TPU v7x, 32 devices: a whole 2x2x4 slice. The times are simulated.
32 devices in a mesh: span: 8 (over z, x), plane: 4 (over y, core).
Axes of the slice: x: 2, y: 2, z: 4, core: 2. Of those that a mesh axis runs over, the one named last changes fastest.
Arguments:
- rhs: float32 [80, 512], P(None, ('span', 'plane')), may hold values from -6 to 6
- blocks: float32 [512, 70400], P(('span', 'plane')), as said below
- columns: int32 [11, 512], P(None, ('span', 'plane')), may hold values from 0 to 511, as said below
- line_slot: int32 [32, 16], P(('span', 'plane')), may hold values from 0 to 15, each once within a row
- line_lower: float32 [512, 6400], P(('span', 'plane')), may hold values from -0.2 to 0.2
- line_upper: float32 [512, 6400], P(('span', 'plane')), may hold values from -0.2 to 0.2
- pivot_inv: float32 [512, 6400], P(('span', 'plane')), as said below
Outputs:
- solution: float32 [80, 512], P(None, ('span', 'plane'))
- residual: float32 [80, 512], P(None, ('span', 'plane'))
Inputs may be any that keep to these rules, and one draw needn't show every extreme that they name: columns[0, i] = i; the other columns name faces on the device itself, on the devices one step along span (wrapping) or one step along plane (not wrapping). Blocks 1 to 4 name faces on the span devices after and before and the plane devices after and before, or on the device itself where no such plane device exists. pivot_inv is a diagonal with entries between about 0.5 and 2.0 plus a full-rank off-diagonal part of small entries. `blocks`: block 0 of every row has an added diagonal of 1 to about 4.06.
All inputs are finite; a program needn't handle non-finite values.
Results may differ from a plain program's by a relative error of at most 0.0065.
Values sent between devices are 32-bit elements; how exact they have to be, the bound alone decides.
No kernel may reach another device: no remote copies, remote signals or barrier semaphores. Data moves between devices by JAX's collectives and lax.ppermute only.
A program may use at most 128 MiB of HBM per device.

v0:
```python
import jax
import jax.numpy as jnp
from jax import lax
from jax.sharding import PartitionSpec as P

ITERS = 3
P_SIZE = 2


HIGH = lax.Precision.HIGHEST


def with_halo(x, sides, width, wrap):
    for axis, dim in sides:
        size, length = (lax.axis_size(axis), x.shape[dim])
        up = [(i, (i + 1) % size) for i in range(size if wrap else size - 1)]
        down = [(j, i) for i, j in up]
        last = lax.slice_in_dim(x, length - width, length, axis=dim)
        first = lax.slice_in_dim(x, 0, width, axis=dim)
        before = lax.ppermute(last, axis, up)
        after = lax.ppermute(first, axis, down)
        x = jnp.concatenate([before, x, after], axis=dim)
    return x


def small_solve(factor, target):
    extent = target.shape[0]
    forward_vals = []
    for row in range(extent):
        running = target[row]
        for inner in range(row):
            running = running - factor[row, inner] * forward_vals[inner]
        forward_vals.append(running / factor[row, row])
    backward_vals = [None] * extent
    for row in reversed(range(extent)):
        running = forward_vals[row]
        for inner in range(row + 1, extent):
            running = running - factor[inner, row] * backward_vals[inner]
        backward_vals[row] = running / factor[row, row]
    return jnp.stack(backward_vals)


def to_sequence(factor_rows, nlines, length, width):
    return jnp.swapaxes(factor_rows.reshape(nlines, length, width, width), 0, 1)


def line_solve(rhs_lines, lseq, useq, pseq):
    rseq = jnp.moveaxis(rhs_lines, 2, 0)

    def forward(prev, items):
        right, low = items
        cur = right - jnp.einsum("mab,bm->am", low, prev, precision=HIGH)
        return (cur, cur)

    start = jnp.zeros(rseq.shape[1:], jnp.float32)
    _, yseq = lax.scan(forward, start, (rseq, lseq))

    def backward(nxt, items):
        yval, upp, piv = items
        inner = yval - jnp.einsum("mab,bm->am", upp, nxt, precision=HIGH)
        cur = jnp.einsum("mab,bm->am", piv, inner, precision=HIGH)
        return (cur, cur)

    _, zseq = lax.scan(backward, start, (yseq, useq, pseq), reverse=True)
    return jnp.moveaxis(zseq, 0, 2)


def on_device(rhs, blocks, columns, line_slot, line_lower, line_upper, pivot_inv):
    width = rhs.shape[0]
    nfaces = rhs.shape[1]
    nblocks = columns.shape[0]
    nspan = lax.axis_size("span")
    nplane = lax.axis_size("plane")
    my_span = lax.axis_index("span")
    my_plane = lax.axis_index("plane")
    device_of = columns // nfaces
    span_of = device_of // nplane
    plane_of = device_of % nplane
    dspan = (span_of - my_span + 1 + nspan) % nspan - 1
    dplane = plane_of - my_plane
    selector = jnp.where(
        dspan == -1,
        1,
        jnp.where(dspan == 1, 2, jnp.where(dplane == -1, 3, jnp.where(dplane == 1, 4, 0))),
    )
    position = selector * nfaces + columns % nfaces
    slot = line_slot[0]
    lines_group = nfaces // P_SIZE
    owned = lines_group // nplane
    length = P_SIZE * nplane
    lower = to_sequence(line_lower, owned, length, width)
    upper = to_sequence(line_upper, owned, length, width)
    pivot = to_sequence(pivot_inv, owned, length, width)
    shaped_blocks = blocks.reshape(nfaces, nblocks, width, width)

    def apply_a(vec):
        shaped = vec.reshape(width, 1, 1, nfaces)
        span_side = with_halo(shaped, (("span", 1),), 1, True)
        plane_side = with_halo(shaped, (("plane", 2),), 1, False)
        below = plane_side[:, 0, 0]
        above = plane_side[:, 0, 2]
        table = jnp.concatenate([vec, span_side[:, 0, 0], span_side[:, 2, 0], below, above], axis=1)
        picked = table[:, position]
        return jnp.einsum("ikab,bki->ai", shaped_blocks, picked, precision=HIGH)

    def apply_m(vec):
        pieces = vec[:, slot].reshape(width, lines_group, P_SIZE)
        whole = lax.all_to_all(pieces, "plane", split_axis=1, concat_axis=2, tiled=True)
        solved = line_solve(whole, lower, upper, pivot)
        every = None
        back = lax.all_to_all(solved, "plane", split_axis=2, concat_axis=1, tiled=True)
        return (jnp.zeros_like(vec).at[:, slot].set(back.reshape(width, nfaces)), every)

    beta = jnp.sqrt(lax.psum(jnp.sum(rhs * rhs), ("span", "plane")) + 1e-06)
    basis = [rhs / beta]
    hcols = []
    for step in range(ITERS):
        precond, lines_held = apply_m(basis[step])
        wvec = apply_a(precond)
        stacked = jnp.stack(basis)
        local_proj = jnp.einsum("jai,ai->j", stacked, wvec, precision=HIGH)
        hvals = lax.psum(local_proj, ("span", "plane"))
        wvec = wvec - jnp.einsum("j,jai->ai", hvals, stacked, precision=HIGH)
        square = lax.psum(jnp.sum(wvec * wvec), ("span", "plane"))
        hnext = jnp.sqrt(square + 1e-06)
        basis.append(wvec / hnext)
        hcols.append(
            jnp.concatenate([hvals, hnext[None], jnp.zeros((ITERS - step - 1,), jnp.float32)])
        )
    hmat = jnp.stack(hcols, axis=1)
    gram_mat = jnp.dot(hmat.T, hmat, precision=HIGH)
    target = beta * hmat[0]
    factor = jnp.linalg.cholesky(gram_mat)
    coef = small_solve(factor, target)
    update = jnp.einsum("j,jai->ai", coef, jnp.stack(basis[:ITERS]), precision=HIGH)
    solution, lines_final = apply_m(update)
    residual = rhs - apply_a(solution)
    return (solution, residual)


def solution(mesh):
    return jax.shard_map(
        on_device,
        mesh=mesh,
        in_specs=(
            P(None, ("span", "plane")),
            P(("span", "plane"), None),
            P(None, ("span", "plane")),
            P(("span", "plane"), None),
            P(("span", "plane"), None),
            P(("span", "plane"), None),
            P(("span", "plane"), None),
        ),
        out_specs=(P(None, ("span", "plane")), P(None, ("span", "plane"))),
        check_vma=False,
    )
```

profile of v0, /device:TPU:0, one launch (start us, length us, event | category | flops | bytes accessed | tf_op | source)
XLA Modules:
  0.0 496.9 jit_solution(17568002625893289630)
XLA Ops:
  2.6 42.2 %psum.49 = f32[]{:T(128)} all-reduce(f32[]{:T(128)} %multiply_reduce_fusion.4), channel_id=1, replica_groups=mesh['span'=8,'plane'=4] {'span','plane'}, use_global_device_ids=true, to_apply=%region_1.2 | all-reduce | flops 1 | bytes 8 | tf_op jit(solution)/shard_map/psum | solution.py:114
  47.4 3.7 all-to-all-start
  59.4 8.6 %while.116 = (s32[]{:T(128)}, f32[80,2]{0,1:T(2,128)S(1)}, f32[8,80,2]{1,2,0:T(2,128)}, f32[8,80,2]{1,2,0:T(2,128)S(1)}, f32[8,2,80,80]{3,2,1,0:T(8,128)S(1)}, /...) while((s32[]{:T(128)}, f32[80,2]{0,1:T(2,128)S(1)}, f32[8,80,2]{1,2,0:T(2,128)}, ...), condition=%wide.region_5.6_spmd, body=%wide.region_4.5_spmd.sunk | while | flops 307363 | bytes 170865 | solution.py:64
  68.0 3.3 all-to-all-start.1
  71.3 8.9 %reshape.115 = f32[16,11,80,80]{3,2,1,0:T(8,128)} reshape(f32[16,70400]{1,0:T(8,128)} %param.24) | data formatting | bytes 9011200 | tf_op jit(solution)/shard_map/reshape | solution.py:94
  88.8 3.4 collective-permute-done.3
  92.9 8.6 %fusion.62 = f32[16,1,80,1]{2,1,3,0:T(1,128)S(1)} fusion(f32[16,11,80,80]{3,2,1,0:T(8,128)} %reshape.115, f32[80,11,16,1]{0,2,1,3:T(8,128)S(1)} %bitcast.517), kind=kOutput, calls=%fused_computation.96 | convolution fusion | flops 13516800 | bytes 4567040 | tf_op jit(solution)/shard_map/ikab,bki->ai/dot_general | solution.py:104
  102.1 38.9 %psum.50 = f32[1]{0:T(128)} all-reduce(f32[1]{0:T(128)} %bitcast.87), channel_id=1, replica_groups=mesh['span'=8,'plane'=4] {'span','plane'}, use_global_device_ids=true, to_apply=%region_7.8 | all-reduce | flops 1 | bytes 8 | tf_op jit(solution)/shard_map/psum | solution.py:122
  142.1 41.8 %psum.51 = f32[]{:T(128)} all-reduce(f32[]{:T(128)} %multiply_reduce_fusion.3), channel_id=1, replica_groups=mesh['span'=8,'plane'=4] {'span','plane'}, use_global_device_ids=true, to_apply=%region_9.10 | all-reduce | flops 1 | bytes 8 | tf_op jit(solution)/shard_map/psum | solution.py:124
  186.3 3.7 all-to-all-start.2
  190.1 3.8 all-to-all-done.2
  196.7 8.6 %while.117 = (s32[]{:T(128)}, f32[80,2]{0,1:T(2,128)S(1)}, f32[8,80,2]{1,2,0:T(2,128)}, f32[8,80,2]{1,2,0:T(2,128)S(1)}, f32[8,2,80,80]{3,2,1,0:T(8,128)S(1)}, /...) while((s32[]{:T(128)}, f32[80,2]{0,1:T(2,128)S(1)}, f32[8,80,2]{1,2,0:T(2,128)}, ...), condition=%wide.region_13.14_spmd, body=%wide.region_12.13_spmd.sunk | while | flops 307363 | bytes 170865 | solution.py:64
  205.3 3.2 all-to-all-start.3
  208.6 3.8 all-to-all-done.3
  214.8 3.0 collective-permute-start.5
  223.0 8.6 %fusion.60 = f32[16,1,80,1]{2,1,3,0:T(1,128)S(1)} fusion(f32[16,11,80,80]{3,2,1,0:T(8,128)} %reshape.115, f32[80,11,16,1]{0,2,1,3:T(8,128)S(1)} %bitcast.518), kind=kOutput, calls=%fused_computation.94 | convolution fusion | flops 13516800 | bytes 4567040 | tf_op jit(solution)/shard_map/ikab,bki->ai/dot_general | solution.py:104
  231.8 37.3 %psum.52 = f32[2]{0:T(128)S(1)} all-reduce(f32[2]{0:T(128)S(1)} %convolution_bitcast_fusion.1), channel_id=1, replica_groups=mesh['span'=8,'plane'=4] {'span','plane'}, use_global_device_ids=true, to_apply=%region_15.16 | all-reduce | flops 2 | bytes 16 | tf_op jit(solution)/shard_map/psum | solution.py:122
  269.9 43.0 %psum.53 = f32[]{:T(128)} all-reduce(f32[]{:T(128)} %get-tuple-element.862), channel_id=1, replica_groups=mesh['span'=8,'plane'=4] {'span','plane'}, use_global_device_ids=true, to_apply=%region_17.18 | all-reduce | flops 1 | bytes 8 | tf_op jit(solution)/shard_map/psum | solution.py:124
  314.8 3.7 all-to-all-start.4
  318.5 3.8 all-to-all-done.4
  325.1 8.6 %while.118 = (s32[]{:T(128)}, f32[80,2]{0,1:T(2,128)S(1)}, f32[8,80,2]{1,2,0:T(2,128)}, f32[8,80,2]{1,2,0:T(2,128)S(1)}, f32[8,2,80,80]{3,2,1,0:T(8,128)S(1)}, /...) while((s32[]{:T(128)}, f32[80,2]{0,1:T(2,128)S(1)}, f32[8,80,2]{1,2,0:T(2,128)}, ...), condition=%wide.region_21.22_spmd, body=%wide.region_20.21_spmd.sunk | while | flops 307363 | bytes 170865 | solution.py:64
  333.8 3.2 all-to-all-start.5
  337.0 3.8 all-to-all-done.5
  343.2 3.0 collective-permute-start.9
  351.5 8.6 %fusion.58 = f32[16,1,80,1]{2,1,3,0:T(1,128)S(1)} fusion(f32[16,11,80,80]{3,2,1,0:T(8,128)} %reshape.115, f32[80,11,16,1]{0,2,1,3:T(8,128)S(1)} %bitcast.519), kind=kOutput, calls=%fused_computation.92 | convolution fusion | flops 13516800 | bytes 4567040 | tf_op jit(solution)/shard_map/ikab,bki->ai/dot_general | solution.py:104
  361.0 37.2 %psum.54 = f32[3]{0:T(128)S(1)} all-reduce(f32[3]{0:T(128)S(1)} %convolution_bitcast_fusion), channel_id=1, replica_groups=mesh['span'=8,'plane'=4] {'span','plane'}, use_global_device_ids=true, to_apply=%region_23.24 | all-reduce | flops 3 | bytes 24 | tf_op jit(solution)/shard_map/psum | solution.py:122
  399.1 43.0 %psum.55 = f32[]{:T(128)} all-reduce(f32[]{:T(128)} %multiply_reduce_fusion.1), channel_id=1, replica_groups=mesh['span'=8,'plane'=4] {'span','plane'}, use_global_device_ids=true, to_apply=%region_25.26 | all-reduce | flops 1 | bytes 8 | tf_op jit(solution)/shard_map/psum | solution.py:124
  456.9 3.7 all-to-all-start.6
  460.6 3.8 all-to-all-done.6
  466.6 4.2 while.119
  470.8 6.2 %all_to_all.132 = f32[80,2,8]{0,1,2:T(2,128)S(1)} all-to-all(f32[80,2,8]{0,1,2:T(2,128)S(1)} %bitcast.580), channel_id=1, replica_groups=mesh['span'=8,'plane'=4] {'plane'}, dimensions={2} | all-to-all | bytes 10240 | tf_op jit(solution)/shard_map/all_to_all | solution.py:111
  487.7 8.6 %fusion.56 = f32[16,1,80,1]{2,1,3,0:T(1,128)S(1)} fusion(f32[16,11,80,80]{3,2,1,0:T(8,128)} %reshape.115, f32[80,11,16,1]{0,2,1,3:T(8,128)S(1)} %bitcast.516), kind=kOutput, calls=%fused_computation.90 | convolution fusion | flops 13516800 | bytes 4567040 | tf_op jit(solution)/shard_map/ikab,bki->ai/dot_general | solution.py:104
  (363 shorter events, 105.9 us)
Async XLA Ops:
  47.4 9.2 %all-to-all-start = ((f32[80,8,2]{0,2,1:T(2,128)}), f32[80,8,2]{0,2,1:T(2,128)S(1)}, u32[]{:S(2)}, u32[]{:S(2)}) async-start(f32[80,8,2]{0,2,1:T(2,128)} %bitcast.63), calls=%async_computation | async-start | bytes 16384 | tf_op jit(solution)/shard_map/all_to_all | solution.py:108
  68.0 12.2 %all-to-all-start.1 = ((f32[80,2,8]{0,1,2:T(2,128)}), f32[80,2,8]{0,1,2:T(2,128)S(1)}, u32[]{:S(2)}, u32[]{:S(2)}) async-start(f32[80,2,8]{0,1,2:T(2,128)} %bitcast.71), calls=%async_computation.1 | async-start | bytes 16384 | tf_op jit(solution)/shard_map/all_to_all | solution.py:111
  80.2 21.3 %copy-start = (f32[80,16]{0,1:T(8,128)S(1)}, f32[80,16]{0,1:T(8,128)}, u32[]{:S(2)}) copy-start(f32[80,16]{0,1:T(8,128)} %param.23) | copy-start | bytes 15364
  80.8 7.9 %collective-permute-start = (f32[80,1,1,16]{0,3,2,1:T(8,128)S(1)}, f32[80,1,1,16]{0,3,2,1:T(8,128)S(1)}, u32[]{:S(2)}, u32[]{:S(2)}) collective-permute-start(f32[80,1,1,16]{0,3,2,1:T(8,128)S(1)} %bitcast.562), channel_id=1, source_target_pairs={{0,4},{4,8},{8,12},{12,16},{16,20},{20,24},{24,28},{28,0},{1,5},{5... | collective-permute-start | bytes 15368 | tf_op jit(solution)/shard_map/ppermute | solution.py:20
  82.6 6.1 %collective-permute-start.1 = (f32[80,1,1,16]{0,3,2,1:T(8,128)S(1)}, f32[80,1,1,16]{0,3,2,1:T(8,128)S(1)}, u32[]{:S(2)}, u32[]{:S(2)}) collective-permute-start(f32[80,1,1,16]{0,3,2,1:T(8,128)S(1)} %bitcast.563), channel_id=1, source_target_pairs={{4,0},{8,4},{12,8},{16,12},{20,16},{24,20},{28,24},{0,28},{5,1},{9... | collective-permute-start | bytes 15368 | tf_op jit(solution)/shard_map/ppermute | solution.py:21
  85.6 3.2 collective-permute-start.2
  87.4 4.8 collective-permute-start.3
  186.3 7.6 %all-to-all-start.2 = ((f32[80,8,2]{0,2,1:T(2,128)}), f32[80,8,2]{0,2,1:T(2,128)S(1)}, u32[]{:S(2)}, u32[]{:S(2)}) async-start(f32[80,8,2]{0,2,1:T(2,128)} %bitcast.96), calls=%async_computation.2 | async-start | bytes 16384 | tf_op jit(solution)/shard_map/all_to_all | solution.py:108
  205.3 7.0 %all-to-all-start.3 = ((f32[80,2,8]{0,1,2:T(2,128)}), f32[80,2,8]{0,1,2:T(2,128)S(1)}, u32[]{:S(2)}, u32[]{:S(2)}) async-start(f32[80,2,8]{0,1,2:T(2,128)} %bitcast.101), calls=%async_computation.3 | async-start | bytes 16384 | tf_op jit(solution)/shard_map/all_to_all | solution.py:111
  213.0 7.5 %collective-permute-start.4 = (f32[80,1,1,16]{0,3,2,1:T(8,128)S(1)}, f32[80,1,1,16]{0,3,2,1:T(8,128)S(1)}, u32[]{:S(2)}, u32[]{:S(2)}) collective-permute-start(f32[80,1,1,16]{0,3,2,1:T(8,128)S(1)} %bitcast.566), channel_id=1, source_target_pairs={{0,4},{4,8},{8,12},{12,16},{16,20},{20,24},{24,28},{28,0},{1,5},{5... | collective-permute-start | bytes 15368 | tf_op jit(solution)/shard_map/ppermute | solution.py:20
  214.8 5.8 %collective-permute-start.5 = (f32[80,1,1,16]{0,3,2,1:T(8,128)S(1)}, f32[80,1,1,16]{0,3,2,1:T(8,128)S(1)}, u32[]{:S(2)}, u32[]{:S(2)}) collective-permute-start(f32[80,1,1,16]{0,3,2,1:T(8,128)S(1)} %bitcast.567), channel_id=1, source_target_pairs={{4,0},{8,4},{12,8},{16,12},{20,16},{24,20},{28,24},{0,28},{5,1},{9... | collective-permute-start | bytes 15368 | tf_op jit(solution)/shard_map/ppermute | solution.py:21
  217.7 2.8 collective-permute-start.6
  219.0 3.3 collective-permute-start.7
  314.8 7.6 %all-to-all-start.4 = ((f32[80,8,2]{0,2,1:T(2,128)}), f32[80,8,2]{0,2,1:T(2,128)S(1)}, u32[]{:S(2)}, u32[]{:S(2)}) async-start(f32[80,8,2]{0,2,1:T(2,128)} %bitcast.128), calls=%async_computation.4 | async-start | bytes 16384 | tf_op jit(solution)/shard_map/all_to_all | solution.py:108
  333.8 7.0 %all-to-all-start.5 = ((f32[80,2,8]{0,1,2:T(2,128)}), f32[80,2,8]{0,1,2:T(2,128)S(1)}, u32[]{:S(2)}, u32[]{:S(2)}) async-start(f32[80,2,8]{0,1,2:T(2,128)} %bitcast.133), calls=%async_computation.5 | async-start | bytes 16384 | tf_op jit(solution)/shard_map/all_to_all | solution.py:111
  341.4 7.4 %collective-permute-start.8 = (f32[80,1,1,16]{0,3,2,1:T(8,128)S(1)}, f32[80,1,1,16]{0,3,2,1:T(8,128)S(1)}, u32[]{:S(2)}, u32[]{:S(2)}) collective-permute-start(f32[80,1,1,16]{0,3,2,1:T(8,128)S(1)} %bitcast.570), channel_id=1, source_target_pairs={{0,4},{4,8},{8,12},{12,16},{16,20},{20,24},{24,28},{28,0},{1,5},{5... | collective-permute-start | bytes 15368 | tf_op jit(solution)/shard_map/ppermute | solution.py:20
  343.2 5.6 %collective-permute-start.9 = (f32[80,1,1,16]{0,3,2,1:T(8,128)S(1)}, f32[80,1,1,16]{0,3,2,1:T(8,128)S(1)}, u32[]{:S(2)}, u32[]{:S(2)}) collective-permute-start(f32[80,1,1,16]{0,3,2,1:T(8,128)S(1)} %bitcast.571), channel_id=1, source_target_pairs={{4,0},{8,4},{12,8},{16,12},{20,16},{24,20},{28,24},{0,28},{5,1},{9... | collective-permute-start | bytes 15368 | tf_op jit(solution)/shard_map/ppermute | solution.py:21
  346.2 2.6 collective-permute-start.10
  347.5 3.3 collective-permute-start.11
  456.9 7.5 %all-to-all-start.6 = ((f32[80,8,2]{0,2,1:T(2,128)}), f32[80,8,2]{0,2,1:T(2,128)S(1)}, u32[]{:S(2)}, u32[]{:S(2)}) async-start(f32[80,8,2]{0,2,1:T(2,128)} %bitcast.174), calls=%async_computation.6 | async-start | bytes 16384 | tf_op jit(solution)/shard_map/all_to_all | solution.py:108
  477.6 19.3 %copy-start.1 = (f32[80,16]{0,1:T(8,128)}, f32[80,16]{0,1:T(8,128)S(1)}, u32[]{:S(2)}) copy-start(f32[80,16]{0,1:T(8,128)S(1)} %scatter_custom_fusion.3) | copy-start | bytes 15364
  477.6 7.6 %collective-permute-start.12 = (f32[80,1,1,16]{0,3,2,1:T(8,128)S(1)}, f32[80,1,1,16]{0,3,2,1:T(8,128)S(1)}, u32[]{:S(2)}, u32[]{:S(2)}) collective-permute-start(f32[80,1,1,16]{0,3,2,1:T(8,128)S(1)} %bitcast.557), channel_id=1, source_target_pairs={{0,4},{4,8},{8,12},{12,16},{16,20},{20,24},{24,28},{28,0},{1,5},{5... | collective-permute-start | bytes 15368 | tf_op jit(solution)/shard_map/ppermute | solution.py:20
  479.4 5.8 %collective-permute-start.13 = (f32[80,1,1,16]{0,3,2,1:T(8,128)S(1)}, f32[80,1,1,16]{0,3,2,1:T(8,128)S(1)}, u32[]{:S(2)}, u32[]{:S(2)}) collective-permute-start(f32[80,1,1,16]{0,3,2,1:T(8,128)S(1)} %bitcast.558), channel_id=1, source_target_pairs={{4,0},{8,4},{12,8},{16,12},{20,16},{24,20},{28,24},{0,28},{5,1},{9... | collective-permute-start | bytes 15368 | tf_op jit(solution)/shard_map/ppermute | solution.py:21
  482.4 2.9 collective-permute-start.14
  483.7 3.3 collective-permute-start.15
where the time goes:
time: 501 us; the launch traced here: 497 us
  blocking collectives  290 us (58%)
  matrix products  58.7 us (12%)
  starting transfers between devices  55.1 us (11%)
  local copies, waits for them, and re-layouts  40.8 us (8%)
  waiting for transfers between devices  27.9 us (6%)
  between operations  13.5 us (3%)
  other arithmetic  10.9 us (2%)
    psum x3, blocking collectives, on_device(): square = lax.psum(jnp.sum(wvec * wvec), ('span', 'plane'))  128 us
    psum x3, blocking collectives, on_device(): hvals = lax.psum(local_proj, ('span', 'plane'))  113 us
    psum x1, blocking collectives, on_device(): beta = jnp.sqrt(lax.psum(jnp.sum(rhs * rhs), ('span', 'plane')) + 1e-06)  42.2 us
    dot_general x4, matrix products, apply_a(): return jnp.einsum('ikab,bki->ai', shaped_blocks, picked, precision=HIGH)  34.2 us
    ppermute x8, starting transfers between devices, with_halo(): after = lax.ppermute(first, axis, down)  17.4 us
    all_to_all x4, starting transfers between devices, apply_m(): lax.all_to_all(pieces, 'plane', split_axis=1, concat_axis=2, tiled=True)  14.9 us
    dynamic_update_slice x32, local copies, waits for them, and re-layouts, line_solve(): _, yseq = lax.scan(forward, start, (rseq, lseq))  14.1 us
    ppermute x8, starting transfers between devices, with_halo(): before = lax.ppermute(last, axis, up)  12.9 us
  transfers between devices with their start and end apart: 23, of which 9 were waited for; matrix products, arithmetic and copies ran while one was open for 3% of the time, Pallas kernels for 0%

commit v1 on v0

v1 whole, which is shorter than its diff:
```python
import functools
import math

import jax
import jax.numpy as jnp
import numpy as np
from jax import lax
from jax.experimental import pallas as pl
from jax.experimental.pallas import tpu as pltpu
from jax.sharding import PartitionSpec as P

ITERS = 3
P_SIZE = 2
SHIFT = 2.0
EPS = 1e-6
VMEM_LIMIT = 16 * 1024 * 1024
HIGH = lax.Precision.HIGHEST
F32, BF16 = jnp.float32, jnp.bfloat16


def with_halo(x, sides, width, wrap):
    for axis, dim in sides:
        size, length = (lax.axis_size(axis), x.shape[dim])
        up = [(i, (i + 1) % size) for i in range(size if wrap else size - 1)]
        down = [(j, i) for i, j in up]
        last = lax.slice_in_dim(x, length - width, length, axis=dim)
        first = lax.slice_in_dim(x, 0, width, axis=dim)
        before = lax.ppermute(last, axis, up)
        after = lax.ppermute(first, axis, down)
        x = jnp.concatenate([before, x, after], axis=dim)
    return x


def small_solve(factor, target):
    extent = target.shape[0]
    forward_vals = []
    for row in range(extent):
        running = target[row]
        for inner in range(row):
            running = running - factor[row, inner] * forward_vals[inner]
        forward_vals.append(running / factor[row, row])
    backward_vals = [None] * extent
    for row in reversed(range(extent)):
        running = forward_vals[row]
        for inner in range(row + 1, extent):
            running = running - factor[inner, row] * backward_vals[inner]
        backward_vals[row] = running / factor[row, row]
    return jnp.stack(backward_vals)


def to_sequence(factor_rows, nlines, length, width):
    return jnp.swapaxes(factor_rows.reshape(nlines, length, width, width), 0, 1)


def line_solve(rhs_lines, lseq, useq, pseq):
    rseq = jnp.moveaxis(rhs_lines, 2, 0)

    def forward(prev, items):
        right, low = items
        cur = right - jnp.einsum("mab,bm->am", low, prev, precision=HIGH)
        return (cur, cur)

    start = jnp.zeros(rseq.shape[1:], F32)
    _, yseq = lax.scan(forward, start, (rseq, lseq))

    def backward(nxt, items):
        yval, upp, piv = items
        inner = yval - jnp.einsum("mab,bm->am", upp, nxt, precision=HIGH)
        cur = jnp.einsum("mab,bm->am", piv, inner, precision=HIGH)
        return (cur, cur)

    _, zseq = lax.scan(backward, start, (yseq, useq, pseq), reverse=True)
    return jnp.moveaxis(zseq, 0, 2)


def table_positions(columns, nfaces):
    nspan, nplane = lax.axis_size("span"), lax.axis_size("plane")
    my_span, my_plane = lax.axis_index("span"), lax.axis_index("plane")
    device_of = columns // nfaces
    span_of = device_of // nplane
    plane_of = device_of % nplane
    dspan = (span_of - my_span + 1 + nspan) % nspan - 1
    dplane = plane_of - my_plane
    selector = jnp.where(
        dspan == -1,
        1,
        jnp.where(dspan == 1, 2, jnp.where(dplane == -1, 3, jnp.where(dplane == 1, 4, 0))),
    )
    return selector * nfaces + columns % nfaces


def step_by_step(rhs, blocks, columns, line_slot, line_lower, line_upper, pivot_inv):
    width, nfaces = rhs.shape
    nblocks = columns.shape[0]
    nplane = lax.axis_size("plane")
    position = table_positions(columns, nfaces)
    slot = line_slot[0]
    lines_group = nfaces // P_SIZE
    owned = lines_group // nplane
    length = P_SIZE * nplane
    lower = to_sequence(line_lower, owned, length, width)
    upper = to_sequence(line_upper, owned, length, width)
    pivot = to_sequence(pivot_inv, owned, length, width)
    shaped_blocks = blocks.reshape(nfaces, nblocks, width, width)

    def apply_a(vec):
        shaped = vec.reshape(width, 1, 1, nfaces)
        span_side = with_halo(shaped, (("span", 1),), 1, True)
        plane_side = with_halo(shaped, (("plane", 2),), 1, False)
        below = plane_side[:, 0, 0]
        above = plane_side[:, 0, 2]
        table = jnp.concatenate([vec, span_side[:, 0, 0], span_side[:, 2, 0], below, above], axis=1)
        return jnp.einsum("ikab,bki->ai", shaped_blocks, table[:, position], precision=HIGH)

    def apply_m(vec):
        pieces = vec[:, slot].reshape(width, lines_group, P_SIZE)
        whole = lax.all_to_all(pieces, "plane", split_axis=1, concat_axis=2, tiled=True)
        solved = line_solve(whole, lower, upper, pivot)
        back = lax.all_to_all(solved, "plane", split_axis=2, concat_axis=1, tiled=True)
        return jnp.zeros_like(vec).at[:, slot].set(back.reshape(width, nfaces))

    beta = jnp.sqrt(lax.psum(jnp.sum(rhs * rhs), ("span", "plane")) + EPS)
    basis = [rhs / beta]
    hcols = []
    for step in range(ITERS):
        wvec = apply_a(apply_m(basis[step]))
        stacked = jnp.stack(basis)
        hvals = lax.psum(jnp.einsum("jai,ai->j", stacked, wvec, precision=HIGH), ("span", "plane"))
        wvec = wvec - jnp.einsum("j,jai->ai", hvals, stacked, precision=HIGH)
        hnext = jnp.sqrt(lax.psum(jnp.sum(wvec * wvec), ("span", "plane")) + EPS)
        basis.append(wvec / hnext)
        hcols.append(jnp.concatenate([hvals, hnext[None], jnp.zeros((ITERS - step - 1,), F32)]))
    hmat = jnp.stack(hcols, axis=1)
    factor = jnp.linalg.cholesky(jnp.dot(hmat.T, hmat, precision=HIGH))
    coef = small_solve(factor, beta * hmat[0])
    update = jnp.einsum("j,jai->ai", coef, jnp.stack(basis[:ITERS]), precision=HIGH)
    solution = apply_m(update)
    return solution, rhs - apply_a(solution)


def partner(me, k, size):
    if size & (size - 1) == 0:
        return me ^ k, me ^ k
    return (me + k) % size, (me + size - k) % size


def exchange(x, axis, k):
    size = lax.axis_size(axis)
    return lax.ppermute(x, axis, [(i, partner(i, k, size)[0]) for i in range(size)])


def start_kernel(nplane, me_ref, slot_ref, u_ref, tail_ref, *outs):
    per = slot_ref.shape[1] // nplane
    for k in range(nplane):
        to, _ = partner(me_ref[0], k, nplane)
        for i in range(per):
            outs[k][pl.ds(i, 1), :] = u_ref[pl.ds(slot_ref[0, to * per + i], 1), :]
        outs[k][pl.ds(per, 1), :] = tail_ref[...]


def line_kernel(nplane, nlines, me_ref, *refs):
    msgs, (low, low_t, upp, piv_t, z_ref, r_scr) = refs[:nplane], refs[nplane:]
    width = z_ref.shape[1]
    length = z_ref.shape[0] // nlines
    for k in range(nplane):
        _, source = partner(me_ref[0], k, nplane)
        for m in range(nlines):
            for q in range(P_SIZE):
                r_scr[m, pl.ds(source * P_SIZE + q, 1), :] = msgs[k][pl.ds(m * P_SIZE + q, 1), :]
    eye = lax.broadcasted_iota(jnp.int32, (width, width), 0) == lax.broadcasted_iota(jnp.int32, (width, width), 1)

    def column(row):
        return jnp.sum(jnp.where(eye, row, 0.0), axis=1, keepdims=True)

    rows = [[r_scr[m, pl.ds(j, 1), :] for m in range(nlines)] for j in range(length)]
    y_cols = [[None] * nlines for _ in range(length)]
    carry = [None] * nlines
    for j in range(length):
        for m in range(nlines):
            at = m * length + j
            if j == 0:
                carry[m] = rows[j][m]
            elif j % 2:
                carry[m] = column(rows[j][m]) - jnp.sum(low[at] * carry[m], axis=1, keepdims=True)
            else:
                carry[m] = rows[j][m] - jnp.sum(low_t[at] * carry[m], axis=0, keepdims=True)
            y_cols[j][m] = carry[m] if j % 2 else column(carry[m])
    after = [None] * nlines
    for j in reversed(range(length)):
        for m in range(nlines):
            at = m * length + j
            inner = y_cols[j][m]
            if j < length - 1:
                inner = inner - jnp.sum(upp[at] * after[m], axis=1, keepdims=True)
            after[m] = jnp.sum(piv_t[at] * inner, axis=0, keepdims=True)
            z_ref[pl.ds(at, 1), :] = after[m]


def faces_kernel(nplane, nlines, me_ref, slots_ref, *refs):
    solved, (mine_ref, sides_ref) = refs[:nplane], refs[nplane:]
    nfaces = mine_ref.shape[0]
    length = nfaces // nlines
    per = nlines * P_SIZE
    me = me_ref[0]
    for side, dplane in enumerate((0, -1, 1)):
        there = me + dplane
        safe = jnp.clip(there, 0, nplane - 1)
        for k in range(nplane):
            _, owner = partner(me, k, nplane)
            for i in range(per):
                face = slots_ref[safe, owner * per + i]
                row = solved[k][pl.ds((i // P_SIZE) * length + safe * P_SIZE + i % P_SIZE, 1), :]
                if side == 0:
                    mine_ref[pl.ds(face, 1), :] = row
                else:
                    sides_ref[pl.ds((side - 1) * nfaces + face, 1), :] = row


def apply_kernel(nplane, last, *refs):
    (me_ref, slot_ref, blocks, pick, seg, mine, before, after, sides), refs = refs[:9], refs[9:]
    nold = ITERS if last else 1
    olds, refs = refs[:nold], refs[nold:]
    next_ref, refs = refs[0], refs[1:]
    nfaces, width = mine.shape
    area = width * width
    nblocks = blocks.shape[1] // area
    chunk = seg.shape[0]
    copies = chunk // width
    table = jnp.concatenate([mine[...], before[...], after[...], sides[...]], axis=0)
    high = table.astype(BF16).astype(F32)
    both = jnp.concatenate([high, table - high], axis=0)
    wide = jnp.concatenate([both] * copies, axis=1).astype(BF16)
    x_scr = refs[-1]
    x_scr[...] = jnp.dot(pick[...], wide, preferred_element_type=F32)
    masks = lax.broadcasted_iota(jnp.int32, (nfaces, seg.shape[1]), 1) // copies
    total = jnp.zeros((nfaces, seg.shape[1]), F32)
    parts = []
    for c in range(area // chunk):
        acc = None
        for k in range(nblocks):
            at = k * area + c * chunk
            term = blocks[:, at : at + chunk] * x_scr[k * nfaces : (k + 1) * nfaces, :]
            acc = term if acc is None else acc + term
        acc_high = acc.astype(BF16)
        parts += [acc_high, (acc - acc_high.astype(F32)).astype(BF16)]
    sums = jnp.dot(jnp.concatenate(parts, axis=0), seg[...], preferred_element_type=F32)
    for c in range(area // chunk):
        pair = sums[2 * c * nfaces : (2 * c + 1) * nfaces] + sums[(2 * c + 1) * nfaces : (2 * c + 2) * nfaces]
        total = total + jnp.where(masks == c, pair, 0.0)
    u_next = total[:, :width] - SHIFT * olds[-1][...]
    next_ref[...] = u_next
    if last:
        gram_ref = refs[0]
        basis = [old[...] for old in olds] + [u_next]
        row = 0
        for i in range(ITERS + 1):
            for j in range(i, ITERS + 1):
                value = jnp.sum(jnp.sum(basis[i] * basis[j], axis=1, keepdims=True), axis=0, keepdims=True)
                gram_ref[pl.ds(row, 1), :] = jnp.broadcast_to(value, (1, gram_ref.shape[1]))
                row += 1
    else:
        outs = refs[:nplane]
        per = nfaces // nplane
        for k in range(nplane):
            to, _ = partner(me_ref[0], k, nplane)
            for i in range(per):
                outs[k][pl.ds(i, 1), :] = next_ref[pl.ds(slot_ref[0, to * per + i], 1), :]


def finish_kernel(gram_ref, *refs):
    us, zs = refs[: ITERS + 1], refs[ITERS + 1 : 2 * ITERS + 1]
    sol_ref, res_ref, ok_ref = refs[2 * ITERS + 1 :]
    width = sol_ref.shape[1]
    gram, row = {}, 0
    for i in range(ITERS + 1):
        for j in range(i, ITERS + 1):
            gram[i, j] = gram[j, i] = gram_ref[pl.ds(row, 1), :]
            row += 1
    largest = functools.reduce(jnp.maximum, [jnp.abs(g) for g in gram.values()])
    ok = largest < 1e30
    beta = jnp.sqrt(gram[0, 0] + EPS)
    basis = [[1.0 / beta]]
    hmat = {}
    for step in range(ITERS):
        own = basis[step]
        wvec = [SHIFT * own[0]] + [own[i] + SHIFT * own[i + 1] for i in range(step)] + [own[step]]
        images = [sum(gram[i, j] * wvec[j] for j in range(step + 2)) for i in range(step + 1)]
        for i in range(step + 1):
            hmat[i, step] = sum(basis[i][m] * images[m] for m in range(i + 1))
        for i in range(step + 1):
            for m in range(i + 1):
                wvec[m] = wvec[m] - hmat[i, step] * basis[i][m]
        terms = [wvec[i] * wvec[j] * gram[i, j] for i in range(step + 2) for j in range(step + 2)]
        square = jnp.maximum(sum(terms), 0.0)
        ok = ok & (square + EPS >= 2e-3 * sum(jnp.abs(term) for term in terms))
        hmat[step + 1, step] = jnp.sqrt(square + EPS)
        scale = 1.0 / hmat[step + 1, step]
        basis.append([w * scale for w in wvec])
    normal = {
        (i, j): sum(hmat[m, i] * hmat[m, j] for m in range(j + 2) if (m, i) in hmat and (m, j) in hmat)
        for i in range(ITERS)
        for j in range(i + 1)
    }
    factor, inverse = {}, []
    for j in range(ITERS):
        diag = jnp.sqrt(normal[j, j] - sum(factor[j, m] * factor[j, m] for m in range(j)))
        inverse.append(1.0 / diag)
        for i in range(j + 1, ITERS):
            factor[i, j] = (normal[i, j] - sum(factor[i, m] * factor[j, m] for m in range(j))) * inverse[j]
    forward = []
    for i in range(ITERS):
        forward.append((beta * hmat[0, i] - sum(factor[i, m] * forward[m] for m in range(i))) * inverse[i])
    coef = [None] * ITERS
    for i in reversed(range(ITERS)):
        coef[i] = (forward[i] - sum(factor[m, i] * coef[m] for m in range(i + 1, ITERS))) * inverse[i]
    mix = [sum(coef[s] * basis[s][m] for s in range(m, ITERS))[:, :width] for m in range(ITERS)]
    sol_ref[...] = sum(mix[m] * zs[m][...] for m in range(ITERS))
    image = sum(mix[m] * (us[m + 1][...] + SHIFT * us[m][...]) for m in range(ITERS))
    res_ref[...] = us[0][...] - image
    ok = ok & (functools.reduce(jnp.maximum, [jnp.abs(c) for c in coef]) < 1e30)
    ok_ref[...] = jnp.where(ok, 1.0, 0.0)


def call(kernel, args, outs, scratch=(), flops=0, pinned=True):
    spaces = [pltpu.SMEM if x.dtype == jnp.int32 else pltpu.VMEM for x in args]
    args = [x if s is pltpu.SMEM else pltpu.with_memory_space_constraint(x, s) for x, s in zip(args, spaces)]
    size = sum(4 * math.prod(x.shape) for x in args)
    return pl.pallas_call(
        kernel,
        out_shape=[pltpu.VMEM(shape, F32) if pinned else jax.ShapeDtypeStruct(shape, F32) for shape in outs],
        in_specs=[pl.BlockSpec(memory_space=s) for s in spaces],
        out_specs=[pl.BlockSpec(memory_space=pltpu.VMEM) for _ in outs],
        scratch_shapes=scratch,
        compiler_params=pltpu.CompilerParams(vmem_limit_bytes=VMEM_LIMIT),
        cost_estimate=pl.CostEstimate(flops=flops, bytes_accessed=size, transcendentals=0),
    )(*args)


def add_up(x, axis):
    size = lax.axis_size(axis)
    if size & (size - 1):
        return lax.psum(x, axis)
    step = 1
    while step < size:
        x = x + exchange(x, axis, step)
        step *= 2
    return x


def on_device(rhs, blocks, columns, line_slot, line_lower, line_upper, pivot_inv):
    width, nfaces = rhs.shape
    nblocks = columns.shape[0]
    nspan, nplane = lax.axis_size("span"), lax.axis_size("plane")
    owned = nfaces // P_SIZE // nplane
    length = P_SIZE * nplane
    per = owned * P_SIZE
    me = lax.axis_index("plane").astype(jnp.int32)[None]
    shape = (nfaces, width)

    position = table_positions(columns, nfaces).reshape(nblocks * nfaces, 1)
    places = 5 * nfaces
    pick = (lax.broadcasted_iota(jnp.int32, (1, 2 * places), 1) % places == position).astype(BF16)
    chunk = math.lcm(width, 128)
    seg = (np.arange(chunk)[:, None] // width == np.arange(128)[None, :] % (chunk // width)).astype(np.float32)
    seg = jnp.asarray(seg, BF16)
    low = line_lower.reshape(nfaces, width, width)
    low_t = jnp.swapaxes(low, 1, 2)
    upp = line_upper.reshape(nfaces, width, width)
    piv_t = jnp.swapaxes(pivot_inv.reshape(nfaces, width, width), 1, 2)

    us = [rhs.T]
    zs = []
    tail = jnp.pad(line_slot.astype(F32), ((0, 0), (0, width - nfaces)))
    send = call(
        functools.partial(start_kernel, nplane), [me, line_slot, us[0], tail], [(per + 1, width)] * nplane
    )
    up = [(i, (i + 1) % nspan) for i in range(nspan)]
    down = [(j, i) for i, j in up]
    slots = None
    for step in range(ITERS):
        got = [send[0]] + [exchange(send[k], "plane", k) for k in range(1, nplane)]
        if step == 0:
            owners = jnp.stack([partner(me[0], k, nplane)[1] for k in range(nplane)])
            known = jnp.concatenate([g[per:, :nfaces] for g in got], axis=0).astype(jnp.int32)
            slots = jnp.sum(
                jnp.where(owners[None, :, None] == jnp.arange(nplane)[:, None, None], known[None], 0), axis=1
            ).astype(jnp.int32)
        (solved,) = call(
            functools.partial(line_kernel, nplane, owned),
            [me, *got, low, low_t, upp, piv_t],
            [shape],
            [pltpu.VMEM((owned, length, width), F32)],
            flops=6 * nfaces * width * width,
        )
        pieces = [solved] + [exchange(solved, "plane", k) for k in range(1, nplane)]
        mine, sides = call(
            functools.partial(faces_kernel, nplane, owned), [me, slots, *pieces], [shape, (2 * nfaces, width)]
        )
        zs.append(mine)
        before = lax.ppermute(mine, "span", up)
        after = lax.ppermute(mine, "span", down)
        last = step == ITERS - 1
        out = call(
            functools.partial(apply_kernel, nplane, last),
            [me, line_slot, blocks, pick, seg, mine, before, after, sides, *(us if last else us[-1:])],
            [shape] + ([(16, 128)] if last else [(per, width)] * nplane),
            [pltpu.VMEM((nblocks * nfaces, chunk), F32)],
            flops=2 * nblocks * nfaces * width * width,
        )
        us.append(out[0])
        send = out[1:]
    gram = add_up(add_up(send[0], "plane"), "span")
    sol, res, ok = call(finish_kernel, [gram, *us, *zs], [shape, shape, (1, 128)], pinned=False)
    return lax.cond(
        ok[0, 0] > 0.5,
        lambda *_: (sol.T, res.T),
        step_by_step,
        rhs, blocks, columns, line_slot, line_lower, line_upper, pivot_inv,
    )


def solution(mesh):
    both = ("span", "plane")
    return jax.shard_map(
        on_device,
        mesh=mesh,
        in_specs=(
            P(None, both),
            P(both, None),
            P(None, both),
            P(both, None),
            P(both, None),
            P(both, None),
            P(both, None),
        ),
        out_specs=(P(None, both), P(None, both)),
        check_vma=False,
    )
```

time: 501 us -> 87.1 us (0.17)
  blocking collectives: 290 us -> 0 us
  matrix products: 58.7 us -> 0 us
  local copies, waits for them, and re-layouts: 40.8 us -> 6.95 us
  starting transfers between devices: 55.1 us -> 30.2 us
  Pallas kernels: 0 us -> 15.9 us
  between operations: 13.5 us -> 0.92 us
  other arithmetic: 10.9 us -> 1.73 us
    psum x7 -> x0, blocking collectives: 283 us -> none  [the longest x3 128 us: on_device(): square = lax.psum(jnp.sum(wvec * wvec), ('span', 'plane'))]
    dot_general x106 -> x0, matrix products: 58.7 us -> none  [the longest x4 34.2 us: apply_a(): return jnp.einsum('ikab,bki->ai', shaped_blocks, picked, precision=HIGH)]
    all_to_all x7 -> x0, starting transfers between devices: 24.7 us -> none  [the longest x4 14.9 us: apply_m(): lax.all_to_all(pieces, 'plane', split_axis=1, concat_axis=2, tiled=True)]
    ppermute x16 -> x29, waiting for transfers between devices: 8.92 us -> 30.9 us  [the longest x23 26.3 us: exchange(): lax.ppermute(x, axis, [(i, partner(i, k, size)[0]) for i in range(size)])]
    all_to_all x7 -> x0, waiting for transfers between devices: 19 us -> none  [the longest x4 11.4 us: apply_m(): lax.all_to_all(pieces, 'plane', split_axis=1, concat_axis=2, tiled=True)]
    pallas_call x0 -> x11, Pallas kernels: none -> 15.9 us  [call(): pl.pallas_call(kernel, out_shape=[pltpu.VMEM(shape, F32) if pinned else j...]
    dynamic_update_slice x32 -> x0, local copies, waits for them, and re-layouts: 14.1 us -> none  [line_solve(): _, yseq = lax.scan(forward, start, (rseq, lseq))]
    reshape x4 -> x5, local copies, waits for them, and re-layouts: 13.4 us -> 4.93 us  [the longest x2 1.72 us: on_device(): piv_t = jnp.swapaxes(pivot_inv.reshape(nfaces, width, width), 1, 2)]
  transfers between devices with their start and end apart: 23 -> 29, of which waited for: 9 -> 17; matrix products, arithmetic and copies ran while one was open for 3% -> 7% of each run, Pallas kernels for 0% -> 0%
where the time goes in v1:
time: 87.1 us; the launch traced here: 86.6 us
  waiting for transfers between devices  30.9 us (35%)
  starting transfers between devices  30.2 us (35%)
  Pallas kernels  15.9 us (18%)
  local copies, waits for them, and re-layouts  6.95 us (8%)
  other arithmetic  1.73 us (2%)
  between operations  0.92 us (1%)
    ppermute x23, waiting for transfers between devices, exchange(): lax.ppermute(x, axis, [(i, partner(i, k, size)[0]) for i in range(size)])  26.3 us
    pallas_call x11, Pallas kernels, call(): pl.pallas_call(kernel, out_shape=[pltpu.VMEM(shape, F32) if pinned else j...  15.9 us
    ppermute x23, starting transfers between devices, exchange(): lax.ppermute(x, axis, [(i, partner(i, k, size)[0]) for i in range(size)])  15.7 us
    ppermute x3, starting transfers between devices, on_device(): after = lax.ppermute(mine, 'span', down)  11.4 us
    ppermute x3, waiting for transfers between devices, on_device(): before = lax.ppermute(mine, 'span', up)  4.66 us
    ppermute x3, starting transfers between devices, on_device(): before = lax.ppermute(mine, 'span', up)  3.07 us
  transfers between devices with their start and end apart: 29, of which 17 were waited for; matrix products, arithmetic and copies ran while one was open for 7% of the time, Pallas kernels for 0%

profile of v1, /device:TPU:0, one launch (start us, length us, event | category | flops | bytes accessed | tf_op | source)
XLA Modules:
  0.0 86.6 jit_solution(4913671386849157816)
XLA Ops:
  3.4 2.6 %collective-permute-start.17 = (f32[5,80]{1,0:T(8,128)S(1)}, f32[5,80]{1,0:T(8,128)S(1)}, u32[]{:S(2)}, u32[]{:S(2)}) collective-permute-start(f32[5,80]{1,0:T(8,128)S(1)} %get-tuple-element.652), channel_id=1, source_target_pairs={{0,2},{1,3},{2,0},{3,1},{4,6},{5,7},{6,4},{7,5},{8,10},{9,11},{10,... | collective-permute-start | bytes 4808 | tf_op jit(solution)/shard_map/ppermute | solution.py:149
  6.9 1.5 %reshape.190.refs_4_ = f32[16,80,80]{2,1,0:T(8,128)S(1)} reshape(f32[16,6400]{1,0:T(8,128)} %param.30) | data formatting | bytes 819200 | tf_op jit(solution)/shard_map/reshape | solution.py:366
  8.6 1.5 %reshape.192 = f32[16,80,80]{2,1,0:T(8,128)S(1)} reshape(f32[16,6400]{1,0:T(8,128)} %param.32) | data formatting | bytes 819200 | tf_op jit(solution)/shard_map/reshape | solution.py:369
  10.4 1.5 %reshape.191.refs_6_ = f32[16,80,80]{2,1,0:T(8,128)S(1)} reshape(f32[16,6400]{1,0:T(8,128)} %param.31) | data formatting | bytes 819200 | tf_op jit(solution)/shard_map/reshape | solution.py:368
  12.0 1.2 %shard_map.98.refs_0_ = f32[16,80]{1,0:T(8,128)S(1)} custom-call(s32[1]{0:T(128)} %bitcast.197.me_ref.refs_0_, f32[5,80]{1,0:T(8,128)S(1)} %get-tuple-element.650.refs_0_, f32[5,80]{1,0:T(8,128)S(1)} %collective-permute-done.16.refs_1_, f32[5,80]{1,0:T(8,128)S(1)} %collective-permute-done.17.refs_2_, f32[5,80]{1,0:T(8,128)S(1)} %collective-permute-done.18.refs_3_, ...), custom_call_target="tpu_custom_call" | custom-call | flops 614400 | bytes 1644804 | tf_op jit(solution)/shard_map/pallas_call | solution.py:328
  13.4 1.9 %collective-permute-start.20 = (f32[16,80]{1,0:T(8,128)S(1)}, f32[16,80]{1,0:T(8,128)S(1)}, u32[]{:S(2)}, u32[]{:S(2)}) collective-permute-start(f32[16,80]{1,0:T(8,128)S(1)} %shard_map.98.refs_0_), channel_id=1, source_target_pairs={{0,2},{1,3},{2,0},{3,1},{4,6},{5,7},{6,4},{7,5},{8,10},{9,11},{10,... | collective-permute-start | bytes 15368 | tf_op jit(solution)/shard_map/ppermute | solution.py:149
  15.5 1.6 %collective-permute-done.20.refs_2_ = f32[16,80]{1,0:T(8,128)S(1)} collective-permute-done((f32[16,80]{1,0:T(8,128)S(1)}, f32[16,80]{1,0:T(8,128)S(1)}, u32[]{:S(2)}, u32[]{:S(2)}) %collective-permute-start.20) | collective-permute-done | bytes 5152 | tf_op jit(solution)/shard_map/ppermute | solution.py:149
  17.1 1.4 %collective-permute-done.21.refs_3_ = f32[16,80]{1,0:T(8,128)S(1)} collective-permute-done((f32[16,80]{1,0:T(8,128)S(1)}, f32[16,80]{1,0:T(8,128)S(1)}, u32[]{:S(2)}, u32[]{:S(2)}) %collective-permute-start.21) | collective-permute-done | bytes 5152 | tf_op jit(solution)/shard_map/ppermute | solution.py:149
  19.1 1.6 %collective-permute-start.22 = (f32[16,80]{1,0:T(8,128)S(1)}, f32[16,80]{1,0:T(8,128)S(1)}, u32[]{:S(2)}, u32[]{:S(2)}) collective-permute-start(f32[16,80]{1,0:T(8,128)S(1)} %get-tuple-element.654.refs_5_.refs_4_), channel_id=1, source_target_pairs={{0,4},{4,8},{8,12},{12,16},{16,20},{20,24},{24,28},{28,0},{1,5},{5... | collective-permute-start | bytes 15368 | tf_op jit(solution)/shard_map/ppermute | solution.py:400
  20.7 3.2 %collective-permute-start.23 = (f32[16,80]{1,0:T(8,128)S(1)}, f32[16,80]{1,0:T(8,128)S(1)}, u32[]{:S(2)}, u32[]{:S(2)}) collective-permute-start(f32[16,80]{1,0:T(8,128)S(1)} %get-tuple-element.654.refs_5_.refs_4_), channel_id=1, source_target_pairs={{4,0},{8,4},{12,8},{16,12},{20,16},{24,20},{28,24},{0,28},{5,1},{9... | collective-permute-start | bytes 15368 | tf_op jit(solution)/shard_map/ppermute | solution.py:401
  24.0 1.5 %collective-permute-done.22.refs_6_ = f32[16,80]{1,0:T(8,128)S(1)} collective-permute-done((f32[16,80]{1,0:T(8,128)S(1)}, f32[16,80]{1,0:T(8,128)S(1)}, u32[]{:S(2)}, u32[]{:S(2)}) %collective-permute-start.22) | collective-permute-done | bytes 5152 | tf_op jit(solution)/shard_map/ppermute | solution.py:400
  25.6 3.0 %shard_map.100 = (f32[16,80]{1,0:T(8,128)S(1)}, f32[4,80]{1,0:T(4,128)S(1)}, f32[4,80]{1,0:T(4,128)S(1)}, f32[4,80]{1,0:T(4,128)S(1)}, f32[4,80]{1,0:T(4,128)S(1)}) custom-call(s32[1]{0:T(128)} %bitcast.197.me_ref.refs_0_, s32[1,16]{1,0:T(1,128)S(1)} %copy-done.6, f32[16,70400]{1,0:T(8,128)} %refs_2_.5, bf16[176,160]{1,0:T(8,128)(2,1)S(1)} %compare_convert_fusion.refs_3_, ...), custom_call_target="tpu_custom_call" | custom-call | flops 2252800 | bytes 4976708 | tf_op jit(solution)/shard_map/pallas_call | solution.py:328
  30.5 1.8 %collective-permute-done.25.refs_2_ = f32[4,80]{1,0:T(4,128)S(1)} collective-permute-done((f32[4,80]{1,0:T(4,128)S(1)}, f32[4,80]{1,0:T(4,128)S(1)}, u32[]{:S(2)}, u32[]{:S(2)}) %collective-permute-start.25) | collective-permute-done | bytes 1312 | tf_op jit(solution)/shard_map/ppermute | solution.py:149
  32.3 1.2 %shard_map.101.refs_0_ = f32[16,80]{1,0:T(8,128)S(1)} custom-call(s32[1]{0:T(128)} %bitcast.197.me_ref.refs_0_, f32[4,80]{1,0:T(4,128)S(1)} %get-tuple-element.656.refs_0_, f32[4,80]{1,0:T(4,128)S(1)} %collective-permute-done.24.refs_1_, f32[4,80]{1,0:T(4,128)S(1)} %collective-permute-done.25.refs_2_, f32[4,80]{1,0:T(4,128)S(1)} %collective-permute-done.26.refs_3_, ...), custom_call_target="tpu_custom_call" | custom-call | flops 614400 | bytes 1643524 | tf_op jit(solution)/shard_map/pallas_call | solution.py:328
  33.8 1.5 %collective-permute-start.28 = (f32[16,80]{1,0:T(8,128)S(1)}, f32[16,80]{1,0:T(8,128)S(1)}, u32[]{:S(2)}, u32[]{:S(2)}) collective-permute-start(f32[16,80]{1,0:T(8,128)S(1)} %shard_map.101.refs_0_), channel_id=1, source_target_pairs={{0,2},{1,3},{2,0},{3,1},{4,6},{5,7},{6,4},{7,5},{8,10},{9,11},{10,... | collective-permute-start | bytes 15368 | tf_op jit(solution)/shard_map/ppermute | solution.py:149
  35.5 1.9 %collective-permute-done.28.refs_2_ = f32[16,80]{1,0:T(8,128)S(1)} collective-permute-done((f32[16,80]{1,0:T(8,128)S(1)}, f32[16,80]{1,0:T(8,128)S(1)}, u32[]{:S(2)}, u32[]{:S(2)}) %collective-permute-start.28) | collective-permute-done | bytes 5152 | tf_op jit(solution)/shard_map/ppermute | solution.py:149
  39.0 1.3 %collective-permute-start.30 = (f32[16,80]{1,0:T(8,128)S(1)}, f32[16,80]{1,0:T(8,128)S(1)}, u32[]{:S(2)}, u32[]{:S(2)}) collective-permute-start(f32[16,80]{1,0:T(8,128)S(1)} %get-tuple-element.660.refs_5_), channel_id=1, source_target_pairs={{0,4},{4,8},{8,12},{12,16},{16,20},{20,24},{24,28},{28,0},{1,5},{5... | collective-permute-start | bytes 15368 | tf_op jit(solution)/shard_map/ppermute | solution.py:400
  40.4 3.5 %collective-permute-start.31 = (f32[16,80]{1,0:T(8,128)S(1)}, f32[16,80]{1,0:T(8,128)S(1)}, u32[]{:S(2)}, u32[]{:S(2)}) collective-permute-start(f32[16,80]{1,0:T(8,128)S(1)} %get-tuple-element.660.refs_5_), channel_id=1, source_target_pairs={{4,0},{8,4},{12,8},{16,12},{20,16},{24,20},{28,24},{0,28},{5,1},{9... | collective-permute-start | bytes 15368 | tf_op jit(solution)/shard_map/ppermute | solution.py:401
  43.9 1.6 %collective-permute-done.30.refs_6_ = f32[16,80]{1,0:T(8,128)S(1)} collective-permute-done((f32[16,80]{1,0:T(8,128)S(1)}, f32[16,80]{1,0:T(8,128)S(1)}, u32[]{:S(2)}, u32[]{:S(2)}) %collective-permute-start.30) | collective-permute-done | bytes 5152 | tf_op jit(solution)/shard_map/ppermute | solution.py:400
  45.4 3.0 %shard_map.103 = (f32[16,80]{1,0:T(8,128)S(1)}, f32[4,80]{1,0:T(4,128)S(1)}, f32[4,80]{1,0:T(4,128)S(1)}, f32[4,80]{1,0:T(4,128)S(1)}, f32[4,80]{1,0:T(4,128)S(1)}) custom-call(s32[1]{0:T(128)} %bitcast.197.me_ref.refs_0_, s32[1,16]{1,0:T(1,128)S(1)} %copy-done.6, f32[16,70400]{1,0:T(8,128)} %refs_2_.5, bf16[176,160]{1,0:T(8,128)(2,1)S(1)} %compare_convert_fusion.refs_3_, ...), custom_call_target="tpu_custom_call" | custom-call | flops 2252800 | bytes 4976708 | tf_op jit(solution)/shard_map/pallas_call | solution.py:328
  50.4 1.8 %collective-permute-done.33.refs_2_ = f32[4,80]{1,0:T(4,128)S(1)} collective-permute-done((f32[4,80]{1,0:T(4,128)S(1)}, f32[4,80]{1,0:T(4,128)S(1)}, u32[]{:S(2)}, u32[]{:S(2)}) %collective-permute-start.33) | collective-permute-done | bytes 1312 | tf_op jit(solution)/shard_map/ppermute | solution.py:149
  52.3 1.2 %shard_map.104.refs_0_ = f32[16,80]{1,0:T(8,128)S(1)} custom-call(s32[1]{0:T(128)} %bitcast.197.me_ref.refs_0_, f32[4,80]{1,0:T(4,128)S(1)} %get-tuple-element.663.refs_0_, f32[4,80]{1,0:T(4,128)S(1)} %collective-permute-done.32.refs_1_, f32[4,80]{1,0:T(4,128)S(1)} %collective-permute-done.33.refs_2_, f32[4,80]{1,0:T(4,128)S(1)} %collective-permute-done.34.refs_3_, ...), custom_call_target="tpu_custom_call" | custom-call | flops 614400 | bytes 1643524 | tf_op jit(solution)/shard_map/pallas_call | solution.py:328
  53.8 1.4 %collective-permute-start.36 = (f32[16,80]{1,0:T(8,128)S(1)}, f32[16,80]{1,0:T(8,128)S(1)}, u32[]{:S(2)}, u32[]{:S(2)}) collective-permute-start(f32[16,80]{1,0:T(8,128)S(1)} %shard_map.104.refs_0_), channel_id=1, source_target_pairs={{0,2},{1,3},{2,0},{3,1},{4,6},{5,7},{6,4},{7,5},{8,10},{9,11},{10,... | collective-permute-start | bytes 15368 | tf_op jit(solution)/shard_map/ppermute | solution.py:149
  55.5 2.0 %collective-permute-done.36.refs_2_ = f32[16,80]{1,0:T(8,128)S(1)} collective-permute-done((f32[16,80]{1,0:T(8,128)S(1)}, f32[16,80]{1,0:T(8,128)S(1)}, u32[]{:S(2)}, u32[]{:S(2)}) %collective-permute-start.36) | collective-permute-done | bytes 5152 | tf_op jit(solution)/shard_map/ppermute | solution.py:149
  59.0 4.8 %collective-permute-start.39 = (f32[16,80]{1,0:T(8,128)S(1)}, f32[16,80]{1,0:T(8,128)S(1)}, u32[]{:S(2)}, u32[]{:S(2)}) collective-permute-start(f32[16,80]{1,0:T(8,128)S(1)} %get-tuple-element.667.refs_5_.refs_6_), channel_id=1, source_target_pairs={{4,0},{8,4},{12,8},{16,12},{20,16},{24,20},{28,24},{0,28},{5,1},{9... | collective-permute-start | bytes 15368 | tf_op jit(solution)/shard_map/ppermute | solution.py:401
  63.8 1.6 %collective-permute-done.38.refs_6_ = f32[16,80]{1,0:T(8,128)S(1)} collective-permute-done((f32[16,80]{1,0:T(8,128)S(1)}, f32[16,80]{1,0:T(8,128)S(1)}, u32[]{:S(2)}, u32[]{:S(2)}) %collective-permute-start.38) | collective-permute-done | bytes 5152 | tf_op jit(solution)/shard_map/ppermute | solution.py:400
  65.4 3.1 %shard_map.106 = (f32[16,80]{1,0:T(8,128)S(1)}, f32[16,128]{1,0:T(8,128)S(1)}) custom-call(s32[1]{0:T(128)} %bitcast.197.me_ref.refs_0_, s32[1,16]{1,0:T(1,128)S(1)} %copy-done.6, f32[16,70400]{1,0:T(8,128)} %refs_2_.5, bf16[176,160]{1,0:T(8,128)(2,1)S(1)} %compare_convert_fusion.refs_3_, bf16[640,128]{1,0:T(8,128)(2,1)S(1)} %copy-done, ...), custom_call_target="tpu_custom_call" | custom-call | flops 2252800 | bytes 4986948 | tf_op jit(solution)/shard_map/pallas_call | solution.py:328
  70.4 3.0 %collective-permute-done.41 = f32[16,128]{1,0:T(8,128)S(1)} collective-permute-done((f32[16,128]{1,0:T(8,128)S(1)}, f32[16,128]{1,0:T(8,128)S(1)}, u32[]{:S(2)}, u32[]{:S(2)}) %collective-permute-start.41) | collective-permute-done | bytes 8224 | tf_op jit(solution)/shard_map/ppermute | solution.py:149
  73.4 3.6 %collective-permute-done.42 = f32[16,128]{1,0:T(8,128)S(1)} collective-permute-done((f32[16,128]{1,0:T(8,128)S(1)}, f32[16,128]{1,0:T(8,128)S(1)}, u32[]{:S(2)}, u32[]{:S(2)}) %collective-permute-start.42) | collective-permute-done | bytes 8224 | tf_op jit(solution)/shard_map/ppermute | solution.py:149
  77.0 3.6 %collective-permute-done.43 = f32[16,128]{1,0:T(8,128)S(1)} collective-permute-done((f32[16,128]{1,0:T(8,128)S(1)}, f32[16,128]{1,0:T(8,128)S(1)}, u32[]{:S(2)}, u32[]{:S(2)}) %collective-permute-start.43) | collective-permute-done | bytes 8224 | tf_op jit(solution)/shard_map/ppermute | solution.py:149
  80.7 1.9 %collective-permute-start.44 = (f32[16,128]{1,0:T(8,128)S(1)}, f32[16,128]{1,0:T(8,128)S(1)}, u32[]{:S(2)}, u32[]{:S(2)}) collective-permute-start(f32[16,128]{1,0:T(8,128)S(1)} %add.226), channel_id=1, source_target_pairs={{0,16},{4,20},{8,24},{12,28},{16,0},{20,4},{24,8},{28,12},{1,17},{... | collective-permute-start | bytes 24584 | tf_op jit(solution)/shard_map/ppermute | solution.py:149
  82.6 2.6 %collective-permute-done.44 = f32[16,128]{1,0:T(8,128)S(1)} collective-permute-done((f32[16,128]{1,0:T(8,128)S(1)}, f32[16,128]{1,0:T(8,128)S(1)}, u32[]{:S(2)}, u32[]{:S(2)}) %collective-permute-start.44) | collective-permute-done | bytes 8224 | tf_op jit(solution)/shard_map/ppermute | solution.py:149
  (76 shorter events, 17.3 us)
Async XLA Ops:
  0.6 24.9 %copy-start = (bf16[640,128]{1,0:T(8,128)(2,1)S(1)}, bf16[640,128]{1,0:T(8,128)(2,1)}, u32[]{:S(2)}) copy-start(bf16[640,128]{1,0:T(8,128)(2,1)} %constant.403.clone.refs_4_) | copy-start | bytes 491524
  2.9 9.1 %collective-permute-start.16 = (f32[5,80]{1,0:T(8,128)S(1)}, f32[5,80]{1,0:T(8,128)S(1)}, u32[]{:S(2)}, u32[]{:S(2)}) collective-permute-start(f32[5,80]{1,0:T(8,128)S(1)} %get-tuple-element.651), channel_id=1, source_target_pairs={{0,1},{1,0},{2,3},{3,2},{4,5},{5,4},{6,7},{7,6},{8,9},{9,8},{10,11... | collective-permute-start | bytes 4808 | tf_op jit(solution)/shard_map/ppermute | solution.py:149
  3.4 8.6 %collective-permute-start.17 = (f32[5,80]{1,0:T(8,128)S(1)}, f32[5,80]{1,0:T(8,128)S(1)}, u32[]{:S(2)}, u32[]{:S(2)}) collective-permute-start(f32[5,80]{1,0:T(8,128)S(1)} %get-tuple-element.652), channel_id=1, source_target_pairs={{0,2},{1,3},{2,0},{3,1},{4,6},{5,7},{6,4},{7,5},{8,10},{9,11},{10,... | collective-permute-start | bytes 4808 | tf_op jit(solution)/shard_map/ppermute | solution.py:149
  6.0 6.0 %collective-permute-start.18 = (f32[5,80]{1,0:T(8,128)S(1)}, f32[5,80]{1,0:T(8,128)S(1)}, u32[]{:S(2)}, u32[]{:S(2)}) collective-permute-start(f32[5,80]{1,0:T(8,128)S(1)} %get-tuple-element.653), channel_id=1, source_target_pairs={{0,3},{1,2},{2,1},{3,0},{4,7},{5,6},{6,5},{7,4},{8,11},{9,10},{10,... | collective-permute-start | bytes 4808 | tf_op jit(solution)/shard_map/ppermute | solution.py:149
  13.2 2.3 %collective-permute-start.19 = (f32[16,80]{1,0:T(8,128)S(1)}, f32[16,80]{1,0:T(8,128)S(1)}, u32[]{:S(2)}, u32[]{:S(2)}) collective-permute-start(f32[16,80]{1,0:T(8,128)S(1)} %shard_map.98.refs_0_), channel_id=1, source_target_pairs={{0,1},{1,0},{2,3},{3,2},{4,5},{5,4},{6,7},{7,6},{8,9},{9,8},{10,11... | collective-permute-start | bytes 15368 | tf_op jit(solution)/shard_map/ppermute | solution.py:149
  13.4 3.7 %collective-permute-start.20 = (f32[16,80]{1,0:T(8,128)S(1)}, f32[16,80]{1,0:T(8,128)S(1)}, u32[]{:S(2)}, u32[]{:S(2)}) collective-permute-start(f32[16,80]{1,0:T(8,128)S(1)} %shard_map.98.refs_0_), channel_id=1, source_target_pairs={{0,2},{1,3},{2,0},{3,1},{4,6},{5,7},{6,4},{7,5},{8,10},{9,11},{10,... | collective-permute-start | bytes 15368 | tf_op jit(solution)/shard_map/ppermute | solution.py:149
  15.4 3.1 %collective-permute-start.21 = (f32[16,80]{1,0:T(8,128)S(1)}, f32[16,80]{1,0:T(8,128)S(1)}, u32[]{:S(2)}, u32[]{:S(2)}) collective-permute-start(f32[16,80]{1,0:T(8,128)S(1)} %shard_map.98.refs_0_), channel_id=1, source_target_pairs={{0,3},{1,2},{2,1},{3,0},{4,7},{5,6},{6,5},{7,4},{8,11},{9,10},{10,... | collective-permute-start | bytes 15368 | tf_op jit(solution)/shard_map/ppermute | solution.py:149
  19.1 6.4 %collective-permute-start.22 = (f32[16,80]{1,0:T(8,128)S(1)}, f32[16,80]{1,0:T(8,128)S(1)}, u32[]{:S(2)}, u32[]{:S(2)}) collective-permute-start(f32[16,80]{1,0:T(8,128)S(1)} %get-tuple-element.654.refs_5_.refs_4_), channel_id=1, source_target_pairs={{0,4},{4,8},{8,12},{12,16},{16,20},{20,24},{24,28},{28,0},{1,5},{5... | collective-permute-start | bytes 15368 | tf_op jit(solution)/shard_map/ppermute | solution.py:400
  20.7 4.8 %collective-permute-start.23 = (f32[16,80]{1,0:T(8,128)S(1)}, f32[16,80]{1,0:T(8,128)S(1)}, u32[]{:S(2)}, u32[]{:S(2)}) collective-permute-start(f32[16,80]{1,0:T(8,128)S(1)} %get-tuple-element.654.refs_5_.refs_4_), channel_id=1, source_target_pairs={{4,0},{8,4},{12,8},{16,12},{20,16},{24,20},{28,24},{0,28},{5,1},{9... | collective-permute-start | bytes 15368 | tf_op jit(solution)/shard_map/ppermute | solution.py:401
  28.6 1.9 %collective-permute-start.24 = (f32[4,80]{1,0:T(4,128)S(1)}, f32[4,80]{1,0:T(4,128)S(1)}, u32[]{:S(2)}, u32[]{:S(2)}) collective-permute-start(f32[4,80]{1,0:T(4,128)S(1)} %get-tuple-element.657), channel_id=1, source_target_pairs={{0,1},{1,0},{2,3},{3,2},{4,5},{5,4},{6,7},{7,6},{8,9},{9,8},{10,11... | collective-permute-start | bytes 3848 | tf_op jit(solution)/shard_map/ppermute | solution.py:149
  28.7 3.7 %collective-permute-start.25 = (f32[4,80]{1,0:T(4,128)S(1)}, f32[4,80]{1,0:T(4,128)S(1)}, u32[]{:S(2)}, u32[]{:S(2)}) collective-permute-start(f32[4,80]{1,0:T(4,128)S(1)} %get-tuple-element.658), channel_id=1, source_target_pairs={{0,2},{1,3},{2,0},{3,1},{4,6},{5,7},{6,4},{7,5},{8,10},{9,11},{10,... | collective-permute-start | bytes 3848 | tf_op jit(solution)/shard_map/ppermute | solution.py:149
  29.3 3.0 %collective-permute-start.26 = (f32[4,80]{1,0:T(4,128)S(1)}, f32[4,80]{1,0:T(4,128)S(1)}, u32[]{:S(2)}, u32[]{:S(2)}) collective-permute-start(f32[4,80]{1,0:T(4,128)S(1)} %get-tuple-element.659), channel_id=1, source_target_pairs={{0,3},{1,2},{2,1},{3,0},{4,7},{5,6},{6,5},{7,4},{8,11},{9,10},{10,... | collective-permute-start | bytes 3848 | tf_op jit(solution)/shard_map/ppermute | solution.py:149
  32.3 53.7 %copy-start.3 = (f32[16,6400]{1,0:T(8,128)S(1)}, f32[16,6400]{1,0:T(8,128)}, u32[]{:S(2)}) copy-start(f32[16,6400]{1,0:T(8,128)} %param.30) | copy-start | bytes 1228804
  32.3 53.7 %copy-start.4 = (s32[11,16]{1,0:T(8,128)S(1)}, s32[11,16]{1,0:T(8,128)}, u32[]{:S(2)}) copy-start(s32[11,16]{1,0:T(8,128)} %param.28) | copy-start | bytes 2116
  33.6 1.9 %collective-permute-start.27 = (f32[16,80]{1,0:T(8,128)S(1)}, f32[16,80]{1,0:T(8,128)S(1)}, u32[]{:S(2)}, u32[]{:S(2)}) collective-permute-start(f32[16,80]{1,0:T(8,128)S(1)} %shard_map.101.refs_0_), channel_id=1, source_target_pairs={{0,1},{1,0},{2,3},{3,2},{4,5},{5,4},{6,7},{7,6},{8,9},{9,8},{10,11... | collective-permute-start | bytes 15368 | tf_op jit(solution)/shard_map/ppermute | solution.py:149
  33.8 3.7 %collective-permute-start.28 = (f32[16,80]{1,0:T(8,128)S(1)}, f32[16,80]{1,0:T(8,128)S(1)}, u32[]{:S(2)}, u32[]{:S(2)}) collective-permute-start(f32[16,80]{1,0:T(8,128)S(1)} %shard_map.101.refs_0_), channel_id=1, source_target_pairs={{0,2},{1,3},{2,0},{3,1},{4,6},{5,7},{6,4},{7,5},{8,10},{9,11},{10,... | collective-permute-start | bytes 15368 | tf_op jit(solution)/shard_map/ppermute | solution.py:149
  35.3 3.1 %collective-permute-start.29 = (f32[16,80]{1,0:T(8,128)S(1)}, f32[16,80]{1,0:T(8,128)S(1)}, u32[]{:S(2)}, u32[]{:S(2)}) collective-permute-start(f32[16,80]{1,0:T(8,128)S(1)} %shard_map.101.refs_0_), channel_id=1, source_target_pairs={{0,3},{1,2},{2,1},{3,0},{4,7},{5,6},{6,5},{7,4},{8,11},{9,10},{10,... | collective-permute-start | bytes 15368 | tf_op jit(solution)/shard_map/ppermute | solution.py:149
  39.0 6.4 %collective-permute-start.30 = (f32[16,80]{1,0:T(8,128)S(1)}, f32[16,80]{1,0:T(8,128)S(1)}, u32[]{:S(2)}, u32[]{:S(2)}) collective-permute-start(f32[16,80]{1,0:T(8,128)S(1)} %get-tuple-element.660.refs_5_), channel_id=1, source_target_pairs={{0,4},{4,8},{8,12},{12,16},{16,20},{20,24},{24,28},{28,0},{1,5},{5... | collective-permute-start | bytes 15368 | tf_op jit(solution)/shard_map/ppermute | solution.py:400
  40.4 5.1 %collective-permute-start.31 = (f32[16,80]{1,0:T(8,128)S(1)}, f32[16,80]{1,0:T(8,128)S(1)}, u32[]{:S(2)}, u32[]{:S(2)}) collective-permute-start(f32[16,80]{1,0:T(8,128)S(1)} %get-tuple-element.660.refs_5_), channel_id=1, source_target_pairs={{4,0},{8,4},{12,8},{16,12},{20,16},{24,20},{28,24},{0,28},{5,1},{9... | collective-permute-start | bytes 15368 | tf_op jit(solution)/shard_map/ppermute | solution.py:401
  48.5 1.9 %collective-permute-start.32 = (f32[4,80]{1,0:T(4,128)S(1)}, f32[4,80]{1,0:T(4,128)S(1)}, u32[]{:S(2)}, u32[]{:S(2)}) collective-permute-start(f32[4,80]{1,0:T(4,128)S(1)} %get-tuple-element.664), channel_id=1, source_target_pairs={{0,1},{1,0},{2,3},{3,2},{4,5},{5,4},{6,7},{7,6},{8,9},{9,8},{10,11... | collective-permute-start | bytes 3848 | tf_op jit(solution)/shard_map/ppermute | solution.py:149
  48.5 3.7 %collective-permute-start.33 = (f32[4,80]{1,0:T(4,128)S(1)}, f32[4,80]{1,0:T(4,128)S(1)}, u32[]{:S(2)}, u32[]{:S(2)}) collective-permute-start(f32[4,80]{1,0:T(4,128)S(1)} %get-tuple-element.665), channel_id=1, source_target_pairs={{0,2},{1,3},{2,0},{3,1},{4,6},{5,7},{6,4},{7,5},{8,10},{9,11},{10,... | collective-permute-start | bytes 3848 | tf_op jit(solution)/shard_map/ppermute | solution.py:149
  49.3 3.0 %collective-permute-start.34 = (f32[4,80]{1,0:T(4,128)S(1)}, f32[4,80]{1,0:T(4,128)S(1)}, u32[]{:S(2)}, u32[]{:S(2)}) collective-permute-start(f32[4,80]{1,0:T(4,128)S(1)} %get-tuple-element.666), channel_id=1, source_target_pairs={{0,3},{1,2},{2,1},{3,0},{4,7},{5,6},{6,5},{7,4},{8,11},{9,10},{10,... | collective-permute-start | bytes 3848 | tf_op jit(solution)/shard_map/ppermute | solution.py:149
  53.5 1.9 %collective-permute-start.35 = (f32[16,80]{1,0:T(8,128)S(1)}, f32[16,80]{1,0:T(8,128)S(1)}, u32[]{:S(2)}, u32[]{:S(2)}) collective-permute-start(f32[16,80]{1,0:T(8,128)S(1)} %shard_map.104.refs_0_), channel_id=1, source_target_pairs={{0,1},{1,0},{2,3},{3,2},{4,5},{5,4},{6,7},{7,6},{8,9},{9,8},{10,11... | collective-permute-start | bytes 15368 | tf_op jit(solution)/shard_map/ppermute | solution.py:149
  53.8 3.7 %collective-permute-start.36 = (f32[16,80]{1,0:T(8,128)S(1)}, f32[16,80]{1,0:T(8,128)S(1)}, u32[]{:S(2)}, u32[]{:S(2)}) collective-permute-start(f32[16,80]{1,0:T(8,128)S(1)} %shard_map.104.refs_0_), channel_id=1, source_target_pairs={{0,2},{1,3},{2,0},{3,1},{4,6},{5,7},{6,4},{7,5},{8,10},{9,11},{10,... | collective-permute-start | bytes 15368 | tf_op jit(solution)/shard_map/ppermute | solution.py:149
  55.1 3.1 %collective-permute-start.37 = (f32[16,80]{1,0:T(8,128)S(1)}, f32[16,80]{1,0:T(8,128)S(1)}, u32[]{:S(2)}, u32[]{:S(2)}) collective-permute-start(f32[16,80]{1,0:T(8,128)S(1)} %shard_map.104.refs_0_), channel_id=1, source_target_pairs={{0,3},{1,2},{2,1},{3,0},{4,7},{5,6},{6,5},{7,4},{8,11},{9,10},{10,... | collective-permute-start | bytes 15368 | tf_op jit(solution)/shard_map/ppermute | solution.py:149
  58.9 6.5 %collective-permute-start.38 = (f32[16,80]{1,0:T(8,128)S(1)}, f32[16,80]{1,0:T(8,128)S(1)}, u32[]{:S(2)}, u32[]{:S(2)}) collective-permute-start(f32[16,80]{1,0:T(8,128)S(1)} %get-tuple-element.667.refs_5_.refs_6_), channel_id=1, source_target_pairs={{0,4},{4,8},{8,12},{12,16},{16,20},{20,24},{24,28},{28,0},{1,5},{5... | collective-permute-start | bytes 15368 | tf_op jit(solution)/shard_map/ppermute | solution.py:400
  59.0 6.3 %collective-permute-start.39 = (f32[16,80]{1,0:T(8,128)S(1)}, f32[16,80]{1,0:T(8,128)S(1)}, u32[]{:S(2)}, u32[]{:S(2)}) collective-permute-start(f32[16,80]{1,0:T(8,128)S(1)} %get-tuple-element.667.refs_5_.refs_6_), channel_id=1, source_target_pairs={{4,0},{8,4},{12,8},{16,12},{20,16},{24,20},{28,24},{0,28},{5,1},{9... | collective-permute-start | bytes 15368 | tf_op jit(solution)/shard_map/ppermute | solution.py:401
  68.5 1.2 %collective-permute-start.40 = (f32[16,128]{1,0:T(8,128)S(1)}, f32[16,128]{1,0:T(8,128)S(1)}, u32[]{:S(2)}, u32[]{:S(2)}) collective-permute-start(f32[16,128]{1,0:T(8,128)S(1)} %get-tuple-element.670), channel_id=1, source_target_pairs={{0,1},{1,0},{2,3},{3,2},{4,5},{5,4},{6,7},{7,6},{8,9},{9,8},{10,11... | collective-permute-start | bytes 24584 | tf_op jit(solution)/shard_map/ppermute | solution.py:149
  69.7 3.7 %collective-permute-start.41 = (f32[16,128]{1,0:T(8,128)S(1)}, f32[16,128]{1,0:T(8,128)S(1)}, u32[]{:S(2)}, u32[]{:S(2)}) collective-permute-start(f32[16,128]{1,0:T(8,128)S(1)} %add.223), channel_id=1, source_target_pairs={{0,2},{1,3},{2,0},{3,1},{4,6},{5,7},{6,4},{7,5},{8,10},{9,11},{10,... | collective-permute-start | bytes 24584 | tf_op jit(solution)/shard_map/ppermute | solution.py:149
  73.4 3.7 %collective-permute-start.42 = (f32[16,128]{1,0:T(8,128)S(1)}, f32[16,128]{1,0:T(8,128)S(1)}, u32[]{:S(2)}, u32[]{:S(2)}) collective-permute-start(f32[16,128]{1,0:T(8,128)S(1)} %add.224), channel_id=1, source_target_pairs={{0,4},{4,0},{8,12},{12,8},{16,20},{20,16},{24,28},{28,24},{1,5},{5... | collective-permute-start | bytes 24584 | tf_op jit(solution)/shard_map/ppermute | solution.py:149
  77.0 3.7 %collective-permute-start.43 = (f32[16,128]{1,0:T(8,128)S(1)}, f32[16,128]{1,0:T(8,128)S(1)}, u32[]{:S(2)}, u32[]{:S(2)}) collective-permute-start(f32[16,128]{1,0:T(8,128)S(1)} %add.225), channel_id=1, source_target_pairs={{0,8},{4,12},{8,0},{12,4},{16,24},{20,28},{24,16},{28,20},{1,9},{5... | collective-permute-start | bytes 24584 | tf_op jit(solution)/shard_map/ppermute | solution.py:149
  80.7 4.5 %collective-permute-start.44 = (f32[16,128]{1,0:T(8,128)S(1)}, f32[16,128]{1,0:T(8,128)S(1)}, u32[]{:S(2)}, u32[]{:S(2)}) collective-permute-start(f32[16,128]{1,0:T(8,128)S(1)} %add.226), channel_id=1, source_target_pairs={{0,16},{4,20},{8,24},{12,28},{16,0},{20,4},{24,8},{28,12},{1,17},{... | collective-permute-start | bytes 24584 | tf_op jit(solution)/shard_map/ppermute | solution.py:149
  (3 other events, 47.7 us)

commit v2 on v1

--- a/solution.py
+++ b/solution.py
@@ -149,21 +149,52 @@
     return lax.ppermute(x, axis, [(i, partner(i, k, size)[0]) for i in range(size)])
 
 
-def start_kernel(nplane, me_ref, slot_ref, u_ref, tail_ref, *outs):
-    per = slot_ref.shape[1] // nplane
+def split(x, parts):
+    out = []
+    for _ in range(parts):
+        out.append(x.astype(BF16).astype(F32))
+        x = x - out[-1]
+    return jnp.concatenate(out, axis=0)
+
+
+def start_kernel(nplane, slot_ref, u_ref, *outs):
+    nfaces, width = u_ref.shape
+    per = nfaces // nplane
+    me = lax.axis_index("plane")
+    lane = lax.broadcasted_iota(jnp.int32, (1, width), 1)
+    tail = jnp.zeros((1, width), F32)
+    for t in range(nfaces):
+        tail = jnp.where(lane == t, slot_ref[0, t].astype(F32), tail)
     for k in range(nplane):
-        to, _ = partner(me_ref[0], k, nplane)
+        to, _ = partner(me, k, nplane)
         for i in range(per):
             outs[k][pl.ds(i, 1), :] = u_ref[pl.ds(slot_ref[0, to * per + i], 1), :]
-        outs[k][pl.ds(per, 1), :] = tail_ref[...]
-
-
-def line_kernel(nplane, nlines, me_ref, *refs):
-    msgs, (low, low_t, upp, piv_t, z_ref, r_scr) = refs[:nplane], refs[nplane:]
+        outs[k][pl.ds(per, 1), :] = tail
+
+
+def square_kernel(length, low, upp, piv, low_out, upp_out, piv_out):
+    nrows, width = low.shape[0], low_out.shape[1]
+    chunk = math.lcm(width, 128)
+    for src, dst in ((low, low_out), (upp, upp_out), (piv, piv_out)):
+        for c in range(width * width // chunk):
+            piece = src[:, c * chunk : (c + 1) * chunk]
+            for r in range(chunk // width):
+                a = c * (chunk // width) + r
+                dst[pl.ds(a, nrows, stride=width), :] = piece[:, r * width : (r + 1) * width]
+    for at in range(nrows):
+        here = slice(at * width, (at + 1) * width)
+        if at % length % 2 == 0 and at % length:
+            low_out[here, :] = low_out[here, :].T
+        piv_out[here, :] = piv_out[here, :].T
+
+
+def line_kernel(nplane, nlines, *refs):
+    msgs, (low, upp, piv_t, z_ref, r_scr) = refs[:nplane], refs[nplane:]
     width = z_ref.shape[1]
     length = z_ref.shape[0] // nlines
+    me = lax.axis_index("plane")
     for k in range(nplane):
-        _, source = partner(me_ref[0], k, nplane)
+        _, source = partner(me, k, nplane)
         for m in range(nlines):
             for q in range(P_SIZE):
                 r_scr[m, pl.ds(source * P_SIZE + q, 1), :] = msgs[k][pl.ds(m * P_SIZE + q, 1), :]
@@ -183,7 +214,7 @@
             elif j % 2:
                 carry[m] = column(rows[j][m]) - jnp.sum(low[at] * carry[m], axis=1, keepdims=True)
             else:
-                carry[m] = rows[j][m] - jnp.sum(low_t[at] * carry[m], axis=0, keepdims=True)
+                carry[m] = rows[j][m] - jnp.sum(low[at] * carry[m], axis=0, keepdims=True)
             y_cols[j][m] = carry[m] if j % 2 else column(carry[m])
     after = [None] * nlines
     for j in reversed(range(length)):
@@ -196,86 +227,109 @@
             z_ref[pl.ds(at, 1), :] = after[m]
 
 
-def faces_kernel(nplane, nlines, me_ref, slots_ref, *refs):
+def faces_kernel(nplane, choose, *refs):
     solved, (mine_ref, sides_ref) = refs[:nplane], refs[nplane:]
     nfaces = mine_ref.shape[0]
-    length = nfaces // nlines
-    per = nlines * P_SIZE
-    me = me_ref[0]
-    for side, dplane in enumerate((0, -1, 1)):
-        there = me + dplane
-        safe = jnp.clip(there, 0, nplane - 1)
-        for k in range(nplane):
-            _, owner = partner(me, k, nplane)
-            for i in range(per):
-                face = slots_ref[safe, owner * per + i]
-                row = solved[k][pl.ds((i // P_SIZE) * length + safe * P_SIZE + i % P_SIZE, 1), :]
-                if side == 0:
-                    mine_ref[pl.ds(face, 1), :] = row
-                else:
-                    sides_ref[pl.ds((side - 1) * nfaces + face, 1), :] = row
-
-
-def apply_kernel(nplane, last, *refs):
-    (me_ref, slot_ref, blocks, pick, seg, mine, before, after, sides), refs = refs[:9], refs[9:]
+    table = split(jnp.concatenate([s[...] for s in solved], axis=0), 3).astype(BF16)
+    out = jnp.dot(choose[...], table, preferred_element_type=F32)
+    mine_ref[...] = out[:nfaces]
+    sides_ref[...] = out[nfaces:]
+
+
+def fetch_and_apply(ks, blocks, pick, seg, faces, scratch):
+    buf, x_scr, acc, sems = scratch
+    nfaces, width = faces[0].shape
+    area = width * width
+    chunk = seg.shape[0]
+    copies = chunk // width
+
+    def fetch(n):
+        return pltpu.make_async_copy(
+            blocks.at[:, pl.ds(ks[n] * area, area)], buf.at[:, pl.ds(n * area, area)], sems.at[n]
+        )
+
+    for n in range(len(ks)):
+        fetch(n).start()
+    both = split(jnp.concatenate([f[...] for f in faces], axis=0), 2)
+    wide = jnp.concatenate([both] * copies, axis=1).astype(BF16)
+    x_scr[...] = jnp.dot(pick[...], wide, preferred_element_type=F32)
+    group = 3
+    for first in range(0, len(ks), group):
+        some = range(first, min(first + group, len(ks)))
+        for n in some:
+            fetch(n).wait()
+        for v in range(0, chunk, 128):
+            xs = [x_scr[n * nfaces : (n + 1) * nfaces, v : v + 128] for n in some]
+            for c in range(area // chunk):
+                at = c * chunk + v
+                total = None if first == 0 else acc[:, at : at + 128]
+                for n, x in zip(some, xs):
+                    term = buf[:, n * area + at : n * area + at + 128] * x
+                    total = term if total is None else total + term
+                acc[:, at : at + 128] = total
+    parts = []
+    for c in range(area // chunk):
+        value = acc[:, c * chunk : (c + 1) * chunk]
+        high = value.astype(BF16)
+        parts += [high, (value - high.astype(F32)).astype(BF16)]
+    sums = jnp.dot(jnp.concatenate(parts, axis=0), seg[...], preferred_element_type=F32)
+    place = lax.broadcasted_iota(jnp.int32, (nfaces, seg.shape[1]), 1) // copies
+    total = jnp.zeros((nfaces, seg.shape[1]), F32)
+    for c in range(area // chunk):
+        at = 2 * c * nfaces
+        total = total + jnp.where(place == c, sums[at : at + nfaces] + sums[at + nfaces : at + 2 * nfaces], 0.0)
+    return total[:, :width]
+
+
+def near_kernel(ks, blocks, pick, seg, mine, sides, out_ref, *scratch):
+    out_ref[...] = fetch_and_apply(ks, blocks, pick, seg, [mine, sides], scratch)
+
+
+def far_kernel(ks, nplane, last, *refs):
+    (blocks, slot, pick, seg, pair, other, near), refs = refs[:7], refs[7:]
     nold = ITERS if last else 1
     olds, refs = refs[:nold], refs[nold:]
     next_ref, refs = refs[0], refs[1:]
-    nfaces, width = mine.shape
-    area = width * width
-    nblocks = blocks.shape[1] // area
-    chunk = seg.shape[0]
-    copies = chunk // width
-    table = jnp.concatenate([mine[...], before[...], after[...], sides[...]], axis=0)
-    high = table.astype(BF16).astype(F32)
-    both = jnp.concatenate([high, table - high], axis=0)
-    wide = jnp.concatenate([both] * copies, axis=1).astype(BF16)
-    x_scr = refs[-1]
-    x_scr[...] = jnp.dot(pick[...], wide, preferred_element_type=F32)
-    masks = lax.broadcasted_iota(jnp.int32, (nfaces, seg.shape[1]), 1) // copies
-    total = jnp.zeros((nfaces, seg.shape[1]), F32)
-    parts = []
-    for c in range(area // chunk):
-        acc = None
-        for k in range(nblocks):
-            at = k * area + c * chunk
-            term = blocks[:, at : at + chunk] * x_scr[k * nfaces : (k + 1) * nfaces, :]
-            acc = term if acc is None else acc + term
-        acc_high = acc.astype(BF16)
-        parts += [acc_high, (acc - acc_high.astype(F32)).astype(BF16)]
-    sums = jnp.dot(jnp.concatenate(parts, axis=0), seg[...], preferred_element_type=F32)
-    for c in range(area // chunk):
-        pair = sums[2 * c * nfaces : (2 * c + 1) * nfaces] + sums[(2 * c + 1) * nfaces : (2 * c + 2) * nfaces]
-        total = total + jnp.where(masks == c, pair, 0.0)
-    u_next = total[:, :width] - SHIFT * olds[-1][...]
+    nfaces = next_ref.shape[0]
+    if not last:
+        slot_scr, slot_sem = refs[-2:]
+        refs = refs[:-2]
+        slots = pltpu.make_async_copy(slot, slot_scr, slot_sem)
+        slots.start()
+    far = fetch_and_apply(ks, blocks, pick, seg, [pair, other], refs[-4:])
+    u_next = near[...] + far - SHIFT * olds[-1][...]
     next_ref[...] = u_next
     if last:
         gram_ref = refs[0]
         basis = [old[...] for old in olds] + [u_next]
-        row = 0
+        lane = lax.broadcasted_iota(jnp.int32, gram_ref.shape, 1)
+        gram, at = jnp.zeros(gram_ref.shape, F32), 0
         for i in range(ITERS + 1):
             for j in range(i, ITERS + 1):
-                value = jnp.sum(jnp.sum(basis[i] * basis[j], axis=1, keepdims=True), axis=0, keepdims=True)
-                gram_ref[pl.ds(row, 1), :] = jnp.broadcast_to(value, (1, gram_ref.shape[1]))
-                row += 1
+                value = jnp.sum(jnp.sum(basis[i] * basis[j], axis=0, keepdims=True), axis=1, keepdims=True)
+                gram, at = jnp.where(lane == at, value, gram), at + 1
+        gram_ref[...] = gram
     else:
-        outs = refs[:nplane]
         per = nfaces // nplane
+        me = lax.axis_index("plane")
+        slots.wait()
         for k in range(nplane):
-            to, _ = partner(me_ref[0], k, nplane)
+            to, _ = partner(me, k, nplane)
             for i in range(per):
-                outs[k][pl.ds(i, 1), :] = next_ref[pl.ds(slot_ref[0, to * per + i], 1), :]
+                refs[k][pl.ds(i, 1), :] = next_ref[pl.ds(slot_scr[0, to * per + i], 1), :]
 
 
 def finish_kernel(gram_ref, *refs):
     us, zs = refs[: ITERS + 1], refs[ITERS + 1 : 2 * ITERS + 1]
     sol_ref, res_ref, ok_ref = refs[2 * ITERS + 1 :]
     width = sol_ref.shape[1]
-    gram, row = {}, 0
+    lane = lax.broadcasted_iota(jnp.int32, gram_ref.shape, 1)
+    gram, at = {}, 0
     for i in range(ITERS + 1):
         for j in range(i, ITERS + 1):
-            gram[i, j] = gram[j, i] = gram_ref[pl.ds(row, 1), :]
-            row += 1
+            value = jnp.sum(jnp.where(lane == at, gram_ref[...], 0.0), axis=1, keepdims=True)
+            gram[i, j] = gram[j, i] = jnp.broadcast_to(value, gram_ref.shape)
+            at += 1
     largest = functools.reduce(jnp.maximum, [jnp.abs(g) for g in gram.values()])
     ok = largest < 1e30
     beta = jnp.sqrt(gram[0, 0] + EPS)
@@ -321,10 +375,11 @@
     ok_ref[...] = jnp.where(ok, 1.0, 0.0)
 
 
-def call(kernel, args, outs, scratch=(), flops=0, pinned=True):
-    spaces = [pltpu.SMEM if x.dtype == jnp.int32 else pltpu.VMEM for x in args]
-    args = [x if s is pltpu.SMEM else pltpu.with_memory_space_constraint(x, s) for x, s in zip(args, spaces)]
-    size = sum(4 * math.prod(x.shape) for x in args)
+def call(kernel, args, outs, spaces=None, scratch=(), flops=0, pinned=True, ready=True):
+    spaces = [pltpu.VMEM] * len(args) if spaces is None else spaces
+    if ready:
+        args = [pltpu.with_memory_space_constraint(x, s) if s is pltpu.VMEM else x for x, s in zip(args, spaces)]
+    size = sum(x.dtype.itemsize * math.prod(x.shape) for x in args)
     return pl.pallas_call(
         kernel,
         out_shape=[pltpu.VMEM(shape, F32) if pinned else jax.ShapeDtypeStruct(shape, F32) for shape in outs],
@@ -336,15 +391,20 @@
     )(*args)
 
 
-def add_up(x, axis):
-    size = lax.axis_size(axis)
-    if size & (size - 1):
-        return lax.psum(x, axis)
+def add_up(x):
+    count = lax.axis_size("span") * lax.axis_size("plane")
+    if count & (count - 1):
+        return lax.psum(x, ("span", "plane"))
     step = 1
-    while step < size:
-        x = x + exchange(x, axis, step)
+    while step < count:
+        x = x + lax.ppermute(x, ("span", "plane"), [(i, i ^ step) for i in range(count)])
         step *= 2
     return x
+
+
+def one_hot(index, count, copies):
+    lanes = lax.broadcasted_iota(jnp.int32, (1, copies * count), 1) % count
+    return (lanes == index.reshape(-1, 1)).astype(BF16)
 
 
 def on_device(rhs, blocks, columns, line_slot, line_lower, line_upper, pivot_inv):
@@ -354,69 +414,120 @@
     owned = nfaces // P_SIZE // nplane
     length = P_SIZE * nplane
     per = owned * P_SIZE
-    me = lax.axis_index("plane").astype(jnp.int32)[None]
+    me = lax.axis_index("plane")
     shape = (nfaces, width)
-
-    position = table_positions(columns, nfaces).reshape(nblocks * nfaces, 1)
-    places = 5 * nfaces
-    pick = (lax.broadcasted_iota(jnp.int32, (1, 2 * places), 1) % places == position).astype(BF16)
+    area = width * width
+
+    us = [rhs.T]
+    send = call(
+        functools.partial(start_kernel, nplane),
+        [line_slot, us[0]],
+        [(per + 1, width)] * nplane,
+        [pltpu.SMEM, pltpu.VMEM],
+        ready=False,
+    )
+
+    if nspan % 2 == 0:
+        pairs = [(i, i ^ 1) for i in range(nspan)]
+        others = [(i, (i + 1 if i % 2 else i - 1) % nspan) for i in range(nspan)]
+        before_first = lax.axis_index("span") % 2 == 1
+    else:
+        pairs = [(i, (i + 1) % nspan) for i in range(nspan)]
+        others = [(i, (i - 1) % nspan) for i in range(nspan)]
+        before_first = True
+
     chunk = math.lcm(width, 128)
     seg = (np.arange(chunk)[:, None] // width == np.arange(128)[None, :] % (chunk // width)).astype(np.float32)
     seg = jnp.asarray(seg, BF16)
-    low = line_lower.reshape(nfaces, width, width)
-    low_t = jnp.swapaxes(low, 1, 2)
-    upp = line_upper.reshape(nfaces, width, width)
-    piv_t = jnp.swapaxes(pivot_inv.reshape(nfaces, width, width), 1, 2)
-
-    us = [rhs.T]
+
+    factors = call(
+        functools.partial(square_kernel, length),
+        [line_lower, line_upper, pivot_inv],
+        [(nfaces * width, width)] * 3,
+        flops=nfaces * area,
+        ready=False,
+    )
+    factors = [x.reshape(nfaces, width, width) for x in factors]
+
+    def scratch(count):
+        return [
+            pltpu.VMEM((nfaces, count * area), F32),
+            pltpu.VMEM((count * nfaces, chunk), F32),
+            pltpu.VMEM((nfaces, area), F32),
+            pltpu.SemaphoreType.DMA((count,)),
+        ]
+
+    near_ks = [0] + list(range(3, nblocks))
+    far_ks = [1, 2] + list(range(5, nblocks))
     zs = []
-    tail = jnp.pad(line_slot.astype(F32), ((0, 0), (0, width - nfaces)))
-    send = call(
-        functools.partial(start_kernel, nplane), [me, line_slot, us[0], tail], [(per + 1, width)] * nplane
-    )
-    up = [(i, (i + 1) % nspan) for i in range(nspan)]
-    down = [(j, i) for i, j in up]
-    slots = None
+    choose = near_pick = far_pick = None
     for step in range(ITERS):
         got = [send[0]] + [exchange(send[k], "plane", k) for k in range(1, nplane)]
         if step == 0:
-            owners = jnp.stack([partner(me[0], k, nplane)[1] for k in range(nplane)])
+            owners = jnp.stack([jnp.asarray(partner(me, k, nplane)[1], jnp.int32) for k in range(nplane)])
             known = jnp.concatenate([g[per:, :nfaces] for g in got], axis=0).astype(jnp.int32)
-            slots = jnp.sum(
-                jnp.where(owners[None, :, None] == jnp.arange(nplane)[:, None, None], known[None], 0), axis=1
-            ).astype(jnp.int32)
+            places = jnp.arange(nplane, dtype=jnp.int32)
+            slots = jnp.sum(jnp.where(owners[None, :, None] == places[:, None, None], known[None], 0), axis=1)
+            slots = slots.reshape(1, nplane, nplane, owned, P_SIZE)
+            by_owner = jnp.where(owners[:, None, None, None, None] == places[None, None, :, None, None], slots, 0)
+            face_row = jnp.swapaxes(jnp.sum(by_owner, axis=2), 1, 2).reshape(1, 1, -1)
+            device_row = jnp.broadcast_to(places[None, None, :, None], (nplane, owned, nplane, P_SIZE)).reshape(1, 1, -1)
+            there = jnp.clip(me + jnp.array([0, -1, 1], jnp.int32), 0, nplane - 1)[:, None, None]
+            choose = (device_row == there) & (face_row == jnp.arange(nfaces, dtype=jnp.int32)[None, :, None])
+            choose = jnp.tile(choose.reshape(3 * nfaces, -1), (1, 3)).astype(BF16)
         (solved,) = call(
             functools.partial(line_kernel, nplane, owned),
-            [me, *got, low, low_t, upp, piv_t],
+            [*got, *factors],
             [shape],
-            [pltpu.VMEM((owned, length, width), F32)],
-            flops=6 * nfaces * width * width,
+            scratch=[pltpu.VMEM((owned, length, width), F32)],
+            flops=6 * nfaces * area,
         )
-        pieces = [solved] + [exchange(solved, "plane", k) for k in range(1, nplane)]
+        if step == 0:
+            position = table_positions(lax.optimization_barrier((columns, solved))[0], nfaces)
+            selector, face = position // nfaces, position % nfaces
+            near_at = jnp.where(selector == 0, 0, jnp.where(selector >= 3, selector - 2, -nfaces)) * nfaces + face
+            far_at = jnp.where(
+                (selector == 1) | (selector == 2), jnp.where((selector == 1) == before_first, 0, 1), -nfaces
+            ) * nfaces + face
+            near_pick = one_hot(jnp.concatenate([near_at[:1], near_at[3:]], axis=0), 3 * nfaces, 2)
+            far_pick = one_hot(jnp.concatenate([far_at[1:3], far_at[5:]], axis=0), 2 * nfaces, 2)
+        pieces = [solved]
+        for k in range(1, nplane):
+            relayed = k % 2 and k > 1 and nplane & (nplane - 1) == 0
+            pieces.append(exchange(pieces[k - 1], "plane", 1) if relayed else exchange(solved, "plane", k))
         mine, sides = call(
-            functools.partial(faces_kernel, nplane, owned), [me, slots, *pieces], [shape, (2 * nfaces, width)]
+            functools.partial(faces_kernel, nplane), [choose, *pieces], [shape, (2 * nfaces, width)]
         )
         zs.append(mine)
-        before = lax.ppermute(mine, "span", up)
-        after = lax.ppermute(mine, "span", down)
+        other = lax.ppermute(mine, "span", others)
+        pair = lax.ppermute(mine, "span", pairs)
+        (near,) = call(
+            functools.partial(near_kernel, near_ks),
+            [blocks, near_pick, seg, mine, sides],
+            [shape],
+            [pl.ANY] + [pltpu.VMEM] * 4,
+            scratch(len(near_ks)),
+            flops=2 * len(near_ks) * nfaces * area,
+        )
         last = step == ITERS - 1
+        args = [blocks, line_slot, far_pick, seg, pair, other, near, *(us if last else us[-1:])]
         out = call(
-            functools.partial(apply_kernel, nplane, last),
-            [me, line_slot, blocks, pick, seg, mine, before, after, sides, *(us if last else us[-1:])],
-            [shape] + ([(16, 128)] if last else [(per, width)] * nplane),
-            [pltpu.VMEM((nblocks * nfaces, chunk), F32)],
-            flops=2 * nblocks * nfaces * width * width,
+            functools.partial(far_kernel, far_ks, nplane, last),
+            args,
+            [shape] + ([(1, 128)] if last else [(per, width)] * nplane),
+            [pl.ANY] + [pltpu.VMEM] * (len(args) - 1),
+            scratch(len(far_ks)) + ([] if last else [pltpu.SMEM(line_slot.shape, jnp.int32), pltpu.SemaphoreType.DMA]),
+            flops=2 * len(far_ks) * nfaces * area,
         )
         us.append(out[0])
         send = out[1:]
-    gram = add_up(add_up(send[0], "plane"), "span")
+    gram = add_up(send[0])
     sol, res, ok = call(finish_kernel, [gram, *us, *zs], [shape, shape, (1, 128)], pinned=False)
-    return lax.cond(
-        ok[0, 0] > 0.5,
-        lambda *_: (sol.T, res.T),
-        step_by_step,
-        rhs, blocks, columns, line_slot, line_lower, line_upper, pivot_inv,
+    given = (rhs, blocks, columns, line_slot, line_lower, line_upper, pivot_inv)
+    _, sol, res = lax.while_loop(
+        lambda state: state[0], lambda _: (jnp.array(False), *step_by_step(*given)), (ok[0, 0] < 0.5, sol.T, res.T)
     )
+    return sol, res
 
 
 def solution(mesh):

time: 87.1 us -> 82.3 us (0.945)
  Pallas kernels: 15.9 us -> 22.8 us
  starting transfers between devices: 30.2 us -> 24 us
  local copies, waits for them, and re-layouts: 6.95 us -> 1.81 us
  waiting for transfers between devices: 30.9 us -> 29.5 us
    ppermute x23 -> x18, waiting for transfers between devices: 26.3 us -> 12.7 us  [exchange(): lax.ppermute(x, axis, [(i, partner(i, k, size)[0]) for i in range(size)])]
    ppermute x6 -> x11, waiting for transfers between devices: 4.67 us -> 16.8 us  [the longest x5 14.7 us: add_up(): lax.ppermute(x, ('span', 'plane'), [(i, i ^ step) for i in range(count)])]
    pallas_call x11 -> x15, Pallas kernels: 15.9 us -> 22.8 us  [call(): pl.pallas_call(kernel, out_shape=[pltpu.VMEM(shape, F32) if pinned else j...]
    reshape x5 -> x0, local copies, waits for them, and re-layouts: 4.93 us -> none  [the longest x2 1.72 us: on_device(): piv_t = jnp.swapaxes(pivot_inv.reshape(nfaces, width, width), 1, 2)]
    ppermute x23 -> x18, starting transfers between devices: 15.7 us -> 11.6 us  [exchange(): lax.ppermute(x, axis, [(i, partner(i, k, size)[0]) for i in range(size)])]
    ppermute x6 -> x11, starting transfers between devices: 14.5 us -> 12.4 us  [the longest x3 9.21 us: on_device(): other = lax.ppermute(mine, 'span', others)]
  transfers between devices with their start and end apart: 29 -> 29, of which waited for: 17 -> 15; matrix products, arithmetic and copies ran while one was open for 7% -> 4% of each run, Pallas kernels for 0% -> 12%
where the time goes in v2:
time: 82.3 us; the launch traced here: 82 us
  waiting for transfers between devices  29.5 us (36%)
  starting transfers between devices  24 us (29%)
  Pallas kernels  22.8 us (28%)
  other arithmetic  2.35 us (3%)
  local copies, waits for them, and re-layouts  1.81 us (2%)
  between operations  1.27 us (2%)
    pallas_call x15, Pallas kernels, call(): pl.pallas_call(kernel, out_shape=[pltpu.VMEM(shape, F32) if pinned else j...  22.8 us
    ppermute x5, waiting for transfers between devices, add_up(): lax.ppermute(x, ('span', 'plane'), [(i, i ^ step) for i in range(count)])  14.7 us
    ppermute x18, waiting for transfers between devices, exchange(): lax.ppermute(x, axis, [(i, partner(i, k, size)[0]) for i in range(size)])  12.7 us
    ppermute x18, starting transfers between devices, exchange(): lax.ppermute(x, axis, [(i, partner(i, k, size)[0]) for i in range(size)])  11.6 us
    ppermute x3, starting transfers between devices, on_device(): other = lax.ppermute(mine, 'span', others)  9.21 us
    ppermute x3, waiting for transfers between devices, on_device(): other = lax.ppermute(mine, 'span', others)  2.08 us
    ppermute x3, starting transfers between devices, on_device(): pair = lax.ppermute(mine, 'span', pairs)  1.72 us
  transfers between devices with their start and end apart: 29, of which 15 were waited for; matrix products, arithmetic and copies ran while one was open for 4% of the time, Pallas kernels for 12%

profile of v2, /device:TPU:0, one launch (start us, length us, event | category | flops | bytes accessed | tf_op | source)
XLA Modules:
  0.0 82.0 jit_solution(16317137646225574597)
XLA Ops:
  2.0 2.6 %collective-permute-start.17 = (f32[5,80]{1,0:T(8,128)S(1)}, f32[5,80]{1,0:T(8,128)S(1)}, u32[]{:S(2)}, u32[]{:S(2)}) collective-permute-start(f32[5,80]{1,0:T(8,128)S(1)} %get-tuple-element.679), channel_id=1, source_target_pairs={{0,2},{1,3},{2,0},{3,1},{4,6},{5,7},{6,4},{7,5},{8,10},{9,11},{10,... | collective-permute-start | bytes 4808 | tf_op jit(solution)/shard_map/ppermute | solution.py:149
  5.7 2.3 %shard_map.105 = (f32[1280,80]{1,0:T(8,128)S(1)}, f32[1280,80]{1,0:T(8,128)S(1)}, f32[1280,80]{1,0:T(8,128)S(1)}) custom-call(f32[16,6400]{1,0:T(8,128)} %low.1, f32[16,6400]{1,0:T(8,128)} %upp.1, f32[16,6400]{1,0:T(8,128)} %piv.1), custom_call_target="tpu_custom_call" | custom-call | flops 102400 | bytes 1228800 | tf_op jit(solution)/shard_map/pallas_call | solution.py:383
  8.1 1.2 %shard_map.106.refs_0_ = f32[16,80]{1,0:T(8,128)S(1)} custom-call(f32[5,80]{1,0:T(8,128)S(1)} %get-tuple-element.677.refs_0_, f32[5,80]{1,0:T(8,128)S(1)} %collective-permute-done.16.refs_1_, f32[5,80]{1,0:T(8,128)S(1)} %collective-permute-done.17.refs_2_, f32[5,80]{1,0:T(8,128)S(1)} %collective-permute-done.18.refs_3_, f32[16,80,80]{2,1,0:T(8,128)S(1)} %bitcast.552, ...), custom_call_target="tpu_custom_call" | custom-call | flops 614400 | bytes 1235200 | tf_op jit(solution)/shard_map/pallas_call | solution.py:383
  9.3 1.8 %collective-permute-start.20 = (f32[16,80]{1,0:T(8,128)S(1)}, f32[16,80]{1,0:T(8,128)S(1)}, u32[]{:S(2)}, u32[]{:S(2)}) collective-permute-start(f32[16,80]{1,0:T(8,128)S(1)} %shard_map.106.refs_0_), channel_id=1, source_target_pairs={{0,2},{1,3},{2,0},{3,1},{4,6},{5,7},{6,4},{7,5},{8,10},{9,11},{10,... | collective-permute-start | bytes 15368 | tf_op jit(solution)/shard_map/ppermute | solution.py:149
  14.7 1.5 %collective-permute-start.22 = (f32[16,80]{1,0:T(8,128)S(1)}, f32[16,80]{1,0:T(8,128)S(1)}, u32[]{:S(2)}, u32[]{:S(2)}) collective-permute-start(f32[16,80]{1,0:T(8,128)S(1)} %get-tuple-element.685.mine.refs_4_), channel_id=1, source_target_pairs={{0,4},{4,0},{8,12},{12,8},{16,20},{20,16},{24,28},{28,24},{1,5},{5... | collective-permute-start | bytes 15368 | tf_op jit(solution)/shard_map/ppermute | solution.py:503
  16.2 3.6 %collective-permute-start.23 = (f32[16,80]{1,0:T(8,128)S(1)}, f32[16,80]{1,0:T(8,128)S(1)}, u32[]{:S(2)}, u32[]{:S(2)}) collective-permute-start(f32[16,80]{1,0:T(8,128)S(1)} %get-tuple-element.685.mine.refs_4_), channel_id=1, source_target_pairs={{0,28},{4,8},{8,4},{12,16},{16,12},{20,24},{24,20},{28,0},{1,29},{... | collective-permute-start | bytes 15368 | tf_op jit(solution)/shard_map/ppermute | solution.py:502
  20.7 2.5 %shard_map.108.refs_6_ = f32[16,80]{1,0:T(8,128)S(1)} custom-call(f32[16,70400]{1,0:T(8,128)} %refs_0_.5, bf16[144,96]{1,0:T(8,128)(2,1)S(1)} %compare_convert_fusion.pick, bf16[640,128]{1,0:T(8,128)(2,1)S(1)} %copy-done.1, f32[16,80]{1,0:T(8,128)S(1)} %get-tuple-element.685.mine.refs_4_, f32[32,80]{1,0:T(8,128)S(1)} %get-tuple-element.686.sides), custom_call_target="tpu_custom_call" | custom-call | flops 1843200 | bytes 4712448 | tf_op jit(solution)/shard_map/pallas_call | solution.py:383
  23.3 2.4 %shard_map.109 = (f32[16,80]{1,0:T(8,128)S(1)}, f32[4,80]{1,0:T(4,128)S(1)}, f32[4,80]{1,0:T(4,128)S(1)}, f32[4,80]{1,0:T(4,128)S(1)}, f32[4,80]{1,0:T(4,128)S(1)}) custom-call(f32[16,70400]{1,0:T(8,128)} %refs_0_.5, s32[1,16]{1,0:T(1,128)S(1)} %copy-done.3, bf16[128,64]{1,0:T(8,128)(2,1)S(1)} %compare_convert_fusion.1.refs_2_, ...), custom_call_target="tpu_custom_call" | custom-call | flops 1638400 | bytes 4706368 | tf_op jit(solution)/shard_map/pallas_call | solution.py:383
  25.8 1.5 %collective-permute-start.25 = (f32[4,80]{1,0:T(4,128)S(1)}, f32[4,80]{1,0:T(4,128)S(1)}, u32[]{:S(2)}, u32[]{:S(2)}) collective-permute-start(f32[4,80]{1,0:T(4,128)S(1)} %get-tuple-element.689), channel_id=1, source_target_pairs={{0,2},{1,3},{2,0},{3,1},{4,6},{5,7},{6,4},{7,5},{8,10},{9,11},{10,... | collective-permute-start | bytes 3848 | tf_op jit(solution)/shard_map/ppermute | solution.py:149
  27.6 1.8 %collective-permute-done.25.refs_2_ = f32[4,80]{1,0:T(4,128)S(1)} collective-permute-done((f32[4,80]{1,0:T(4,128)S(1)}, f32[4,80]{1,0:T(4,128)S(1)}, u32[]{:S(2)}, u32[]{:S(2)}) %collective-permute-start.25) | collective-permute-done | bytes 1312 | tf_op jit(solution)/shard_map/ppermute | solution.py:149
  30.2 1.2 %shard_map.110.refs_0_ = f32[16,80]{1,0:T(8,128)S(1)} custom-call(f32[4,80]{1,0:T(4,128)S(1)} %get-tuple-element.687.refs_0_, f32[4,80]{1,0:T(4,128)S(1)} %collective-permute-done.24.refs_1_, f32[4,80]{1,0:T(4,128)S(1)} %collective-permute-done.25.refs_2_, f32[4,80]{1,0:T(4,128)S(1)} %collective-permute-done.26.refs_3_, f32[16,80,80]{2,1,0:T(8,128)S(1)} %bitcast.553, ...), custom_call_target="tpu_custom_call" | custom-call | flops 614400 | bytes 1233920 | tf_op jit(solution)/shard_map/pallas_call | solution.py:383
  32.2 3.0 %collective-permute-done.28.refs_2_ = f32[16,80]{1,0:T(8,128)S(1)} collective-permute-done((f32[16,80]{1,0:T(8,128)S(1)}, f32[16,80]{1,0:T(8,128)S(1)}, u32[]{:S(2)}, u32[]{:S(2)}) %collective-permute-start.28) | collective-permute-done | bytes 5152 | tf_op jit(solution)/shard_map/ppermute | solution.py:149
  35.2 1.2 %collective-permute-done.29.refs_3_ = f32[16,80]{1,0:T(8,128)S(1)} collective-permute-done((f32[16,80]{1,0:T(8,128)S(1)}, f32[16,80]{1,0:T(8,128)S(1)}, u32[]{:S(2)}, u32[]{:S(2)}) %collective-permute-start.29) | collective-permute-done | bytes 5152 | tf_op jit(solution)/shard_map/ppermute | solution.py:149
  36.5 2.8 %collective-permute-start.31 = (f32[16,80]{1,0:T(8,128)S(1)}, f32[16,80]{1,0:T(8,128)S(1)}, u32[]{:S(2)}, u32[]{:S(2)}) collective-permute-start(f32[16,80]{1,0:T(8,128)S(1)} %get-tuple-element.691.mine.refs_5_), channel_id=1, source_target_pairs={{0,28},{4,8},{8,4},{12,16},{16,12},{20,24},{24,20},{28,0},{1,29},{... | collective-permute-start | bytes 15368 | tf_op jit(solution)/shard_map/ppermute | solution.py:502
  39.3 2.5 %shard_map.112.refs_6_ = f32[16,80]{1,0:T(8,128)S(1)} custom-call(f32[16,70400]{1,0:T(8,128)} %refs_0_.5, bf16[144,96]{1,0:T(8,128)(2,1)S(1)} %compare_convert_fusion.pick, bf16[640,128]{1,0:T(8,128)(2,1)S(1)} %copy-done.2, f32[16,80]{1,0:T(8,128)S(1)} %get-tuple-element.691.mine.refs_5_, f32[32,80]{1,0:T(8,128)S(1)} %get-tuple-element.692.sides), custom_call_target="tpu_custom_call" | custom-call | flops 1843200 | bytes 4712448 | tf_op jit(solution)/shard_map/pallas_call | solution.py:383
  41.9 1.0 %collective-permute-done.31.refs_5_ = f32[16,80]{1,0:T(8,128)S(1)} collective-permute-done((f32[16,80]{1,0:T(8,128)S(1)}, f32[16,80]{1,0:T(8,128)S(1)}, u32[]{:S(2)}, u32[]{:S(2)}) %collective-permute-start.31) | collective-permute-done | bytes 5152 | tf_op jit(solution)/shard_map/ppermute | solution.py:502
  42.9 2.4 %shard_map.113 = (f32[16,80]{1,0:T(8,128)S(1)}, f32[4,80]{1,0:T(4,128)S(1)}, f32[4,80]{1,0:T(4,128)S(1)}, f32[4,80]{1,0:T(4,128)S(1)}, f32[4,80]{1,0:T(4,128)S(1)}) custom-call(f32[16,70400]{1,0:T(8,128)} %refs_0_.5, s32[1,16]{1,0:T(1,128)S(1)} %copy-done.3, bf16[128,64]{1,0:T(8,128)(2,1)S(1)} %compare_convert_fusion.1.refs_2_, ...), custom_call_target="tpu_custom_call" | custom-call | flops 1638400 | bytes 4706368 | tf_op jit(solution)/shard_map/pallas_call | solution.py:383
  46.1 1.2 %collective-permute-start.34 = (f32[4,80]{1,0:T(4,128)S(1)}, f32[4,80]{1,0:T(4,128)S(1)}, u32[]{:S(2)}, u32[]{:S(2)}) collective-permute-start(f32[4,80]{1,0:T(4,128)S(1)} %get-tuple-element.697), channel_id=1, source_target_pairs={{0,3},{1,2},{2,1},{3,0},{4,7},{5,6},{6,5},{7,4},{8,11},{9,10},{10,... | collective-permute-start | bytes 3848 | tf_op jit(solution)/shard_map/ppermute | solution.py:149
  47.3 1.8 %collective-permute-done.33.refs_2_ = f32[4,80]{1,0:T(4,128)S(1)} collective-permute-done((f32[4,80]{1,0:T(4,128)S(1)}, f32[4,80]{1,0:T(4,128)S(1)}, u32[]{:S(2)}, u32[]{:S(2)}) %collective-permute-start.33) | collective-permute-done | bytes 1312 | tf_op jit(solution)/shard_map/ppermute | solution.py:149
  49.1 1.2 %shard_map.114.refs_0_ = f32[16,80]{1,0:T(8,128)S(1)} custom-call(f32[4,80]{1,0:T(4,128)S(1)} %get-tuple-element.694.refs_0_, f32[4,80]{1,0:T(4,128)S(1)} %collective-permute-done.32.refs_1_, f32[4,80]{1,0:T(4,128)S(1)} %collective-permute-done.33.refs_2_, f32[4,80]{1,0:T(4,128)S(1)} %collective-permute-done.34.refs_3_, f32[16,80,80]{2,1,0:T(8,128)S(1)} %bitcast.554, ...), custom_call_target="tpu_custom_call" | custom-call | flops 614400 | bytes 1233920 | tf_op jit(solution)/shard_map/pallas_call | solution.py:383
  50.4 1.5 %collective-permute-start.36 = (f32[16,80]{1,0:T(8,128)S(1)}, f32[16,80]{1,0:T(8,128)S(1)}, u32[]{:S(2)}, u32[]{:S(2)}) collective-permute-start(f32[16,80]{1,0:T(8,128)S(1)} %shard_map.114.refs_0_), channel_id=1, source_target_pairs={{0,2},{1,3},{2,0},{3,1},{4,6},{5,7},{6,4},{7,5},{8,10},{9,11},{10,... | collective-permute-start | bytes 15368 | tf_op jit(solution)/shard_map/ppermute | solution.py:149
  51.8 2.2 %collective-permute-done.36.refs_2_ = f32[16,80]{1,0:T(8,128)S(1)} collective-permute-done((f32[16,80]{1,0:T(8,128)S(1)}, f32[16,80]{1,0:T(8,128)S(1)}, u32[]{:S(2)}, u32[]{:S(2)}) %collective-permute-start.36) | collective-permute-done | bytes 5152 | tf_op jit(solution)/shard_map/ppermute | solution.py:149
  54.1 1.2 %collective-permute-done.37.refs_3_ = f32[16,80]{1,0:T(8,128)S(1)} collective-permute-done((f32[16,80]{1,0:T(8,128)S(1)}, f32[16,80]{1,0:T(8,128)S(1)}, u32[]{:S(2)}, u32[]{:S(2)}) %collective-permute-start.37) | collective-permute-done | bytes 5152 | tf_op jit(solution)/shard_map/ppermute | solution.py:149
  55.6 2.8 %collective-permute-start.39 = (f32[16,80]{1,0:T(8,128)S(1)}, f32[16,80]{1,0:T(8,128)S(1)}, u32[]{:S(2)}, u32[]{:S(2)}) collective-permute-start(f32[16,80]{1,0:T(8,128)S(1)} %get-tuple-element.698.mine.refs_6_), channel_id=1, source_target_pairs={{0,28},{4,8},{8,4},{12,16},{16,12},{20,24},{24,20},{28,0},{1,29},{... | collective-permute-start | bytes 15368 | tf_op jit(solution)/shard_map/ppermute | solution.py:502
  58.4 2.5 %shard_map.116.refs_6_ = f32[16,80]{1,0:T(8,128)S(1)} custom-call(f32[16,70400]{1,0:T(8,128)} %refs_0_.5, bf16[144,96]{1,0:T(8,128)(2,1)S(1)} %compare_convert_fusion.pick, bf16[640,128]{1,0:T(8,128)(2,1)S(1)} %copy-done.2, f32[16,80]{1,0:T(8,128)S(1)} %get-tuple-element.698.mine.refs_6_, f32[32,80]{1,0:T(8,128)S(1)} %get-tuple-element.699.sides), custom_call_target="tpu_custom_call" | custom-call | flops 1843200 | bytes 4712448 | tf_op jit(solution)/shard_map/pallas_call | solution.py:383
  61.9 2.4 %shard_map.117 = (f32[16,80]{1,0:T(8,128)S(1)}, f32[1,128]{1,0:T(1,128)S(1)}) custom-call(f32[16,70400]{1,0:T(8,128)} %refs_0_.5, s32[1,16]{1,0:T(1,128)S(1)} %copy-done.3, bf16[128,64]{1,0:T(8,128)(2,1)S(1)} %compare_convert_fusion.1.refs_2_, bf16[640,128]{1,0:T(8,128)(2,1)S(1)} %copy-done.2, f32[16,80]{1,0:T(8,128)S(1)} %collective-permute-done.38.refs_4_, ...), custom_call_target="tpu_custom_call" | custom-call | flops 1638400 | bytes 4716608 | tf_op jit(solution)/shard_map/pallas_call | solution.py:383
  64.5 1.1 %collective-permute-done.40 = f32[1,128]{1,0:T(1,128)S(1)} collective-permute-done((f32[1,128]{1,0:T(1,128)S(1)}, f32[1,128]{1,0:T(1,128)S(1)}, u32[]{:S(2)}, u32[]{:S(2)}) %collective-permute-start.40) | collective-permute-done | bytes 544 | tf_op jit(solution)/shard_map/ppermute | solution.py:400
  65.6 1.4 %collective-permute-start.41 = (f32[1,128]{1,0:T(1,128)S(1)}, f32[1,128]{1,0:T(1,128)S(1)}, u32[]{:S(2)}, u32[]{:S(2)}) collective-permute-start(f32[1,128]{1,0:T(1,128)S(1)} %add.326), channel_id=1, source_target_pairs={{0,2},{1,3},{2,0},{3,1},{4,6},{5,7},{6,4},{7,5},{8,10},{9,11},{10,... | collective-permute-start | bytes 1544 | tf_op jit(solution)/shard_map/ppermute | solution.py:400
  67.0 2.1 %collective-permute-done.41 = f32[1,128]{1,0:T(1,128)S(1)} collective-permute-done((f32[1,128]{1,0:T(1,128)S(1)}, f32[1,128]{1,0:T(1,128)S(1)}, u32[]{:S(2)}, u32[]{:S(2)}) %collective-permute-start.41) | collective-permute-done | bytes 544 | tf_op jit(solution)/shard_map/ppermute | solution.py:400
  69.1 3.5 %collective-permute-done.42 = f32[1,128]{1,0:T(1,128)S(1)} collective-permute-done((f32[1,128]{1,0:T(1,128)S(1)}, f32[1,128]{1,0:T(1,128)S(1)}, u32[]{:S(2)}, u32[]{:S(2)}) %collective-permute-start.42) | collective-permute-done | bytes 544 | tf_op jit(solution)/shard_map/ppermute | solution.py:400
  72.7 3.5 %collective-permute-done.43 = f32[1,128]{1,0:T(1,128)S(1)} collective-permute-done((f32[1,128]{1,0:T(1,128)S(1)}, f32[1,128]{1,0:T(1,128)S(1)}, u32[]{:S(2)}, u32[]{:S(2)}) %collective-permute-start.43) | collective-permute-done | bytes 544 | tf_op jit(solution)/shard_map/ppermute | solution.py:400
  76.2 4.4 %collective-permute-done.44 = f32[1,128]{1,0:T(1,128)S(1)} collective-permute-done((f32[1,128]{1,0:T(1,128)S(1)}, f32[1,128]{1,0:T(1,128)S(1)}, u32[]{:S(2)}, u32[]{:S(2)}) %collective-permute-start.44) | collective-permute-done | bytes 544 | tf_op jit(solution)/shard_map/ppermute | solution.py:400
  (96 shorter events, 12.4 us)
Async XLA Ops:
  1.5 6.5 %collective-permute-start.16 = (f32[5,80]{1,0:T(8,128)S(1)}, f32[5,80]{1,0:T(8,128)S(1)}, u32[]{:S(2)}, u32[]{:S(2)}) collective-permute-start(f32[5,80]{1,0:T(8,128)S(1)} %get-tuple-element.678), channel_id=1, source_target_pairs={{0,1},{1,0},{2,3},{3,2},{4,5},{5,4},{6,7},{7,6},{8,9},{9,8},{10,11... | collective-permute-start | bytes 4808 | tf_op jit(solution)/shard_map/ppermute | solution.py:149
  2.0 6.0 %collective-permute-start.17 = (f32[5,80]{1,0:T(8,128)S(1)}, f32[5,80]{1,0:T(8,128)S(1)}, u32[]{:S(2)}, u32[]{:S(2)}) collective-permute-start(f32[5,80]{1,0:T(8,128)S(1)} %get-tuple-element.679), channel_id=1, source_target_pairs={{0,2},{1,3},{2,0},{3,1},{4,6},{5,7},{6,4},{7,5},{8,10},{9,11},{10,... | collective-permute-start | bytes 4808 | tf_op jit(solution)/shard_map/ppermute | solution.py:149
  4.6 3.4 %collective-permute-start.18 = (f32[5,80]{1,0:T(8,128)S(1)}, f32[5,80]{1,0:T(8,128)S(1)}, u32[]{:S(2)}, u32[]{:S(2)}) collective-permute-start(f32[5,80]{1,0:T(8,128)S(1)} %get-tuple-element.680), channel_id=1, source_target_pairs={{0,3},{1,2},{2,1},{3,0},{4,7},{5,6},{6,5},{7,4},{8,11},{9,10},{10,... | collective-permute-start | bytes 4808 | tf_op jit(solution)/shard_map/ppermute | solution.py:149
  9.3 3.9 %collective-permute-start.20 = (f32[16,80]{1,0:T(8,128)S(1)}, f32[16,80]{1,0:T(8,128)S(1)}, u32[]{:S(2)}, u32[]{:S(2)}) collective-permute-start(f32[16,80]{1,0:T(8,128)S(1)} %shard_map.106.refs_0_), channel_id=1, source_target_pairs={{0,2},{1,3},{2,0},{3,1},{4,6},{5,7},{6,4},{7,5},{8,10},{9,11},{10,... | collective-permute-start | bytes 15368 | tf_op jit(solution)/shard_map/ppermute | solution.py:149
  11.1 2.8 %collective-permute-start.19 = (f32[16,80]{1,0:T(8,128)S(1)}, f32[16,80]{1,0:T(8,128)S(1)}, u32[]{:S(2)}, u32[]{:S(2)}) collective-permute-start(f32[16,80]{1,0:T(8,128)S(1)} %shard_map.106.refs_0_), channel_id=1, source_target_pairs={{0,1},{1,0},{2,3},{3,2},{4,5},{5,4},{6,7},{7,6},{8,9},{9,8},{10,11... | collective-permute-start | bytes 15368 | tf_op jit(solution)/shard_map/ppermute | solution.py:149
  13.2 1.3 %collective-permute-start.21 = (f32[16,80]{1,0:T(8,128)S(1)}, f32[16,80]{1,0:T(8,128)S(1)}, u32[]{:S(2)}, u32[]{:S(2)}) collective-permute-start(f32[16,80]{1,0:T(8,128)S(1)} %collective-permute-done.20.refs_2_), channel_id=1, source_target_pairs={{0,1},{1,0},{2,3},{3,2},{4,5},{5,4},{6,7},{7,6},{8,9},{9,8},{10,11... | collective-permute-start | bytes 15368 | tf_op jit(solution)/shard_map/ppermute | solution.py:149
  14.7 8.6 %collective-permute-start.22 = (f32[16,80]{1,0:T(8,128)S(1)}, f32[16,80]{1,0:T(8,128)S(1)}, u32[]{:S(2)}, u32[]{:S(2)}) collective-permute-start(f32[16,80]{1,0:T(8,128)S(1)} %get-tuple-element.685.mine.refs_4_), channel_id=1, source_target_pairs={{0,4},{4,0},{8,12},{12,8},{16,20},{20,16},{24,28},{28,24},{1,5},{5... | collective-permute-start | bytes 15368 | tf_op jit(solution)/shard_map/ppermute | solution.py:503
  16.2 7.1 %collective-permute-start.23 = (f32[16,80]{1,0:T(8,128)S(1)}, f32[16,80]{1,0:T(8,128)S(1)}, u32[]{:S(2)}, u32[]{:S(2)}) collective-permute-start(f32[16,80]{1,0:T(8,128)S(1)} %get-tuple-element.685.mine.refs_4_), channel_id=1, source_target_pairs={{0,28},{4,8},{8,4},{12,16},{16,12},{20,24},{24,20},{28,0},{1,29},{... | collective-permute-start | bytes 15368 | tf_op jit(solution)/shard_map/ppermute | solution.py:502
  25.7 1.9 %collective-permute-start.24 = (f32[4,80]{1,0:T(4,128)S(1)}, f32[4,80]{1,0:T(4,128)S(1)}, u32[]{:S(2)}, u32[]{:S(2)}) collective-permute-start(f32[4,80]{1,0:T(4,128)S(1)} %get-tuple-element.688), channel_id=1, source_target_pairs={{0,1},{1,0},{2,3},{3,2},{4,5},{5,4},{6,7},{7,6},{8,9},{9,8},{10,11... | collective-permute-start | bytes 3848 | tf_op jit(solution)/shard_map/ppermute | solution.py:149
  25.8 3.7 %collective-permute-start.25 = (f32[4,80]{1,0:T(4,128)S(1)}, f32[4,80]{1,0:T(4,128)S(1)}, u32[]{:S(2)}, u32[]{:S(2)}) collective-permute-start(f32[4,80]{1,0:T(4,128)S(1)} %get-tuple-element.689), channel_id=1, source_target_pairs={{0,2},{1,3},{2,0},{3,1},{4,6},{5,7},{6,4},{7,5},{8,10},{9,11},{10,... | collective-permute-start | bytes 3848 | tf_op jit(solution)/shard_map/ppermute | solution.py:149
  27.2 3.0 %collective-permute-start.26 = (f32[4,80]{1,0:T(4,128)S(1)}, f32[4,80]{1,0:T(4,128)S(1)}, u32[]{:S(2)}, u32[]{:S(2)}) collective-permute-start(f32[4,80]{1,0:T(4,128)S(1)} %get-tuple-element.690), channel_id=1, source_target_pairs={{0,3},{1,2},{2,1},{3,0},{4,7},{5,6},{6,5},{7,4},{8,11},{9,10},{10,... | collective-permute-start | bytes 3848 | tf_op jit(solution)/shard_map/ppermute | solution.py:149
  31.5 3.7 %collective-permute-start.28 = (f32[16,80]{1,0:T(8,128)S(1)}, f32[16,80]{1,0:T(8,128)S(1)}, u32[]{:S(2)}, u32[]{:S(2)}) collective-permute-start(f32[16,80]{1,0:T(8,128)S(1)} %shard_map.110.refs_0_), channel_id=1, source_target_pairs={{0,2},{1,3},{2,0},{3,1},{4,6},{5,7},{6,4},{7,5},{8,10},{9,11},{10,... | collective-permute-start | bytes 15368 | tf_op jit(solution)/shard_map/ppermute | solution.py:149
  32.2 3.0 %collective-permute-start.27 = (f32[16,80]{1,0:T(8,128)S(1)}, f32[16,80]{1,0:T(8,128)S(1)}, u32[]{:S(2)}, u32[]{:S(2)}) collective-permute-start(f32[16,80]{1,0:T(8,128)S(1)} %shard_map.110.refs_0_), channel_id=1, source_target_pairs={{0,1},{1,0},{2,3},{3,2},{4,5},{5,4},{6,7},{7,6},{8,9},{9,8},{10,11... | collective-permute-start | bytes 15368 | tf_op jit(solution)/shard_map/ppermute | solution.py:149
  35.2 1.2 %collective-permute-start.29 = (f32[16,80]{1,0:T(8,128)S(1)}, f32[16,80]{1,0:T(8,128)S(1)}, u32[]{:S(2)}, u32[]{:S(2)}) collective-permute-start(f32[16,80]{1,0:T(8,128)S(1)} %collective-permute-done.28.refs_2_), channel_id=1, source_target_pairs={{0,1},{1,0},{2,3},{3,2},{4,5},{5,4},{6,7},{7,6},{8,9},{9,8},{10,11... | collective-permute-start | bytes 15368 | tf_op jit(solution)/shard_map/ppermute | solution.py:149
  36.5 5.3 %collective-permute-start.30 = (f32[16,80]{1,0:T(8,128)S(1)}, f32[16,80]{1,0:T(8,128)S(1)}, u32[]{:S(2)}, u32[]{:S(2)}) collective-permute-start(f32[16,80]{1,0:T(8,128)S(1)} %get-tuple-element.691.mine.refs_5_), channel_id=1, source_target_pairs={{0,4},{4,0},{8,12},{12,8},{16,20},{20,16},{24,28},{28,24},{1,5},{5... | collective-permute-start | bytes 15368 | tf_op jit(solution)/shard_map/ppermute | solution.py:503
  36.5 6.4 %collective-permute-start.31 = (f32[16,80]{1,0:T(8,128)S(1)}, f32[16,80]{1,0:T(8,128)S(1)}, u32[]{:S(2)}, u32[]{:S(2)}) collective-permute-start(f32[16,80]{1,0:T(8,128)S(1)} %get-tuple-element.691.mine.refs_5_), channel_id=1, source_target_pairs={{0,28},{4,8},{8,4},{12,16},{16,12},{20,24},{24,20},{28,0},{1,29},{... | collective-permute-start | bytes 15368 | tf_op jit(solution)/shard_map/ppermute | solution.py:502
  42.9 38.6 %copy-start.4 = (f32[16,6400]{1,0:T(8,128)S(1)}, f32[16,6400]{1,0:T(8,128)}, u32[]{:S(2)}) copy-start(f32[16,6400]{1,0:T(8,128)} %low.1) | copy-start | bytes 1228804
  42.9 38.6 %copy-start.5 = (f32[16,6400]{1,0:T(8,128)S(1)}, f32[16,6400]{1,0:T(8,128)}, u32[]{:S(2)}) copy-start(f32[16,6400]{1,0:T(8,128)} %upp.1) | copy-start | bytes 1228804
  42.9 38.6 %copy-start.6 = (s32[11,16]{1,0:T(8,128)S(1)}, s32[11,16]{1,0:T(8,128)}, u32[]{:S(2)}) copy-start(s32[11,16]{1,0:T(8,128)} %param.29) | copy-start | bytes 2116
  45.3 1.9 %collective-permute-start.32 = (f32[4,80]{1,0:T(4,128)S(1)}, f32[4,80]{1,0:T(4,128)S(1)}, u32[]{:S(2)}, u32[]{:S(2)}) collective-permute-start(f32[4,80]{1,0:T(4,128)S(1)} %get-tuple-element.695), channel_id=1, source_target_pairs={{0,1},{1,0},{2,3},{3,2},{4,5},{5,4},{6,7},{7,6},{8,9},{9,8},{10,11... | collective-permute-start | bytes 3848 | tf_op jit(solution)/shard_map/ppermute | solution.py:149
  45.4 3.7 %collective-permute-start.33 = (f32[4,80]{1,0:T(4,128)S(1)}, f32[4,80]{1,0:T(4,128)S(1)}, u32[]{:S(2)}, u32[]{:S(2)}) collective-permute-start(f32[4,80]{1,0:T(4,128)S(1)} %get-tuple-element.696), channel_id=1, source_target_pairs={{0,2},{1,3},{2,0},{3,1},{4,6},{5,7},{6,4},{7,5},{8,10},{9,11},{10,... | collective-permute-start | bytes 3848 | tf_op jit(solution)/shard_map/ppermute | solution.py:149
  46.1 3.0 %collective-permute-start.34 = (f32[4,80]{1,0:T(4,128)S(1)}, f32[4,80]{1,0:T(4,128)S(1)}, u32[]{:S(2)}, u32[]{:S(2)}) collective-permute-start(f32[4,80]{1,0:T(4,128)S(1)} %get-tuple-element.697), channel_id=1, source_target_pairs={{0,3},{1,2},{2,1},{3,0},{4,7},{5,6},{6,5},{7,4},{8,11},{9,10},{10,... | collective-permute-start | bytes 3848 | tf_op jit(solution)/shard_map/ppermute | solution.py:149
  50.4 3.7 %collective-permute-start.36 = (f32[16,80]{1,0:T(8,128)S(1)}, f32[16,80]{1,0:T(8,128)S(1)}, u32[]{:S(2)}, u32[]{:S(2)}) collective-permute-start(f32[16,80]{1,0:T(8,128)S(1)} %shard_map.114.refs_0_), channel_id=1, source_target_pairs={{0,2},{1,3},{2,0},{3,1},{4,6},{5,7},{6,4},{7,5},{8,10},{9,11},{10,... | collective-permute-start | bytes 15368 | tf_op jit(solution)/shard_map/ppermute | solution.py:149
  51.8 2.2 %collective-permute-start.35 = (f32[16,80]{1,0:T(8,128)S(1)}, f32[16,80]{1,0:T(8,128)S(1)}, u32[]{:S(2)}, u32[]{:S(2)}) collective-permute-start(f32[16,80]{1,0:T(8,128)S(1)} %shard_map.114.refs_0_), channel_id=1, source_target_pairs={{0,1},{1,0},{2,3},{3,2},{4,5},{5,4},{6,7},{7,6},{8,9},{9,8},{10,11... | collective-permute-start | bytes 15368 | tf_op jit(solution)/shard_map/ppermute | solution.py:149
  54.1 1.2 %collective-permute-start.37 = (f32[16,80]{1,0:T(8,128)S(1)}, f32[16,80]{1,0:T(8,128)S(1)}, u32[]{:S(2)}, u32[]{:S(2)}) collective-permute-start(f32[16,80]{1,0:T(8,128)S(1)} %collective-permute-done.36.refs_2_), channel_id=1, source_target_pairs={{0,1},{1,0},{2,3},{3,2},{4,5},{5,4},{6,7},{7,6},{8,9},{9,8},{10,11... | collective-permute-start | bytes 15368 | tf_op jit(solution)/shard_map/ppermute | solution.py:149
  55.4 5.5 %collective-permute-start.38 = (f32[16,80]{1,0:T(8,128)S(1)}, f32[16,80]{1,0:T(8,128)S(1)}, u32[]{:S(2)}, u32[]{:S(2)}) collective-permute-start(f32[16,80]{1,0:T(8,128)S(1)} %get-tuple-element.698.mine.refs_6_), channel_id=1, source_target_pairs={{0,4},{4,0},{8,12},{12,8},{16,20},{20,16},{24,28},{28,24},{1,5},{5... | collective-permute-start | bytes 15368 | tf_op jit(solution)/shard_map/ppermute | solution.py:503
  55.6 6.3 %collective-permute-start.39 = (f32[16,80]{1,0:T(8,128)S(1)}, f32[16,80]{1,0:T(8,128)S(1)}, u32[]{:S(2)}, u32[]{:S(2)}) collective-permute-start(f32[16,80]{1,0:T(8,128)S(1)} %get-tuple-element.698.mine.refs_6_), channel_id=1, source_target_pairs={{0,28},{4,8},{8,4},{12,16},{16,12},{20,24},{24,20},{28,0},{1,29},{... | collective-permute-start | bytes 15368 | tf_op jit(solution)/shard_map/ppermute | solution.py:502
  64.4 1.2 %collective-permute-start.40 = (f32[1,128]{1,0:T(1,128)S(1)}, f32[1,128]{1,0:T(1,128)S(1)}, u32[]{:S(2)}, u32[]{:S(2)}) collective-permute-start(f32[1,128]{1,0:T(1,128)S(1)} %get-tuple-element.701), channel_id=1, source_target_pairs={{0,1},{1,0},{2,3},{3,2},{4,5},{5,4},{6,7},{7,6},{8,9},{9,8},{10,11... | collective-permute-start | bytes 1544 | tf_op jit(solution)/shard_map/ppermute | solution.py:400
  65.6 3.5 %collective-permute-start.41 = (f32[1,128]{1,0:T(1,128)S(1)}, f32[1,128]{1,0:T(1,128)S(1)}, u32[]{:S(2)}, u32[]{:S(2)}) collective-permute-start(f32[1,128]{1,0:T(1,128)S(1)} %add.326), channel_id=1, source_target_pairs={{0,2},{1,3},{2,0},{3,1},{4,6},{5,7},{6,4},{7,5},{8,10},{9,11},{10,... | collective-permute-start | bytes 1544 | tf_op jit(solution)/shard_map/ppermute | solution.py:400
  69.1 3.5 %collective-permute-start.42 = (f32[1,128]{1,0:T(1,128)S(1)}, f32[1,128]{1,0:T(1,128)S(1)}, u32[]{:S(2)}, u32[]{:S(2)}) collective-permute-start(f32[1,128]{1,0:T(1,128)S(1)} %add.327), channel_id=1, source_target_pairs={{0,4},{1,5},{2,6},{3,7},{4,0},{5,1},{6,2},{7,3},{8,12},{9,13},{10,... | collective-permute-start | bytes 1544 | tf_op jit(solution)/shard_map/ppermute | solution.py:400
  72.7 3.5 %collective-permute-start.43 = (f32[1,128]{1,0:T(1,128)S(1)}, f32[1,128]{1,0:T(1,128)S(1)}, u32[]{:S(2)}, u32[]{:S(2)}) collective-permute-start(f32[1,128]{1,0:T(1,128)S(1)} %add.328), channel_id=1, source_target_pairs={{0,8},{1,9},{2,10},{3,11},{4,12},{5,13},{6,14},{7,15},{8,0},{9,1},... | collective-permute-start | bytes 1544 | tf_op jit(solution)/shard_map/ppermute | solution.py:400
  76.2 4.4 %collective-permute-start.44 = (f32[1,128]{1,0:T(1,128)S(1)}, f32[1,128]{1,0:T(1,128)S(1)}, u32[]{:S(2)}, u32[]{:S(2)}) collective-permute-start(f32[1,128]{1,0:T(1,128)S(1)} %add.329), channel_id=1, source_target_pairs={{0,16},{1,17},{2,18},{3,19},{4,20},{5,21},{6,22},{7,23},{8,24},{9,... | collective-permute-start | bytes 1544 | tf_op jit(solution)/shard_map/ppermute | solution.py:400
  (4 other events, 68.8 us)

commit v3 on v2

--- a/solution.py
+++ b/solution.py
@@ -158,18 +158,12 @@
 
 
 def start_kernel(nplane, slot_ref, u_ref, *outs):
-    nfaces, width = u_ref.shape
-    per = nfaces // nplane
+    per = outs[0].shape[0]
     me = lax.axis_index("plane")
-    lane = lax.broadcasted_iota(jnp.int32, (1, width), 1)
-    tail = jnp.zeros((1, width), F32)
-    for t in range(nfaces):
-        tail = jnp.where(lane == t, slot_ref[0, t].astype(F32), tail)
     for k in range(nplane):
         to, _ = partner(me, k, nplane)
         for i in range(per):
             outs[k][pl.ds(i, 1), :] = u_ref[pl.ds(slot_ref[0, to * per + i], 1), :]
-        outs[k][pl.ds(per, 1), :] = tail
 
 
 def square_kernel(length, low, upp, piv, low_out, upp_out, piv_out):
@@ -189,9 +183,8 @@
 
 
 def line_kernel(nplane, nlines, *refs):
-    msgs, (low, upp, piv_t, z_ref, r_scr) = refs[:nplane], refs[nplane:]
-    width = z_ref.shape[1]
-    length = z_ref.shape[0] // nlines
+    msgs, (low, upp, piv_t), outs, (r_scr, z_scr) = refs[:nplane], refs[nplane:-nplane-2], refs[-nplane-2:-2], refs[-2:]
+    _, length, width = r_scr.shape
     me = lax.axis_index("plane")
     for k in range(nplane):
         _, source = partner(me, k, nplane)
@@ -224,85 +217,77 @@
             if j < length - 1:
                 inner = inner - jnp.sum(upp[at] * after[m], axis=1, keepdims=True)
             after[m] = jnp.sum(piv_t[at] * inner, axis=0, keepdims=True)
-            z_ref[pl.ds(at, 1), :] = after[m]
-
-
-def faces_kernel(nplane, choose, *refs):
-    solved, (mine_ref, sides_ref) = refs[:nplane], refs[nplane:]
-    nfaces = mine_ref.shape[0]
+            z_scr[m, pl.ds(j, 1), :] = after[m]
+    for k in range(nplane):
+        to, _ = partner(me, k, nplane)
+        for m in range(nlines):
+            for q in range(P_SIZE):
+                outs[k][pl.ds(m * P_SIZE + q, 1), :] = z_scr[m, pl.ds(to * P_SIZE + q, 1), :]
+
+
+def faces_kernel(choose, *refs):
+    solved, mine_ref = refs[:-1], refs[-1]
     table = split(jnp.concatenate([s[...] for s in solved], axis=0), 3).astype(BF16)
-    out = jnp.dot(choose[...], table, preferred_element_type=F32)
-    mine_ref[...] = out[:nfaces]
-    sides_ref[...] = out[nfaces:]
-
-
-def fetch_and_apply(ks, blocks, pick, seg, faces, scratch):
-    buf, x_scr, acc, sems = scratch
+    mine_ref[...] = jnp.dot(choose[...], table, preferred_element_type=F32)
+
+
+def apply_kernel(nplane, nblocks, last, *refs):
+    (blocks, slot, pick), faces, refs = refs[:3], refs[3:8], refs[8:]
+    nold = ITERS if last else 1
+    olds, refs = refs[:nold], refs[nold:]
+    next_ref, outs, (buf, x_scr, parts, sems, slot_scr, slot_sem) = refs[0], refs[1:-6], refs[-6:]
     nfaces, width = faces[0].shape
     area = width * width
-    chunk = seg.shape[0]
-    copies = chunk // width
-
-    def fetch(n):
-        return pltpu.make_async_copy(
-            blocks.at[:, pl.ds(ks[n] * area, area)], buf.at[:, pl.ds(n * area, area)], sems.at[n]
-        )
-
-    for n in range(len(ks)):
-        fetch(n).start()
+    chunk = math.lcm(width, 128)
+    copies, count = chunk // width, area // chunk
+    lane = lax.broadcasted_iota(jnp.int32, (1, 128), 1)
+
+    bounds = [0, 3 * count // 10, 6 * count // 10, 8 * count // 10, count]
+    bounds = sorted(set(bounds))
+    copies_of = []
+    for g, (first, end) in enumerate(zip(bounds, bounds[1:])):
+        some = []
+        for k in range(nblocks):
+            where = pl.ds(k * area + first * chunk, (end - first) * chunk)
+            some.append(pltpu.make_async_copy(blocks.at[:, where], buf.at[:, where], sems.at[g, k]))
+            some[-1].start()
+        copies_of.append(some)
+    if not last:
+        slots = pltpu.make_async_copy(slot, slot_scr, slot_sem)
+        slots.start()
+
     both = split(jnp.concatenate([f[...] for f in faces], axis=0), 2)
     wide = jnp.concatenate([both] * copies, axis=1).astype(BF16)
     x_scr[...] = jnp.dot(pick[...], wide, preferred_element_type=F32)
-    group = 3
-    for first in range(0, len(ks), group):
-        some = range(first, min(first + group, len(ks)))
-        for n in some:
-            fetch(n).wait()
+    seg = [jnp.broadcast_to(jnp.where(lane % copies == r, 1.0, 0.0), (width, 128)) for r in range(copies)]
+    seg = jnp.concatenate(seg, axis=0).astype(BF16)
+    total = jnp.zeros((nfaces, 128), F32)
+    for first, end, some in zip(bounds, bounds[1:], copies_of):
+        for copy in some:
+            copy.wait()
         for v in range(0, chunk, 128):
-            xs = [x_scr[n * nfaces : (n + 1) * nfaces, v : v + 128] for n in some]
-            for c in range(area // chunk):
-                at = c * chunk + v
-                total = None if first == 0 else acc[:, at : at + 128]
-                for n, x in zip(some, xs):
-                    term = buf[:, n * area + at : n * area + at + 128] * x
-                    total = term if total is None else total + term
-                acc[:, at : at + 128] = total
-    parts = []
-    for c in range(area // chunk):
-        value = acc[:, c * chunk : (c + 1) * chunk]
-        high = value.astype(BF16)
-        parts += [high, (value - high.astype(F32)).astype(BF16)]
-    sums = jnp.dot(jnp.concatenate(parts, axis=0), seg[...], preferred_element_type=F32)
-    place = lax.broadcasted_iota(jnp.int32, (nfaces, seg.shape[1]), 1) // copies
-    total = jnp.zeros((nfaces, seg.shape[1]), F32)
-    for c in range(area // chunk):
-        at = 2 * c * nfaces
-        total = total + jnp.where(place == c, sums[at : at + nfaces] + sums[at + nfaces : at + 2 * nfaces], 0.0)
-    return total[:, :width]
-
-
-def near_kernel(ks, blocks, pick, seg, mine, sides, out_ref, *scratch):
-    out_ref[...] = fetch_and_apply(ks, blocks, pick, seg, [mine, sides], scratch)
-
-
-def far_kernel(ks, nplane, last, *refs):
-    (blocks, slot, pick, seg, pair, other, near), refs = refs[:7], refs[7:]
-    nold = ITERS if last else 1
-    olds, refs = refs[:nold], refs[nold:]
-    next_ref, refs = refs[0], refs[1:]
-    nfaces = next_ref.shape[0]
-    if not last:
-        slot_scr, slot_sem = refs[-2:]
-        refs = refs[:-2]
-        slots = pltpu.make_async_copy(slot, slot_scr, slot_sem)
-        slots.start()
-    far = fetch_and_apply(ks, blocks, pick, seg, [pair, other], refs[-4:])
-    u_next = near[...] + far - SHIFT * olds[-1][...]
+            xs = [x_scr[k * nfaces : (k + 1) * nfaces, v : v + 128] for k in range(nblocks)]
+            for c in range(first, end):
+                acc = None
+                for k in range(nblocks):
+                    at = k * area + c * chunk + v
+                    term = buf[:, at : at + 128] * xs[k]
+                    acc = term if acc is None else acc + term
+                high = acc.astype(BF16)
+                at = 2 * c * nfaces
+                parts[at : at + nfaces, v : v + 128] = high
+                parts[at + nfaces : at + 2 * nfaces, v : v + 128] = (acc - high.astype(F32)).astype(BF16)
+        base = 2 * first * nfaces
+        sums = jnp.dot(parts[base : 2 * end * nfaces, :], seg, preferred_element_type=F32)
+        for c in range(first, end):
+            at = 2 * c * nfaces - base
+            both_sums = sums[at : at + nfaces] + sums[at + nfaces : at + 2 * nfaces]
+            total = total + jnp.where(lane // copies == c, both_sums, 0.0)
+    u_next = total[:, :width] - SHIFT * olds[-1][...]
     next_ref[...] = u_next
     if last:
-        gram_ref = refs[0]
+        gram_ref = outs[0]
         basis = [old[...] for old in olds] + [u_next]
-        lane = lax.broadcasted_iota(jnp.int32, gram_ref.shape, 1)
         gram, at = jnp.zeros(gram_ref.shape, F32), 0
         for i in range(ITERS + 1):
             for j in range(i, ITERS + 1):
@@ -316,7 +301,7 @@
         for k in range(nplane):
             to, _ = partner(me, k, nplane)
             for i in range(per):
-                refs[k][pl.ds(i, 1), :] = next_ref[pl.ds(slot_scr[0, to * per + i], 1), :]
+                outs[k][pl.ds(i, 1), :] = next_ref[pl.ds(slot_scr[0, to * per + i], 1), :]
 
 
 def finish_kernel(gram_ref, *refs):
@@ -395,16 +380,24 @@
     count = lax.axis_size("span") * lax.axis_size("plane")
     if count & (count - 1):
         return lax.psum(x, ("span", "plane"))
-    step = 1
-    while step < count:
-        x = x + lax.ppermute(x, ("span", "plane"), [(i, i ^ step) for i in range(count)])
-        step *= 2
+    steps = [1 << i for i in range(count.bit_length() - 1)]
+
+    def of(flip):
+        return lax.ppermute(x, ("span", "plane"), [(i, i ^ flip) for i in range(count)])
+
+    for bits in [steps[:1], steps[1:3], *([step] for step in steps[3:])]:
+        if len(bits) == 2:
+            both, one, other = of(sum(bits)), of(bits[0]), of(bits[1])
+            x = (x + one) + (other + both)
+        elif bits:
+            x = x + of(bits[0])
     return x
 
 
-def one_hot(index, count, copies):
-    lanes = lax.broadcasted_iota(jnp.int32, (1, copies * count), 1) % count
-    return (lanes == index.reshape(-1, 1)).astype(BF16)
+def pairings(size):
+    if size % 2:
+        return [(i, (i + 1) % size) for i in range(size)], [(i, (i - 1) % size) for i in range(size)]
+    return [(i, i ^ 1) for i in range(size)], [(i, (i + 1 if i % 2 else i - 1) % size) for i in range(size)]
 
 
 def on_device(rhs, blocks, columns, line_slot, line_lower, line_upper, pivot_inv):
@@ -414,32 +407,19 @@
     owned = nfaces // P_SIZE // nplane
     length = P_SIZE * nplane
     per = owned * P_SIZE
-    me = lax.axis_index("plane")
+    area = width * width
     shape = (nfaces, width)
-    area = width * width
+    span_pairs, span_others = pairings(nspan)
+    plane_pairs, plane_others = pairings(nplane)
 
     us = [rhs.T]
     send = call(
         functools.partial(start_kernel, nplane),
         [line_slot, us[0]],
-        [(per + 1, width)] * nplane,
+        [(per, width)] * nplane,
         [pltpu.SMEM, pltpu.VMEM],
         ready=False,
     )
-
-    if nspan % 2 == 0:
-        pairs = [(i, i ^ 1) for i in range(nspan)]
-        others = [(i, (i + 1 if i % 2 else i - 1) % nspan) for i in range(nspan)]
-        before_first = lax.axis_index("span") % 2 == 1
-    else:
-        pairs = [(i, (i + 1) % nspan) for i in range(nspan)]
-        others = [(i, (i - 1) % nspan) for i in range(nspan)]
-        before_first = True
-
-    chunk = math.lcm(width, 128)
-    seg = (np.arange(chunk)[:, None] // width == np.arange(128)[None, :] % (chunk // width)).astype(np.float32)
-    seg = jnp.asarray(seg, BF16)
-
     factors = call(
         functools.partial(square_kernel, length),
         [line_lower, line_upper, pivot_inv],
@@ -449,75 +429,61 @@
     )
     factors = [x.reshape(nfaces, width, width) for x in factors]
 
-    def scratch(count):
-        return [
-            pltpu.VMEM((nfaces, count * area), F32),
-            pltpu.VMEM((count * nfaces, chunk), F32),
-            pltpu.VMEM((nfaces, area), F32),
-            pltpu.SemaphoreType.DMA((count,)),
-        ]
-
-    near_ks = [0] + list(range(3, nblocks))
-    far_ks = [1, 2] + list(range(5, nblocks))
     zs = []
-    choose = near_pick = far_pick = None
+    choose = pick = None
     for step in range(ITERS):
         got = [send[0]] + [exchange(send[k], "plane", k) for k in range(1, nplane)]
-        if step == 0:
-            owners = jnp.stack([jnp.asarray(partner(me, k, nplane)[1], jnp.int32) for k in range(nplane)])
-            known = jnp.concatenate([g[per:, :nfaces] for g in got], axis=0).astype(jnp.int32)
-            places = jnp.arange(nplane, dtype=jnp.int32)
-            slots = jnp.sum(jnp.where(owners[None, :, None] == places[:, None, None], known[None], 0), axis=1)
-            slots = slots.reshape(1, nplane, nplane, owned, P_SIZE)
-            by_owner = jnp.where(owners[:, None, None, None, None] == places[None, None, :, None, None], slots, 0)
-            face_row = jnp.swapaxes(jnp.sum(by_owner, axis=2), 1, 2).reshape(1, 1, -1)
-            device_row = jnp.broadcast_to(places[None, None, :, None], (nplane, owned, nplane, P_SIZE)).reshape(1, 1, -1)
-            there = jnp.clip(me + jnp.array([0, -1, 1], jnp.int32), 0, nplane - 1)[:, None, None]
-            choose = (device_row == there) & (face_row == jnp.arange(nfaces, dtype=jnp.int32)[None, :, None])
-            choose = jnp.tile(choose.reshape(3 * nfaces, -1), (1, 3)).astype(BF16)
-        (solved,) = call(
+        solved = call(
             functools.partial(line_kernel, nplane, owned),
             [*got, *factors],
-            [shape],
-            scratch=[pltpu.VMEM((owned, length, width), F32)],
+            [(per, width)] * nplane,
+            scratch=[pltpu.VMEM((owned, length, width), F32)] * 2,
             flops=6 * nfaces * area,
         )
         if step == 0:
-            position = table_positions(lax.optimization_barrier((columns, solved))[0], nfaces)
+            slot = lax.optimization_barrier((line_slot, solved[0]))[0].reshape(nplane, per)
+            me = lax.axis_index("plane")
+            owners = jnp.stack([jnp.asarray(partner(me, k, nplane)[1], jnp.int32) for k in range(nplane)])
+            places = jnp.arange(nplane, dtype=jnp.int32)
+            back = jnp.sum(jnp.where(owners[:, None, None] == places[None, :, None], slot[None], 0), axis=1)
+            back = jnp.tile(back.reshape(1, nfaces), (1, 3))
+            choose = (back == jnp.arange(nfaces, dtype=jnp.int32)[:, None]).astype(BF16)
+        pieces = [solved[0]] + [exchange(solved[k], "plane", k) for k in range(1, nplane)]
+        (mine,) = call(faces_kernel, [choose, *pieces], [shape])
+        zs.append(mine)
+        if step == 0:
+            position = table_positions(lax.optimization_barrier((columns, mine))[0], nfaces)
             selector, face = position // nfaces, position % nfaces
-            near_at = jnp.where(selector == 0, 0, jnp.where(selector >= 3, selector - 2, -nfaces)) * nfaces + face
-            far_at = jnp.where(
-                (selector == 1) | (selector == 2), jnp.where((selector == 1) == before_first, 0, 1), -nfaces
-            ) * nfaces + face
-            near_pick = one_hot(jnp.concatenate([near_at[:1], near_at[3:]], axis=0), 3 * nfaces, 2)
-            far_pick = one_hot(jnp.concatenate([far_at[1:3], far_at[5:]], axis=0), 2 * nfaces, 2)
-        pieces = [solved]
-        for k in range(1, nplane):
-            relayed = k % 2 and k > 1 and nplane & (nplane - 1) == 0
-            pieces.append(exchange(pieces[k - 1], "plane", 1) if relayed else exchange(solved, "plane", k))
-        mine, sides = call(
-            functools.partial(faces_kernel, nplane), [choose, *pieces], [shape, (2 * nfaces, width)]
-        )
-        zs.append(mine)
-        other = lax.ppermute(mine, "span", others)
-        pair = lax.ppermute(mine, "span", pairs)
-        (near,) = call(
-            functools.partial(near_kernel, near_ks),
-            [blocks, near_pick, seg, mine, sides],
-            [shape],
-            [pl.ANY] + [pltpu.VMEM] * 4,
-            scratch(len(near_ks)),
-            flops=2 * len(near_ks) * nfaces * area,
-        )
+            span_first = 1 if nspan % 2 else lax.axis_index("span") % 2
+            plane_first = 1 if nplane % 2 else lax.axis_index("plane") % 2
+            group = jnp.where(selector >= 3, selector - 3 + 1 - plane_first, selector - 1 + 1 - span_first) % 2
+            group = jnp.where(selector == 0, 0, group + jnp.where(selector >= 3, 3, 1))
+            lanes = lax.broadcasted_iota(jnp.int32, (1, 10 * nfaces), 1) % (5 * nfaces)
+            pick = (lanes == (group * nfaces + face).reshape(-1, 1)).astype(BF16)
+        far = lax.ppermute(mine, "span", span_others)
+        faces = [
+            mine,
+            lax.ppermute(mine, "span", span_pairs),
+            far,
+            lax.ppermute(mine, "plane", plane_pairs),
+            lax.ppermute(mine, "plane", plane_others),
+        ]
         last = step == ITERS - 1
-        args = [blocks, line_slot, far_pick, seg, pair, other, near, *(us if last else us[-1:])]
+        args = [blocks, line_slot, pick, *faces, *(us if last else us[-1:])]
         out = call(
-            functools.partial(far_kernel, far_ks, nplane, last),
+            functools.partial(apply_kernel, nplane, nblocks, last),
             args,
             [shape] + ([(1, 128)] if last else [(per, width)] * nplane),
             [pl.ANY] + [pltpu.VMEM] * (len(args) - 1),
-            scratch(len(far_ks)) + ([] if last else [pltpu.SMEM(line_slot.shape, jnp.int32), pltpu.SemaphoreType.DMA]),
-            flops=2 * len(far_ks) * nfaces * area,
+            [
+                pltpu.VMEM((nfaces, nblocks * area), F32),
+                pltpu.VMEM((nblocks * nfaces, math.lcm(width, 128)), F32),
+                pltpu.VMEM((2 * nfaces * area // math.lcm(width, 128), math.lcm(width, 128)), BF16),
+                pltpu.SemaphoreType.DMA((4, nblocks)),
+                pltpu.SMEM(line_slot.shape, jnp.int32),
+                pltpu.SemaphoreType.DMA,
+            ],
+            flops=2 * nblocks * nfaces * area,
         )
         us.append(out[0])
         send = out[1:]

time: 82.3 us -> 83.7 us (1.017)
  starting transfers between devices: 24 us -> 33.1 us
  Pallas kernels: 22.8 us -> 17.4 us
  waiting for transfers between devices: 29.5 us -> 26.8 us
    ppermute x11 -> x18, starting transfers between devices: 12.4 us -> 20.2 us  [the longest x3 9.44 us: on_device(): far = lax.ppermute(mine, 'span', span_others)]
    pallas_call x15 -> x12, Pallas kernels: 22.8 us -> 17.4 us  [call(): pl.pallas_call(kernel, out_shape=[pltpu.VMEM(shape, F32) if pinned else j...]
    ppermute x11 -> x18, waiting for transfers between devices: 16.8 us -> 14.1 us  [the longest x6 7.24 us: of(): lax.ppermute(x, ('span', 'plane'), [(i, i ^ flip) for i in range(count)])]
    optimization_barrier x0 -> x1, other arithmetic: none -> 1.32 us  [on_device(): lax.optimization_barrier((line_slot, solved[0]))[0].reshape(nplane, per)]
    ppermute x18, starting transfers between devices: 11.6 us -> 12.9 us  [exchange(): lax.ppermute(x, axis, [(i, partner(i, k, size)[0]) for i in range(size)])]
  transfers between devices with their start and end apart: 29 -> 36, of which waited for: 15 -> 19; matrix products, arithmetic and copies ran while one was open for 4% -> 1% of each run, Pallas kernels for 12% -> 3%
where the time goes in v3:
time: 83.7 us; the launch traced here: 83.3 us
  starting transfers between devices  33.1 us (40%)
  waiting for transfers between devices  26.8 us (32%)
  Pallas kernels  17.4 us (21%)
  other arithmetic  2.43 us (3%)
  local copies, waits for them, and re-layouts  2.24 us (3%)
  between operations  1.07 us (1%)
    pallas_call x12, Pallas kernels, call(): pl.pallas_call(kernel, out_shape=[pltpu.VMEM(shape, F32) if pinned else j...  17.4 us
    ppermute x18, starting transfers between devices, exchange(): lax.ppermute(x, axis, [(i, partner(i, k, size)[0]) for i in range(size)])  12.9 us
    ppermute x18, waiting for transfers between devices, exchange(): lax.ppermute(x, axis, [(i, partner(i, k, size)[0]) for i in range(size)])  12.7 us
    ppermute x3, starting transfers between devices, on_device(): far = lax.ppermute(mine, 'span', span_others)  9.44 us
    ppermute x6, waiting for transfers between devices, of(): lax.ppermute(x, ('span', 'plane'), [(i, i ^ flip) for i in range(count)])  7.24 us
    ppermute x6, starting transfers between devices, of(): lax.ppermute(x, ('span', 'plane'), [(i, i ^ flip) for i in range(count)])  7.06 us
    ppermute x3, waiting for transfers between devices, on_device(): far = lax.ppermute(mine, 'span', span_others)  6.56 us
    ppermute x3, starting transfers between devices, on_device(): lax.ppermute(mine, 'plane', plane_others)  2.11 us
  transfers between devices with their start and end apart: 36, of which 19 were waited for; matrix products, arithmetic and copies ran while one was open for 1% of the time, Pallas kernels for 3%

profile of v3, /device:TPU:0, one launch (start us, length us, event | category | flops | bytes accessed | tf_op | source)
XLA Modules:
  0.0 83.3 jit_solution(15027433650855150450)
XLA Ops:
  1.9 2.6 %collective-permute-start.17 = (f32[4,80]{1,0:T(4,128)S(1)}, f32[4,80]{1,0:T(4,128)S(1)}, u32[]{:S(2)}, u32[]{:S(2)}) collective-permute-start(f32[4,80]{1,0:T(4,128)S(1)} %get-tuple-element.686), channel_id=1, source_target_pairs={{0,2},{1,3},{2,0},{3,1},{4,6},{5,7},{6,4},{7,5},{8,10},{9,11},{10,... | collective-permute-start | bytes 3848 | tf_op jit(solution)/shard_map/ppermute | solution.py:149
  4.7 2.3 %shard_map.87 = (f32[1280,80]{1,0:T(8,128)S(1)}, f32[1280,80]{1,0:T(8,128)S(1)}, f32[1280,80]{1,0:T(8,128)S(1)}) custom-call(f32[16,6400]{1,0:T(8,128)} %low.1, f32[16,6400]{1,0:T(8,128)} %upp.1, f32[16,6400]{1,0:T(8,128)} %piv.1), custom_call_target="tpu_custom_call" | custom-call | flops 102400 | bytes 1228800 | tf_op jit(solution)/shard_map/pallas_call | solution.py:368
  7.5 1.2 %shard_map.88 = (f32[4,80]{1,0:T(4,128)S(1)}, f32[4,80]{1,0:T(4,128)S(1)}, f32[4,80]{1,0:T(4,128)S(1)}, f32[4,80]{1,0:T(4,128)S(1)}) custom-call(f32[4,80]{1,0:T(4,128)S(1)} %get-tuple-element.684.refs_0_, f32[4,80]{1,0:T(4,128)S(1)} %collective-permute-done.16.refs_1_, f32[4,80]{1,0:T(4,128)S(1)} %collective-permute-done.17.refs_2_, ...), custom_call_target="tpu_custom_call" | custom-call | flops 614400 | bytes 1233920 | tf_op jit(solution)/shard_map/pallas_call | solution.py:368
  9.3 1.3 %reduce.11 = s32[16]{0:T(128)S(1)} reduce(s32[1,16]{1,0:T(1,128)} %refs_1_.5, s32[]{:T(128)} %broadcast.552), dimensions={0}, to_apply=%get-tuple-element.692.reduce_sub_computation.3 | reduce | bytes 132 | tf_op jit(solution)/shard_map/optimization_barrier | solution.py:444
  11.1 1.5 %collective-permute-start.20 = (f32[4,80]{1,0:T(4,128)S(1)}, f32[4,80]{1,0:T(4,128)S(1)}, u32[]{:S(2)}, u32[]{:S(2)}) collective-permute-start(f32[4,80]{1,0:T(4,128)S(1)} %get-tuple-element.694), channel_id=1, source_target_pairs={{0,2},{1,3},{2,0},{3,1},{4,6},{5,7},{6,4},{7,5},{8,10},{9,11},{10,... | collective-permute-start | bytes 3848 | tf_op jit(solution)/shard_map/ppermute | solution.py:149
  12.8 1.9 %collective-permute-done.20.refs_2_ = f32[4,80]{1,0:T(4,128)S(1)} collective-permute-done((f32[4,80]{1,0:T(4,128)S(1)}, f32[4,80]{1,0:T(4,128)S(1)}, u32[]{:S(2)}, u32[]{:S(2)}) %collective-permute-start.20) | collective-permute-done | bytes 1312 | tf_op jit(solution)/shard_map/ppermute | solution.py:149
  15.7 1.5 %collective-permute-start.22 = (f32[16,80]{1,0:T(8,128)S(1)}, f32[16,80]{1,0:T(8,128)S(1)}, u32[]{:S(2)}, u32[]{:S(2)}) collective-permute-start(f32[16,80]{1,0:T(8,128)S(1)} %shard_map.89.refs_3_.refs_4_), channel_id=1, source_target_pairs={{0,4},{4,0},{8,12},{12,8},{16,20},{20,16},{24,28},{28,24},{1,5},{5... | collective-permute-start | bytes 15368 | tf_op jit(solution)/shard_map/ppermute | solution.py:466
  17.2 3.6 %collective-permute-start.23 = (f32[16,80]{1,0:T(8,128)S(1)}, f32[16,80]{1,0:T(8,128)S(1)}, u32[]{:S(2)}, u32[]{:S(2)}) collective-permute-start(f32[16,80]{1,0:T(8,128)S(1)} %shard_map.89.refs_3_.refs_4_), channel_id=1, source_target_pairs={{0,28},{4,8},{8,4},{12,16},{16,12},{20,24},{24,20},{28,0},{1,29},{... | collective-permute-start | bytes 15368 | tf_op jit(solution)/shard_map/ppermute | solution.py:463
  22.4 1.1 %collective-permute-done.23.refs_5_ = f32[16,80]{1,0:T(8,128)S(1)} collective-permute-done((f32[16,80]{1,0:T(8,128)S(1)}, f32[16,80]{1,0:T(8,128)S(1)}, u32[]{:S(2)}, u32[]{:S(2)}) %collective-permute-start.23) | collective-permute-done | bytes 5152 | tf_op jit(solution)/shard_map/ppermute | solution.py:463
  25.2 3.1 %shard_map.90 = (f32[16,80]{1,0:T(8,128)S(1)}, f32[4,80]{1,0:T(4,128)S(1)}, f32[4,80]{1,0:T(4,128)S(1)}, f32[4,80]{1,0:T(4,128)S(1)}, f32[4,80]{1,0:T(4,128)S(1)}) custom-call(f32[16,70400]{1,0:T(8,128)} %refs_0_.5, s32[1,16]{1,0:T(1,128)S(1)} %copy-done.2, bf16[176,160]{1,0:T(8,128)(2,1)S(1)} %compare_convert_fusion.refs_2_, ...), custom_call_target="tpu_custom_call" | custom-call | flops 2252800 | bytes 4592704 | tf_op jit(solution)/shard_map/pallas_call | solution.py:368
  30.4 2.2 %collective-permute-done.27.refs_2_ = f32[4,80]{1,0:T(4,128)S(1)} collective-permute-done((f32[4,80]{1,0:T(4,128)S(1)}, f32[4,80]{1,0:T(4,128)S(1)}, u32[]{:S(2)}, u32[]{:S(2)}) %collective-permute-start.27) | collective-permute-done | bytes 1312 | tf_op jit(solution)/shard_map/ppermute | solution.py:149
  32.6 1.3 %shard_map.91 = (f32[4,80]{1,0:T(4,128)S(1)}, f32[4,80]{1,0:T(4,128)S(1)}, f32[4,80]{1,0:T(4,128)S(1)}, f32[4,80]{1,0:T(4,128)S(1)}) custom-call(f32[4,80]{1,0:T(4,128)S(1)} %get-tuple-element.697.refs_0_, f32[4,80]{1,0:T(4,128)S(1)} %collective-permute-done.26.refs_1_, f32[4,80]{1,0:T(4,128)S(1)} %collective-permute-done.27.refs_2_, ...), custom_call_target="tpu_custom_call" | custom-call | flops 614400 | bytes 1233920 | tf_op jit(solution)/shard_map/pallas_call | solution.py:368
  34.0 1.4 %collective-permute-start.30 = (f32[4,80]{1,0:T(4,128)S(1)}, f32[4,80]{1,0:T(4,128)S(1)}, u32[]{:S(2)}, u32[]{:S(2)}) collective-permute-start(f32[4,80]{1,0:T(4,128)S(1)} %get-tuple-element.703), channel_id=1, source_target_pairs={{0,2},{1,3},{2,0},{3,1},{4,6},{5,7},{6,4},{7,5},{8,10},{9,11},{10,... | collective-permute-start | bytes 3848 | tf_op jit(solution)/shard_map/ppermute | solution.py:149
  35.8 1.8 %collective-permute-done.30.refs_2_ = f32[4,80]{1,0:T(4,128)S(1)} collective-permute-done((f32[4,80]{1,0:T(4,128)S(1)}, f32[4,80]{1,0:T(4,128)S(1)}, u32[]{:S(2)}, u32[]{:S(2)}) %collective-permute-start.30) | collective-permute-done | bytes 1312 | tf_op jit(solution)/shard_map/ppermute | solution.py:149
  38.6 3.0 %collective-permute-start.33 = (f32[16,80]{1,0:T(8,128)S(1)}, f32[16,80]{1,0:T(8,128)S(1)}, u32[]{:S(2)}, u32[]{:S(2)}) collective-permute-start(f32[16,80]{1,0:T(8,128)S(1)} %shard_map.92.refs_3_.refs_5_), channel_id=1, source_target_pairs={{0,28},{4,8},{8,4},{12,16},{16,12},{20,24},{24,20},{28,0},{1,29},{... | collective-permute-start | bytes 15368 | tf_op jit(solution)/shard_map/ppermute | solution.py:463
  42.2 2.7 %collective-permute-done.33.refs_5_ = f32[16,80]{1,0:T(8,128)S(1)} collective-permute-done((f32[16,80]{1,0:T(8,128)S(1)}, f32[16,80]{1,0:T(8,128)S(1)}, u32[]{:S(2)}, u32[]{:S(2)}) %collective-permute-start.33) | collective-permute-done | bytes 5152 | tf_op jit(solution)/shard_map/ppermute | solution.py:463
  45.0 3.1 %shard_map.93 = (f32[16,80]{1,0:T(8,128)S(1)}, f32[4,80]{1,0:T(4,128)S(1)}, f32[4,80]{1,0:T(4,128)S(1)}, f32[4,80]{1,0:T(4,128)S(1)}, f32[4,80]{1,0:T(4,128)S(1)}) custom-call(f32[16,70400]{1,0:T(8,128)} %refs_0_.5, s32[1,16]{1,0:T(1,128)S(1)} %copy-done.2, bf16[176,160]{1,0:T(8,128)(2,1)S(1)} %compare_convert_fusion.refs_2_, ...), custom_call_target="tpu_custom_call" | custom-call | flops 2252800 | bytes 4592704 | tf_op jit(solution)/shard_map/pallas_call | solution.py:368
  48.9 1.1 %collective-permute-start.38 = (f32[4,80]{1,0:T(4,128)S(1)}, f32[4,80]{1,0:T(4,128)S(1)}, u32[]{:S(2)}, u32[]{:S(2)}) collective-permute-start(f32[4,80]{1,0:T(4,128)S(1)} %get-tuple-element.709), channel_id=1, source_target_pairs={{0,3},{1,2},{2,1},{3,0},{4,7},{5,6},{6,5},{7,4},{8,11},{9,10},{10,... | collective-permute-start | bytes 3848 | tf_op jit(solution)/shard_map/ppermute | solution.py:149
  50.0 1.9 %collective-permute-done.37.refs_2_ = f32[4,80]{1,0:T(4,128)S(1)} collective-permute-done((f32[4,80]{1,0:T(4,128)S(1)}, f32[4,80]{1,0:T(4,128)S(1)}, u32[]{:S(2)}, u32[]{:S(2)}) %collective-permute-start.37) | collective-permute-done | bytes 1312 | tf_op jit(solution)/shard_map/ppermute | solution.py:149
  52.0 1.2 %shard_map.94 = (f32[4,80]{1,0:T(4,128)S(1)}, f32[4,80]{1,0:T(4,128)S(1)}, f32[4,80]{1,0:T(4,128)S(1)}, f32[4,80]{1,0:T(4,128)S(1)}) custom-call(f32[4,80]{1,0:T(4,128)S(1)} %get-tuple-element.706.refs_0_, f32[4,80]{1,0:T(4,128)S(1)} %collective-permute-done.36.refs_1_, f32[4,80]{1,0:T(4,128)S(1)} %collective-permute-done.37.refs_2_, ...), custom_call_target="tpu_custom_call" | custom-call | flops 614400 | bytes 1233920 | tf_op jit(solution)/shard_map/pallas_call | solution.py:368
  53.4 1.5 %collective-permute-start.40 = (f32[4,80]{1,0:T(4,128)S(1)}, f32[4,80]{1,0:T(4,128)S(1)}, u32[]{:S(2)}, u32[]{:S(2)}) collective-permute-start(f32[4,80]{1,0:T(4,128)S(1)} %get-tuple-element.712), channel_id=1, source_target_pairs={{0,2},{1,3},{2,0},{3,1},{4,6},{5,7},{6,4},{7,5},{8,10},{9,11},{10,... | collective-permute-start | bytes 3848 | tf_op jit(solution)/shard_map/ppermute | solution.py:149
  55.2 1.8 %collective-permute-done.40.refs_2_ = f32[4,80]{1,0:T(4,128)S(1)} collective-permute-done((f32[4,80]{1,0:T(4,128)S(1)}, f32[4,80]{1,0:T(4,128)S(1)}, u32[]{:S(2)}, u32[]{:S(2)}) %collective-permute-start.40) | collective-permute-done | bytes 1312 | tf_op jit(solution)/shard_map/ppermute | solution.py:149
  58.1 2.9 %collective-permute-start.43 = (f32[16,80]{1,0:T(8,128)S(1)}, f32[16,80]{1,0:T(8,128)S(1)}, u32[]{:S(2)}, u32[]{:S(2)}) collective-permute-start(f32[16,80]{1,0:T(8,128)S(1)} %shard_map.95.refs_3_.refs_6_), channel_id=1, source_target_pairs={{0,28},{4,8},{8,4},{12,16},{16,12},{20,24},{24,20},{28,0},{1,29},{... | collective-permute-start | bytes 15368 | tf_op jit(solution)/shard_map/ppermute | solution.py:463
  61.7 2.7 %collective-permute-done.43.refs_5_ = f32[16,80]{1,0:T(8,128)S(1)} collective-permute-done((f32[16,80]{1,0:T(8,128)S(1)}, f32[16,80]{1,0:T(8,128)S(1)}, u32[]{:S(2)}, u32[]{:S(2)}) %collective-permute-start.43) | collective-permute-done | bytes 5152 | tf_op jit(solution)/shard_map/ppermute | solution.py:463
  64.5 3.2 %shard_map.96 = (f32[16,80]{1,0:T(8,128)S(1)}, f32[1,128]{1,0:T(1,128)S(1)}) custom-call(f32[16,70400]{1,0:T(8,128)} %refs_0_.5, s32[1,16]{1,0:T(1,128)S(1)} %copy-done.3, bf16[176,160]{1,0:T(8,128)(2,1)S(1)} %compare_convert_fusion.refs_2_, f32[16,80]{1,0:T(8,128)S(1)} %shard_map.95.refs_3_.refs_6_, f32[16,80]{1,0:T(8,128)S(1)} %collective-permute-done.42.refs_4_, ...), custom_call_target="tpu_custom_call" | custom-call | flops 2252800 | bytes 4602944 | tf_op jit(solution)/shard_map/pallas_call | solution.py:368
  67.9 1.0 %collective-permute-done.46 = f32[1,128]{1,0:T(1,128)S(1)} collective-permute-done((f32[1,128]{1,0:T(1,128)S(1)}, f32[1,128]{1,0:T(1,128)S(1)}, u32[]{:S(2)}, u32[]{:S(2)}) %collective-permute-start.46) | collective-permute-done | bytes 544 | tf_op jit(solution)/shard_map/ppermute | solution.py:386
  69.6 2.8 %collective-permute-start.49 = (f32[1,128]{1,0:T(1,128)S(1)}, f32[1,128]{1,0:T(1,128)S(1)}, u32[]{:S(2)}, u32[]{:S(2)}) collective-permute-start(f32[1,128]{1,0:T(1,128)S(1)} %add.331), channel_id=1, source_target_pairs={{0,6},{1,7},{2,4},{3,5},{4,2},{5,3},{6,0},{7,1},{8,14},{9,15},{10,... | collective-permute-start | bytes 1544 | tf_op jit(solution)/shard_map/ppermute | solution.py:386
  73.0 1.0 %collective-permute-done.49 = f32[1,128]{1,0:T(1,128)S(1)} collective-permute-done((f32[1,128]{1,0:T(1,128)S(1)}, f32[1,128]{1,0:T(1,128)S(1)}, u32[]{:S(2)}, u32[]{:S(2)}) %collective-permute-start.49) | collective-permute-done | bytes 544 | tf_op jit(solution)/shard_map/ppermute | solution.py:386
  74.0 1.2 %collective-permute-start.50 = (f32[1,128]{1,0:T(1,128)S(1)}, f32[1,128]{1,0:T(1,128)S(1)}, u32[]{:S(2)}, u32[]{:S(2)}) collective-permute-start(f32[1,128]{1,0:T(1,128)S(1)} %add_add_fusion), channel_id=1, source_target_pairs={{0,8},{1,9},{2,10},{3,11},{4,12},{5,13},{6,14},{7,15},{8,0},{9,1},... | collective-permute-start | bytes 1544 | tf_op jit(solution)/shard_map/ppermute | solution.py:386
  75.2 2.3 %collective-permute-done.50 = f32[1,128]{1,0:T(1,128)S(1)} collective-permute-done((f32[1,128]{1,0:T(1,128)S(1)}, f32[1,128]{1,0:T(1,128)S(1)}, u32[]{:S(2)}, u32[]{:S(2)}) %collective-permute-start.50) | collective-permute-done | bytes 544 | tf_op jit(solution)/shard_map/ppermute | solution.py:386
  77.6 2.1 %collective-permute-start.51 = (f32[1,128]{1,0:T(1,128)S(1)}, f32[1,128]{1,0:T(1,128)S(1)}, u32[]{:S(2)}, u32[]{:S(2)}) collective-permute-start(f32[1,128]{1,0:T(1,128)S(1)} %add.335), channel_id=1, source_target_pairs={{0,16},{1,17},{2,18},{3,19},{4,20},{5,21},{6,22},{7,23},{8,24},{9,... | collective-permute-start | bytes 1544 | tf_op jit(solution)/shard_map/ppermute | solution.py:386
  79.7 2.3 %collective-permute-done.51 = f32[1,128]{1,0:T(1,128)S(1)} collective-permute-done((f32[1,128]{1,0:T(1,128)S(1)}, f32[1,128]{1,0:T(1,128)S(1)}, u32[]{:S(2)}, u32[]{:S(2)}) %collective-permute-start.51) | collective-permute-done | bytes 544 | tf_op jit(solution)/shard_map/ppermute | solution.py:386
  (85 shorter events, 17.6 us)
Async XLA Ops:
  1.4 5.7 %collective-permute-start.16 = (f32[4,80]{1,0:T(4,128)S(1)}, f32[4,80]{1,0:T(4,128)S(1)}, u32[]{:S(2)}, u32[]{:S(2)}) collective-permute-start(f32[4,80]{1,0:T(4,128)S(1)} %get-tuple-element.685), channel_id=1, source_target_pairs={{0,1},{1,0},{2,3},{3,2},{4,5},{5,4},{6,7},{7,6},{8,9},{9,8},{10,11... | collective-permute-start | bytes 3848 | tf_op jit(solution)/shard_map/ppermute | solution.py:149
  1.9 5.2 %collective-permute-start.17 = (f32[4,80]{1,0:T(4,128)S(1)}, f32[4,80]{1,0:T(4,128)S(1)}, u32[]{:S(2)}, u32[]{:S(2)}) collective-permute-start(f32[4,80]{1,0:T(4,128)S(1)} %get-tuple-element.686), channel_id=1, source_target_pairs={{0,2},{1,3},{2,0},{3,1},{4,6},{5,7},{6,4},{7,5},{8,10},{9,11},{10,... | collective-permute-start | bytes 3848 | tf_op jit(solution)/shard_map/ppermute | solution.py:149
  4.5 3.0 %collective-permute-start.18 = (f32[4,80]{1,0:T(4,128)S(1)}, f32[4,80]{1,0:T(4,128)S(1)}, u32[]{:S(2)}, u32[]{:S(2)}) collective-permute-start(f32[4,80]{1,0:T(4,128)S(1)} %get-tuple-element.687), channel_id=1, source_target_pairs={{0,3},{1,2},{2,1},{3,0},{4,7},{5,6},{6,5},{7,4},{8,11},{9,10},{10,... | collective-permute-start | bytes 3848 | tf_op jit(solution)/shard_map/ppermute | solution.py:149
  11.1 3.6 %collective-permute-start.20 = (f32[4,80]{1,0:T(4,128)S(1)}, f32[4,80]{1,0:T(4,128)S(1)}, u32[]{:S(2)}, u32[]{:S(2)}) collective-permute-start(f32[4,80]{1,0:T(4,128)S(1)} %get-tuple-element.694), channel_id=1, source_target_pairs={{0,2},{1,3},{2,0},{3,1},{4,6},{5,7},{6,4},{7,5},{8,10},{9,11},{10,... | collective-permute-start | bytes 3848 | tf_op jit(solution)/shard_map/ppermute | solution.py:149
  12.6 3.0 %collective-permute-start.21 = (f32[4,80]{1,0:T(4,128)S(1)}, f32[4,80]{1,0:T(4,128)S(1)}, u32[]{:S(2)}, u32[]{:S(2)}) collective-permute-start(f32[4,80]{1,0:T(4,128)S(1)} %get-tuple-element.695), channel_id=1, source_target_pairs={{0,3},{1,2},{2,1},{3,0},{4,7},{5,6},{6,5},{7,4},{8,11},{9,10},{10,... | collective-permute-start | bytes 3848 | tf_op jit(solution)/shard_map/ppermute | solution.py:149
  15.7 6.7 %collective-permute-start.22 = (f32[16,80]{1,0:T(8,128)S(1)}, f32[16,80]{1,0:T(8,128)S(1)}, u32[]{:S(2)}, u32[]{:S(2)}) collective-permute-start(f32[16,80]{1,0:T(8,128)S(1)} %shard_map.89.refs_3_.refs_4_), channel_id=1, source_target_pairs={{0,4},{4,0},{8,12},{12,8},{16,20},{20,16},{24,28},{28,24},{1,5},{5... | collective-permute-start | bytes 15368 | tf_op jit(solution)/shard_map/ppermute | solution.py:466
  17.2 6.3 %collective-permute-start.23 = (f32[16,80]{1,0:T(8,128)S(1)}, f32[16,80]{1,0:T(8,128)S(1)}, u32[]{:S(2)}, u32[]{:S(2)}) collective-permute-start(f32[16,80]{1,0:T(8,128)S(1)} %shard_map.89.refs_3_.refs_4_), channel_id=1, source_target_pairs={{0,28},{4,8},{8,4},{12,16},{16,12},{20,24},{24,20},{28,0},{1,29},{... | collective-permute-start | bytes 15368 | tf_op jit(solution)/shard_map/ppermute | solution.py:463
  20.8 2.8 %collective-permute-start.24 = (f32[16,80]{1,0:T(8,128)S(1)}, f32[16,80]{1,0:T(8,128)S(1)}, u32[]{:S(2)}, u32[]{:S(2)}) collective-permute-start(f32[16,80]{1,0:T(8,128)S(1)} %shard_map.89.refs_3_.refs_4_), channel_id=1, source_target_pairs={{0,1},{1,0},{2,3},{3,2},{4,5},{5,4},{6,7},{7,6},{8,9},{9,8},{10,11... | collective-permute-start | bytes 15368 | tf_op jit(solution)/shard_map/ppermute | solution.py:468
  20.8 3.1 %collective-permute-start.25 = (f32[16,80]{1,0:T(8,128)S(1)}, f32[16,80]{1,0:T(8,128)S(1)}, u32[]{:S(2)}, u32[]{:S(2)}) collective-permute-start(f32[16,80]{1,0:T(8,128)S(1)} %shard_map.89.refs_3_.refs_4_), channel_id=1, source_target_pairs={{0,3},{1,2},{2,1},{3,0},{4,7},{5,6},{6,5},{7,4},{8,11},{9,10},{10,... | collective-permute-start | bytes 15368 | tf_op jit(solution)/shard_map/ppermute | solution.py:469
  28.4 2.0 %collective-permute-start.26 = (f32[4,80]{1,0:T(4,128)S(1)}, f32[4,80]{1,0:T(4,128)S(1)}, u32[]{:S(2)}, u32[]{:S(2)}) collective-permute-start(f32[4,80]{1,0:T(4,128)S(1)} %get-tuple-element.698), channel_id=1, source_target_pairs={{0,1},{1,0},{2,3},{3,2},{4,5},{5,4},{6,7},{7,6},{8,9},{9,8},{10,11... | collective-permute-start | bytes 3848 | tf_op jit(solution)/shard_map/ppermute | solution.py:149
  29.0 3.6 %collective-permute-start.27 = (f32[4,80]{1,0:T(4,128)S(1)}, f32[4,80]{1,0:T(4,128)S(1)}, u32[]{:S(2)}, u32[]{:S(2)}) collective-permute-start(f32[4,80]{1,0:T(4,128)S(1)} %get-tuple-element.699), channel_id=1, source_target_pairs={{0,2},{1,3},{2,0},{3,1},{4,6},{5,7},{6,4},{7,5},{8,10},{9,11},{10,... | collective-permute-start | bytes 3848 | tf_op jit(solution)/shard_map/ppermute | solution.py:149
  29.6 3.0 %collective-permute-start.28 = (f32[4,80]{1,0:T(4,128)S(1)}, f32[4,80]{1,0:T(4,128)S(1)}, u32[]{:S(2)}, u32[]{:S(2)}) collective-permute-start(f32[4,80]{1,0:T(4,128)S(1)} %get-tuple-element.700), channel_id=1, source_target_pairs={{0,3},{1,2},{2,1},{3,0},{4,7},{5,6},{6,5},{7,4},{8,11},{9,10},{10,... | collective-permute-start | bytes 3848 | tf_op jit(solution)/shard_map/ppermute | solution.py:149
  34.0 3.6 %collective-permute-start.30 = (f32[4,80]{1,0:T(4,128)S(1)}, f32[4,80]{1,0:T(4,128)S(1)}, u32[]{:S(2)}, u32[]{:S(2)}) collective-permute-start(f32[4,80]{1,0:T(4,128)S(1)} %get-tuple-element.703), channel_id=1, source_target_pairs={{0,2},{1,3},{2,0},{3,1},{4,6},{5,7},{6,4},{7,5},{8,10},{9,11},{10,... | collective-permute-start | bytes 3848 | tf_op jit(solution)/shard_map/ppermute | solution.py:149
  35.4 3.0 %collective-permute-start.31 = (f32[4,80]{1,0:T(4,128)S(1)}, f32[4,80]{1,0:T(4,128)S(1)}, u32[]{:S(2)}, u32[]{:S(2)}) collective-permute-start(f32[4,80]{1,0:T(4,128)S(1)} %get-tuple-element.704), channel_id=1, source_target_pairs={{0,3},{1,2},{2,1},{3,0},{4,7},{5,6},{6,5},{7,4},{8,11},{9,10},{10,... | collective-permute-start | bytes 3848 | tf_op jit(solution)/shard_map/ppermute | solution.py:149
  38.6 3.7 %collective-permute-start.32 = (f32[16,80]{1,0:T(8,128)S(1)}, f32[16,80]{1,0:T(8,128)S(1)}, u32[]{:S(2)}, u32[]{:S(2)}) collective-permute-start(f32[16,80]{1,0:T(8,128)S(1)} %shard_map.92.refs_3_.refs_5_), channel_id=1, source_target_pairs={{0,4},{4,0},{8,12},{12,8},{16,20},{20,16},{24,28},{28,24},{1,5},{5... | collective-permute-start | bytes 15368 | tf_op jit(solution)/shard_map/ppermute | solution.py:466
  38.6 6.4 %collective-permute-start.33 = (f32[16,80]{1,0:T(8,128)S(1)}, f32[16,80]{1,0:T(8,128)S(1)}, u32[]{:S(2)}, u32[]{:S(2)}) collective-permute-start(f32[16,80]{1,0:T(8,128)S(1)} %shard_map.92.refs_3_.refs_5_), channel_id=1, source_target_pairs={{0,28},{4,8},{8,4},{12,16},{16,12},{20,24},{24,20},{28,0},{1,29},{... | collective-permute-start | bytes 15368 | tf_op jit(solution)/shard_map/ppermute | solution.py:463
  41.5 3.4 %collective-permute-start.34 = (f32[16,80]{1,0:T(8,128)S(1)}, f32[16,80]{1,0:T(8,128)S(1)}, u32[]{:S(2)}, u32[]{:S(2)}) collective-permute-start(f32[16,80]{1,0:T(8,128)S(1)} %shard_map.92.refs_3_.refs_5_), channel_id=1, source_target_pairs={{0,1},{1,0},{2,3},{3,2},{4,5},{5,4},{6,7},{7,6},{8,9},{9,8},{10,11... | collective-permute-start | bytes 15368 | tf_op jit(solution)/shard_map/ppermute | solution.py:468
  41.5 3.4 %collective-permute-start.35 = (f32[16,80]{1,0:T(8,128)S(1)}, f32[16,80]{1,0:T(8,128)S(1)}, u32[]{:S(2)}, u32[]{:S(2)}) collective-permute-start(f32[16,80]{1,0:T(8,128)S(1)} %shard_map.92.refs_3_.refs_5_), channel_id=1, source_target_pairs={{0,3},{1,2},{2,1},{3,0},{4,7},{5,6},{6,5},{7,4},{8,11},{9,10},{10,... | collective-permute-start | bytes 15368 | tf_op jit(solution)/shard_map/ppermute | solution.py:469
  48.3 3.6 %collective-permute-start.37 = (f32[4,80]{1,0:T(4,128)S(1)}, f32[4,80]{1,0:T(4,128)S(1)}, u32[]{:S(2)}, u32[]{:S(2)}) collective-permute-start(f32[4,80]{1,0:T(4,128)S(1)} %get-tuple-element.708), channel_id=1, source_target_pairs={{0,2},{1,3},{2,0},{3,1},{4,6},{5,7},{6,4},{7,5},{8,10},{9,11},{10,... | collective-permute-start | bytes 3848 | tf_op jit(solution)/shard_map/ppermute | solution.py:149
  48.9 3.0 %collective-permute-start.38 = (f32[4,80]{1,0:T(4,128)S(1)}, f32[4,80]{1,0:T(4,128)S(1)}, u32[]{:S(2)}, u32[]{:S(2)}) collective-permute-start(f32[4,80]{1,0:T(4,128)S(1)} %get-tuple-element.709), channel_id=1, source_target_pairs={{0,3},{1,2},{2,1},{3,0},{4,7},{5,6},{6,5},{7,4},{8,11},{9,10},{10,... | collective-permute-start | bytes 3848 | tf_op jit(solution)/shard_map/ppermute | solution.py:149
  53.2 2.0 %collective-permute-start.39 = (f32[4,80]{1,0:T(4,128)S(1)}, f32[4,80]{1,0:T(4,128)S(1)}, u32[]{:S(2)}, u32[]{:S(2)}) collective-permute-start(f32[4,80]{1,0:T(4,128)S(1)} %get-tuple-element.711), channel_id=1, source_target_pairs={{0,1},{1,0},{2,3},{3,2},{4,5},{5,4},{6,7},{7,6},{8,9},{9,8},{10,11... | collective-permute-start | bytes 3848 | tf_op jit(solution)/shard_map/ppermute | solution.py:149
  53.4 3.6 %collective-permute-start.40 = (f32[4,80]{1,0:T(4,128)S(1)}, f32[4,80]{1,0:T(4,128)S(1)}, u32[]{:S(2)}, u32[]{:S(2)}) collective-permute-start(f32[4,80]{1,0:T(4,128)S(1)} %get-tuple-element.712), channel_id=1, source_target_pairs={{0,2},{1,3},{2,0},{3,1},{4,6},{5,7},{6,4},{7,5},{8,10},{9,11},{10,... | collective-permute-start | bytes 3848 | tf_op jit(solution)/shard_map/ppermute | solution.py:149
  54.8 3.0 %collective-permute-start.41 = (f32[4,80]{1,0:T(4,128)S(1)}, f32[4,80]{1,0:T(4,128)S(1)}, u32[]{:S(2)}, u32[]{:S(2)}) collective-permute-start(f32[4,80]{1,0:T(4,128)S(1)} %get-tuple-element.713), channel_id=1, source_target_pairs={{0,3},{1,2},{2,1},{3,0},{4,7},{5,6},{6,5},{7,4},{8,11},{9,10},{10,... | collective-permute-start | bytes 3848 | tf_op jit(solution)/shard_map/ppermute | solution.py:149
  58.0 3.8 %collective-permute-start.42 = (f32[16,80]{1,0:T(8,128)S(1)}, f32[16,80]{1,0:T(8,128)S(1)}, u32[]{:S(2)}, u32[]{:S(2)}) collective-permute-start(f32[16,80]{1,0:T(8,128)S(1)} %shard_map.95.refs_3_.refs_6_), channel_id=1, source_target_pairs={{0,4},{4,0},{8,12},{12,8},{16,20},{20,16},{24,28},{28,24},{1,5},{5... | collective-permute-start | bytes 15368 | tf_op jit(solution)/shard_map/ppermute | solution.py:466
  58.1 6.3 %collective-permute-start.43 = (f32[16,80]{1,0:T(8,128)S(1)}, f32[16,80]{1,0:T(8,128)S(1)}, u32[]{:S(2)}, u32[]{:S(2)}) collective-permute-start(f32[16,80]{1,0:T(8,128)S(1)} %shard_map.95.refs_3_.refs_6_), channel_id=1, source_target_pairs={{0,28},{4,8},{8,4},{12,16},{16,12},{20,24},{24,20},{28,0},{1,29},{... | collective-permute-start | bytes 15368 | tf_op jit(solution)/shard_map/ppermute | solution.py:463
  61.0 3.4 %collective-permute-start.44 = (f32[16,80]{1,0:T(8,128)S(1)}, f32[16,80]{1,0:T(8,128)S(1)}, u32[]{:S(2)}, u32[]{:S(2)}) collective-permute-start(f32[16,80]{1,0:T(8,128)S(1)} %shard_map.95.refs_3_.refs_6_), channel_id=1, source_target_pairs={{0,1},{1,0},{2,3},{3,2},{4,5},{5,4},{6,7},{7,6},{8,9},{9,8},{10,11... | collective-permute-start | bytes 15368 | tf_op jit(solution)/shard_map/ppermute | solution.py:468
  61.0 3.4 %collective-permute-start.45 = (f32[16,80]{1,0:T(8,128)S(1)}, f32[16,80]{1,0:T(8,128)S(1)}, u32[]{:S(2)}, u32[]{:S(2)}) collective-permute-start(f32[16,80]{1,0:T(8,128)S(1)} %shard_map.95.refs_3_.refs_6_), channel_id=1, source_target_pairs={{0,3},{1,2},{2,1},{3,0},{4,7},{5,6},{6,5},{7,4},{8,11},{9,10},{10,... | collective-permute-start | bytes 15368 | tf_op jit(solution)/shard_map/ppermute | solution.py:469
  68.9 3.5 %collective-permute-start.47 = (f32[1,128]{1,0:T(1,128)S(1)}, f32[1,128]{1,0:T(1,128)S(1)}, u32[]{:S(2)}, u32[]{:S(2)}) collective-permute-start(f32[1,128]{1,0:T(1,128)S(1)} %add.331), channel_id=1, source_target_pairs={{0,2},{1,3},{2,0},{3,1},{4,6},{5,7},{6,4},{7,5},{8,10},{9,11},{10,... | collective-permute-start | bytes 1544 | tf_op jit(solution)/shard_map/ppermute | solution.py:386
  69.5 3.5 %collective-permute-start.48 = (f32[1,128]{1,0:T(1,128)S(1)}, f32[1,128]{1,0:T(1,128)S(1)}, u32[]{:S(2)}, u32[]{:S(2)}) collective-permute-start(f32[1,128]{1,0:T(1,128)S(1)} %add.331), channel_id=1, source_target_pairs={{0,4},{1,5},{2,6},{3,7},{4,0},{5,1},{6,2},{7,3},{8,12},{9,13},{10,... | collective-permute-start | bytes 1544 | tf_op jit(solution)/shard_map/ppermute | solution.py:386
  69.6 4.4 %collective-permute-start.49 = (f32[1,128]{1,0:T(1,128)S(1)}, f32[1,128]{1,0:T(1,128)S(1)}, u32[]{:S(2)}, u32[]{:S(2)}) collective-permute-start(f32[1,128]{1,0:T(1,128)S(1)} %add.331), channel_id=1, source_target_pairs={{0,6},{1,7},{2,4},{3,5},{4,2},{5,3},{6,0},{7,1},{8,14},{9,15},{10,... | collective-permute-start | bytes 1544 | tf_op jit(solution)/shard_map/ppermute | solution.py:386
  74.0 3.5 %collective-permute-start.50 = (f32[1,128]{1,0:T(1,128)S(1)}, f32[1,128]{1,0:T(1,128)S(1)}, u32[]{:S(2)}, u32[]{:S(2)}) collective-permute-start(f32[1,128]{1,0:T(1,128)S(1)} %add_add_fusion), channel_id=1, source_target_pairs={{0,8},{1,9},{2,10},{3,11},{4,12},{5,13},{6,14},{7,15},{8,0},{9,1},... | collective-permute-start | bytes 1544 | tf_op jit(solution)/shard_map/ppermute | solution.py:386
  77.6 4.4 %collective-permute-start.51 = (f32[1,128]{1,0:T(1,128)S(1)}, f32[1,128]{1,0:T(1,128)S(1)}, u32[]{:S(2)}, u32[]{:S(2)}) collective-permute-start(f32[1,128]{1,0:T(1,128)S(1)} %add.335), channel_id=1, source_target_pairs={{0,16},{1,17},{2,18},{3,19},{4,20},{5,21},{6,22},{7,23},{8,24},{9,... | collective-permute-start | bytes 1544 | tf_op jit(solution)/shard_map/ppermute | solution.py:386
  (11 other events, 283.3 us)

commit v4 on v3

--- a/solution.py
+++ b/solution.py
@@ -73,9 +73,7 @@
     return jnp.moveaxis(zseq, 0, 2)
 
 
-def table_positions(columns, nfaces):
-    nspan, nplane = lax.axis_size("span"), lax.axis_size("plane")
-    my_span, my_plane = lax.axis_index("span"), lax.axis_index("plane")
+def table_positions(columns, nfaces, my_span, my_plane, nspan, nplane):
     device_of = columns // nfaces
     span_of = device_of // nplane
     plane_of = device_of % nplane
@@ -93,7 +91,9 @@
     width, nfaces = rhs.shape
     nblocks = columns.shape[0]
     nplane = lax.axis_size("plane")
-    position = table_positions(columns, nfaces)
+    position = table_positions(
+        columns, nfaces, lax.axis_index("span"), lax.axis_index("plane"), lax.axis_size("span"), nplane
+    )
     slot = line_slot[0]
     lines_group = nfaces // P_SIZE
     owned = lines_group // nplane
@@ -157,29 +157,61 @@
     return jnp.concatenate(out, axis=0)
 
 
-def start_kernel(nplane, slot_ref, u_ref, *outs):
-    per = outs[0].shape[0]
+def start_kernel(nplane, slot_ref, u_ref, copy_ref, choose_ref, *outs):
+    nfaces = u_ref.shape[0]
+    per = nfaces // nplane
     me = lax.axis_index("plane")
     for k in range(nplane):
         to, _ = partner(me, k, nplane)
         for i in range(per):
             outs[k][pl.ds(i, 1), :] = u_ref[pl.ds(slot_ref[0, to * per + i], 1), :]
-
-
-def square_kernel(length, low, upp, piv, low_out, upp_out, piv_out):
+    copy_ref[...] = u_ref[...]
+    face = lax.broadcasted_iota(jnp.int32, choose_ref.shape, 0)
+    piece = lax.broadcasted_iota(jnp.int32, choose_ref.shape, 1) % nfaces
+    choose = jnp.zeros(choose_ref.shape, F32)
+    for k in range(nplane):
+        _, source = partner(me, k, nplane)
+        for i in range(per):
+            hit = (face == slot_ref[0, source * per + i]) & (piece == k * per + i)
+            choose = jnp.where(hit, 1.0, choose)
+    choose_ref[...] = choose
+
+
+def square_kernel(length, low, upp, piv, low_out, upp_out, piv_out, low_scr, upp_scr, piv_scr, sems):
     nrows, width = low.shape[0], low_out.shape[1]
     chunk = math.lcm(width, 128)
-    for src, dst in ((low, low_out), (upp, upp_out), (piv, piv_out)):
+    work = ((low, low_scr, low_out), (piv, piv_scr, piv_out), (upp, upp_scr, upp_out))
+    fetches = [pltpu.make_async_copy(src, scr, sems.at[n]) for n, (src, scr, _) in enumerate(work)]
+    for fetch in fetches:
+        fetch.start()
+    for fetch, (src, scr, dst) in zip(fetches, work):
+        fetch.wait()
         for c in range(width * width // chunk):
-            piece = src[:, c * chunk : (c + 1) * chunk]
+            piece = scr[:, c * chunk : (c + 1) * chunk]
             for r in range(chunk // width):
                 a = c * (chunk // width) + r
                 dst[pl.ds(a, nrows, stride=width), :] = piece[:, r * width : (r + 1) * width]
-    for at in range(nrows):
-        here = slice(at * width, (at + 1) * width)
-        if at % length % 2 == 0 and at % length:
-            low_out[here, :] = low_out[here, :].T
-        piv_out[here, :] = piv_out[here, :].T
+        for at in range(nrows):
+            here = slice(at * width, (at + 1) * width)
+            if src is piv or (src is low and at % length % 2 == 0 and at % length):
+                dst[here, :] = dst[here, :].T
+
+
+def pick_kernel(nspan, nplane, columns_ref, pick_ref):
+    nblocks, nfaces = columns_ref.shape
+    span, plane = lax.axis_index("span"), lax.axis_index("plane")
+    position = table_positions(columns_ref[...], nfaces, span, plane, nspan, nplane)
+    selector, face = position // nfaces, position % nfaces
+    span_first = 1 if nspan % 2 else span % 2
+    plane_first = 1 if nplane % 2 else plane % 2
+    group = jnp.where(selector >= 3, selector - 2 - plane_first, selector - span_first)
+    group = jnp.where(group == 2, 0, group) + jnp.where(selector >= 3, 3, 1)
+    at = jnp.where(selector == 0, 0, group) * nfaces + face
+    eye = lax.broadcasted_iota(jnp.int32, (nfaces, nfaces), 0) == lax.broadcasted_iota(jnp.int32, (nfaces, nfaces), 1)
+    lane = lax.broadcasted_iota(jnp.int32, (nfaces, pick_ref.shape[1]), 1) % (pick_ref.shape[1] // 2)
+    for k in range(nblocks):
+        column = jnp.sum(jnp.where(eye, at[k : k + 1, :].astype(F32), 0.0), axis=1, keepdims=True).astype(jnp.int32)
+        pick_ref[k * nfaces : (k + 1) * nfaces, :] = jnp.where(lane == column, 1.0, 0.0)
 
 
 def line_kernel(nplane, nlines, *refs):
@@ -228,61 +260,58 @@
 def faces_kernel(choose, *refs):
     solved, mine_ref = refs[:-1], refs[-1]
     table = split(jnp.concatenate([s[...] for s in solved], axis=0), 3).astype(BF16)
-    mine_ref[...] = jnp.dot(choose[...], table, preferred_element_type=F32)
+    mine_ref[...] = jnp.dot(choose[...].astype(BF16), table, preferred_element_type=F32)
 
 
 def apply_kernel(nplane, nblocks, last, *refs):
     (blocks, slot, pick), faces, refs = refs[:3], refs[3:8], refs[8:]
     nold = ITERS if last else 1
     olds, refs = refs[:nold], refs[nold:]
-    next_ref, outs, (buf, x_scr, parts, sems, slot_scr, slot_sem) = refs[0], refs[1:-6], refs[-6:]
+    next_ref, outs, (buf, x_scr, acc_scr, parts, sems, slot_scr, slot_sem) = refs[0], refs[1:-7], refs[-7:]
     nfaces, width = faces[0].shape
     area = width * width
     chunk = math.lcm(width, 128)
     copies, count = chunk // width, area // chunk
     lane = lax.broadcasted_iota(jnp.int32, (1, 128), 1)
 
-    bounds = [0, 3 * count // 10, 6 * count // 10, 8 * count // 10, count]
-    bounds = sorted(set(bounds))
-    copies_of = []
+    bounds = [0, nblocks - 7, nblocks - 3, nblocks - 1, nblocks]
+    runs = []
     for g, (first, end) in enumerate(zip(bounds, bounds[1:])):
-        some = []
-        for k in range(nblocks):
-            where = pl.ds(k * area + first * chunk, (end - first) * chunk)
-            some.append(pltpu.make_async_copy(blocks.at[:, where], buf.at[:, where], sems.at[g, k]))
-            some[-1].start()
-        copies_of.append(some)
+        where = pl.ds(first * area, (end - first) * area)
+        runs.append(pltpu.make_async_copy(blocks.at[:, where], buf.at[:, where], sems.at[g]))
+        runs[-1].start()
     if not last:
         slots = pltpu.make_async_copy(slot, slot_scr, slot_sem)
         slots.start()
 
-    both = split(jnp.concatenate([f[...] for f in faces], axis=0), 2)
-    wide = jnp.concatenate([both] * copies, axis=1).astype(BF16)
-    x_scr[...] = jnp.dot(pick[...], wide, preferred_element_type=F32)
+    both = split(jnp.concatenate([f[...] for f in faces], axis=0), 2).astype(BF16)
+    picked = jnp.dot(pick[...].astype(BF16), both, preferred_element_type=F32)
+    x_scr[...] = jnp.concatenate([picked] * copies, axis=1)
     seg = [jnp.broadcast_to(jnp.where(lane % copies == r, 1.0, 0.0), (width, 128)) for r in range(copies)]
     seg = jnp.concatenate(seg, axis=0).astype(BF16)
+    for first, end, run in zip(bounds, bounds[1:], runs):
+        run.wait()
+        for v in range(0, chunk, 128):
+            xs = [x_scr[k * nfaces : (k + 1) * nfaces, v : v + 128] for k in range(first, end)]
+            for c in range(count):
+                at = c * chunk + v
+                total = None if first == 0 else acc_scr[:, at : at + 128]
+                for k in range(first, end):
+                    term = buf[:, k * area + at : k * area + at + 128] * xs[k - first]
+                    total = term if total is None else total + term
+                if end < nblocks:
+                    acc_scr[:, at : at + 128] = total
+                else:
+                    high = total.astype(BF16)
+                    row = 2 * c * nfaces
+                    parts[row : row + nfaces, v : v + 128] = high
+                    parts[row + nfaces : row + 2 * nfaces, v : v + 128] = (total - high.astype(F32)).astype(BF16)
+    sums = jnp.dot(parts[...], seg, preferred_element_type=F32)
     total = jnp.zeros((nfaces, 128), F32)
-    for first, end, some in zip(bounds, bounds[1:], copies_of):
-        for copy in some:
-            copy.wait()
-        for v in range(0, chunk, 128):
-            xs = [x_scr[k * nfaces : (k + 1) * nfaces, v : v + 128] for k in range(nblocks)]
-            for c in range(first, end):
-                acc = None
-                for k in range(nblocks):
-                    at = k * area + c * chunk + v
-                    term = buf[:, at : at + 128] * xs[k]
-                    acc = term if acc is None else acc + term
-                high = acc.astype(BF16)
-                at = 2 * c * nfaces
-                parts[at : at + nfaces, v : v + 128] = high
-                parts[at + nfaces : at + 2 * nfaces, v : v + 128] = (acc - high.astype(F32)).astype(BF16)
-        base = 2 * first * nfaces
-        sums = jnp.dot(parts[base : 2 * end * nfaces, :], seg, preferred_element_type=F32)
-        for c in range(first, end):
-            at = 2 * c * nfaces - base
-            both_sums = sums[at : at + nfaces] + sums[at + nfaces : at + 2 * nfaces]
-            total = total + jnp.where(lane // copies == c, both_sums, 0.0)
+    for c in range(count):
+        at = 2 * c * nfaces
+        pair = sums[at : at + nfaces] + sums[at + nfaces : at + 2 * nfaces]
+        total = total + jnp.where(lane // copies == c, pair, 0.0)
     u_next = total[:, :width] - SHIFT * olds[-1][...]
     next_ref[...] = u_next
     if last:
@@ -308,12 +337,13 @@
     us, zs = refs[: ITERS + 1], refs[ITERS + 1 : 2 * ITERS + 1]
     sol_ref, res_ref, ok_ref = refs[2 * ITERS + 1 :]
     width = sol_ref.shape[1]
-    lane = lax.broadcasted_iota(jnp.int32, gram_ref.shape, 1)
+    rows = jnp.sum(gram_ref[...], axis=0, keepdims=True)
+    lane = lax.broadcasted_iota(jnp.int32, rows.shape, 1)
     gram, at = {}, 0
     for i in range(ITERS + 1):
         for j in range(i, ITERS + 1):
-            value = jnp.sum(jnp.where(lane == at, gram_ref[...], 0.0), axis=1, keepdims=True)
-            gram[i, j] = gram[j, i] = jnp.broadcast_to(value, gram_ref.shape)
+            value = jnp.sum(jnp.where(lane == at, rows, 0.0), axis=1, keepdims=True)
+            gram[i, j] = gram[j, i] = jnp.broadcast_to(value, rows.shape)
             at += 1
     largest = functools.reduce(jnp.maximum, [jnp.abs(g) for g in gram.values()])
     ok = largest < 1e30
@@ -378,20 +408,8 @@
 
 def add_up(x):
     count = lax.axis_size("span") * lax.axis_size("plane")
-    if count & (count - 1):
-        return lax.psum(x, ("span", "plane"))
-    steps = [1 << i for i in range(count.bit_length() - 1)]
-
-    def of(flip):
-        return lax.ppermute(x, ("span", "plane"), [(i, i ^ flip) for i in range(count)])
-
-    for bits in [steps[:1], steps[1:3], *([step] for step in steps[3:])]:
-        if len(bits) == 2:
-            both, one, other = of(sum(bits)), of(bits[0]), of(bits[1])
-            x = (x + one) + (other + both)
-        elif bits:
-            x = x + of(bits[0])
-    return x
+    rows = jnp.broadcast_to(x, (count, x.shape[1]))
+    return lax.all_to_all(rows, ("span", "plane"), split_axis=0, concat_axis=0, tiled=True)
 
 
 def pairings(size):
@@ -412,25 +430,26 @@
     span_pairs, span_others = pairings(nspan)
     plane_pairs, plane_others = pairings(nplane)
 
-    us = [rhs.T]
-    send = call(
+    u_first, choose, *send = call(
         functools.partial(start_kernel, nplane),
-        [line_slot, us[0]],
-        [(per, width)] * nplane,
+        [line_slot, rhs.T],
+        [shape, (nfaces, 3 * nfaces)] + [(per, width)] * nplane,
         [pltpu.SMEM, pltpu.VMEM],
         ready=False,
     )
+    us = [u_first]
     factors = call(
         functools.partial(square_kernel, length),
         [line_lower, line_upper, pivot_inv],
         [(nfaces * width, width)] * 3,
+        [pl.ANY] * 3,
+        [pltpu.VMEM((nfaces, area), F32)] * 3 + [pltpu.SemaphoreType.DMA((3,))],
         flops=nfaces * area,
-        ready=False,
     )
     factors = [x.reshape(nfaces, width, width) for x in factors]
 
     zs = []
-    choose = pick = None
+    pick = None
     for step in range(ITERS):
         got = [send[0]] + [exchange(send[k], "plane", k) for k in range(1, nplane)]
         solved = call(
@@ -441,25 +460,15 @@
             flops=6 * nfaces * area,
         )
         if step == 0:
-            slot = lax.optimization_barrier((line_slot, solved[0]))[0].reshape(nplane, per)
-            me = lax.axis_index("plane")
-            owners = jnp.stack([jnp.asarray(partner(me, k, nplane)[1], jnp.int32) for k in range(nplane)])
-            places = jnp.arange(nplane, dtype=jnp.int32)
-            back = jnp.sum(jnp.where(owners[:, None, None] == places[None, :, None], slot[None], 0), axis=1)
-            back = jnp.tile(back.reshape(1, nfaces), (1, 3))
-            choose = (back == jnp.arange(nfaces, dtype=jnp.int32)[:, None]).astype(BF16)
+            (pick,) = call(
+                functools.partial(pick_kernel, nspan, nplane),
+                [lax.optimization_barrier((columns, solved[0]))[0]],
+                [(nblocks * nfaces, 10 * nfaces)],
+                ready=False,
+            )
         pieces = [solved[0]] + [exchange(solved[k], "plane", k) for k in range(1, nplane)]
         (mine,) = call(faces_kernel, [choose, *pieces], [shape])
         zs.append(mine)
-        if step == 0:
-            position = table_positions(lax.optimization_barrier((columns, mine))[0], nfaces)
-            selector, face = position // nfaces, position % nfaces
-            span_first = 1 if nspan % 2 else lax.axis_index("span") % 2
-            plane_first = 1 if nplane % 2 else lax.axis_index("plane") % 2
-            group = jnp.where(selector >= 3, selector - 3 + 1 - plane_first, selector - 1 + 1 - span_first) % 2
-            group = jnp.where(selector == 0, 0, group + jnp.where(selector >= 3, 3, 1))
-            lanes = lax.broadcasted_iota(jnp.int32, (1, 10 * nfaces), 1) % (5 * nfaces)
-            pick = (lanes == (group * nfaces + face).reshape(-1, 1)).astype(BF16)
         far = lax.ppermute(mine, "span", span_others)
         faces = [
             mine,
@@ -474,12 +483,13 @@
             functools.partial(apply_kernel, nplane, nblocks, last),
             args,
             [shape] + ([(1, 128)] if last else [(per, width)] * nplane),
-            [pl.ANY] + [pltpu.VMEM] * (len(args) - 1),
+            [pl.ANY] * 2 + [pltpu.VMEM] * (len(args) - 2),
             [
                 pltpu.VMEM((nfaces, nblocks * area), F32),
                 pltpu.VMEM((nblocks * nfaces, math.lcm(width, 128)), F32),
+                pltpu.VMEM((nfaces, area), F32),
                 pltpu.VMEM((2 * nfaces * area // math.lcm(width, 128), math.lcm(width, 128)), BF16),
-                pltpu.SemaphoreType.DMA((4, nblocks)),
+                pltpu.SemaphoreType.DMA((4,)),
                 pltpu.SMEM(line_slot.shape, jnp.int32),
                 pltpu.SemaphoreType.DMA,
             ],

time: 83.7 us -> 74.8 us (0.89)
  blocking collectives: 0 us -> 10.4 us
  waiting for transfers between devices: 26.8 us -> 19.2 us
  starting transfers between devices: 33.1 us -> 26.6 us
  other arithmetic: 2.43 us -> 0 us
  local copies, waits for them, and re-layouts: 2.24 us -> 0.04 us
    all_to_all x0 -> x1, blocking collectives: none -> 10.4 us  [add_up(): lax.all_to_all(rows, ('span', 'plane'), split_axis=0, concat_axis=0, tile...]
    ppermute x6 -> x0, waiting for transfers between devices: 7.24 us -> none  [of(): lax.ppermute(x, ('span', 'plane'), [(i, i ^ flip) for i in range(count)])]
    ppermute x6 -> x0, starting transfers between devices: 7.06 us -> none  [of(): lax.ppermute(x, ('span', 'plane'), [(i, i ^ flip) for i in range(count)])]
    unnamed x14 -> x10, local copies, waits for them, and re-layouts: 1.38 us -> 0.03 us
    optimization_barrier x1 -> x0, other arithmetic: 1.32 us -> none  [on_device(): lax.optimization_barrier((line_slot, solved[0]))[0].reshape(nplane, per)]
    pallas_call x12 -> x13, Pallas kernels: 17.4 us -> 17 us  [call(): pl.pallas_call(kernel, out_shape=[pltpu.VMEM(shape, F32) if pinned else j...]
  transfers between devices with their start and end apart: 36 -> 30, of which waited for: 19 -> 15; matrix products, arithmetic and copies ran while one was open for 1% -> 0% of each run, Pallas kernels for 3% -> 4%
where the time goes in v4:
time: 74.8 us; the launch traced here: 74.5 us
  starting transfers between devices  26.6 us (36%)
  waiting for transfers between devices  19.2 us (26%)
  Pallas kernels  17 us (23%)
  blocking collectives  10.4 us (14%)
  between operations  1.05 us (1%)
    pallas_call x13, Pallas kernels, call(): pl.pallas_call(kernel, out_shape=[pltpu.VMEM(shape, F32) if pinned else j...  17 us
    ppermute x18, starting transfers between devices, exchange(): lax.ppermute(x, axis, [(i, partner(i, k, size)[0]) for i in range(size)])  12.9 us
    ppermute x18, waiting for transfers between devices, exchange(): lax.ppermute(x, axis, [(i, partner(i, k, size)[0]) for i in range(size)])  12.7 us
    all_to_all x1, blocking collectives, add_up(): lax.all_to_all(rows, ('span', 'plane'), split_axis=0, concat_axis=0, tile...  10.4 us
    ppermute x3, starting transfers between devices, on_device(): far = lax.ppermute(mine, 'span', span_others)  9.48 us
    ppermute x3, waiting for transfers between devices, on_device(): far = lax.ppermute(mine, 'span', span_others)  6.2 us
    ppermute x3, starting transfers between devices, on_device(): lax.ppermute(mine, 'plane', plane_others)  2.52 us
    ppermute x3, starting transfers between devices, on_device(): lax.ppermute(mine, 'span', span_pairs)  1.63 us
  transfers between devices with their start and end apart: 30, of which 15 were waited for; matrix products, arithmetic and copies ran while one was open for 0% of the time, Pallas kernels for 4%

profile of v4, /device:TPU:0, one launch (start us, length us, event | category | flops | bytes accessed | tf_op | source)
XLA Modules:
  0.0 74.5 jit_solution(8680505852608727571)
XLA Ops:
  0.6 0.8 %shard_map.86 = (f32[16,80]{1,0:T(8,128)S(1)}, f32[16,48]{1,0:T(8,128)S(1)}, f32[4,80]{1,0:T(4,128)S(1)}, f32[4,80]{1,0:T(4,128)S(1)}, f32[4,80]{1,0:T(4,128)S(1)}, /*index=5*/f32[4,80]{1,0:T(4,128)S(1)}) custom-call(s32[1,16]{1,0:T(1,128)} %refs_1_.5, f32[16,80]{1,0:T(8,128)} %bitcast.565), custom_call_target="tpu_custom_call" | custom-call | bytes 5184 | tf_op jit(solution)/shard_map/pallas_call | solution.py:398
  2.0 2.6 %collective-permute-start.17 = (f32[4,80]{1,0:T(4,128)S(1)}, f32[4,80]{1,0:T(4,128)S(1)}, u32[]{:S(2)}, u32[]{:S(2)}) collective-permute-start(f32[4,80]{1,0:T(4,128)S(1)} %get-tuple-element.687), channel_id=1, source_target_pairs={{0,2},{1,3},{2,0},{3,1},{4,6},{5,7},{6,4},{7,5},{8,10},{9,11},{10,... | collective-permute-start | bytes 3848 | tf_op jit(solution)/shard_map/ppermute | solution.py:149
  4.7 2.3 %shard_map.87 = (f32[1280,80]{1,0:T(8,128)S(1)}, f32[1280,80]{1,0:T(8,128)S(1)}, f32[1280,80]{1,0:T(8,128)S(1)}) custom-call(f32[16,6400]{1,0:T(8,128)} %low.1, f32[16,6400]{1,0:T(8,128)} %upp.1, f32[16,6400]{1,0:T(8,128)} %piv.1), custom_call_target="tpu_custom_call" | custom-call | flops 102400 | bytes 1228800 | tf_op jit(solution)/shard_map/pallas_call | solution.py:398
  7.6 1.2 %shard_map.88 = (f32[4,80]{1,0:T(4,128)S(1)}, f32[4,80]{1,0:T(4,128)S(1)}, f32[4,80]{1,0:T(4,128)S(1)}, f32[4,80]{1,0:T(4,128)S(1)}) custom-call(f32[4,80]{1,0:T(4,128)S(1)} %get-tuple-element.685.refs_0_, f32[4,80]{1,0:T(4,128)S(1)} %collective-permute-done.16.refs_1_, f32[4,80]{1,0:T(4,128)S(1)} %collective-permute-done.17.refs_2_, ...), custom_call_target="tpu_custom_call" | custom-call | flops 614400 | bytes 1233920 | tf_op jit(solution)/shard_map/pallas_call | solution.py:398
  9.1 1.3 %collective-permute-start.20 = (f32[4,80]{1,0:T(4,128)S(1)}, f32[4,80]{1,0:T(4,128)S(1)}, u32[]{:S(2)}, u32[]{:S(2)}) collective-permute-start(f32[4,80]{1,0:T(4,128)S(1)} %get-tuple-element.696), channel_id=1, source_target_pairs={{0,2},{1,3},{2,0},{3,1},{4,6},{5,7},{6,4},{7,5},{8,10},{9,11},{10,... | collective-permute-start | bytes 3848 | tf_op jit(solution)/shard_map/ppermute | solution.py:149
  10.8 1.9 %collective-permute-done.20.refs_2_ = f32[4,80]{1,0:T(4,128)S(1)} collective-permute-done((f32[4,80]{1,0:T(4,128)S(1)}, f32[4,80]{1,0:T(4,128)S(1)}, u32[]{:S(2)}, u32[]{:S(2)}) %collective-permute-start.20) | collective-permute-done | bytes 1312 | tf_op jit(solution)/shard_map/ppermute | solution.py:149
  13.5 1.5 %collective-permute-start.22 = (f32[16,80]{1,0:T(8,128)S(1)}, f32[16,80]{1,0:T(8,128)S(1)}, u32[]{:S(2)}, u32[]{:S(2)}) collective-permute-start(f32[16,80]{1,0:T(8,128)S(1)} %shard_map.90.refs_3_.refs_4_), channel_id=1, source_target_pairs={{0,4},{4,0},{8,12},{12,8},{16,20},{20,16},{24,28},{28,24},{1,5},{5... | collective-permute-start | bytes 15368 | tf_op jit(solution)/shard_map/ppermute | solution.py:475
  15.0 3.6 %collective-permute-start.23 = (f32[16,80]{1,0:T(8,128)S(1)}, f32[16,80]{1,0:T(8,128)S(1)}, u32[]{:S(2)}, u32[]{:S(2)}) collective-permute-start(f32[16,80]{1,0:T(8,128)S(1)} %shard_map.90.refs_3_.refs_4_), channel_id=1, source_target_pairs={{0,28},{4,8},{8,4},{12,16},{16,12},{20,24},{24,20},{28,0},{1,29},{... | collective-permute-start | bytes 15368 | tf_op jit(solution)/shard_map/ppermute | solution.py:472
  18.6 0.8 %collective-permute-start.25 = (f32[16,80]{1,0:T(8,128)S(1)}, f32[16,80]{1,0:T(8,128)S(1)}, u32[]{:S(2)}, u32[]{:S(2)}) collective-permute-start(f32[16,80]{1,0:T(8,128)S(1)} %shard_map.90.refs_3_.refs_4_), channel_id=1, source_target_pairs={{0,3},{1,2},{2,1},{3,0},{4,7},{5,6},{6,5},{7,4},{8,11},{9,10},{10,... | collective-permute-start | bytes 15368 | tf_op jit(solution)/shard_map/ppermute | solution.py:478
  19.4 0.8 %shard_map.89.refs_2_ = f32[176,160]{1,0:T(8,128)S(1)} custom-call(s32[11,16]{1,0:T(8,128)} %columns_ref), custom_call_target="tpu_custom_call" | custom-call | bytes 704 | tf_op jit(solution)/shard_map/pallas_call | solution.py:398
  20.3 1.1 %collective-permute-done.23.refs_5_ = f32[16,80]{1,0:T(8,128)S(1)} collective-permute-done((f32[16,80]{1,0:T(8,128)S(1)}, f32[16,80]{1,0:T(8,128)S(1)}, u32[]{:S(2)}, u32[]{:S(2)}) %collective-permute-start.23) | collective-permute-done | bytes 5152 | tf_op jit(solution)/shard_map/ppermute | solution.py:472
  21.7 2.7 %shard_map.91 = (f32[16,80]{1,0:T(8,128)S(1)}, f32[4,80]{1,0:T(4,128)S(1)}, f32[4,80]{1,0:T(4,128)S(1)}, f32[4,80]{1,0:T(4,128)S(1)}, f32[4,80]{1,0:T(4,128)S(1)}) custom-call(f32[16,70400]{1,0:T(8,128)} %refs_0_.5, s32[1,16]{1,0:T(1,128)} %refs_1_.5, f32[176,160]{1,0:T(8,128)S(1)} %shard_map.89.refs_2_, f32[16,80]{1,0:T(8,128)S(1)} %shard_map.90.refs_3_.refs_4_, ...), custom_call_target="tpu_custom_call" | custom-call | flops 2252800 | bytes 4649024 | tf_op jit(solution)/shard_map/pallas_call | solution.py:398
  26.4 2.2 %collective-permute-done.27.refs_2_ = f32[4,80]{1,0:T(4,128)S(1)} collective-permute-done((f32[4,80]{1,0:T(4,128)S(1)}, f32[4,80]{1,0:T(4,128)S(1)}, u32[]{:S(2)}, u32[]{:S(2)}) %collective-permute-start.27) | collective-permute-done | bytes 1312 | tf_op jit(solution)/shard_map/ppermute | solution.py:149
  28.7 1.2 %shard_map.92 = (f32[4,80]{1,0:T(4,128)S(1)}, f32[4,80]{1,0:T(4,128)S(1)}, f32[4,80]{1,0:T(4,128)S(1)}, f32[4,80]{1,0:T(4,128)S(1)}) custom-call(f32[4,80]{1,0:T(4,128)S(1)} %get-tuple-element.699.refs_0_, f32[4,80]{1,0:T(4,128)S(1)} %collective-permute-done.26.refs_1_, f32[4,80]{1,0:T(4,128)S(1)} %collective-permute-done.27.refs_2_, ...), custom_call_target="tpu_custom_call" | custom-call | flops 614400 | bytes 1233920 | tf_op jit(solution)/shard_map/pallas_call | solution.py:398
  30.0 1.4 %collective-permute-start.30 = (f32[4,80]{1,0:T(4,128)S(1)}, f32[4,80]{1,0:T(4,128)S(1)}, u32[]{:S(2)}, u32[]{:S(2)}) collective-permute-start(f32[4,80]{1,0:T(4,128)S(1)} %get-tuple-element.705), channel_id=1, source_target_pairs={{0,2},{1,3},{2,0},{3,1},{4,6},{5,7},{6,4},{7,5},{8,10},{9,11},{10,... | collective-permute-start | bytes 3848 | tf_op jit(solution)/shard_map/ppermute | solution.py:149
  31.9 1.8 %collective-permute-done.30.refs_2_ = f32[4,80]{1,0:T(4,128)S(1)} collective-permute-done((f32[4,80]{1,0:T(4,128)S(1)}, f32[4,80]{1,0:T(4,128)S(1)}, u32[]{:S(2)}, u32[]{:S(2)}) %collective-permute-start.30) | collective-permute-done | bytes 1312 | tf_op jit(solution)/shard_map/ppermute | solution.py:149
  34.5 3.0 %collective-permute-start.33 = (f32[16,80]{1,0:T(8,128)S(1)}, f32[16,80]{1,0:T(8,128)S(1)}, u32[]{:S(2)}, u32[]{:S(2)}) collective-permute-start(f32[16,80]{1,0:T(8,128)S(1)} %shard_map.93.refs_3_.refs_5_), channel_id=1, source_target_pairs={{0,28},{4,8},{8,4},{12,16},{16,12},{20,24},{24,20},{28,0},{1,29},{... | collective-permute-start | bytes 15368 | tf_op jit(solution)/shard_map/ppermute | solution.py:472
  37.5 0.8 %collective-permute-start.35 = (f32[16,80]{1,0:T(8,128)S(1)}, f32[16,80]{1,0:T(8,128)S(1)}, u32[]{:S(2)}, u32[]{:S(2)}) collective-permute-start(f32[16,80]{1,0:T(8,128)S(1)} %shard_map.93.refs_3_.refs_5_), channel_id=1, source_target_pairs={{0,3},{1,2},{2,1},{3,0},{4,7},{5,6},{6,5},{7,4},{8,11},{9,10},{10,... | collective-permute-start | bytes 15368 | tf_op jit(solution)/shard_map/ppermute | solution.py:478
  38.4 2.6 %collective-permute-done.33.refs_5_ = f32[16,80]{1,0:T(8,128)S(1)} collective-permute-done((f32[16,80]{1,0:T(8,128)S(1)}, f32[16,80]{1,0:T(8,128)S(1)}, u32[]{:S(2)}, u32[]{:S(2)}) %collective-permute-start.33) | collective-permute-done | bytes 5152 | tf_op jit(solution)/shard_map/ppermute | solution.py:472
  40.9 2.7 %shard_map.94 = (f32[16,80]{1,0:T(8,128)S(1)}, f32[4,80]{1,0:T(4,128)S(1)}, f32[4,80]{1,0:T(4,128)S(1)}, f32[4,80]{1,0:T(4,128)S(1)}, f32[4,80]{1,0:T(4,128)S(1)}) custom-call(f32[16,70400]{1,0:T(8,128)} %refs_0_.5, s32[1,16]{1,0:T(1,128)S(1)} %copy-done.5, f32[176,160]{1,0:T(8,128)S(1)} %shard_map.89.refs_2_, f32[16,80]{1,0:T(8,128)S(1)} %shard_map.93.refs_3_.refs_5_, ...), custom_call_target="tpu_custom_call" | custom-call | flops 2252800 | bytes 4649024 | tf_op jit(solution)/shard_map/pallas_call | solution.py:398
  44.6 1.0 %collective-permute-start.38 = (f32[4,80]{1,0:T(4,128)S(1)}, f32[4,80]{1,0:T(4,128)S(1)}, u32[]{:S(2)}, u32[]{:S(2)}) collective-permute-start(f32[4,80]{1,0:T(4,128)S(1)} %get-tuple-element.711), channel_id=1, source_target_pairs={{0,3},{1,2},{2,1},{3,0},{4,7},{5,6},{6,5},{7,4},{8,11},{9,10},{10,... | collective-permute-start | bytes 3848 | tf_op jit(solution)/shard_map/ppermute | solution.py:149
  45.6 1.9 %collective-permute-done.37.refs_2_ = f32[4,80]{1,0:T(4,128)S(1)} collective-permute-done((f32[4,80]{1,0:T(4,128)S(1)}, f32[4,80]{1,0:T(4,128)S(1)}, u32[]{:S(2)}, u32[]{:S(2)}) %collective-permute-start.37) | collective-permute-done | bytes 1312 | tf_op jit(solution)/shard_map/ppermute | solution.py:149
  47.6 1.2 %shard_map.95 = (f32[4,80]{1,0:T(4,128)S(1)}, f32[4,80]{1,0:T(4,128)S(1)}, f32[4,80]{1,0:T(4,128)S(1)}, f32[4,80]{1,0:T(4,128)S(1)}) custom-call(f32[4,80]{1,0:T(4,128)S(1)} %get-tuple-element.708.refs_0_, f32[4,80]{1,0:T(4,128)S(1)} %collective-permute-done.36.refs_1_, f32[4,80]{1,0:T(4,128)S(1)} %collective-permute-done.37.refs_2_, ...), custom_call_target="tpu_custom_call" | custom-call | flops 614400 | bytes 1233920 | tf_op jit(solution)/shard_map/pallas_call | solution.py:398
  49.0 1.3 %collective-permute-start.40 = (f32[4,80]{1,0:T(4,128)S(1)}, f32[4,80]{1,0:T(4,128)S(1)}, u32[]{:S(2)}, u32[]{:S(2)}) collective-permute-start(f32[4,80]{1,0:T(4,128)S(1)} %get-tuple-element.714), channel_id=1, source_target_pairs={{0,2},{1,3},{2,0},{3,1},{4,6},{5,7},{6,4},{7,5},{8,10},{9,11},{10,... | collective-permute-start | bytes 3848 | tf_op jit(solution)/shard_map/ppermute | solution.py:149
  50.8 1.8 %collective-permute-done.40.refs_2_ = f32[4,80]{1,0:T(4,128)S(1)} collective-permute-done((f32[4,80]{1,0:T(4,128)S(1)}, f32[4,80]{1,0:T(4,128)S(1)}, u32[]{:S(2)}, u32[]{:S(2)}) %collective-permute-start.40) | collective-permute-done | bytes 1312 | tf_op jit(solution)/shard_map/ppermute | solution.py:149
  52.6 0.8 %collective-permute-done.41.refs_3_ = f32[4,80]{1,0:T(4,128)S(1)} collective-permute-done((f32[4,80]{1,0:T(4,128)S(1)}, f32[4,80]{1,0:T(4,128)S(1)}, u32[]{:S(2)}, u32[]{:S(2)}) %collective-permute-start.41) | collective-permute-done | bytes 1312 | tf_op jit(solution)/shard_map/ppermute | solution.py:149
  53.6 2.9 %collective-permute-start.43 = (f32[16,80]{1,0:T(8,128)S(1)}, f32[16,80]{1,0:T(8,128)S(1)}, u32[]{:S(2)}, u32[]{:S(2)}) collective-permute-start(f32[16,80]{1,0:T(8,128)S(1)} %shard_map.96.refs_3_.refs_6_), channel_id=1, source_target_pairs={{0,28},{4,8},{8,4},{12,16},{16,12},{20,24},{24,20},{28,0},{1,29},{... | collective-permute-start | bytes 15368 | tf_op jit(solution)/shard_map/ppermute | solution.py:472
  56.6 0.8 %collective-permute-start.45 = (f32[16,80]{1,0:T(8,128)S(1)}, f32[16,80]{1,0:T(8,128)S(1)}, u32[]{:S(2)}, u32[]{:S(2)}) collective-permute-start(f32[16,80]{1,0:T(8,128)S(1)} %shard_map.96.refs_3_.refs_6_), channel_id=1, source_target_pairs={{0,3},{1,2},{2,1},{3,0},{4,7},{5,6},{6,5},{7,4},{8,11},{9,10},{10,... | collective-permute-start | bytes 15368 | tf_op jit(solution)/shard_map/ppermute | solution.py:478
  57.4 2.6 %collective-permute-done.43.refs_5_ = f32[16,80]{1,0:T(8,128)S(1)} collective-permute-done((f32[16,80]{1,0:T(8,128)S(1)}, f32[16,80]{1,0:T(8,128)S(1)}, u32[]{:S(2)}, u32[]{:S(2)}) %collective-permute-start.43) | collective-permute-done | bytes 5152 | tf_op jit(solution)/shard_map/ppermute | solution.py:472
  60.0 2.7 %shard_map.97 = (f32[16,80]{1,0:T(8,128)S(1)}, f32[1,128]{1,0:T(1,128)S(1)}) custom-call(f32[16,70400]{1,0:T(8,128)} %refs_0_.5, s32[1,16]{1,0:T(1,128)S(1)} %copy-done.5, f32[176,160]{1,0:T(8,128)S(1)} %shard_map.89.refs_2_, f32[16,80]{1,0:T(8,128)S(1)} %shard_map.96.refs_3_.refs_6_, f32[16,80]{1,0:T(8,128)S(1)} %collective-permute-done.42.refs_4_, ...), custom_call_target="tpu_custom_call" | custom-call | flops 2252800 | bytes 4659264 | tf_op jit(solution)/shard_map/pallas_call | solution.py:398
  62.7 10.4 %all_to_all.112 = f32[32,1,128]{2,1,0:T(1,128)S(1)} all-to-all(f32[32,1,128]{2,1,0:T(1,128)S(1)} %broadcast_in_dim.83), channel_id=1, replica_groups=mesh['span'=8,'plane'=4] {'span','plane'}, dimensions={0} | all-to-all | bytes 32768 | tf_op jit(solution)/shard_map/all_to_all | solution.py:412
  73.2 0.8 %shard_map.98 = (f32[16,80]{1,0:T(8,128)}, f32[16,80]{1,0:T(8,128)}, f32[1,128]{1,0:T(1,128)S(1)}) custom-call(f32[32,128]{1,0:T(8,128)S(1)} %bitcast.552, f32[16,80]{1,0:T(8,128)S(1)} %get-tuple-element.698.refs_8_.refs_0_, f32[16,80]{1,0:T(8,128)S(1)} %get-tuple-element.707.refs_8_.refs_9_.refs_1_, f32[16,80]{1,0:T(8,128)S(1)} %get-tuple-element.716.refs_10_.refs_2_, ...), custom_call_target="tpu_custom_call" | custom-call | bytes 52224 | tf_op jit(solution)/shard_map/pallas_call | solution.py:398
  (54 shorter events, 8.9 us)
Async XLA Ops:
  1.5 5.5 %collective-permute-start.16 = (f32[4,80]{1,0:T(4,128)S(1)}, f32[4,80]{1,0:T(4,128)S(1)}, u32[]{:S(2)}, u32[]{:S(2)}) collective-permute-start(f32[4,80]{1,0:T(4,128)S(1)} %get-tuple-element.686), channel_id=1, source_target_pairs={{0,1},{1,0},{2,3},{3,2},{4,5},{5,4},{6,7},{7,6},{8,9},{9,8},{10,11... | collective-permute-start | bytes 3848 | tf_op jit(solution)/shard_map/ppermute | solution.py:149
  2.0 5.0 %collective-permute-start.17 = (f32[4,80]{1,0:T(4,128)S(1)}, f32[4,80]{1,0:T(4,128)S(1)}, u32[]{:S(2)}, u32[]{:S(2)}) collective-permute-start(f32[4,80]{1,0:T(4,128)S(1)} %get-tuple-element.687), channel_id=1, source_target_pairs={{0,2},{1,3},{2,0},{3,1},{4,6},{5,7},{6,4},{7,5},{8,10},{9,11},{10,... | collective-permute-start | bytes 3848 | tf_op jit(solution)/shard_map/ppermute | solution.py:149
  4.6 3.0 %collective-permute-start.18 = (f32[4,80]{1,0:T(4,128)S(1)}, f32[4,80]{1,0:T(4,128)S(1)}, u32[]{:S(2)}, u32[]{:S(2)}) collective-permute-start(f32[4,80]{1,0:T(4,128)S(1)} %get-tuple-element.688), channel_id=1, source_target_pairs={{0,3},{1,2},{2,1},{3,0},{4,7},{5,6},{6,5},{7,4},{8,11},{9,10},{10,... | collective-permute-start | bytes 3848 | tf_op jit(solution)/shard_map/ppermute | solution.py:149
  8.9 1.9 %collective-permute-start.19 = (f32[4,80]{1,0:T(4,128)S(1)}, f32[4,80]{1,0:T(4,128)S(1)}, u32[]{:S(2)}, u32[]{:S(2)}) collective-permute-start(f32[4,80]{1,0:T(4,128)S(1)} %get-tuple-element.695), channel_id=1, source_target_pairs={{0,1},{1,0},{2,3},{3,2},{4,5},{5,4},{6,7},{7,6},{8,9},{9,8},{10,11... | collective-permute-start | bytes 3848 | tf_op jit(solution)/shard_map/ppermute | solution.py:149
  9.1 3.6 %collective-permute-start.20 = (f32[4,80]{1,0:T(4,128)S(1)}, f32[4,80]{1,0:T(4,128)S(1)}, u32[]{:S(2)}, u32[]{:S(2)}) collective-permute-start(f32[4,80]{1,0:T(4,128)S(1)} %get-tuple-element.696), channel_id=1, source_target_pairs={{0,2},{1,3},{2,0},{3,1},{4,6},{5,7},{6,4},{7,5},{8,10},{9,11},{10,... | collective-permute-start | bytes 3848 | tf_op jit(solution)/shard_map/ppermute | solution.py:149
  10.4 3.0 %collective-permute-start.21 = (f32[4,80]{1,0:T(4,128)S(1)}, f32[4,80]{1,0:T(4,128)S(1)}, u32[]{:S(2)}, u32[]{:S(2)}) collective-permute-start(f32[4,80]{1,0:T(4,128)S(1)} %get-tuple-element.697), channel_id=1, source_target_pairs={{0,3},{1,2},{2,1},{3,0},{4,7},{5,6},{6,5},{7,4},{8,11},{9,10},{10,... | collective-permute-start | bytes 3848 | tf_op jit(solution)/shard_map/ppermute | solution.py:149
  13.5 6.8 %collective-permute-start.22 = (f32[16,80]{1,0:T(8,128)S(1)}, f32[16,80]{1,0:T(8,128)S(1)}, u32[]{:S(2)}, u32[]{:S(2)}) collective-permute-start(f32[16,80]{1,0:T(8,128)S(1)} %shard_map.90.refs_3_.refs_4_), channel_id=1, source_target_pairs={{0,4},{4,0},{8,12},{12,8},{16,20},{20,16},{24,28},{28,24},{1,5},{5... | collective-permute-start | bytes 15368 | tf_op jit(solution)/shard_map/ppermute | solution.py:475
  15.0 6.3 %collective-permute-start.23 = (f32[16,80]{1,0:T(8,128)S(1)}, f32[16,80]{1,0:T(8,128)S(1)}, u32[]{:S(2)}, u32[]{:S(2)}) collective-permute-start(f32[16,80]{1,0:T(8,128)S(1)} %shard_map.90.refs_3_.refs_4_), channel_id=1, source_target_pairs={{0,28},{4,8},{8,4},{12,16},{16,12},{20,24},{24,20},{28,0},{1,29},{... | collective-permute-start | bytes 15368 | tf_op jit(solution)/shard_map/ppermute | solution.py:472
  18.6 2.8 %collective-permute-start.24 = (f32[16,80]{1,0:T(8,128)S(1)}, f32[16,80]{1,0:T(8,128)S(1)}, u32[]{:S(2)}, u32[]{:S(2)}) collective-permute-start(f32[16,80]{1,0:T(8,128)S(1)} %shard_map.90.refs_3_.refs_4_), channel_id=1, source_target_pairs={{0,1},{1,0},{2,3},{3,2},{4,5},{5,4},{6,7},{7,6},{8,9},{9,8},{10,11... | collective-permute-start | bytes 15368 | tf_op jit(solution)/shard_map/ppermute | solution.py:477
  18.6 3.1 %collective-permute-start.25 = (f32[16,80]{1,0:T(8,128)S(1)}, f32[16,80]{1,0:T(8,128)S(1)}, u32[]{:S(2)}, u32[]{:S(2)}) collective-permute-start(f32[16,80]{1,0:T(8,128)S(1)} %shard_map.90.refs_3_.refs_4_), channel_id=1, source_target_pairs={{0,3},{1,2},{2,1},{3,0},{4,7},{5,6},{6,5},{7,4},{8,11},{9,10},{10,... | collective-permute-start | bytes 15368 | tf_op jit(solution)/shard_map/ppermute | solution.py:478
  24.4 49.7 %copy-start = (f32[16,6400]{1,0:T(8,128)S(1)}, f32[16,6400]{1,0:T(8,128)}, u32[]{:S(2)}) copy-start(f32[16,6400]{1,0:T(8,128)} %low.1) | copy-start | bytes 1228804
  24.4 49.7 %copy-start.1 = (f32[16,6400]{1,0:T(8,128)S(1)}, f32[16,6400]{1,0:T(8,128)}, u32[]{:S(2)}) copy-start(f32[16,6400]{1,0:T(8,128)} %upp.1) | copy-start | bytes 1228804
  24.4 2.0 %collective-permute-start.26 = (f32[4,80]{1,0:T(4,128)S(1)}, f32[4,80]{1,0:T(4,128)S(1)}, u32[]{:S(2)}, u32[]{:S(2)}) collective-permute-start(f32[4,80]{1,0:T(4,128)S(1)} %get-tuple-element.700), channel_id=1, source_target_pairs={{0,1},{1,0},{2,3},{3,2},{4,5},{5,4},{6,7},{7,6},{8,9},{9,8},{10,11... | collective-permute-start | bytes 3848 | tf_op jit(solution)/shard_map/ppermute | solution.py:149
  25.0 3.6 %collective-permute-start.27 = (f32[4,80]{1,0:T(4,128)S(1)}, f32[4,80]{1,0:T(4,128)S(1)}, u32[]{:S(2)}, u32[]{:S(2)}) collective-permute-start(f32[4,80]{1,0:T(4,128)S(1)} %get-tuple-element.701), channel_id=1, source_target_pairs={{0,2},{1,3},{2,0},{3,1},{4,6},{5,7},{6,4},{7,5},{8,10},{9,11},{10,... | collective-permute-start | bytes 3848 | tf_op jit(solution)/shard_map/ppermute | solution.py:149
  25.7 3.0 %collective-permute-start.28 = (f32[4,80]{1,0:T(4,128)S(1)}, f32[4,80]{1,0:T(4,128)S(1)}, u32[]{:S(2)}, u32[]{:S(2)}) collective-permute-start(f32[4,80]{1,0:T(4,128)S(1)} %get-tuple-element.702), channel_id=1, source_target_pairs={{0,3},{1,2},{2,1},{3,0},{4,7},{5,6},{6,5},{7,4},{8,11},{9,10},{10,... | collective-permute-start | bytes 3848 | tf_op jit(solution)/shard_map/ppermute | solution.py:149
  30.0 1.9 %collective-permute-start.29 = (f32[4,80]{1,0:T(4,128)S(1)}, f32[4,80]{1,0:T(4,128)S(1)}, u32[]{:S(2)}, u32[]{:S(2)}) collective-permute-start(f32[4,80]{1,0:T(4,128)S(1)} %get-tuple-element.704), channel_id=1, source_target_pairs={{0,1},{1,0},{2,3},{3,2},{4,5},{5,4},{6,7},{7,6},{8,9},{9,8},{10,11... | collective-permute-start | bytes 3848 | tf_op jit(solution)/shard_map/ppermute | solution.py:149
  30.0 3.7 %collective-permute-start.30 = (f32[4,80]{1,0:T(4,128)S(1)}, f32[4,80]{1,0:T(4,128)S(1)}, u32[]{:S(2)}, u32[]{:S(2)}) collective-permute-start(f32[4,80]{1,0:T(4,128)S(1)} %get-tuple-element.705), channel_id=1, source_target_pairs={{0,2},{1,3},{2,0},{3,1},{4,6},{5,7},{6,4},{7,5},{8,10},{9,11},{10,... | collective-permute-start | bytes 3848 | tf_op jit(solution)/shard_map/ppermute | solution.py:149
  31.4 3.0 %collective-permute-start.31 = (f32[4,80]{1,0:T(4,128)S(1)}, f32[4,80]{1,0:T(4,128)S(1)}, u32[]{:S(2)}, u32[]{:S(2)}) collective-permute-start(f32[4,80]{1,0:T(4,128)S(1)} %get-tuple-element.706), channel_id=1, source_target_pairs={{0,3},{1,2},{2,1},{3,0},{4,7},{5,6},{6,5},{7,4},{8,11},{9,10},{10,... | collective-permute-start | bytes 3848 | tf_op jit(solution)/shard_map/ppermute | solution.py:149
  34.5 3.8 %collective-permute-start.32 = (f32[16,80]{1,0:T(8,128)S(1)}, f32[16,80]{1,0:T(8,128)S(1)}, u32[]{:S(2)}, u32[]{:S(2)}) collective-permute-start(f32[16,80]{1,0:T(8,128)S(1)} %shard_map.93.refs_3_.refs_5_), channel_id=1, source_target_pairs={{0,4},{4,0},{8,12},{12,8},{16,20},{20,16},{24,28},{28,24},{1,5},{5... | collective-permute-start | bytes 15368 | tf_op jit(solution)/shard_map/ppermute | solution.py:475
  34.5 6.4 %collective-permute-start.33 = (f32[16,80]{1,0:T(8,128)S(1)}, f32[16,80]{1,0:T(8,128)S(1)}, u32[]{:S(2)}, u32[]{:S(2)}) collective-permute-start(f32[16,80]{1,0:T(8,128)S(1)} %shard_map.93.refs_3_.refs_5_), channel_id=1, source_target_pairs={{0,28},{4,8},{8,4},{12,16},{16,12},{20,24},{24,20},{28,0},{1,29},{... | collective-permute-start | bytes 15368 | tf_op jit(solution)/shard_map/ppermute | solution.py:472
  37.5 3.4 %collective-permute-start.34 = (f32[16,80]{1,0:T(8,128)S(1)}, f32[16,80]{1,0:T(8,128)S(1)}, u32[]{:S(2)}, u32[]{:S(2)}) collective-permute-start(f32[16,80]{1,0:T(8,128)S(1)} %shard_map.93.refs_3_.refs_5_), channel_id=1, source_target_pairs={{0,1},{1,0},{2,3},{3,2},{4,5},{5,4},{6,7},{7,6},{8,9},{9,8},{10,11... | collective-permute-start | bytes 15368 | tf_op jit(solution)/shard_map/ppermute | solution.py:477
  37.5 3.4 %collective-permute-start.35 = (f32[16,80]{1,0:T(8,128)S(1)}, f32[16,80]{1,0:T(8,128)S(1)}, u32[]{:S(2)}, u32[]{:S(2)}) collective-permute-start(f32[16,80]{1,0:T(8,128)S(1)} %shard_map.93.refs_3_.refs_5_), channel_id=1, source_target_pairs={{0,3},{1,2},{2,1},{3,0},{4,7},{5,6},{6,5},{7,4},{8,11},{9,10},{10,... | collective-permute-start | bytes 15368 | tf_op jit(solution)/shard_map/ppermute | solution.py:478
  43.6 1.9 %collective-permute-start.36 = (f32[4,80]{1,0:T(4,128)S(1)}, f32[4,80]{1,0:T(4,128)S(1)}, u32[]{:S(2)}, u32[]{:S(2)}) collective-permute-start(f32[4,80]{1,0:T(4,128)S(1)} %get-tuple-element.709), channel_id=1, source_target_pairs={{0,1},{1,0},{2,3},{3,2},{4,5},{5,4},{6,7},{7,6},{8,9},{9,8},{10,11... | collective-permute-start | bytes 3848 | tf_op jit(solution)/shard_map/ppermute | solution.py:149
  43.8 3.6 %collective-permute-start.37 = (f32[4,80]{1,0:T(4,128)S(1)}, f32[4,80]{1,0:T(4,128)S(1)}, u32[]{:S(2)}, u32[]{:S(2)}) collective-permute-start(f32[4,80]{1,0:T(4,128)S(1)} %get-tuple-element.710), channel_id=1, source_target_pairs={{0,2},{1,3},{2,0},{3,1},{4,6},{5,7},{6,4},{7,5},{8,10},{9,11},{10,... | collective-permute-start | bytes 3848 | tf_op jit(solution)/shard_map/ppermute | solution.py:149
  44.6 3.0 %collective-permute-start.38 = (f32[4,80]{1,0:T(4,128)S(1)}, f32[4,80]{1,0:T(4,128)S(1)}, u32[]{:S(2)}, u32[]{:S(2)}) collective-permute-start(f32[4,80]{1,0:T(4,128)S(1)} %get-tuple-element.711), channel_id=1, source_target_pairs={{0,3},{1,2},{2,1},{3,0},{4,7},{5,6},{6,5},{7,4},{8,11},{9,10},{10,... | collective-permute-start | bytes 3848 | tf_op jit(solution)/shard_map/ppermute | solution.py:149
  48.8 2.0 %collective-permute-start.39 = (f32[4,80]{1,0:T(4,128)S(1)}, f32[4,80]{1,0:T(4,128)S(1)}, u32[]{:S(2)}, u32[]{:S(2)}) collective-permute-start(f32[4,80]{1,0:T(4,128)S(1)} %get-tuple-element.713), channel_id=1, source_target_pairs={{0,1},{1,0},{2,3},{3,2},{4,5},{5,4},{6,7},{7,6},{8,9},{9,8},{10,11... | collective-permute-start | bytes 3848 | tf_op jit(solution)/shard_map/ppermute | solution.py:149
  49.0 3.6 %collective-permute-start.40 = (f32[4,80]{1,0:T(4,128)S(1)}, f32[4,80]{1,0:T(4,128)S(1)}, u32[]{:S(2)}, u32[]{:S(2)}) collective-permute-start(f32[4,80]{1,0:T(4,128)S(1)} %get-tuple-element.714), channel_id=1, source_target_pairs={{0,2},{1,3},{2,0},{3,1},{4,6},{5,7},{6,4},{7,5},{8,10},{9,11},{10,... | collective-permute-start | bytes 3848 | tf_op jit(solution)/shard_map/ppermute | solution.py:149
  50.4 3.0 %collective-permute-start.41 = (f32[4,80]{1,0:T(4,128)S(1)}, f32[4,80]{1,0:T(4,128)S(1)}, u32[]{:S(2)}, u32[]{:S(2)}) collective-permute-start(f32[4,80]{1,0:T(4,128)S(1)} %get-tuple-element.715), channel_id=1, source_target_pairs={{0,3},{1,2},{2,1},{3,0},{4,7},{5,6},{6,5},{7,4},{8,11},{9,10},{10,... | collective-permute-start | bytes 3848 | tf_op jit(solution)/shard_map/ppermute | solution.py:149
  53.5 3.9 %collective-permute-start.42 = (f32[16,80]{1,0:T(8,128)S(1)}, f32[16,80]{1,0:T(8,128)S(1)}, u32[]{:S(2)}, u32[]{:S(2)}) collective-permute-start(f32[16,80]{1,0:T(8,128)S(1)} %shard_map.96.refs_3_.refs_6_), channel_id=1, source_target_pairs={{0,4},{4,0},{8,12},{12,8},{16,20},{20,16},{24,28},{28,24},{1,5},{5... | collective-permute-start | bytes 15368 | tf_op jit(solution)/shard_map/ppermute | solution.py:475
  53.6 6.3 %collective-permute-start.43 = (f32[16,80]{1,0:T(8,128)S(1)}, f32[16,80]{1,0:T(8,128)S(1)}, u32[]{:S(2)}, u32[]{:S(2)}) collective-permute-start(f32[16,80]{1,0:T(8,128)S(1)} %shard_map.96.refs_3_.refs_6_), channel_id=1, source_target_pairs={{0,28},{4,8},{8,4},{12,16},{16,12},{20,24},{24,20},{28,0},{1,29},{... | collective-permute-start | bytes 15368 | tf_op jit(solution)/shard_map/ppermute | solution.py:472
  56.6 3.4 %collective-permute-start.44 = (f32[16,80]{1,0:T(8,128)S(1)}, f32[16,80]{1,0:T(8,128)S(1)}, u32[]{:S(2)}, u32[]{:S(2)}) collective-permute-start(f32[16,80]{1,0:T(8,128)S(1)} %shard_map.96.refs_3_.refs_6_), channel_id=1, source_target_pairs={{0,1},{1,0},{2,3},{3,2},{4,5},{5,4},{6,7},{7,6},{8,9},{9,8},{10,11... | collective-permute-start | bytes 15368 | tf_op jit(solution)/shard_map/ppermute | solution.py:477
  56.6 3.4 %collective-permute-start.45 = (f32[16,80]{1,0:T(8,128)S(1)}, f32[16,80]{1,0:T(8,128)S(1)}, u32[]{:S(2)}, u32[]{:S(2)}) collective-permute-start(f32[16,80]{1,0:T(8,128)S(1)} %shard_map.96.refs_3_.refs_6_), channel_id=1, source_target_pairs={{0,3},{1,2},{2,1},{3,0},{4,7},{5,6},{6,5},{7,4},{8,11},{9,10},{10,... | collective-permute-start | bytes 15368 | tf_op jit(solution)/shard_map/ppermute | solution.py:478
  (3 other events, 139.7 us)

commit v5 on v4

--- a/solution.py
+++ b/solution.py
@@ -177,7 +177,7 @@
     choose_ref[...] = choose
 
 
-def square_kernel(length, low, upp, piv, low_out, upp_out, piv_out, low_scr, upp_scr, piv_scr, sems):
+def square_kernel(length, low, upp, piv, _, low_out, upp_out, piv_out, low_scr, upp_scr, piv_scr, sems):
     nrows, width = low.shape[0], low_out.shape[1]
     chunk = math.lcm(width, 128)
     work = ((low, low_scr, low_out), (piv, piv_scr, piv_out), (upp, upp_scr, upp_out))
@@ -197,21 +197,34 @@
                 dst[here, :] = dst[here, :].T
 
 
-def pick_kernel(nspan, nplane, columns_ref, pick_ref):
+def parities():
+    return [1 if lax.axis_size(a) % 2 else lax.axis_index(a) % 2 for a in ("span", "plane")]
+
+
+def early_blocks():
+    span_odd, plane_odd = parities()
+    return (1 + span_odd, 3 + plane_odd), (2 - span_odd, 4 - plane_odd)
+
+
+def pick_kernel(nspan, nplane, columns_ref, early_ref, late_ref):
     nblocks, nfaces = columns_ref.shape
     span, plane = lax.axis_index("span"), lax.axis_index("plane")
     position = table_positions(columns_ref[...], nfaces, span, plane, nspan, nplane)
     selector, face = position // nfaces, position % nfaces
-    span_first = 1 if nspan % 2 else span % 2
-    plane_first = 1 if nplane % 2 else plane % 2
-    group = jnp.where(selector >= 3, selector - 2 - plane_first, selector - span_first)
-    group = jnp.where(group == 2, 0, group) + jnp.where(selector >= 3, 3, 1)
-    at = jnp.where(selector == 0, 0, group) * nfaces + face
+    span_odd, plane_odd = [parity == 1 for parity in parities()]
+    of_span = jnp.where((selector == 1) == span_odd, 1, 3)
+    of_plane = jnp.where((selector == 3) == plane_odd, 2, 4)
+    group = jnp.where(selector == 0, 0, jnp.where(selector <= 2, of_span, of_plane))
+    at = (group * nfaces + face).astype(F32)
     eye = lax.broadcasted_iota(jnp.int32, (nfaces, nfaces), 0) == lax.broadcasted_iota(jnp.int32, (nfaces, nfaces), 1)
-    lane = lax.broadcasted_iota(jnp.int32, (nfaces, pick_ref.shape[1]), 1) % (pick_ref.shape[1] // 2)
-    for k in range(nblocks):
-        column = jnp.sum(jnp.where(eye, at[k : k + 1, :].astype(F32), 0.0), axis=1, keepdims=True).astype(jnp.int32)
-        pick_ref[k * nfaces : (k + 1) * nfaces, :] = jnp.where(lane == column, 1.0, 0.0)
+    first, second = jnp.where(span_odd, at[2:3], at[1:2]), jnp.where(span_odd, at[1:2], at[2:3])
+    third, fourth = jnp.where(plane_odd, at[4:5], at[3:4]), jnp.where(plane_odd, at[3:4], at[4:5])
+    rest = [at[k : k + 1] for k in range(5, nblocks)]
+    for ref, rows in ((early_ref, [at[0:1], first, third]), (late_ref, [second, fourth, *rest])):
+        lane = lax.broadcasted_iota(jnp.int32, (nfaces, ref.shape[1]), 1) % (ref.shape[1] // 2)
+        for n, row in enumerate(rows):
+            column = jnp.sum(jnp.where(eye, row, 0.0), axis=1, keepdims=True).astype(jnp.int32)
+            ref[n * nfaces : (n + 1) * nfaces, :] = jnp.where(lane == column, 1.0, 0.0).astype(BF16)
 
 
 def line_kernel(nplane, nlines, *refs):
@@ -263,59 +276,97 @@
     mine_ref[...] = jnp.dot(choose[...].astype(BF16), table, preferred_element_type=F32)
 
 
-def apply_kernel(nplane, nblocks, last, *refs):
-    (blocks, slot, pick), faces, refs = refs[:3], refs[3:8], refs[8:]
+def repeat_faces(faces, pick, copies):
+    both = split(jnp.concatenate([f[...] for f in faces], axis=0), 2).astype(BF16)
+    picked = jnp.dot(pick[...], both, preferred_element_type=F32)
+    return jnp.concatenate([picked] * copies, axis=1)
+
+
+def add_products(work, x_scr, acc_scr, parts, width):
+    nfaces, area = acc_scr.shape
+    chunk = x_scr.shape[1]
+    copies, count = chunk // width, area // chunk
+    lane = lax.broadcasted_iota(jnp.int32, (1, 128), 1)
+    seg = [jnp.broadcast_to(jnp.where(lane % copies == r, 1.0, 0.0), (width, 128)) for r in range(copies)]
+    seg = jnp.concatenate(seg, axis=0).astype(BF16)
+    total = jnp.zeros((nfaces, 128), F32)
+    done = 0
+    for n, (places, fetch) in enumerate(work):
+        if fetch is not None:
+            fetch.wait()
+        last = n == len(work) - 1
+        for half in ((0, count // 2), (count // 2, count)):
+            for v in range(0, chunk, 128):
+                rows = range(done * nfaces, (done + len(places)) * nfaces, nfaces)
+                xs = [x_scr[row : row + nfaces, v : v + 128] for row in rows]
+                for c in range(*half):
+                    at = c * chunk + v
+                    value = acc_scr[:, at : at + 128] if n else None
+                    for (ref, column), x in zip(places, xs):
+                        term = ref[:, column + at : column + at + 128] * x
+                        value = term if value is None else value + term
+                    if not last:
+                        acc_scr[:, at : at + 128] = value
+                        continue
+                    high = value.astype(BF16)
+                    row = 2 * c * nfaces
+                    parts[row : row + nfaces, v : v + 128] = high
+                    parts[row + nfaces : row + 2 * nfaces, v : v + 128] = (value - high.astype(F32)).astype(BF16)
+            if last:
+                base = 2 * half[0] * nfaces
+                sums = jnp.dot(parts[base : 2 * half[1] * nfaces, :], seg, preferred_element_type=F32)
+                for c in range(*half):
+                    at = 2 * c * nfaces - base
+                    pair = sums[at : at + nfaces] + sums[at + nfaces : at + 2 * nfaces]
+                    total = total + jnp.where(lane // copies == c, pair, 0.0)
+        done += len(places)
+    return total[:, :width]
+
+
+def early_kernel(nblocks, blocks, pick, *refs):
+    faces, (sum_ref, held, buf, x_scr, acc_scr, parts, sems) = refs[:3], refs[3:]
+    width = faces[0].shape[1]
+    area = width * width
+    early, late = early_blocks()
+
+    def fetch(k, count, dst, column, n):
+        start = pl.multiple_of(k * area, 128) if not isinstance(k, int) else k * area
+        return pltpu.make_async_copy(
+            blocks.at[:, pl.ds(start, count * area)], dst.at[:, pl.ds(column, count * area)], sems.at[n]
+        )
+
+    mine = [fetch(k, 1, buf, n * area, n) for n, k in enumerate((0, *early))]
+    kept = [fetch(late[1], 1, held, 0, 3), fetch(5, nblocks - 5, held, area, 4)]
+    for copy in mine + kept:
+        copy.start()
+    x_scr[...] = repeat_faces(faces, pick, x_scr.shape[1] // width)
+    work = [([(buf, n * area)], copy) for n, copy in enumerate(mine)]
+    sum_ref[...] = add_products(work, x_scr, acc_scr, parts, width)
+    for copy in kept:
+        copy.wait()
+
+
+def late_kernel(nplane, last, *refs):
+    (blocks, slot, held, pick, early_sum), faces, refs = refs[:5], refs[5:10], refs[10:]
     nold = ITERS if last else 1
     olds, refs = refs[:nold], refs[nold:]
-    next_ref, outs, (buf, x_scr, acc_scr, parts, sems, slot_scr, slot_sem) = refs[0], refs[1:-7], refs[-7:]
+    next_ref, outs, (buf, x_scr, acc_scr, parts, sem, slot_scr, slot_sem) = refs[0], refs[1:-7], refs[-7:]
     nfaces, width = faces[0].shape
     area = width * width
-    chunk = math.lcm(width, 128)
-    copies, count = chunk // width, area // chunk
-    lane = lax.broadcasted_iota(jnp.int32, (1, 128), 1)
-
-    bounds = [0, nblocks - 7, nblocks - 3, nblocks - 1, nblocks]
-    runs = []
-    for g, (first, end) in enumerate(zip(bounds, bounds[1:])):
-        where = pl.ds(first * area, (end - first) * area)
-        runs.append(pltpu.make_async_copy(blocks.at[:, where], buf.at[:, where], sems.at[g]))
-        runs[-1].start()
+    _, late = early_blocks()
+    fetch = pltpu.make_async_copy(blocks.at[:, pl.ds(pl.multiple_of(late[0] * area, 128), area)], buf, sem)
+    fetch.start()
     if not last:
         slots = pltpu.make_async_copy(slot, slot_scr, slot_sem)
         slots.start()
-
-    both = split(jnp.concatenate([f[...] for f in faces], axis=0), 2).astype(BF16)
-    picked = jnp.dot(pick[...].astype(BF16), both, preferred_element_type=F32)
-    x_scr[...] = jnp.concatenate([picked] * copies, axis=1)
-    seg = [jnp.broadcast_to(jnp.where(lane % copies == r, 1.0, 0.0), (width, 128)) for r in range(copies)]
-    seg = jnp.concatenate(seg, axis=0).astype(BF16)
-    for first, end, run in zip(bounds, bounds[1:], runs):
-        run.wait()
-        for v in range(0, chunk, 128):
-            xs = [x_scr[k * nfaces : (k + 1) * nfaces, v : v + 128] for k in range(first, end)]
-            for c in range(count):
-                at = c * chunk + v
-                total = None if first == 0 else acc_scr[:, at : at + 128]
-                for k in range(first, end):
-                    term = buf[:, k * area + at : k * area + at + 128] * xs[k - first]
-                    total = term if total is None else total + term
-                if end < nblocks:
-                    acc_scr[:, at : at + 128] = total
-                else:
-                    high = total.astype(BF16)
-                    row = 2 * c * nfaces
-                    parts[row : row + nfaces, v : v + 128] = high
-                    parts[row + nfaces : row + 2 * nfaces, v : v + 128] = (total - high.astype(F32)).astype(BF16)
-    sums = jnp.dot(parts[...], seg, preferred_element_type=F32)
-    total = jnp.zeros((nfaces, 128), F32)
-    for c in range(count):
-        at = 2 * c * nfaces
-        pair = sums[at : at + nfaces] + sums[at + nfaces : at + 2 * nfaces]
-        total = total + jnp.where(lane // copies == c, pair, 0.0)
-    u_next = total[:, :width] - SHIFT * olds[-1][...]
+    repeated = repeat_faces(faces, pick, x_scr.shape[1] // width)
+    x_scr[...] = jnp.concatenate([repeated[nfaces:], repeated[:nfaces]], axis=0)
+    work = [([(held, column) for column in range(0, held.shape[1], area)], None), ([(buf, 0)], fetch)]
+    u_next = early_sum[...] + add_products(work, x_scr, acc_scr, parts, width) - SHIFT * olds[-1][...]
     next_ref[...] = u_next
     if last:
         gram_ref = outs[0]
+        lane = lax.broadcasted_iota(jnp.int32, gram_ref.shape, 1)
         basis = [old[...] for old in olds] + [u_next]
         gram, at = jnp.zeros(gram_ref.shape, F32), 0
         for i in range(ITERS + 1):
@@ -390,14 +441,14 @@
     ok_ref[...] = jnp.where(ok, 1.0, 0.0)
 
 
-def call(kernel, args, outs, spaces=None, scratch=(), flops=0, pinned=True, ready=True):
+def call(kernel, args, outs, spaces=None, scratch=(), flops=0, pinned=True, ready=True, kind=F32):
     spaces = [pltpu.VMEM] * len(args) if spaces is None else spaces
     if ready:
         args = [pltpu.with_memory_space_constraint(x, s) if s is pltpu.VMEM else x for x, s in zip(args, spaces)]
     size = sum(x.dtype.itemsize * math.prod(x.shape) for x in args)
     return pl.pallas_call(
         kernel,
-        out_shape=[pltpu.VMEM(shape, F32) if pinned else jax.ShapeDtypeStruct(shape, F32) for shape in outs],
+        out_shape=[pltpu.VMEM(shape, kind) if pinned else jax.ShapeDtypeStruct(shape, kind) for shape in outs],
         in_specs=[pl.BlockSpec(memory_space=s) for s in spaces],
         out_specs=[pl.BlockSpec(memory_space=pltpu.VMEM) for _ in outs],
         scratch_shapes=scratch,
@@ -438,19 +489,18 @@
         ready=False,
     )
     us = [u_first]
-    factors = call(
-        functools.partial(square_kernel, length),
-        [line_lower, line_upper, pivot_inv],
-        [(nfaces * width, width)] * 3,
-        [pl.ANY] * 3,
-        [pltpu.VMEM((nfaces, area), F32)] * 3 + [pltpu.SemaphoreType.DMA((3,))],
-        flops=nfaces * area,
-    )
-    factors = [x.reshape(nfaces, width, width) for x in factors]
-
     zs = []
-    pick = None
+    picks = None
     for step in range(ITERS):
+        factors = call(
+            functools.partial(square_kernel, length),
+            [line_lower, line_upper, pivot_inv, us[-1]],
+            [(nfaces * width, width)] * 3,
+            [pl.ANY] * 4,
+            [pltpu.VMEM((nfaces, area), F32)] * 3 + [pltpu.SemaphoreType.DMA((3,))],
+            flops=nfaces * area,
+        )
+        factors = [x.reshape(nfaces, width, width) for x in factors]
         got = [send[0]] + [exchange(send[k], "plane", k) for k in range(1, nplane)]
         solved = call(
             functools.partial(line_kernel, nplane, owned),
@@ -460,39 +510,46 @@
             flops=6 * nfaces * area,
         )
         if step == 0:
-            (pick,) = call(
+            picks = call(
                 functools.partial(pick_kernel, nspan, nplane),
                 [lax.optimization_barrier((columns, solved[0]))[0]],
-                [(nblocks * nfaces, 10 * nfaces)],
+                [(3 * nfaces, 6 * nfaces), ((nblocks - 3) * nfaces, 10 * nfaces)],
                 ready=False,
+                kind=BF16,
             )
         pieces = [solved[0]] + [exchange(solved[k], "plane", k) for k in range(1, nplane)]
         (mine,) = call(faces_kernel, [choose, *pieces], [shape])
         zs.append(mine)
-        far = lax.ppermute(mine, "span", span_others)
-        faces = [
-            mine,
-            lax.ppermute(mine, "span", span_pairs),
-            far,
-            lax.ppermute(mine, "plane", plane_pairs),
-            lax.ppermute(mine, "plane", plane_others),
-        ]
+        other = lax.ppermute(mine, "span", span_others)
+        near = [mine, lax.ppermute(mine, "span", span_pairs), lax.ppermute(mine, "plane", plane_pairs)]
+        far = [other, lax.ppermute(mine, "plane", plane_others)]
+        chunk = math.lcm(width, 128)
+
+        def scratch(count, fetched):
+            return [
+                pltpu.VMEM((nfaces, fetched * area), F32),
+                pltpu.VMEM((count * nfaces, chunk), F32),
+                pltpu.VMEM((nfaces, area), F32),
+                pltpu.VMEM((2 * nfaces * area // chunk, chunk), BF16),
+            ]
+
+        early_sum, held = call(
+            functools.partial(early_kernel, nblocks),
+            [blocks, picks[0], *near],
+            [shape, (nfaces, (nblocks - 4) * area)],
+            [pl.ANY] + [pltpu.VMEM] * 4,
+            scratch(3, 3) + [pltpu.SemaphoreType.DMA((5,))],
+            flops=6 * nfaces * area,
+        )
         last = step == ITERS - 1
-        args = [blocks, line_slot, pick, *faces, *(us if last else us[-1:])]
+        args = [blocks, line_slot, held, picks[1], early_sum, *near, *far, *(us if last else us[-1:])]
         out = call(
-            functools.partial(apply_kernel, nplane, nblocks, last),
+            functools.partial(late_kernel, nplane, last),
             args,
             [shape] + ([(1, 128)] if last else [(per, width)] * nplane),
             [pl.ANY] * 2 + [pltpu.VMEM] * (len(args) - 2),
-            [
-                pltpu.VMEM((nfaces, nblocks * area), F32),
-                pltpu.VMEM((nblocks * nfaces, math.lcm(width, 128)), F32),
-                pltpu.VMEM((nfaces, area), F32),
-                pltpu.VMEM((2 * nfaces * area // math.lcm(width, 128), math.lcm(width, 128)), BF16),
-                pltpu.SemaphoreType.DMA((4,)),
-                pltpu.SMEM(line_slot.shape, jnp.int32),
-                pltpu.SemaphoreType.DMA,
-            ],
+            scratch(nblocks - 3, 1)
+            + [pltpu.SemaphoreType.DMA, pltpu.SMEM(line_slot.shape, jnp.int32), pltpu.SemaphoreType.DMA],
             flops=2 * nblocks * nfaces * area,
         )
         us.append(out[0])

time: 74.8 us -> 72.2 us (0.965)
  Pallas kernels: 17 us -> 25.2 us
  waiting for transfers between devices: 19.2 us -> 11.1 us
  starting transfers between devices: 26.6 us -> 24.2 us
    pallas_call x13 -> x18, Pallas kernels: 17 us -> 25.2 us  [call(): pl.pallas_call(kernel, out_shape=[pltpu.VMEM(shape, kind) if pinned else...]
    ppermute x6, waiting for transfers between devices: 6.51 us -> 0.8 us  [the longest x3 0.8 us: on_device(): other = lax.ppermute(mine, 'span', span_others)]
    ppermute x18, waiting for transfers between devices: 12.7 us -> 8.76 us  [exchange(): lax.ppermute(x, axis, [(i, partner(i, k, size)[0]) for i in range(size)])]
    ppermute x6, starting transfers between devices: 12 us -> 9.7 us  [the longest x3 7.7 us: on_device(): other = lax.ppermute(mine, 'span', span_others)]
    ppermute x3, waiting for transfers between devices: 0.01 us -> 1.52 us  [on_device(): lax.ppermute(mine, 'span', span_pairs)]
  transfers between devices with their start and end apart: 30 -> 30, of which waited for: 15 -> 13; matrix products, arithmetic and copies ran while one was open for 0% -> 0% of each run, Pallas kernels for 4% -> 20%
where the time goes in v5:
time: 72.2 us; the launch traced here: 71.7 us
  Pallas kernels  25.2 us (35%)
  starting transfers between devices  24.2 us (34%)
  waiting for transfers between devices  11.1 us (15%)
  blocking collectives  9.79 us (14%)
  between operations  1.11 us (2%)
    pallas_call x18, Pallas kernels, call(): pl.pallas_call(kernel, out_shape=[pltpu.VMEM(shape, kind) if pinned else...  25.2 us
    ppermute x18, starting transfers between devices, exchange(): lax.ppermute(x, axis, [(i, partner(i, k, size)[0]) for i in range(size)])  12.8 us
    all_to_all x1, blocking collectives, add_up(): lax.all_to_all(rows, ('span', 'plane'), split_axis=0, concat_axis=0, tile...  9.79 us
    ppermute x18, waiting for transfers between devices, exchange(): lax.ppermute(x, axis, [(i, partner(i, k, size)[0]) for i in range(size)])  8.76 us
    ppermute x3, starting transfers between devices, on_device(): other = lax.ppermute(mine, 'span', span_others)  7.7 us
    ppermute x3, starting transfers between devices, on_device(): far = [other, lax.ppermute(mine, 'plane', plane_others)]  2 us
    ppermute x3, starting transfers between devices, on_device(): lax.ppermute(mine, 'span', span_pairs)  1.57 us
    ppermute x3, waiting for transfers between devices, on_device(): lax.ppermute(mine, 'span', span_pairs)  1.52 us
  transfers between devices with their start and end apart: 30, of which 13 were waited for; matrix products, arithmetic and copies ran while one was open for 0% of the time, Pallas kernels for 20%

profile of v5, /device:TPU:0, one launch (start us, length us, event | category | flops | bytes accessed | tf_op | source)
XLA Modules:
  0.0 71.7 jit_solution(18149466370431566174)
XLA Ops:
  0.6 0.8 %shard_map.86 = (f32[16,80]{1,0:T(8,128)S(1)}, f32[16,48]{1,0:T(8,128)S(1)}, f32[4,80]{1,0:T(4,128)S(1)}, f32[4,80]{1,0:T(4,128)S(1)}, f32[4,80]{1,0:T(4,128)S(1)}, /*index=5*/f32[4,80]{1,0:T(4,128)S(1)}) custom-call(s32[1,16]{1,0:T(1,128)} %refs_1_.5, f32[16,80]{1,0:T(8,128)} %bitcast.571), custom_call_target="tpu_custom_call" | custom-call | bytes 5184 | tf_op jit(solution)/shard_map/pallas_call | solution.py:449
  2.0 2.6 %collective-permute-start.17 = (f32[4,80]{1,0:T(4,128)S(1)}, f32[4,80]{1,0:T(4,128)S(1)}, u32[]{:S(2)}, u32[]{:S(2)}) collective-permute-start(f32[4,80]{1,0:T(4,128)S(1)} %get-tuple-element.701), channel_id=1, source_target_pairs={{0,2},{1,3},{2,0},{3,1},{4,6},{5,7},{6,4},{7,5},{8,10},{9,11},{10,... | collective-permute-start | bytes 3848 | tf_op jit(solution)/shard_map/ppermute | solution.py:149
  4.7 2.3 %shard_map.87 = (f32[1280,80]{1,0:T(8,128)S(1)}, f32[1280,80]{1,0:T(8,128)S(1)}, f32[1280,80]{1,0:T(8,128)S(1)}) custom-call(f32[16,6400]{1,0:T(8,128)} %low.5, f32[16,6400]{1,0:T(8,128)} %upp.5, f32[16,6400]{1,0:T(8,128)} %piv.5, f32[16,80]{1,0:T(8,128)S(1)} %get-tuple-element.703._.refs_10_.refs_0_), custom_call_target="tpu_custom_call" | custom-call | flops 102400 | bytes 1233920 | tf_op jit(solution)/shard_map/pallas_call | solution.py:449
  7.6 1.3 %shard_map.88 = (f32[4,80]{1,0:T(4,128)S(1)}, f32[4,80]{1,0:T(4,128)S(1)}, f32[4,80]{1,0:T(4,128)S(1)}, f32[4,80]{1,0:T(4,128)S(1)}) custom-call(f32[4,80]{1,0:T(4,128)S(1)} %get-tuple-element.699.refs_0_, f32[4,80]{1,0:T(4,128)S(1)} %collective-permute-done.16.refs_1_, f32[4,80]{1,0:T(4,128)S(1)} %collective-permute-done.17.refs_2_, ...), custom_call_target="tpu_custom_call" | custom-call | flops 614400 | bytes 1233920 | tf_op jit(solution)/shard_map/pallas_call | solution.py:449
  9.1 1.3 %collective-permute-start.20 = (f32[4,80]{1,0:T(4,128)S(1)}, f32[4,80]{1,0:T(4,128)S(1)}, u32[]{:S(2)}, u32[]{:S(2)}) collective-permute-start(f32[4,80]{1,0:T(4,128)S(1)} %get-tuple-element.712), channel_id=1, source_target_pairs={{0,2},{1,3},{2,0},{3,1},{4,6},{5,7},{6,4},{7,5},{8,10},{9,11},{10,... | collective-permute-start | bytes 3848 | tf_op jit(solution)/shard_map/ppermute | solution.py:149
  10.8 1.9 %collective-permute-done.20.refs_2_ = f32[4,80]{1,0:T(4,128)S(1)} collective-permute-done((f32[4,80]{1,0:T(4,128)S(1)}, f32[4,80]{1,0:T(4,128)S(1)}, u32[]{:S(2)}, u32[]{:S(2)}) %collective-permute-start.20) | collective-permute-done | bytes 1312 | tf_op jit(solution)/shard_map/ppermute | solution.py:149
  13.5 1.5 %collective-permute-start.22 = (f32[16,80]{1,0:T(8,128)S(1)}, f32[16,80]{1,0:T(8,128)S(1)}, u32[]{:S(2)}, u32[]{:S(2)}) collective-permute-start(f32[16,80]{1,0:T(8,128)S(1)} %shard_map.90.refs_0_.refs_5_.refs_4_), channel_id=1, source_target_pairs={{0,4},{4,0},{8,12},{12,8},{16,20},{20,16},{24,28},{28,24},{1,5},{5... | collective-permute-start | bytes 15368 | tf_op jit(solution)/shard_map/ppermute | solution.py:524
  15.0 3.6 %collective-permute-start.24 = (f32[16,80]{1,0:T(8,128)S(1)}, f32[16,80]{1,0:T(8,128)S(1)}, u32[]{:S(2)}, u32[]{:S(2)}) collective-permute-start(f32[16,80]{1,0:T(8,128)S(1)} %shard_map.90.refs_0_.refs_5_.refs_4_), channel_id=1, source_target_pairs={{0,28},{4,8},{8,4},{12,16},{16,12},{20,24},{24,20},{28,0},{1,29},{... | collective-permute-start | bytes 15368 | tf_op jit(solution)/shard_map/ppermute | solution.py:523
  19.1 0.8 %shard_map.89 = (bf16[48,96]{1,0:T(8,128)(2,1)S(1)}, bf16[128,160]{1,0:T(8,128)(2,1)S(1)}) custom-call(s32[11,16]{1,0:T(8,128)} %columns_ref), custom_call_target="tpu_custom_call" | custom-call | bytes 704 | tf_op jit(solution)/shard_map/pallas_call | solution.py:449
  20.0 2.4 %shard_map.91 = (f32[16,80]{1,0:T(8,128)S(1)}, f32[16,44800]{1,0:T(8,128)S(1)}) custom-call(f32[16,70400]{1,0:T(8,128)} %refs_0_.5, bf16[48,96]{1,0:T(8,128)(2,1)S(1)} %get-tuple-element.709.pick, f32[16,80]{1,0:T(8,128)S(1)} %shard_map.90.refs_0_.refs_5_.refs_4_, f32[16,80]{1,0:T(8,128)S(1)} %collective-permute-done.22.refs_1_.refs_6_, ...), custom_call_target="tpu_custom_call" | custom-call | flops 614400 | bytes 4530176 | tf_op jit(solution)/shard_map/pallas_call | solution.py:449
  22.5 1.6 %shard_map.92 = (f32[16,80]{1,0:T(8,128)S(1)}, f32[4,80]{1,0:T(4,128)S(1)}, f32[4,80]{1,0:T(4,128)S(1)}, f32[4,80]{1,0:T(4,128)S(1)}, f32[4,80]{1,0:T(4,128)S(1)}) custom-call(f32[16,70400]{1,0:T(8,128)} %refs_0_.5, s32[1,16]{1,0:T(1,128)S(1)} %copy-done.5, f32[16,44800]{1,0:T(8,128)S(1)} %get-tuple-element.714.refs_2_, ...), custom_call_target="tpu_custom_call" | custom-call | flops 2252800 | bytes 7449664 | tf_op jit(solution)/shard_map/pallas_call | solution.py:449
  24.5 1.3 %collective-permute-start.27 = (f32[4,80]{1,0:T(4,128)S(1)}, f32[4,80]{1,0:T(4,128)S(1)}, u32[]{:S(2)}, u32[]{:S(2)}) collective-permute-start(f32[4,80]{1,0:T(4,128)S(1)} %get-tuple-element.719), channel_id=1, source_target_pairs={{0,2},{1,3},{2,0},{3,1},{4,6},{5,7},{6,4},{7,5},{8,10},{9,11},{10,... | collective-permute-start | bytes 3848 | tf_op jit(solution)/shard_map/ppermute | solution.py:149
  26.1 2.1 %shard_map.93 = (f32[1280,80]{1,0:T(8,128)S(1)}, f32[1280,80]{1,0:T(8,128)S(1)}, f32[1280,80]{1,0:T(8,128)S(1)}) custom-call(f32[16,6400]{1,0:T(8,128)S(1)} %copy-done, f32[16,6400]{1,0:T(8,128)S(1)} %copy-done.1, f32[16,6400]{1,0:T(8,128)} %piv.5, f32[16,80]{1,0:T(8,128)S(1)} %get-tuple-element.721._.refs_10_.refs_11_.refs_1_), custom_call_target="tpu_custom_call" | custom-call | flops 102400 | bytes 1233920 | tf_op jit(solution)/shard_map/pallas_call | solution.py:449
  28.8 1.2 %shard_map.94 = (f32[4,80]{1,0:T(4,128)S(1)}, f32[4,80]{1,0:T(4,128)S(1)}, f32[4,80]{1,0:T(4,128)S(1)}, f32[4,80]{1,0:T(4,128)S(1)}) custom-call(f32[4,80]{1,0:T(4,128)S(1)} %get-tuple-element.717.refs_0_, f32[4,80]{1,0:T(4,128)S(1)} %collective-permute-done.26.refs_1_, f32[4,80]{1,0:T(4,128)S(1)} %collective-permute-done.27.refs_2_, ...), custom_call_target="tpu_custom_call" | custom-call | flops 614400 | bytes 1233920 | tf_op jit(solution)/shard_map/pallas_call | solution.py:449
  30.2 1.1 %collective-permute-start.30 = (f32[4,80]{1,0:T(4,128)S(1)}, f32[4,80]{1,0:T(4,128)S(1)}, u32[]{:S(2)}, u32[]{:S(2)}) collective-permute-start(f32[4,80]{1,0:T(4,128)S(1)} %get-tuple-element.727), channel_id=1, source_target_pairs={{0,2},{1,3},{2,0},{3,1},{4,6},{5,7},{6,4},{7,5},{8,10},{9,11},{10,... | collective-permute-start | bytes 3848 | tf_op jit(solution)/shard_map/ppermute | solution.py:149
  32.0 1.8 %collective-permute-done.30.refs_2_ = f32[4,80]{1,0:T(4,128)S(1)} collective-permute-done((f32[4,80]{1,0:T(4,128)S(1)}, f32[4,80]{1,0:T(4,128)S(1)}, u32[]{:S(2)}, u32[]{:S(2)}) %collective-permute-start.30) | collective-permute-done | bytes 1312 | tf_op jit(solution)/shard_map/ppermute | solution.py:149
  34.5 2.1 %collective-permute-start.34 = (f32[16,80]{1,0:T(8,128)S(1)}, f32[16,80]{1,0:T(8,128)S(1)}, u32[]{:S(2)}, u32[]{:S(2)}) collective-permute-start(f32[16,80]{1,0:T(8,128)S(1)} %shard_map.95.refs_0_.refs_5_), channel_id=1, source_target_pairs={{0,28},{4,8},{8,4},{12,16},{16,12},{20,24},{24,20},{28,0},{1,29},{... | collective-permute-start | bytes 15368 | tf_op jit(solution)/shard_map/ppermute | solution.py:523
  36.6 0.8 %collective-permute-start.35 = (f32[16,80]{1,0:T(8,128)S(1)}, f32[16,80]{1,0:T(8,128)S(1)}, u32[]{:S(2)}, u32[]{:S(2)}) collective-permute-start(f32[16,80]{1,0:T(8,128)S(1)} %shard_map.95.refs_0_.refs_5_), channel_id=1, source_target_pairs={{0,3},{1,2},{2,1},{3,0},{4,7},{5,6},{6,5},{7,4},{8,11},{9,10},{10,... | collective-permute-start | bytes 15368 | tf_op jit(solution)/shard_map/ppermute | solution.py:525
  37.4 0.8 %collective-permute-done.32.refs_1_.refs_6_ = f32[16,80]{1,0:T(8,128)S(1)} collective-permute-done((f32[16,80]{1,0:T(8,128)S(1)}, f32[16,80]{1,0:T(8,128)S(1)}, u32[]{:S(2)}, u32[]{:S(2)}) %collective-permute-start.32) | collective-permute-done | bytes 5152 | tf_op jit(solution)/shard_map/ppermute | solution.py:524
  38.2 2.4 %shard_map.96 = (f32[16,80]{1,0:T(8,128)S(1)}, f32[16,44800]{1,0:T(8,128)S(1)}) custom-call(f32[16,70400]{1,0:T(8,128)} %refs_0_.5, bf16[48,96]{1,0:T(8,128)(2,1)S(1)} %get-tuple-element.709.pick, f32[16,80]{1,0:T(8,128)S(1)} %shard_map.95.refs_0_.refs_5_, f32[16,80]{1,0:T(8,128)S(1)} %collective-permute-done.32.refs_1_.refs_6_, ...), custom_call_target="tpu_custom_call" | custom-call | flops 614400 | bytes 4530176 | tf_op jit(solution)/shard_map/pallas_call | solution.py:449
  41.0 1.6 %shard_map.97 = (f32[16,80]{1,0:T(8,128)S(1)}, f32[4,80]{1,0:T(4,128)S(1)}, f32[4,80]{1,0:T(4,128)S(1)}, f32[4,80]{1,0:T(4,128)S(1)}, f32[4,80]{1,0:T(4,128)S(1)}) custom-call(f32[16,70400]{1,0:T(8,128)} %refs_0_.5, s32[1,16]{1,0:T(1,128)S(1)} %copy-done.5, f32[16,44800]{1,0:T(8,128)S(1)} %get-tuple-element.729.refs_2_, ...), custom_call_target="tpu_custom_call" | custom-call | flops 2252800 | bytes 7449664 | tf_op jit(solution)/shard_map/pallas_call | solution.py:449
  42.7 1.0 %collective-permute-start.37 = (f32[4,80]{1,0:T(4,128)S(1)}, f32[4,80]{1,0:T(4,128)S(1)}, u32[]{:S(2)}, u32[]{:S(2)}) collective-permute-start(f32[4,80]{1,0:T(4,128)S(1)} %get-tuple-element.733), channel_id=1, source_target_pairs={{0,2},{1,3},{2,0},{3,1},{4,6},{5,7},{6,4},{7,5},{8,10},{9,11},{10,... | collective-permute-start | bytes 3848 | tf_op jit(solution)/shard_map/ppermute | solution.py:149
  43.7 0.8 %collective-permute-start.38 = (f32[4,80]{1,0:T(4,128)S(1)}, f32[4,80]{1,0:T(4,128)S(1)}, u32[]{:S(2)}, u32[]{:S(2)}) collective-permute-start(f32[4,80]{1,0:T(4,128)S(1)} %get-tuple-element.734), channel_id=1, source_target_pairs={{0,3},{1,2},{2,1},{3,0},{4,7},{5,6},{6,5},{7,4},{8,11},{9,10},{10,... | collective-permute-start | bytes 3848 | tf_op jit(solution)/shard_map/ppermute | solution.py:149
  44.5 2.1 %shard_map.98 = (f32[1280,80]{1,0:T(8,128)S(1)}, f32[1280,80]{1,0:T(8,128)S(1)}, f32[1280,80]{1,0:T(8,128)S(1)}) custom-call(f32[16,6400]{1,0:T(8,128)S(1)} %copy-done, f32[16,6400]{1,0:T(8,128)S(1)} %copy-done.1, f32[16,6400]{1,0:T(8,128)} %piv.5, f32[16,80]{1,0:T(8,128)S(1)} %get-tuple-element.735._.refs_12_.refs_2_), custom_call_target="tpu_custom_call" | custom-call | flops 102400 | bytes 1233920 | tf_op jit(solution)/shard_map/pallas_call | solution.py:449
  46.7 1.2 %shard_map.99 = (f32[4,80]{1,0:T(4,128)S(1)}, f32[4,80]{1,0:T(4,128)S(1)}, f32[4,80]{1,0:T(4,128)S(1)}, f32[4,80]{1,0:T(4,128)S(1)}) custom-call(f32[4,80]{1,0:T(4,128)S(1)} %get-tuple-element.731.refs_0_, f32[4,80]{1,0:T(4,128)S(1)} %collective-permute-done.36.refs_1_, f32[4,80]{1,0:T(4,128)S(1)} %collective-permute-done.37.refs_2_, ...), custom_call_target="tpu_custom_call" | custom-call | flops 614400 | bytes 1233920 | tf_op jit(solution)/shard_map/pallas_call | solution.py:449
  48.3 1.0 %collective-permute-start.40 = (f32[4,80]{1,0:T(4,128)S(1)}, f32[4,80]{1,0:T(4,128)S(1)}, u32[]{:S(2)}, u32[]{:S(2)}) collective-permute-start(f32[4,80]{1,0:T(4,128)S(1)} %get-tuple-element.741), channel_id=1, source_target_pairs={{0,2},{1,3},{2,0},{3,1},{4,6},{5,7},{6,4},{7,5},{8,10},{9,11},{10,... | collective-permute-start | bytes 3848 | tf_op jit(solution)/shard_map/ppermute | solution.py:149
  49.9 2.0 %collective-permute-done.40.refs_2_ = f32[4,80]{1,0:T(4,128)S(1)} collective-permute-done((f32[4,80]{1,0:T(4,128)S(1)}, f32[4,80]{1,0:T(4,128)S(1)}, u32[]{:S(2)}, u32[]{:S(2)}) %collective-permute-start.40) | collective-permute-done | bytes 1312 | tf_op jit(solution)/shard_map/ppermute | solution.py:149
  52.6 2.1 %collective-permute-start.44 = (f32[16,80]{1,0:T(8,128)S(1)}, f32[16,80]{1,0:T(8,128)S(1)}, u32[]{:S(2)}, u32[]{:S(2)}) collective-permute-start(f32[16,80]{1,0:T(8,128)S(1)} %shard_map.100.refs_0_.refs_5_.refs_6_), channel_id=1, source_target_pairs={{0,28},{4,8},{8,4},{12,16},{16,12},{20,24},{24,20},{28,0},{1,29},{... | collective-permute-start | bytes 15368 | tf_op jit(solution)/shard_map/ppermute | solution.py:523
  56.1 2.4 %shard_map.101 = (f32[16,80]{1,0:T(8,128)S(1)}, f32[16,44800]{1,0:T(8,128)S(1)}) custom-call(f32[16,70400]{1,0:T(8,128)} %refs_0_.5, bf16[48,96]{1,0:T(8,128)(2,1)S(1)} %get-tuple-element.709.pick, f32[16,80]{1,0:T(8,128)S(1)} %shard_map.100.refs_0_.refs_5_.refs_6_, f32[16,80]{1,0:T(8,128)S(1)} %collective-permute-done.42.refs_1_.refs_6_, ...), custom_call_target="tpu_custom_call" | custom-call | flops 614400 | bytes 4530176 | tf_op jit(solution)/shard_map/pallas_call | solution.py:449
  59.0 1.7 %shard_map.102 = (f32[16,80]{1,0:T(8,128)S(1)}, f32[1,128]{1,0:T(1,128)S(1)}) custom-call(f32[16,70400]{1,0:T(8,128)} %refs_0_.5, s32[1,16]{1,0:T(1,128)S(1)} %copy-done.5, f32[16,44800]{1,0:T(8,128)S(1)} %get-tuple-element.743.refs_2_, bf16[128,160]{1,0:T(8,128)(2,1)S(1)} %get-tuple-element.715.refs_3_, f32[16,80]{1,0:T(8,128)S(1)} %get-tuple-element.744.refs_4_, ...), custom_call_target="tpu_custom_call" | custom-call | flops 2252800 | bytes 7459904 | tf_op jit(solution)/shard_map/pallas_call | solution.py:449
  60.7 9.8 %all_to_all.112 = f32[32,1,128]{2,1,0:T(1,128)S(1)} all-to-all(f32[32,1,128]{2,1,0:T(1,128)S(1)} %broadcast_in_dim.83), channel_id=1, replica_groups=mesh['span'=8,'plane'=4] {'span','plane'}, dimensions={0} | all-to-all | bytes 32768 | tf_op jit(solution)/shard_map/all_to_all | solution.py:463
  70.4 0.8 %shard_map.103 = (f32[16,80]{1,0:T(8,128)}, f32[16,80]{1,0:T(8,128)}, f32[1,128]{1,0:T(1,128)S(1)}) custom-call(f32[32,128]{1,0:T(8,128)S(1)} %bitcast.558, f32[16,80]{1,0:T(8,128)S(1)} %get-tuple-element.703._.refs_10_.refs_0_, f32[16,80]{1,0:T(8,128)S(1)} %get-tuple-element.721._.refs_10_.refs_11_.refs_1_, ...), custom_call_target="tpu_custom_call" | custom-call | bytes 52224 | tf_op jit(solution)/shard_map/pallas_call | solution.py:449
  (59 shorter events, 10.3 us)
Async XLA Ops:
  1.5 5.5 %collective-permute-start.16 = (f32[4,80]{1,0:T(4,128)S(1)}, f32[4,80]{1,0:T(4,128)S(1)}, u32[]{:S(2)}, u32[]{:S(2)}) collective-permute-start(f32[4,80]{1,0:T(4,128)S(1)} %get-tuple-element.700), channel_id=1, source_target_pairs={{0,1},{1,0},{2,3},{3,2},{4,5},{5,4},{6,7},{7,6},{8,9},{9,8},{10,11... | collective-permute-start | bytes 3848 | tf_op jit(solution)/shard_map/ppermute | solution.py:149
  2.0 5.0 %collective-permute-start.17 = (f32[4,80]{1,0:T(4,128)S(1)}, f32[4,80]{1,0:T(4,128)S(1)}, u32[]{:S(2)}, u32[]{:S(2)}) collective-permute-start(f32[4,80]{1,0:T(4,128)S(1)} %get-tuple-element.701), channel_id=1, source_target_pairs={{0,2},{1,3},{2,0},{3,1},{4,6},{5,7},{6,4},{7,5},{8,10},{9,11},{10,... | collective-permute-start | bytes 3848 | tf_op jit(solution)/shard_map/ppermute | solution.py:149
  4.6 3.0 %collective-permute-start.18 = (f32[4,80]{1,0:T(4,128)S(1)}, f32[4,80]{1,0:T(4,128)S(1)}, u32[]{:S(2)}, u32[]{:S(2)}) collective-permute-start(f32[4,80]{1,0:T(4,128)S(1)} %get-tuple-element.702), channel_id=1, source_target_pairs={{0,3},{1,2},{2,1},{3,0},{4,7},{5,6},{6,5},{7,4},{8,11},{9,10},{10,... | collective-permute-start | bytes 3848 | tf_op jit(solution)/shard_map/ppermute | solution.py:149
  8.9 1.9 %collective-permute-start.19 = (f32[4,80]{1,0:T(4,128)S(1)}, f32[4,80]{1,0:T(4,128)S(1)}, u32[]{:S(2)}, u32[]{:S(2)}) collective-permute-start(f32[4,80]{1,0:T(4,128)S(1)} %get-tuple-element.711), channel_id=1, source_target_pairs={{0,1},{1,0},{2,3},{3,2},{4,5},{5,4},{6,7},{7,6},{8,9},{9,8},{10,11... | collective-permute-start | bytes 3848 | tf_op jit(solution)/shard_map/ppermute | solution.py:149
  9.1 3.6 %collective-permute-start.20 = (f32[4,80]{1,0:T(4,128)S(1)}, f32[4,80]{1,0:T(4,128)S(1)}, u32[]{:S(2)}, u32[]{:S(2)}) collective-permute-start(f32[4,80]{1,0:T(4,128)S(1)} %get-tuple-element.712), channel_id=1, source_target_pairs={{0,2},{1,3},{2,0},{3,1},{4,6},{5,7},{6,4},{7,5},{8,10},{9,11},{10,... | collective-permute-start | bytes 3848 | tf_op jit(solution)/shard_map/ppermute | solution.py:149
  10.4 3.0 %collective-permute-start.21 = (f32[4,80]{1,0:T(4,128)S(1)}, f32[4,80]{1,0:T(4,128)S(1)}, u32[]{:S(2)}, u32[]{:S(2)}) collective-permute-start(f32[4,80]{1,0:T(4,128)S(1)} %get-tuple-element.713), channel_id=1, source_target_pairs={{0,3},{1,2},{2,1},{3,0},{4,7},{5,6},{6,5},{7,4},{8,11},{9,10},{10,... | collective-permute-start | bytes 3848 | tf_op jit(solution)/shard_map/ppermute | solution.py:149
  13.5 6.5 %collective-permute-start.22 = (f32[16,80]{1,0:T(8,128)S(1)}, f32[16,80]{1,0:T(8,128)S(1)}, u32[]{:S(2)}, u32[]{:S(2)}) collective-permute-start(f32[16,80]{1,0:T(8,128)S(1)} %shard_map.90.refs_0_.refs_5_.refs_4_), channel_id=1, source_target_pairs={{0,4},{4,0},{8,12},{12,8},{16,20},{20,16},{24,28},{28,24},{1,5},{5... | collective-permute-start | bytes 15368 | tf_op jit(solution)/shard_map/ppermute | solution.py:524
  15.0 5.0 %collective-permute-start.23 = (f32[16,80]{1,0:T(8,128)S(1)}, f32[16,80]{1,0:T(8,128)S(1)}, u32[]{:S(2)}, u32[]{:S(2)}) collective-permute-start(f32[16,80]{1,0:T(8,128)S(1)} %shard_map.90.refs_0_.refs_5_.refs_4_), channel_id=1, source_target_pairs={{0,1},{1,0},{2,3},{3,2},{4,5},{5,4},{6,7},{7,6},{8,9},{9,8},{10,11... | collective-permute-start | bytes 15368 | tf_op jit(solution)/shard_map/ppermute | solution.py:524
  15.0 7.4 %collective-permute-start.24 = (f32[16,80]{1,0:T(8,128)S(1)}, f32[16,80]{1,0:T(8,128)S(1)}, u32[]{:S(2)}, u32[]{:S(2)}) collective-permute-start(f32[16,80]{1,0:T(8,128)S(1)} %shard_map.90.refs_0_.refs_5_.refs_4_), channel_id=1, source_target_pairs={{0,28},{4,8},{8,4},{12,16},{16,12},{20,24},{24,20},{28,0},{1,29},{... | collective-permute-start | bytes 15368 | tf_op jit(solution)/shard_map/ppermute | solution.py:523
  18.6 3.8 %collective-permute-start.25 = (f32[16,80]{1,0:T(8,128)S(1)}, f32[16,80]{1,0:T(8,128)S(1)}, u32[]{:S(2)}, u32[]{:S(2)}) collective-permute-start(f32[16,80]{1,0:T(8,128)S(1)} %shard_map.90.refs_0_.refs_5_.refs_4_), channel_id=1, source_target_pairs={{0,3},{1,2},{2,1},{3,0},{4,7},{5,6},{6,5},{7,4},{8,11},{9,10},{10,... | collective-permute-start | bytes 15368 | tf_op jit(solution)/shard_map/ppermute | solution.py:525
  24.1 4.0 %collective-permute-start.26 = (f32[4,80]{1,0:T(4,128)S(1)}, f32[4,80]{1,0:T(4,128)S(1)}, u32[]{:S(2)}, u32[]{:S(2)}) collective-permute-start(f32[4,80]{1,0:T(4,128)S(1)} %get-tuple-element.718), channel_id=1, source_target_pairs={{0,1},{1,0},{2,3},{3,2},{4,5},{5,4},{6,7},{7,6},{8,9},{9,8},{10,11... | collective-permute-start | bytes 3848 | tf_op jit(solution)/shard_map/ppermute | solution.py:149
  24.5 3.7 %collective-permute-start.27 = (f32[4,80]{1,0:T(4,128)S(1)}, f32[4,80]{1,0:T(4,128)S(1)}, u32[]{:S(2)}, u32[]{:S(2)}) collective-permute-start(f32[4,80]{1,0:T(4,128)S(1)} %get-tuple-element.719), channel_id=1, source_target_pairs={{0,2},{1,3},{2,0},{3,1},{4,6},{5,7},{6,4},{7,5},{8,10},{9,11},{10,... | collective-permute-start | bytes 3848 | tf_op jit(solution)/shard_map/ppermute | solution.py:149
  25.8 3.0 %collective-permute-start.28 = (f32[4,80]{1,0:T(4,128)S(1)}, f32[4,80]{1,0:T(4,128)S(1)}, u32[]{:S(2)}, u32[]{:S(2)}) collective-permute-start(f32[4,80]{1,0:T(4,128)S(1)} %get-tuple-element.720), channel_id=1, source_target_pairs={{0,3},{1,2},{2,1},{3,0},{4,7},{5,6},{6,5},{7,4},{8,11},{9,10},{10,... | collective-permute-start | bytes 3848 | tf_op jit(solution)/shard_map/ppermute | solution.py:149
  30.0 2.0 %collective-permute-start.29 = (f32[4,80]{1,0:T(4,128)S(1)}, f32[4,80]{1,0:T(4,128)S(1)}, u32[]{:S(2)}, u32[]{:S(2)}) collective-permute-start(f32[4,80]{1,0:T(4,128)S(1)} %get-tuple-element.726), channel_id=1, source_target_pairs={{0,1},{1,0},{2,3},{3,2},{4,5},{5,4},{6,7},{7,6},{8,9},{9,8},{10,11... | collective-permute-start | bytes 3848 | tf_op jit(solution)/shard_map/ppermute | solution.py:149
  30.2 3.6 %collective-permute-start.30 = (f32[4,80]{1,0:T(4,128)S(1)}, f32[4,80]{1,0:T(4,128)S(1)}, u32[]{:S(2)}, u32[]{:S(2)}) collective-permute-start(f32[4,80]{1,0:T(4,128)S(1)} %get-tuple-element.727), channel_id=1, source_target_pairs={{0,2},{1,3},{2,0},{3,1},{4,6},{5,7},{6,4},{7,5},{8,10},{9,11},{10,... | collective-permute-start | bytes 3848 | tf_op jit(solution)/shard_map/ppermute | solution.py:149
  31.4 3.0 %collective-permute-start.31 = (f32[4,80]{1,0:T(4,128)S(1)}, f32[4,80]{1,0:T(4,128)S(1)}, u32[]{:S(2)}, u32[]{:S(2)}) collective-permute-start(f32[4,80]{1,0:T(4,128)S(1)} %get-tuple-element.728), channel_id=1, source_target_pairs={{0,3},{1,2},{2,1},{3,0},{4,7},{5,6},{6,5},{7,4},{8,11},{9,10},{10,... | collective-permute-start | bytes 3848 | tf_op jit(solution)/shard_map/ppermute | solution.py:149
  34.5 3.7 %collective-permute-start.32 = (f32[16,80]{1,0:T(8,128)S(1)}, f32[16,80]{1,0:T(8,128)S(1)}, u32[]{:S(2)}, u32[]{:S(2)}) collective-permute-start(f32[16,80]{1,0:T(8,128)S(1)} %shard_map.95.refs_0_.refs_5_), channel_id=1, source_target_pairs={{0,4},{4,0},{8,12},{12,8},{16,20},{20,16},{24,28},{28,24},{1,5},{5... | collective-permute-start | bytes 15368 | tf_op jit(solution)/shard_map/ppermute | solution.py:524
  34.5 3.7 %collective-permute-start.33 = (f32[16,80]{1,0:T(8,128)S(1)}, f32[16,80]{1,0:T(8,128)S(1)}, u32[]{:S(2)}, u32[]{:S(2)}) collective-permute-start(f32[16,80]{1,0:T(8,128)S(1)} %shard_map.95.refs_0_.refs_5_), channel_id=1, source_target_pairs={{0,1},{1,0},{2,3},{3,2},{4,5},{5,4},{6,7},{7,6},{8,9},{9,8},{10,11... | collective-permute-start | bytes 15368 | tf_op jit(solution)/shard_map/ppermute | solution.py:524
  34.5 6.4 %collective-permute-start.34 = (f32[16,80]{1,0:T(8,128)S(1)}, f32[16,80]{1,0:T(8,128)S(1)}, u32[]{:S(2)}, u32[]{:S(2)}) collective-permute-start(f32[16,80]{1,0:T(8,128)S(1)} %shard_map.95.refs_0_.refs_5_), channel_id=1, source_target_pairs={{0,28},{4,8},{8,4},{12,16},{16,12},{20,24},{24,20},{28,0},{1,29},{... | collective-permute-start | bytes 15368 | tf_op jit(solution)/shard_map/ppermute | solution.py:523
  36.6 4.4 %collective-permute-start.35 = (f32[16,80]{1,0:T(8,128)S(1)}, f32[16,80]{1,0:T(8,128)S(1)}, u32[]{:S(2)}, u32[]{:S(2)}) collective-permute-start(f32[16,80]{1,0:T(8,128)S(1)} %shard_map.95.refs_0_.refs_5_), channel_id=1, source_target_pairs={{0,3},{1,2},{2,1},{3,0},{4,7},{5,6},{6,5},{7,4},{8,11},{9,10},{10,... | collective-permute-start | bytes 15368 | tf_op jit(solution)/shard_map/ppermute | solution.py:525
  42.6 4.0 %collective-permute-start.36 = (f32[4,80]{1,0:T(4,128)S(1)}, f32[4,80]{1,0:T(4,128)S(1)}, u32[]{:S(2)}, u32[]{:S(2)}) collective-permute-start(f32[4,80]{1,0:T(4,128)S(1)} %get-tuple-element.732), channel_id=1, source_target_pairs={{0,1},{1,0},{2,3},{3,2},{4,5},{5,4},{6,7},{7,6},{8,9},{9,8},{10,11... | collective-permute-start | bytes 3848 | tf_op jit(solution)/shard_map/ppermute | solution.py:149
  42.7 4.0 %collective-permute-start.37 = (f32[4,80]{1,0:T(4,128)S(1)}, f32[4,80]{1,0:T(4,128)S(1)}, u32[]{:S(2)}, u32[]{:S(2)}) collective-permute-start(f32[4,80]{1,0:T(4,128)S(1)} %get-tuple-element.733), channel_id=1, source_target_pairs={{0,2},{1,3},{2,0},{3,1},{4,6},{5,7},{6,4},{7,5},{8,10},{9,11},{10,... | collective-permute-start | bytes 3848 | tf_op jit(solution)/shard_map/ppermute | solution.py:149
  43.7 3.0 %collective-permute-start.38 = (f32[4,80]{1,0:T(4,128)S(1)}, f32[4,80]{1,0:T(4,128)S(1)}, u32[]{:S(2)}, u32[]{:S(2)}) collective-permute-start(f32[4,80]{1,0:T(4,128)S(1)} %get-tuple-element.734), channel_id=1, source_target_pairs={{0,3},{1,2},{2,1},{3,0},{4,7},{5,6},{6,5},{7,4},{8,11},{9,10},{10,... | collective-permute-start | bytes 3848 | tf_op jit(solution)/shard_map/ppermute | solution.py:149
  46.6 24.7 %copy-start.2 = (f32[80,16]{0,1:T(8,128)S(1)}, f32[80,16]{0,1:T(8,128)}, u32[]{:S(2)}) copy-start(f32[80,16]{0,1:T(8,128)} %param.25) | copy-start | bytes 15364
  46.6 24.7 %copy-start.3 = (s32[11,16]{1,0:T(8,128)S(1)}, s32[11,16]{1,0:T(8,128)}, u32[]{:S(2)}) copy-start(s32[11,16]{1,0:T(8,128)} %columns_ref) | copy-start | bytes 2116
  48.0 1.9 %collective-permute-start.39 = (f32[4,80]{1,0:T(4,128)S(1)}, f32[4,80]{1,0:T(4,128)S(1)}, u32[]{:S(2)}, u32[]{:S(2)}) collective-permute-start(f32[4,80]{1,0:T(4,128)S(1)} %get-tuple-element.740), channel_id=1, source_target_pairs={{0,1},{1,0},{2,3},{3,2},{4,5},{5,4},{6,7},{7,6},{8,9},{9,8},{10,11... | collective-permute-start | bytes 3848 | tf_op jit(solution)/shard_map/ppermute | solution.py:149
  48.3 3.6 %collective-permute-start.40 = (f32[4,80]{1,0:T(4,128)S(1)}, f32[4,80]{1,0:T(4,128)S(1)}, u32[]{:S(2)}, u32[]{:S(2)}) collective-permute-start(f32[4,80]{1,0:T(4,128)S(1)} %get-tuple-element.741), channel_id=1, source_target_pairs={{0,2},{1,3},{2,0},{3,1},{4,6},{5,7},{6,4},{7,5},{8,10},{9,11},{10,... | collective-permute-start | bytes 3848 | tf_op jit(solution)/shard_map/ppermute | solution.py:149
  49.3 3.0 %collective-permute-start.41 = (f32[4,80]{1,0:T(4,128)S(1)}, f32[4,80]{1,0:T(4,128)S(1)}, u32[]{:S(2)}, u32[]{:S(2)}) collective-permute-start(f32[4,80]{1,0:T(4,128)S(1)} %get-tuple-element.742), channel_id=1, source_target_pairs={{0,3},{1,2},{2,1},{3,0},{4,7},{5,6},{6,5},{7,4},{8,11},{9,10},{10,... | collective-permute-start | bytes 3848 | tf_op jit(solution)/shard_map/ppermute | solution.py:149
  52.5 3.7 %collective-permute-start.42 = (f32[16,80]{1,0:T(8,128)S(1)}, f32[16,80]{1,0:T(8,128)S(1)}, u32[]{:S(2)}, u32[]{:S(2)}) collective-permute-start(f32[16,80]{1,0:T(8,128)S(1)} %shard_map.100.refs_0_.refs_5_.refs_6_), channel_id=1, source_target_pairs={{0,4},{4,0},{8,12},{12,8},{16,20},{20,16},{24,28},{28,24},{1,5},{5... | collective-permute-start | bytes 15368 | tf_op jit(solution)/shard_map/ppermute | solution.py:524
  52.5 3.6 %collective-permute-start.43 = (f32[16,80]{1,0:T(8,128)S(1)}, f32[16,80]{1,0:T(8,128)S(1)}, u32[]{:S(2)}, u32[]{:S(2)}) collective-permute-start(f32[16,80]{1,0:T(8,128)S(1)} %shard_map.100.refs_0_.refs_5_.refs_6_), channel_id=1, source_target_pairs={{0,1},{1,0},{2,3},{3,2},{4,5},{5,4},{6,7},{7,6},{8,9},{9,8},{10,11... | collective-permute-start | bytes 15368 | tf_op jit(solution)/shard_map/ppermute | solution.py:524
  52.6 6.3 %collective-permute-start.44 = (f32[16,80]{1,0:T(8,128)S(1)}, f32[16,80]{1,0:T(8,128)S(1)}, u32[]{:S(2)}, u32[]{:S(2)}) collective-permute-start(f32[16,80]{1,0:T(8,128)S(1)} %shard_map.100.refs_0_.refs_5_.refs_6_), channel_id=1, source_target_pairs={{0,28},{4,8},{8,4},{12,16},{16,12},{20,24},{24,20},{28,0},{1,29},{... | collective-permute-start | bytes 15368 | tf_op jit(solution)/shard_map/ppermute | solution.py:523
  54.7 4.3 %collective-permute-start.45 = (f32[16,80]{1,0:T(8,128)S(1)}, f32[16,80]{1,0:T(8,128)S(1)}, u32[]{:S(2)}, u32[]{:S(2)}) collective-permute-start(f32[16,80]{1,0:T(8,128)S(1)} %shard_map.100.refs_0_.refs_5_.refs_6_), channel_id=1, source_target_pairs={{0,3},{1,2},{2,1},{3,0},{4,7},{5,6},{6,5},{7,4},{8,11},{9,10},{10,... | collective-permute-start | bytes 15368 | tf_op jit(solution)/shard_map/ppermute | solution.py:525
  (3 other events, 60.0 us)

commit v6 on v5

--- a/solution.py
+++ b/solution.py
@@ -336,7 +336,8 @@
         )
 
     mine = [fetch(k, 1, buf, n * area, n) for n, k in enumerate((0, *early))]
-    kept = [fetch(late[1], 1, held, 0, 3), fetch(5, nblocks - 5, held, area, 4)]
+    kept = [fetch(k, 1, held, n * area, 3 + n) for n, k in enumerate(late)]
+    kept.append(fetch(5, nblocks - 5, held, 2 * area, 5))
     for copy in mine + kept:
         copy.start()
     x_scr[...] = repeat_faces(faces, pick, x_scr.shape[1] // width)
@@ -347,21 +348,17 @@
 
 
 def late_kernel(nplane, last, *refs):
-    (blocks, slot, held, pick, early_sum), faces, refs = refs[:5], refs[5:10], refs[10:]
+    (slot, held, pick, early_sum), faces, refs = refs[:4], refs[4:9], refs[9:]
     nold = ITERS if last else 1
     olds, refs = refs[:nold], refs[nold:]
-    next_ref, outs, (buf, x_scr, acc_scr, parts, sem, slot_scr, slot_sem) = refs[0], refs[1:-7], refs[-7:]
+    next_ref, outs, (x_scr, acc_scr, parts, slot_scr, slot_sem) = refs[0], refs[1:-5], refs[-5:]
     nfaces, width = faces[0].shape
     area = width * width
-    _, late = early_blocks()
-    fetch = pltpu.make_async_copy(blocks.at[:, pl.ds(pl.multiple_of(late[0] * area, 128), area)], buf, sem)
-    fetch.start()
     if not last:
         slots = pltpu.make_async_copy(slot, slot_scr, slot_sem)
         slots.start()
-    repeated = repeat_faces(faces, pick, x_scr.shape[1] // width)
-    x_scr[...] = jnp.concatenate([repeated[nfaces:], repeated[:nfaces]], axis=0)
-    work = [([(held, column) for column in range(0, held.shape[1], area)], None), ([(buf, 0)], fetch)]
+    x_scr[...] = repeat_faces(faces, pick, x_scr.shape[1] // width)
+    work = [([(held, column) for column in range(0, held.shape[1], area)], None)]
     u_next = early_sum[...] + add_products(work, x_scr, acc_scr, parts, width) - SHIFT * olds[-1][...]
     next_ref[...] = u_next
     if last:
@@ -458,9 +455,7 @@
 
 
 def add_up(x):
-    count = lax.axis_size("span") * lax.axis_size("plane")
-    rows = jnp.broadcast_to(x, (count, x.shape[1]))
-    return lax.all_to_all(rows, ("span", "plane"), split_axis=0, concat_axis=0, tiled=True)
+    return lax.all_gather(x, ("span", "plane"), axis=0, tiled=True)
 
 
 def pairings(size):
@@ -525,9 +520,8 @@
         far = [other, lax.ppermute(mine, "plane", plane_others)]
         chunk = math.lcm(width, 128)
 
-        def scratch(count, fetched):
+        def scratch(count):
             return [
-                pltpu.VMEM((nfaces, fetched * area), F32),
                 pltpu.VMEM((count * nfaces, chunk), F32),
                 pltpu.VMEM((nfaces, area), F32),
                 pltpu.VMEM((2 * nfaces * area // chunk, chunk), BF16),
@@ -536,20 +530,19 @@
         early_sum, held = call(
             functools.partial(early_kernel, nblocks),
             [blocks, picks[0], *near],
-            [shape, (nfaces, (nblocks - 4) * area)],
+            [shape, (nfaces, (nblocks - 3) * area)],
             [pl.ANY] + [pltpu.VMEM] * 4,
-            scratch(3, 3) + [pltpu.SemaphoreType.DMA((5,))],
+            [pltpu.VMEM((nfaces, 3 * area), F32)] + scratch(3) + [pltpu.SemaphoreType.DMA((6,))],
             flops=6 * nfaces * area,
         )
         last = step == ITERS - 1
-        args = [blocks, line_slot, held, picks[1], early_sum, *near, *far, *(us if last else us[-1:])]
+        args = [line_slot, held, picks[1], early_sum, *near, *far, *(us if last else us[-1:])]
         out = call(
             functools.partial(late_kernel, nplane, last),
             args,
             [shape] + ([(1, 128)] if last else [(per, width)] * nplane),
-            [pl.ANY] * 2 + [pltpu.VMEM] * (len(args) - 2),
-            scratch(nblocks - 3, 1)
-            + [pltpu.SemaphoreType.DMA, pltpu.SMEM(line_slot.shape, jnp.int32), pltpu.SemaphoreType.DMA],
+            [pl.ANY] + [pltpu.VMEM] * (len(args) - 1),
+            scratch(nblocks - 3) + [pltpu.SMEM(line_slot.shape, jnp.int32), pltpu.SemaphoreType.DMA],
             flops=2 * nblocks * nfaces * area,
         )
         us.append(out[0])

time: 72.2 us -> 98.4 us (1.36)
  blocking collectives: 9.79 us -> 38.5 us
  Pallas kernels: 25.2 us -> 23 us
    all_gather x0 -> x1, blocking collectives: none -> 38.5 us  [add_up(): return lax.all_gather(x, ('span', 'plane'), axis=0, tiled=True)]
    all_to_all x1 -> x0, blocking collectives: 9.79 us -> none  [add_up(): lax.all_to_all(rows, ('span', 'plane'), split_axis=0, concat_axis=0, tile...]
    pallas_call x18, Pallas kernels: 25.2 us -> 23 us  [call(): pl.pallas_call(kernel, out_shape=[pltpu.VMEM(shape, kind) if pinned else...]
  transfers between devices with their start and end apart: 30 -> 30, of which waited for: 13 -> 13; matrix products, arithmetic and copies ran while one was open for 0% -> 0% of each run, Pallas kernels for 20% -> 15%
where the time goes in v6:
time: 98.4 us; the launch traced here: 98.1 us
  blocking collectives  38.5 us (39%)
  starting transfers between devices  24.2 us (25%)
  Pallas kernels  23 us (23%)
  waiting for transfers between devices  11.1 us (11%)
  between operations  1.09 us (1%)
    all_gather x1, blocking collectives, add_up(): return lax.all_gather(x, ('span', 'plane'), axis=0, tiled=True)  38.5 us
    pallas_call x18, Pallas kernels, call(): pl.pallas_call(kernel, out_shape=[pltpu.VMEM(shape, kind) if pinned else...  23 us
    ppermute x18, starting transfers between devices, exchange(): lax.ppermute(x, axis, [(i, partner(i, k, size)[0]) for i in range(size)])  12.8 us
    ppermute x18, waiting for transfers between devices, exchange(): lax.ppermute(x, axis, [(i, partner(i, k, size)[0]) for i in range(size)])  8.73 us
    ppermute x3, starting transfers between devices, on_device(): other = lax.ppermute(mine, 'span', span_others)  7.6 us
    ppermute x3, starting transfers between devices, on_device(): far = [other, lax.ppermute(mine, 'plane', plane_others)]  2.06 us
  transfers between devices with their start and end apart: 30, of which 13 were waited for; matrix products, arithmetic and copies ran while one was open for 0% of the time, Pallas kernels for 15%

profile of v6, /device:TPU:0, one launch (start us, length us, event | category | flops | bytes accessed | tf_op | source)
XLA Modules:
  0.0 98.1 jit_solution(11016757042054861672)
XLA Ops:
  0.7 0.8 shard_map.86
  2.0 2.6 %collective-permute-start.17 = (f32[4,80]{1,0:T(4,128)S(1)}, f32[4,80]{1,0:T(4,128)S(1)}, u32[]{:S(2)}, u32[]{:S(2)}) collective-permute-start(f32[4,80]{1,0:T(4,128)S(1)} %get-tuple-element.701), channel_id=1, source_target_pairs={{0,2},{1,3},{2,0},{3,1},{4,6},{5,7},{6,4},{7,5},{8,10},{9,11},{10,... | collective-permute-start | bytes 3848 | tf_op jit(solution)/shard_map/ppermute | solution.py:149
  4.7 2.3 %shard_map.87 = (f32[1280,80]{1,0:T(8,128)S(1)}, f32[1280,80]{1,0:T(8,128)S(1)}, f32[1280,80]{1,0:T(8,128)S(1)}) custom-call(f32[16,6400]{1,0:T(8,128)} %low.5, f32[16,6400]{1,0:T(8,128)} %upp.5, f32[16,6400]{1,0:T(8,128)} %piv.5, f32[16,80]{1,0:T(8,128)S(1)} %get-tuple-element.703._.refs_9_.refs_0_), custom_call_target="tpu_custom_call" | custom-call | flops 102400 | bytes 1233920 | tf_op jit(solution)/shard_map/pallas_call | solution.py:446
  7.6 1.3 %shard_map.88 = (f32[4,80]{1,0:T(4,128)S(1)}, f32[4,80]{1,0:T(4,128)S(1)}, f32[4,80]{1,0:T(4,128)S(1)}, f32[4,80]{1,0:T(4,128)S(1)}) custom-call(f32[4,80]{1,0:T(4,128)S(1)} %get-tuple-element.699.refs_0_, f32[4,80]{1,0:T(4,128)S(1)} %collective-permute-done.16.refs_1_, f32[4,80]{1,0:T(4,128)S(1)} %collective-permute-done.17.refs_2_, ...), custom_call_target="tpu_custom_call" | custom-call | flops 614400 | bytes 1233920 | tf_op jit(solution)/shard_map/pallas_call | solution.py:446
  9.1 1.3 %collective-permute-start.20 = (f32[4,80]{1,0:T(4,128)S(1)}, f32[4,80]{1,0:T(4,128)S(1)}, u32[]{:S(2)}, u32[]{:S(2)}) collective-permute-start(f32[4,80]{1,0:T(4,128)S(1)} %get-tuple-element.712), channel_id=1, source_target_pairs={{0,2},{1,3},{2,0},{3,1},{4,6},{5,7},{6,4},{7,5},{8,10},{9,11},{10,... | collective-permute-start | bytes 3848 | tf_op jit(solution)/shard_map/ppermute | solution.py:149
  10.8 1.9 %collective-permute-done.20.refs_2_ = f32[4,80]{1,0:T(4,128)S(1)} collective-permute-done((f32[4,80]{1,0:T(4,128)S(1)}, f32[4,80]{1,0:T(4,128)S(1)}, u32[]{:S(2)}, u32[]{:S(2)}) %collective-permute-start.20) | collective-permute-done | bytes 1312 | tf_op jit(solution)/shard_map/ppermute | solution.py:149
  13.5 1.5 %collective-permute-start.22 = (f32[16,80]{1,0:T(8,128)S(1)}, f32[16,80]{1,0:T(8,128)S(1)}, u32[]{:S(2)}, u32[]{:S(2)}) collective-permute-start(f32[16,80]{1,0:T(8,128)S(1)} %shard_map.90.refs_0_.refs_4_), channel_id=1, source_target_pairs={{0,4},{4,0},{8,12},{12,8},{16,20},{20,16},{24,28},{28,24},{1,5},{5... | collective-permute-start | bytes 15368 | tf_op jit(solution)/shard_map/ppermute | solution.py:519
  15.0 3.6 %collective-permute-start.24 = (f32[16,80]{1,0:T(8,128)S(1)}, f32[16,80]{1,0:T(8,128)S(1)}, u32[]{:S(2)}, u32[]{:S(2)}) collective-permute-start(f32[16,80]{1,0:T(8,128)S(1)} %shard_map.90.refs_0_.refs_4_), channel_id=1, source_target_pairs={{0,28},{4,8},{8,4},{12,16},{16,12},{20,24},{24,20},{28,0},{1,29},{... | collective-permute-start | bytes 15368 | tf_op jit(solution)/shard_map/ppermute | solution.py:518
  19.2 0.8 shard_map.89
  20.0 2.5 %shard_map.91 = (f32[16,80]{1,0:T(8,128)S(1)}, f32[16,51200]{1,0:T(8,128)S(1)}) custom-call(f32[16,70400]{1,0:T(8,128)} %blocks.5, bf16[48,96]{1,0:T(8,128)(2,1)S(1)} %get-tuple-element.709.pick, f32[16,80]{1,0:T(8,128)S(1)} %shard_map.90.refs_0_.refs_4_, f32[16,80]{1,0:T(8,128)S(1)} %collective-permute-done.22.refs_1_.refs_5_, ...), custom_call_target="tpu_custom_call" | custom-call | flops 614400 | bytes 4530176 | tf_op jit(solution)/shard_map/pallas_call | solution.py:446
  22.5 0.9 shard_map.92
  23.7 1.3 %collective-permute-start.27 = (f32[4,80]{1,0:T(4,128)S(1)}, f32[4,80]{1,0:T(4,128)S(1)}, u32[]{:S(2)}, u32[]{:S(2)}) collective-permute-start(f32[4,80]{1,0:T(4,128)S(1)} %get-tuple-element.719), channel_id=1, source_target_pairs={{0,2},{1,3},{2,0},{3,1},{4,6},{5,7},{6,4},{7,5},{8,10},{9,11},{10,... | collective-permute-start | bytes 3848 | tf_op jit(solution)/shard_map/ppermute | solution.py:149
  25.3 2.1 %shard_map.93 = (f32[1280,80]{1,0:T(8,128)S(1)}, f32[1280,80]{1,0:T(8,128)S(1)}, f32[1280,80]{1,0:T(8,128)S(1)}) custom-call(f32[16,6400]{1,0:T(8,128)S(1)} %copy-done, f32[16,6400]{1,0:T(8,128)S(1)} %copy-done.1, f32[16,6400]{1,0:T(8,128)} %piv.5, f32[16,80]{1,0:T(8,128)S(1)} %get-tuple-element.721._.refs_9_.refs_10_.refs_1_), custom_call_target="tpu_custom_call" | custom-call | flops 102400 | bytes 1233920 | tf_op jit(solution)/shard_map/pallas_call | solution.py:446
  28.0 1.2 %shard_map.94 = (f32[4,80]{1,0:T(4,128)S(1)}, f32[4,80]{1,0:T(4,128)S(1)}, f32[4,80]{1,0:T(4,128)S(1)}, f32[4,80]{1,0:T(4,128)S(1)}) custom-call(f32[4,80]{1,0:T(4,128)S(1)} %get-tuple-element.717.refs_0_, f32[4,80]{1,0:T(4,128)S(1)} %collective-permute-done.26.refs_1_, f32[4,80]{1,0:T(4,128)S(1)} %collective-permute-done.27.refs_2_, ...), custom_call_target="tpu_custom_call" | custom-call | flops 614400 | bytes 1233920 | tf_op jit(solution)/shard_map/pallas_call | solution.py:446
  29.5 1.1 %collective-permute-start.30 = (f32[4,80]{1,0:T(4,128)S(1)}, f32[4,80]{1,0:T(4,128)S(1)}, u32[]{:S(2)}, u32[]{:S(2)}) collective-permute-start(f32[4,80]{1,0:T(4,128)S(1)} %get-tuple-element.727), channel_id=1, source_target_pairs={{0,2},{1,3},{2,0},{3,1},{4,6},{5,7},{6,4},{7,5},{8,10},{9,11},{10,... | collective-permute-start | bytes 3848 | tf_op jit(solution)/shard_map/ppermute | solution.py:149
  31.3 1.8 %collective-permute-done.30.refs_2_ = f32[4,80]{1,0:T(4,128)S(1)} collective-permute-done((f32[4,80]{1,0:T(4,128)S(1)}, f32[4,80]{1,0:T(4,128)S(1)}, u32[]{:S(2)}, u32[]{:S(2)}) %collective-permute-start.30) | collective-permute-done | bytes 1312 | tf_op jit(solution)/shard_map/ppermute | solution.py:149
  33.8 2.0 %collective-permute-start.34 = (f32[16,80]{1,0:T(8,128)S(1)}, f32[16,80]{1,0:T(8,128)S(1)}, u32[]{:S(2)}, u32[]{:S(2)}) collective-permute-start(f32[16,80]{1,0:T(8,128)S(1)} %shard_map.95.refs_0_.refs_4_.refs_5_), channel_id=1, source_target_pairs={{0,28},{4,8},{8,4},{12,16},{16,12},{20,24},{24,20},{28,0},{1,29},{... | collective-permute-start | bytes 15368 | tf_op jit(solution)/shard_map/ppermute | solution.py:518
  35.8 0.8 collective-permute-start.35
  36.6 0.8 collective-permute-done.32.refs_1_.refs_5_
  37.4 2.5 %shard_map.96 = (f32[16,80]{1,0:T(8,128)S(1)}, f32[16,51200]{1,0:T(8,128)S(1)}) custom-call(f32[16,70400]{1,0:T(8,128)} %blocks.5, bf16[48,96]{1,0:T(8,128)(2,1)S(1)} %get-tuple-element.709.pick, f32[16,80]{1,0:T(8,128)S(1)} %shard_map.95.refs_0_.refs_4_.refs_5_, f32[16,80]{1,0:T(8,128)S(1)} %collective-permute-done.32.refs_1_.refs_5_, ...), custom_call_target="tpu_custom_call" | custom-call | flops 614400 | bytes 4530176 | tf_op jit(solution)/shard_map/pallas_call | solution.py:446
  40.2 0.8 shard_map.97
  41.1 1.1 %collective-permute-start.37 = (f32[4,80]{1,0:T(4,128)S(1)}, f32[4,80]{1,0:T(4,128)S(1)}, u32[]{:S(2)}, u32[]{:S(2)}) collective-permute-start(f32[4,80]{1,0:T(4,128)S(1)} %get-tuple-element.733), channel_id=1, source_target_pairs={{0,2},{1,3},{2,0},{3,1},{4,6},{5,7},{6,4},{7,5},{8,10},{9,11},{10,... | collective-permute-start | bytes 3848 | tf_op jit(solution)/shard_map/ppermute | solution.py:149
  42.2 0.8 collective-permute-start.38
  43.0 2.1 %shard_map.98 = (f32[1280,80]{1,0:T(8,128)S(1)}, f32[1280,80]{1,0:T(8,128)S(1)}, f32[1280,80]{1,0:T(8,128)S(1)}) custom-call(f32[16,6400]{1,0:T(8,128)S(1)} %copy-done, f32[16,6400]{1,0:T(8,128)S(1)} %copy-done.1, f32[16,6400]{1,0:T(8,128)} %piv.5, f32[16,80]{1,0:T(8,128)S(1)} %get-tuple-element.735._.refs_11_.refs_2_), custom_call_target="tpu_custom_call" | custom-call | flops 102400 | bytes 1233920 | tf_op jit(solution)/shard_map/pallas_call | solution.py:446
  45.2 1.2 %shard_map.99 = (f32[4,80]{1,0:T(4,128)S(1)}, f32[4,80]{1,0:T(4,128)S(1)}, f32[4,80]{1,0:T(4,128)S(1)}, f32[4,80]{1,0:T(4,128)S(1)}) custom-call(f32[4,80]{1,0:T(4,128)S(1)} %get-tuple-element.731.refs_0_, f32[4,80]{1,0:T(4,128)S(1)} %collective-permute-done.36.refs_1_, f32[4,80]{1,0:T(4,128)S(1)} %collective-permute-done.37.refs_2_, ...), custom_call_target="tpu_custom_call" | custom-call | flops 614400 | bytes 1233920 | tf_op jit(solution)/shard_map/pallas_call | solution.py:446
  46.8 1.0 %collective-permute-start.40 = (f32[4,80]{1,0:T(4,128)S(1)}, f32[4,80]{1,0:T(4,128)S(1)}, u32[]{:S(2)}, u32[]{:S(2)}) collective-permute-start(f32[4,80]{1,0:T(4,128)S(1)} %get-tuple-element.741), channel_id=1, source_target_pairs={{0,2},{1,3},{2,0},{3,1},{4,6},{5,7},{6,4},{7,5},{8,10},{9,11},{10,... | collective-permute-start | bytes 3848 | tf_op jit(solution)/shard_map/ppermute | solution.py:149
  48.4 2.0 %collective-permute-done.40.refs_2_ = f32[4,80]{1,0:T(4,128)S(1)} collective-permute-done((f32[4,80]{1,0:T(4,128)S(1)}, f32[4,80]{1,0:T(4,128)S(1)}, u32[]{:S(2)}, u32[]{:S(2)}) %collective-permute-start.40) | collective-permute-done | bytes 1312 | tf_op jit(solution)/shard_map/ppermute | solution.py:149
  51.0 2.0 %collective-permute-start.44 = (f32[16,80]{1,0:T(8,128)S(1)}, f32[16,80]{1,0:T(8,128)S(1)}, u32[]{:S(2)}, u32[]{:S(2)}) collective-permute-start(f32[16,80]{1,0:T(8,128)S(1)} %shard_map.100.refs_0_.refs_4_.refs_6_), channel_id=1, source_target_pairs={{0,28},{4,8},{8,4},{12,16},{16,12},{20,24},{24,20},{28,0},{1,29},{... | collective-permute-start | bytes 15368 | tf_op jit(solution)/shard_map/ppermute | solution.py:518
  54.5 2.5 %shard_map.101 = (f32[16,80]{1,0:T(8,128)S(1)}, f32[16,51200]{1,0:T(8,128)S(1)}) custom-call(f32[16,70400]{1,0:T(8,128)} %blocks.5, bf16[48,96]{1,0:T(8,128)(2,1)S(1)} %get-tuple-element.709.pick, f32[16,80]{1,0:T(8,128)S(1)} %shard_map.100.refs_0_.refs_4_.refs_6_, f32[16,80]{1,0:T(8,128)S(1)} %collective-permute-done.42.refs_1_.refs_5_, ...), custom_call_target="tpu_custom_call" | custom-call | flops 614400 | bytes 4530176 | tf_op jit(solution)/shard_map/pallas_call | solution.py:446
  57.4 0.9 shard_map.102
  58.3 38.5 %all-gather = f32[32,1,128]{2,1,0:T(1,128)S(1)} all-gather(f32[1,1,128]{2,1,0:T(1,128)S(1)} %bitcast.559), channel_id=1, replica_groups=mesh['span'=8,'plane'=4] {'span','plane'}, dimensions={0}, use_global_device_ids=true | all-gather | bytes 16896 | tf_op jit(solution)/shard_map/all_gather | solution.py:458
  96.8 0.8 shard_map.103
  (58 shorter events, 10.3 us)
Async XLA Ops:
  1.5 5.5 %collective-permute-start.16 = (f32[4,80]{1,0:T(4,128)S(1)}, f32[4,80]{1,0:T(4,128)S(1)}, u32[]{:S(2)}, u32[]{:S(2)}) collective-permute-start(f32[4,80]{1,0:T(4,128)S(1)} %get-tuple-element.700), channel_id=1, source_target_pairs={{0,1},{1,0},{2,3},{3,2},{4,5},{5,4},{6,7},{7,6},{8,9},{9,8},{10,11... | collective-permute-start | bytes 3848 | tf_op jit(solution)/shard_map/ppermute | solution.py:149
  2.0 5.0 %collective-permute-start.17 = (f32[4,80]{1,0:T(4,128)S(1)}, f32[4,80]{1,0:T(4,128)S(1)}, u32[]{:S(2)}, u32[]{:S(2)}) collective-permute-start(f32[4,80]{1,0:T(4,128)S(1)} %get-tuple-element.701), channel_id=1, source_target_pairs={{0,2},{1,3},{2,0},{3,1},{4,6},{5,7},{6,4},{7,5},{8,10},{9,11},{10,... | collective-permute-start | bytes 3848 | tf_op jit(solution)/shard_map/ppermute | solution.py:149
  4.6 3.0 %collective-permute-start.18 = (f32[4,80]{1,0:T(4,128)S(1)}, f32[4,80]{1,0:T(4,128)S(1)}, u32[]{:S(2)}, u32[]{:S(2)}) collective-permute-start(f32[4,80]{1,0:T(4,128)S(1)} %get-tuple-element.702), channel_id=1, source_target_pairs={{0,3},{1,2},{2,1},{3,0},{4,7},{5,6},{6,5},{7,4},{8,11},{9,10},{10,... | collective-permute-start | bytes 3848 | tf_op jit(solution)/shard_map/ppermute | solution.py:149
  8.9 1.9 %collective-permute-start.19 = (f32[4,80]{1,0:T(4,128)S(1)}, f32[4,80]{1,0:T(4,128)S(1)}, u32[]{:S(2)}, u32[]{:S(2)}) collective-permute-start(f32[4,80]{1,0:T(4,128)S(1)} %get-tuple-element.711), channel_id=1, source_target_pairs={{0,1},{1,0},{2,3},{3,2},{4,5},{5,4},{6,7},{7,6},{8,9},{9,8},{10,11... | collective-permute-start | bytes 3848 | tf_op jit(solution)/shard_map/ppermute | solution.py:149
  9.1 3.6 %collective-permute-start.20 = (f32[4,80]{1,0:T(4,128)S(1)}, f32[4,80]{1,0:T(4,128)S(1)}, u32[]{:S(2)}, u32[]{:S(2)}) collective-permute-start(f32[4,80]{1,0:T(4,128)S(1)} %get-tuple-element.712), channel_id=1, source_target_pairs={{0,2},{1,3},{2,0},{3,1},{4,6},{5,7},{6,4},{7,5},{8,10},{9,11},{10,... | collective-permute-start | bytes 3848 | tf_op jit(solution)/shard_map/ppermute | solution.py:149
  10.4 3.0 %collective-permute-start.21 = (f32[4,80]{1,0:T(4,128)S(1)}, f32[4,80]{1,0:T(4,128)S(1)}, u32[]{:S(2)}, u32[]{:S(2)}) collective-permute-start(f32[4,80]{1,0:T(4,128)S(1)} %get-tuple-element.713), channel_id=1, source_target_pairs={{0,3},{1,2},{2,1},{3,0},{4,7},{5,6},{6,5},{7,4},{8,11},{9,10},{10,... | collective-permute-start | bytes 3848 | tf_op jit(solution)/shard_map/ppermute | solution.py:149
  13.5 6.5 %collective-permute-start.22 = (f32[16,80]{1,0:T(8,128)S(1)}, f32[16,80]{1,0:T(8,128)S(1)}, u32[]{:S(2)}, u32[]{:S(2)}) collective-permute-start(f32[16,80]{1,0:T(8,128)S(1)} %shard_map.90.refs_0_.refs_4_), channel_id=1, source_target_pairs={{0,4},{4,0},{8,12},{12,8},{16,20},{20,16},{24,28},{28,24},{1,5},{5... | collective-permute-start | bytes 15368 | tf_op jit(solution)/shard_map/ppermute | solution.py:519
  15.0 5.0 %collective-permute-start.23 = (f32[16,80]{1,0:T(8,128)S(1)}, f32[16,80]{1,0:T(8,128)S(1)}, u32[]{:S(2)}, u32[]{:S(2)}) collective-permute-start(f32[16,80]{1,0:T(8,128)S(1)} %shard_map.90.refs_0_.refs_4_), channel_id=1, source_target_pairs={{0,1},{1,0},{2,3},{3,2},{4,5},{5,4},{6,7},{7,6},{8,9},{9,8},{10,11... | collective-permute-start | bytes 15368 | tf_op jit(solution)/shard_map/ppermute | solution.py:519
  15.0 7.5 %collective-permute-start.24 = (f32[16,80]{1,0:T(8,128)S(1)}, f32[16,80]{1,0:T(8,128)S(1)}, u32[]{:S(2)}, u32[]{:S(2)}) collective-permute-start(f32[16,80]{1,0:T(8,128)S(1)} %shard_map.90.refs_0_.refs_4_), channel_id=1, source_target_pairs={{0,28},{4,8},{8,4},{12,16},{16,12},{20,24},{24,20},{28,0},{1,29},{... | collective-permute-start | bytes 15368 | tf_op jit(solution)/shard_map/ppermute | solution.py:518
  18.6 3.9 %collective-permute-start.25 = (f32[16,80]{1,0:T(8,128)S(1)}, f32[16,80]{1,0:T(8,128)S(1)}, u32[]{:S(2)}, u32[]{:S(2)}) collective-permute-start(f32[16,80]{1,0:T(8,128)S(1)} %shard_map.90.refs_0_.refs_4_), channel_id=1, source_target_pairs={{0,3},{1,2},{2,1},{3,0},{4,7},{5,6},{6,5},{7,4},{8,11},{9,10},{10,... | collective-permute-start | bytes 15368 | tf_op jit(solution)/shard_map/ppermute | solution.py:520
  23.4 4.0 %collective-permute-start.26 = (f32[4,80]{1,0:T(4,128)S(1)}, f32[4,80]{1,0:T(4,128)S(1)}, u32[]{:S(2)}, u32[]{:S(2)}) collective-permute-start(f32[4,80]{1,0:T(4,128)S(1)} %get-tuple-element.718), channel_id=1, source_target_pairs={{0,1},{1,0},{2,3},{3,2},{4,5},{5,4},{6,7},{7,6},{8,9},{9,8},{10,11... | collective-permute-start | bytes 3848 | tf_op jit(solution)/shard_map/ppermute | solution.py:149
  23.7 3.7 %collective-permute-start.27 = (f32[4,80]{1,0:T(4,128)S(1)}, f32[4,80]{1,0:T(4,128)S(1)}, u32[]{:S(2)}, u32[]{:S(2)}) collective-permute-start(f32[4,80]{1,0:T(4,128)S(1)} %get-tuple-element.719), channel_id=1, source_target_pairs={{0,2},{1,3},{2,0},{3,1},{4,6},{5,7},{6,4},{7,5},{8,10},{9,11},{10,... | collective-permute-start | bytes 3848 | tf_op jit(solution)/shard_map/ppermute | solution.py:149
  25.0 3.0 %collective-permute-start.28 = (f32[4,80]{1,0:T(4,128)S(1)}, f32[4,80]{1,0:T(4,128)S(1)}, u32[]{:S(2)}, u32[]{:S(2)}) collective-permute-start(f32[4,80]{1,0:T(4,128)S(1)} %get-tuple-element.720), channel_id=1, source_target_pairs={{0,3},{1,2},{2,1},{3,0},{4,7},{5,6},{6,5},{7,4},{8,11},{9,10},{10,... | collective-permute-start | bytes 3848 | tf_op jit(solution)/shard_map/ppermute | solution.py:149
  29.3 2.0 %collective-permute-start.29 = (f32[4,80]{1,0:T(4,128)S(1)}, f32[4,80]{1,0:T(4,128)S(1)}, u32[]{:S(2)}, u32[]{:S(2)}) collective-permute-start(f32[4,80]{1,0:T(4,128)S(1)} %get-tuple-element.726), channel_id=1, source_target_pairs={{0,1},{1,0},{2,3},{3,2},{4,5},{5,4},{6,7},{7,6},{8,9},{9,8},{10,11... | collective-permute-start | bytes 3848 | tf_op jit(solution)/shard_map/ppermute | solution.py:149
  29.5 3.6 %collective-permute-start.30 = (f32[4,80]{1,0:T(4,128)S(1)}, f32[4,80]{1,0:T(4,128)S(1)}, u32[]{:S(2)}, u32[]{:S(2)}) collective-permute-start(f32[4,80]{1,0:T(4,128)S(1)} %get-tuple-element.727), channel_id=1, source_target_pairs={{0,2},{1,3},{2,0},{3,1},{4,6},{5,7},{6,4},{7,5},{8,10},{9,11},{10,... | collective-permute-start | bytes 3848 | tf_op jit(solution)/shard_map/ppermute | solution.py:149
  30.6 3.0 %collective-permute-start.31 = (f32[4,80]{1,0:T(4,128)S(1)}, f32[4,80]{1,0:T(4,128)S(1)}, u32[]{:S(2)}, u32[]{:S(2)}) collective-permute-start(f32[4,80]{1,0:T(4,128)S(1)} %get-tuple-element.728), channel_id=1, source_target_pairs={{0,3},{1,2},{2,1},{3,0},{4,7},{5,6},{6,5},{7,4},{8,11},{9,10},{10,... | collective-permute-start | bytes 3848 | tf_op jit(solution)/shard_map/ppermute | solution.py:149
  33.7 3.7 %collective-permute-start.32 = (f32[16,80]{1,0:T(8,128)S(1)}, f32[16,80]{1,0:T(8,128)S(1)}, u32[]{:S(2)}, u32[]{:S(2)}) collective-permute-start(f32[16,80]{1,0:T(8,128)S(1)} %shard_map.95.refs_0_.refs_4_.refs_5_), channel_id=1, source_target_pairs={{0,4},{4,0},{8,12},{12,8},{16,20},{20,16},{24,28},{28,24},{1,5},{5... | collective-permute-start | bytes 15368 | tf_op jit(solution)/shard_map/ppermute | solution.py:519
  33.7 3.7 %collective-permute-start.33 = (f32[16,80]{1,0:T(8,128)S(1)}, f32[16,80]{1,0:T(8,128)S(1)}, u32[]{:S(2)}, u32[]{:S(2)}) collective-permute-start(f32[16,80]{1,0:T(8,128)S(1)} %shard_map.95.refs_0_.refs_4_.refs_5_), channel_id=1, source_target_pairs={{0,1},{1,0},{2,3},{3,2},{4,5},{5,4},{6,7},{7,6},{8,9},{9,8},{10,11... | collective-permute-start | bytes 15368 | tf_op jit(solution)/shard_map/ppermute | solution.py:519
  33.8 6.4 %collective-permute-start.34 = (f32[16,80]{1,0:T(8,128)S(1)}, f32[16,80]{1,0:T(8,128)S(1)}, u32[]{:S(2)}, u32[]{:S(2)}) collective-permute-start(f32[16,80]{1,0:T(8,128)S(1)} %shard_map.95.refs_0_.refs_4_.refs_5_), channel_id=1, source_target_pairs={{0,28},{4,8},{8,4},{12,16},{16,12},{20,24},{24,20},{28,0},{1,29},{... | collective-permute-start | bytes 15368 | tf_op jit(solution)/shard_map/ppermute | solution.py:518
  35.8 4.4 %collective-permute-start.35 = (f32[16,80]{1,0:T(8,128)S(1)}, f32[16,80]{1,0:T(8,128)S(1)}, u32[]{:S(2)}, u32[]{:S(2)}) collective-permute-start(f32[16,80]{1,0:T(8,128)S(1)} %shard_map.95.refs_0_.refs_4_.refs_5_), channel_id=1, source_target_pairs={{0,3},{1,2},{2,1},{3,0},{4,7},{5,6},{6,5},{7,4},{8,11},{9,10},{10,... | collective-permute-start | bytes 15368 | tf_op jit(solution)/shard_map/ppermute | solution.py:520
  40.2 57.5 %copy-start.2 = (f32[80,16]{0,1:T(8,128)S(1)}, f32[80,16]{0,1:T(8,128)}, u32[]{:S(2)}) copy-start(f32[80,16]{0,1:T(8,128)} %param.25) | copy-start | bytes 15364
  40.2 57.5 %copy-start.3 = (s32[11,16]{1,0:T(8,128)S(1)}, s32[11,16]{1,0:T(8,128)}, u32[]{:S(2)}) copy-start(s32[11,16]{1,0:T(8,128)} %columns_ref) | copy-start | bytes 2116
  41.1 4.0 %collective-permute-start.36 = (f32[4,80]{1,0:T(4,128)S(1)}, f32[4,80]{1,0:T(4,128)S(1)}, u32[]{:S(2)}, u32[]{:S(2)}) collective-permute-start(f32[4,80]{1,0:T(4,128)S(1)} %get-tuple-element.732), channel_id=1, source_target_pairs={{0,1},{1,0},{2,3},{3,2},{4,5},{5,4},{6,7},{7,6},{8,9},{9,8},{10,11... | collective-permute-start | bytes 3848 | tf_op jit(solution)/shard_map/ppermute | solution.py:149
  41.1 3.9 %collective-permute-start.37 = (f32[4,80]{1,0:T(4,128)S(1)}, f32[4,80]{1,0:T(4,128)S(1)}, u32[]{:S(2)}, u32[]{:S(2)}) collective-permute-start(f32[4,80]{1,0:T(4,128)S(1)} %get-tuple-element.733), channel_id=1, source_target_pairs={{0,2},{1,3},{2,0},{3,1},{4,6},{5,7},{6,4},{7,5},{8,10},{9,11},{10,... | collective-permute-start | bytes 3848 | tf_op jit(solution)/shard_map/ppermute | solution.py:149
  42.2 3.0 %collective-permute-start.38 = (f32[4,80]{1,0:T(4,128)S(1)}, f32[4,80]{1,0:T(4,128)S(1)}, u32[]{:S(2)}, u32[]{:S(2)}) collective-permute-start(f32[4,80]{1,0:T(4,128)S(1)} %get-tuple-element.734), channel_id=1, source_target_pairs={{0,3},{1,2},{2,1},{3,0},{4,7},{5,6},{6,5},{7,4},{8,11},{9,10},{10,... | collective-permute-start | bytes 3848 | tf_op jit(solution)/shard_map/ppermute | solution.py:149
  46.4 1.9 %collective-permute-start.39 = (f32[4,80]{1,0:T(4,128)S(1)}, f32[4,80]{1,0:T(4,128)S(1)}, u32[]{:S(2)}, u32[]{:S(2)}) collective-permute-start(f32[4,80]{1,0:T(4,128)S(1)} %get-tuple-element.740), channel_id=1, source_target_pairs={{0,1},{1,0},{2,3},{3,2},{4,5},{5,4},{6,7},{7,6},{8,9},{9,8},{10,11... | collective-permute-start | bytes 3848 | tf_op jit(solution)/shard_map/ppermute | solution.py:149
  46.8 3.6 %collective-permute-start.40 = (f32[4,80]{1,0:T(4,128)S(1)}, f32[4,80]{1,0:T(4,128)S(1)}, u32[]{:S(2)}, u32[]{:S(2)}) collective-permute-start(f32[4,80]{1,0:T(4,128)S(1)} %get-tuple-element.741), channel_id=1, source_target_pairs={{0,2},{1,3},{2,0},{3,1},{4,6},{5,7},{6,4},{7,5},{8,10},{9,11},{10,... | collective-permute-start | bytes 3848 | tf_op jit(solution)/shard_map/ppermute | solution.py:149
  47.7 3.0 %collective-permute-start.41 = (f32[4,80]{1,0:T(4,128)S(1)}, f32[4,80]{1,0:T(4,128)S(1)}, u32[]{:S(2)}, u32[]{:S(2)}) collective-permute-start(f32[4,80]{1,0:T(4,128)S(1)} %get-tuple-element.742), channel_id=1, source_target_pairs={{0,3},{1,2},{2,1},{3,0},{4,7},{5,6},{6,5},{7,4},{8,11},{9,10},{10,... | collective-permute-start | bytes 3848 | tf_op jit(solution)/shard_map/ppermute | solution.py:149
  50.9 3.7 %collective-permute-start.42 = (f32[16,80]{1,0:T(8,128)S(1)}, f32[16,80]{1,0:T(8,128)S(1)}, u32[]{:S(2)}, u32[]{:S(2)}) collective-permute-start(f32[16,80]{1,0:T(8,128)S(1)} %shard_map.100.refs_0_.refs_4_.refs_6_), channel_id=1, source_target_pairs={{0,4},{4,0},{8,12},{12,8},{16,20},{20,16},{24,28},{28,24},{1,5},{5... | collective-permute-start | bytes 15368 | tf_op jit(solution)/shard_map/ppermute | solution.py:519
  51.0 3.6 %collective-permute-start.43 = (f32[16,80]{1,0:T(8,128)S(1)}, f32[16,80]{1,0:T(8,128)S(1)}, u32[]{:S(2)}, u32[]{:S(2)}) collective-permute-start(f32[16,80]{1,0:T(8,128)S(1)} %shard_map.100.refs_0_.refs_4_.refs_6_), channel_id=1, source_target_pairs={{0,1},{1,0},{2,3},{3,2},{4,5},{5,4},{6,7},{7,6},{8,9},{9,8},{10,11... | collective-permute-start | bytes 15368 | tf_op jit(solution)/shard_map/ppermute | solution.py:519
  51.0 6.3 %collective-permute-start.44 = (f32[16,80]{1,0:T(8,128)S(1)}, f32[16,80]{1,0:T(8,128)S(1)}, u32[]{:S(2)}, u32[]{:S(2)}) collective-permute-start(f32[16,80]{1,0:T(8,128)S(1)} %shard_map.100.refs_0_.refs_4_.refs_6_), channel_id=1, source_target_pairs={{0,28},{4,8},{8,4},{12,16},{16,12},{20,24},{24,20},{28,0},{1,29},{... | collective-permute-start | bytes 15368 | tf_op jit(solution)/shard_map/ppermute | solution.py:518
  53.1 4.3 %collective-permute-start.45 = (f32[16,80]{1,0:T(8,128)S(1)}, f32[16,80]{1,0:T(8,128)S(1)}, u32[]{:S(2)}, u32[]{:S(2)}) collective-permute-start(f32[16,80]{1,0:T(8,128)S(1)} %shard_map.100.refs_0_.refs_4_.refs_6_), channel_id=1, source_target_pairs={{0,3},{1,2},{2,1},{3,0},{4,7},{5,6},{6,5},{7,4},{8,11},{9,10},{10,... | collective-permute-start | bytes 15368 | tf_op jit(solution)/shard_map/ppermute | solution.py:520
  (3 other events, 71.2 us)

commit v7 on v6

--- a/solution.py
+++ b/solution.py
@@ -144,6 +144,10 @@
     return (me + k) % size, (me + size - k) % size
 
 
+def far_first(size):
+    return list(reversed(range(size)))
+
+
 def exchange(x, axis, k):
     size = lax.axis_size(axis)
     return lax.ppermute(x, axis, [(i, partner(i, k, size)[0]) for i in range(size)])
@@ -169,10 +173,10 @@
     face = lax.broadcasted_iota(jnp.int32, choose_ref.shape, 0)
     piece = lax.broadcasted_iota(jnp.int32, choose_ref.shape, 1) % nfaces
     choose = jnp.zeros(choose_ref.shape, F32)
-    for k in range(nplane):
+    for n, k in enumerate(far_first(nplane)):
         _, source = partner(me, k, nplane)
         for i in range(per):
-            hit = (face == slot_ref[0, source * per + i]) & (piece == k * per + i)
+            hit = (face == slot_ref[0, source * per + i]) & (piece == n * per + i)
             choose = jnp.where(hit, 1.0, choose)
     choose_ref[...] = choose
 
@@ -231,11 +235,11 @@
     msgs, (low, upp, piv_t), outs, (r_scr, z_scr) = refs[:nplane], refs[nplane:-nplane-2], refs[-nplane-2:-2], refs[-2:]
     _, length, width = r_scr.shape
     me = lax.axis_index("plane")
-    for k in range(nplane):
+    for k, msg in zip(far_first(nplane), msgs):
         _, source = partner(me, k, nplane)
         for m in range(nlines):
             for q in range(P_SIZE):
-                r_scr[m, pl.ds(source * P_SIZE + q, 1), :] = msgs[k][pl.ds(m * P_SIZE + q, 1), :]
+                r_scr[m, pl.ds(source * P_SIZE + q, 1), :] = msg[pl.ds(m * P_SIZE + q, 1), :]
     eye = lax.broadcasted_iota(jnp.int32, (width, width), 0) == lax.broadcasted_iota(jnp.int32, (width, width), 1)
 
     def column(row):
@@ -270,8 +274,8 @@
                 outs[k][pl.ds(m * P_SIZE + q, 1), :] = z_scr[m, pl.ds(to * P_SIZE + q, 1), :]
 
 
-def faces_kernel(choose, *refs):
-    solved, mine_ref = refs[:-1], refs[-1]
+def faces_kernel(nplane, choose, *refs):
+    solved, mine_ref = refs[:nplane], refs[-1]
     table = split(jnp.concatenate([s[...] for s in solved], axis=0), 3).astype(BF16)
     mine_ref[...] = jnp.dot(choose[...].astype(BF16), table, preferred_element_type=F32)
 
@@ -455,7 +459,9 @@
 
 
 def add_up(x):
-    return lax.all_gather(x, ("span", "plane"), axis=0, tiled=True)
+    count = lax.axis_size("span") * lax.axis_size("plane")
+    rows = jnp.broadcast_to(x, (count, x.shape[1]))
+    return lax.all_to_all(rows, ("span", "plane"), split_axis=0, concat_axis=0, tiled=True)
 
 
 def pairings(size):
@@ -496,7 +502,7 @@
             flops=nfaces * area,
         )
         factors = [x.reshape(nfaces, width, width) for x in factors]
-        got = [send[0]] + [exchange(send[k], "plane", k) for k in range(1, nplane)]
+        got = [exchange(send[k], "plane", k) if k else send[0] for k in far_first(nplane)]
         solved = call(
             functools.partial(line_kernel, nplane, owned),
             [*got, *factors],
@@ -512,8 +518,10 @@
                 ready=False,
                 kind=BF16,
             )
-        pieces = [solved[0]] + [exchange(solved[k], "plane", k) for k in range(1, nplane)]
-        (mine,) = call(faces_kernel, [choose, *pieces], [shape])
+        pieces = [exchange(solved[k], "plane", k) if k else solved[0] for k in far_first(nplane)]
+        args = [choose, *pieces, *(picks if step == 0 else ())]
+        spaces = [pltpu.VMEM] * (nplane + 1) + [pl.ANY] * (len(args) - nplane - 1)
+        (mine,) = call(functools.partial(faces_kernel, nplane), args, [shape], spaces)
         zs.append(mine)
         other = lax.ppermute(mine, "span", span_others)
         near = [mine, lax.ppermute(mine, "span", span_pairs), lax.ppermute(mine, "plane", plane_pairs)]

time: 98.4 us -> 69.1 us (0.70)
  blocking collectives: 38.5 us -> 10.2 us
  waiting for transfers between devices: 11.1 us -> 9.26 us
    all_gather x1 -> x0, blocking collectives: 38.5 us -> none  [add_up(): return lax.all_gather(x, ('span', 'plane'), axis=0, tiled=True)]
    all_to_all x0 -> x1, blocking collectives: none -> 10.2 us  [add_up(): lax.all_to_all(rows, ('span', 'plane'), split_axis=0, concat_axis=0, tile...]
  transfers between devices with their start and end apart: 30 -> 30, of which waited for: 13 -> 13; matrix products, arithmetic and copies ran while one was open for 0% -> 0% of each run, Pallas kernels for 15% -> 21%
where the time goes in v7:
time: 69.1 us; the launch traced here: 68.7 us
  starting transfers between devices  25 us (36%)
  Pallas kernels  23 us (33%)
  blocking collectives  10.2 us (15%)
  waiting for transfers between devices  9.26 us (13%)
  between operations  1.06 us (2%)
    pallas_call x18, Pallas kernels, call(): pl.pallas_call(kernel, out_shape=[pltpu.VMEM(shape, kind) if pinned else...  23 us
    ppermute x18, starting transfers between devices, exchange(): lax.ppermute(x, axis, [(i, partner(i, k, size)[0]) for i in range(size)])  12.8 us
    all_to_all x1, blocking collectives, add_up(): lax.all_to_all(rows, ('span', 'plane'), split_axis=0, concat_axis=0, tile...  10.2 us
    ppermute x3, starting transfers between devices, on_device(): other = lax.ppermute(mine, 'span', span_others)  8.44 us
    ppermute x18, waiting for transfers between devices, exchange(): lax.ppermute(x, axis, [(i, partner(i, k, size)[0]) for i in range(size)])  7.82 us
    ppermute x3, starting transfers between devices, on_device(): far = [other, lax.ppermute(mine, 'plane', plane_others)]  2.2 us
    ppermute x3, starting transfers between devices, on_device(): lax.ppermute(mine, 'span', span_pairs)  1.55 us
  transfers between devices with their start and end apart: 30, of which 13 were waited for; matrix products, arithmetic and copies ran while one was open for 0% of the time, Pallas kernels for 21%

profile of v7, /device:TPU:0, one launch (start us, length us, event | category | flops | bytes accessed | tf_op | source)
XLA Modules:
  0.0 68.7 jit_solution(8627780280280531210)
XLA Ops:
  0.7 0.8 %shard_map.86 = (f32[16,80]{1,0:T(8,128)S(1)}, f32[16,48]{1,0:T(8,128)S(1)}, f32[4,80]{1,0:T(4,128)S(1)}, f32[4,80]{1,0:T(4,128)S(1)}, f32[4,80]{1,0:T(4,128)S(1)}, /*index=5*/f32[4,80]{1,0:T(4,128)S(1)}) custom-call(s32[1,16]{1,0:T(1,128)} %refs_0_.5, f32[16,80]{1,0:T(8,128)} %bitcast.571), custom_call_target="tpu_custom_call" | custom-call | bytes 5184 | tf_op jit(solution)/shard_map/pallas_call | solution.py:450
  1.5 2.5 %collective-permute-start.16 = (f32[4,80]{1,0:T(4,128)S(1)}, f32[4,80]{1,0:T(4,128)S(1)}, u32[]{:S(2)}, u32[]{:S(2)}) collective-permute-start(f32[4,80]{1,0:T(4,128)S(1)} %get-tuple-element.699), channel_id=1, source_target_pairs={{0,3},{1,2},{2,1},{3,0},{4,7},{5,6},{6,5},{7,4},{8,11},{9,10},{10,... | collective-permute-start | bytes 3848 | tf_op jit(solution)/shard_map/ppermute | solution.py:153
  4.7 2.3 %shard_map.87 = (f32[1280,80]{1,0:T(8,128)S(1)}, f32[1280,80]{1,0:T(8,128)S(1)}, f32[1280,80]{1,0:T(8,128)S(1)}) custom-call(f32[16,6400]{1,0:T(8,128)} %low.5, f32[16,6400]{1,0:T(8,128)} %upp.5, f32[16,6400]{1,0:T(8,128)} %piv.5, f32[16,80]{1,0:T(8,128)S(1)} %get-tuple-element.703._.refs_9_.refs_0_), custom_call_target="tpu_custom_call" | custom-call | flops 102400 | bytes 1233920 | tf_op jit(solution)/shard_map/pallas_call | solution.py:450
  7.6 1.2 %shard_map.88 = (f32[4,80]{1,0:T(4,128)S(1)}, f32[4,80]{1,0:T(4,128)S(1)}, f32[4,80]{1,0:T(4,128)S(1)}, f32[4,80]{1,0:T(4,128)S(1)}) custom-call(f32[4,80]{1,0:T(4,128)S(1)} %collective-permute-done.16.refs_0_, f32[4,80]{1,0:T(4,128)S(1)} %collective-permute-done.17.refs_1_, f32[4,80]{1,0:T(4,128)S(1)} %collective-permute-done.18.refs_2_, ...), custom_call_target="tpu_custom_call" | custom-call | flops 614400 | bytes 1233920 | tf_op jit(solution)/shard_map/pallas_call | solution.py:450
  8.8 0.9 %collective-permute-start.19 = (f32[4,80]{1,0:T(4,128)S(1)}, f32[4,80]{1,0:T(4,128)S(1)}, u32[]{:S(2)}, u32[]{:S(2)}) collective-permute-start(f32[4,80]{1,0:T(4,128)S(1)} %get-tuple-element.711), channel_id=1, source_target_pairs={{0,3},{1,2},{2,1},{3,0},{4,7},{5,6},{6,5},{7,4},{8,11},{9,10},{10,... | collective-permute-start | bytes 3848 | tf_op jit(solution)/shard_map/ppermute | solution.py:153
  10.7 0.8 %shard_map.89 = (bf16[48,96]{1,0:T(8,128)(2,1)S(1)}, bf16[128,160]{1,0:T(8,128)(2,1)S(1)}) custom-call(s32[11,16]{1,0:T(8,128)} %columns_ref), custom_call_target="tpu_custom_call" | custom-call | bytes 704 | tf_op jit(solution)/shard_map/pallas_call | solution.py:450
  11.9 1.4 %collective-permute-done.20.refs_1_ = f32[4,80]{1,0:T(4,128)S(1)} collective-permute-done((f32[4,80]{1,0:T(4,128)S(1)}, f32[4,80]{1,0:T(4,128)S(1)}, u32[]{:S(2)}, u32[]{:S(2)}) %collective-permute-start.20) | collective-permute-done | bytes 1312 | tf_op jit(solution)/shard_map/ppermute | solution.py:153
  13.5 1.5 %collective-permute-start.22 = (f32[16,80]{1,0:T(8,128)S(1)}, f32[16,80]{1,0:T(8,128)S(1)}, u32[]{:S(2)}, u32[]{:S(2)}) collective-permute-start(f32[16,80]{1,0:T(8,128)S(1)} %shard_map.90.refs_0_.refs_4_), channel_id=1, source_target_pairs={{0,4},{4,0},{8,12},{12,8},{16,20},{20,16},{24,28},{28,24},{1,5},{5... | collective-permute-start | bytes 15368 | tf_op jit(solution)/shard_map/ppermute | solution.py:527
  15.0 3.6 %collective-permute-start.24 = (f32[16,80]{1,0:T(8,128)S(1)}, f32[16,80]{1,0:T(8,128)S(1)}, u32[]{:S(2)}, u32[]{:S(2)}) collective-permute-start(f32[16,80]{1,0:T(8,128)S(1)} %shard_map.90.refs_0_.refs_4_), channel_id=1, source_target_pairs={{0,28},{4,8},{8,4},{12,16},{16,12},{20,24},{24,20},{28,0},{1,29},{... | collective-permute-start | bytes 15368 | tf_op jit(solution)/shard_map/ppermute | solution.py:526
  19.0 2.5 %shard_map.91 = (f32[16,80]{1,0:T(8,128)S(1)}, f32[16,51200]{1,0:T(8,128)S(1)}) custom-call(f32[16,70400]{1,0:T(8,128)} %blocks.5, bf16[48,96]{1,0:T(8,128)(2,1)S(1)} %get-tuple-element.709.refs_4_.pick, f32[16,80]{1,0:T(8,128)S(1)} %shard_map.90.refs_0_.refs_4_, f32[16,80]{1,0:T(8,128)S(1)} %collective-permute-done.22.refs_1_.refs_5_, ...), custom_call_target="tpu_custom_call" | custom-call | flops 614400 | bytes 4530176 | tf_op jit(solution)/shard_map/pallas_call | solution.py:450
  21.6 0.8 %shard_map.92 = (f32[16,80]{1,0:T(8,128)S(1)}, f32[4,80]{1,0:T(4,128)S(1)}, f32[4,80]{1,0:T(4,128)S(1)}, f32[4,80]{1,0:T(4,128)S(1)}, f32[4,80]{1,0:T(4,128)S(1)}) custom-call(s32[1,16]{1,0:T(1,128)S(1)} %copy-done.5, f32[16,51200]{1,0:T(8,128)S(1)} %get-tuple-element.715.refs_1_, bf16[128,160]{1,0:T(8,128)(2,1)S(1)} %get-tuple-element.714.refs_5_.refs_2_, ...), custom_call_target="tpu_custom_call" | custom-call | flops 2252800 | bytes 3353664 | tf_op jit(solution)/shard_map/pallas_call | solution.py:450
  22.5 1.2 %collective-permute-start.26 = (f32[4,80]{1,0:T(4,128)S(1)}, f32[4,80]{1,0:T(4,128)S(1)}, u32[]{:S(2)}, u32[]{:S(2)}) collective-permute-start(f32[4,80]{1,0:T(4,128)S(1)} %get-tuple-element.717), channel_id=1, source_target_pairs={{0,3},{1,2},{2,1},{3,0},{4,7},{5,6},{6,5},{7,4},{8,11},{9,10},{10,... | collective-permute-start | bytes 3848 | tf_op jit(solution)/shard_map/ppermute | solution.py:153
  24.4 2.1 %shard_map.93 = (f32[1280,80]{1,0:T(8,128)S(1)}, f32[1280,80]{1,0:T(8,128)S(1)}, f32[1280,80]{1,0:T(8,128)S(1)}) custom-call(f32[16,6400]{1,0:T(8,128)S(1)} %copy-done, f32[16,6400]{1,0:T(8,128)S(1)} %copy-done.1, f32[16,6400]{1,0:T(8,128)} %piv.5, f32[16,80]{1,0:T(8,128)S(1)} %get-tuple-element.721._.refs_9_.refs_10_.refs_1_), custom_call_target="tpu_custom_call" | custom-call | flops 102400 | bytes 1233920 | tf_op jit(solution)/shard_map/pallas_call | solution.py:450
  26.5 0.8 %collective-permute-done.27.refs_1_ = f32[4,80]{1,0:T(4,128)S(1)} collective-permute-done((f32[4,80]{1,0:T(4,128)S(1)}, f32[4,80]{1,0:T(4,128)S(1)}, u32[]{:S(2)}, u32[]{:S(2)}) %collective-permute-start.27) | collective-permute-done | bytes 1312 | tf_op jit(solution)/shard_map/ppermute | solution.py:153
  27.3 1.2 %shard_map.94 = (f32[4,80]{1,0:T(4,128)S(1)}, f32[4,80]{1,0:T(4,128)S(1)}, f32[4,80]{1,0:T(4,128)S(1)}, f32[4,80]{1,0:T(4,128)S(1)}) custom-call(f32[4,80]{1,0:T(4,128)S(1)} %collective-permute-done.26.refs_0_, f32[4,80]{1,0:T(4,128)S(1)} %collective-permute-done.27.refs_1_, f32[4,80]{1,0:T(4,128)S(1)} %collective-permute-done.28.refs_2_, ...), custom_call_target="tpu_custom_call" | custom-call | flops 614400 | bytes 1233920 | tf_op jit(solution)/shard_map/pallas_call | solution.py:450
  30.5 1.1 %collective-permute-done.29.refs_0_ = f32[4,80]{1,0:T(4,128)S(1)} collective-permute-done((f32[4,80]{1,0:T(4,128)S(1)}, f32[4,80]{1,0:T(4,128)S(1)}, u32[]{:S(2)}, u32[]{:S(2)}) %collective-permute-start.29) | collective-permute-done | bytes 1312 | tf_op jit(solution)/shard_map/ppermute | solution.py:153
  31.6 1.2 %collective-permute-done.30.refs_1_ = f32[4,80]{1,0:T(4,128)S(1)} collective-permute-done((f32[4,80]{1,0:T(4,128)S(1)}, f32[4,80]{1,0:T(4,128)S(1)}, u32[]{:S(2)}, u32[]{:S(2)}) %collective-permute-start.30) | collective-permute-done | bytes 1312 | tf_op jit(solution)/shard_map/ppermute | solution.py:153
  33.0 2.2 %collective-permute-start.34 = (f32[16,80]{1,0:T(8,128)S(1)}, f32[16,80]{1,0:T(8,128)S(1)}, u32[]{:S(2)}, u32[]{:S(2)}) collective-permute-start(f32[16,80]{1,0:T(8,128)S(1)} %shard_map.95.refs_0_.refs_4_.refs_5_), channel_id=1, source_target_pairs={{0,28},{4,8},{8,4},{12,16},{16,12},{20,24},{24,20},{28,0},{1,29},{... | collective-permute-start | bytes 15368 | tf_op jit(solution)/shard_map/ppermute | solution.py:526
  35.3 1.1 %collective-permute-start.35 = (f32[16,80]{1,0:T(8,128)S(1)}, f32[16,80]{1,0:T(8,128)S(1)}, u32[]{:S(2)}, u32[]{:S(2)}) collective-permute-start(f32[16,80]{1,0:T(8,128)S(1)} %shard_map.95.refs_0_.refs_4_.refs_5_), channel_id=1, source_target_pairs={{0,3},{1,2},{2,1},{3,0},{4,7},{5,6},{6,5},{7,4},{8,11},{9,10},{10,... | collective-permute-start | bytes 15368 | tf_op jit(solution)/shard_map/ppermute | solution.py:528
  36.6 2.5 %shard_map.96 = (f32[16,80]{1,0:T(8,128)S(1)}, f32[16,51200]{1,0:T(8,128)S(1)}) custom-call(f32[16,70400]{1,0:T(8,128)} %blocks.5, bf16[48,96]{1,0:T(8,128)(2,1)S(1)} %get-tuple-element.709.refs_4_.pick, f32[16,80]{1,0:T(8,128)S(1)} %shard_map.95.refs_0_.refs_4_.refs_5_, f32[16,80]{1,0:T(8,128)S(1)} %collective-permute-done.32.refs_1_.refs_5_, ...), custom_call_target="tpu_custom_call" | custom-call | flops 614400 | bytes 4530176 | tf_op jit(solution)/shard_map/pallas_call | solution.py:450
  39.4 0.8 %shard_map.97 = (f32[16,80]{1,0:T(8,128)S(1)}, f32[4,80]{1,0:T(4,128)S(1)}, f32[4,80]{1,0:T(4,128)S(1)}, f32[4,80]{1,0:T(4,128)S(1)}, f32[4,80]{1,0:T(4,128)S(1)}) custom-call(s32[1,16]{1,0:T(1,128)S(1)} %copy-done.5, f32[16,51200]{1,0:T(8,128)S(1)} %get-tuple-element.729.refs_1_, bf16[128,160]{1,0:T(8,128)(2,1)S(1)} %get-tuple-element.714.refs_5_.refs_2_, ...), custom_call_target="tpu_custom_call" | custom-call | flops 2252800 | bytes 3353664 | tf_op jit(solution)/shard_map/pallas_call | solution.py:450
  40.6 1.1 %collective-permute-start.37 = (f32[4,80]{1,0:T(4,128)S(1)}, f32[4,80]{1,0:T(4,128)S(1)}, u32[]{:S(2)}, u32[]{:S(2)}) collective-permute-start(f32[4,80]{1,0:T(4,128)S(1)} %get-tuple-element.732), channel_id=1, source_target_pairs={{0,2},{1,3},{2,0},{3,1},{4,6},{5,7},{6,4},{7,5},{8,10},{9,11},{10,... | collective-permute-start | bytes 3848 | tf_op jit(solution)/shard_map/ppermute | solution.py:153
  42.2 2.1 %shard_map.98 = (f32[1280,80]{1,0:T(8,128)S(1)}, f32[1280,80]{1,0:T(8,128)S(1)}, f32[1280,80]{1,0:T(8,128)S(1)}) custom-call(f32[16,6400]{1,0:T(8,128)S(1)} %copy-done, f32[16,6400]{1,0:T(8,128)S(1)} %copy-done.1, f32[16,6400]{1,0:T(8,128)} %piv.5, f32[16,80]{1,0:T(8,128)S(1)} %get-tuple-element.735._.refs_11_.refs_2_), custom_call_target="tpu_custom_call" | custom-call | flops 102400 | bytes 1233920 | tf_op jit(solution)/shard_map/pallas_call | solution.py:450
  44.3 1.2 %shard_map.99 = (f32[4,80]{1,0:T(4,128)S(1)}, f32[4,80]{1,0:T(4,128)S(1)}, f32[4,80]{1,0:T(4,128)S(1)}, f32[4,80]{1,0:T(4,128)S(1)}) custom-call(f32[4,80]{1,0:T(4,128)S(1)} %collective-permute-done.36.refs_0_, f32[4,80]{1,0:T(4,128)S(1)} %collective-permute-done.37.refs_1_, f32[4,80]{1,0:T(4,128)S(1)} %collective-permute-done.38.refs_2_, ...), custom_call_target="tpu_custom_call" | custom-call | flops 614400 | bytes 1233920 | tf_op jit(solution)/shard_map/pallas_call | solution.py:450
  46.1 1.1 %collective-permute-start.40 = (f32[4,80]{1,0:T(4,128)S(1)}, f32[4,80]{1,0:T(4,128)S(1)}, u32[]{:S(2)}, u32[]{:S(2)}) collective-permute-start(f32[4,80]{1,0:T(4,128)S(1)} %get-tuple-element.740), channel_id=1, source_target_pairs={{0,2},{1,3},{2,0},{3,1},{4,6},{5,7},{6,4},{7,5},{8,10},{9,11},{10,... | collective-permute-start | bytes 3848 | tf_op jit(solution)/shard_map/ppermute | solution.py:153
  47.5 1.1 %collective-permute-done.39.refs_0_ = f32[4,80]{1,0:T(4,128)S(1)} collective-permute-done((f32[4,80]{1,0:T(4,128)S(1)}, f32[4,80]{1,0:T(4,128)S(1)}, u32[]{:S(2)}, u32[]{:S(2)}) %collective-permute-start.39) | collective-permute-done | bytes 1312 | tf_op jit(solution)/shard_map/ppermute | solution.py:153
  48.6 1.1 %collective-permute-done.40.refs_1_ = f32[4,80]{1,0:T(4,128)S(1)} collective-permute-done((f32[4,80]{1,0:T(4,128)S(1)}, f32[4,80]{1,0:T(4,128)S(1)}, u32[]{:S(2)}, u32[]{:S(2)}) %collective-permute-start.40) | collective-permute-done | bytes 1312 | tf_op jit(solution)/shard_map/ppermute | solution.py:153
  49.9 2.6 %collective-permute-start.44 = (f32[16,80]{1,0:T(8,128)S(1)}, f32[16,80]{1,0:T(8,128)S(1)}, u32[]{:S(2)}, u32[]{:S(2)}) collective-permute-start(f32[16,80]{1,0:T(8,128)S(1)} %shard_map.100.refs_0_.refs_4_.refs_6_), channel_id=1, source_target_pairs={{0,28},{4,8},{8,4},{12,16},{16,12},{20,24},{24,20},{28,0},{1,29},{... | collective-permute-start | bytes 15368 | tf_op jit(solution)/shard_map/ppermute | solution.py:526
  53.5 2.5 %shard_map.101 = (f32[16,80]{1,0:T(8,128)S(1)}, f32[16,51200]{1,0:T(8,128)S(1)}) custom-call(f32[16,70400]{1,0:T(8,128)} %blocks.5, bf16[48,96]{1,0:T(8,128)(2,1)S(1)} %get-tuple-element.709.refs_4_.pick, f32[16,80]{1,0:T(8,128)S(1)} %shard_map.100.refs_0_.refs_4_.refs_6_, f32[16,80]{1,0:T(8,128)S(1)} %collective-permute-done.42.refs_1_.refs_5_, ...), custom_call_target="tpu_custom_call" | custom-call | flops 614400 | bytes 4530176 | tf_op jit(solution)/shard_map/pallas_call | solution.py:450
  56.3 0.9 %shard_map.102 = (f32[16,80]{1,0:T(8,128)S(1)}, f32[1,128]{1,0:T(1,128)S(1)}) custom-call(s32[1,16]{1,0:T(1,128)S(1)} %copy-done.5, f32[16,51200]{1,0:T(8,128)S(1)} %get-tuple-element.743.refs_1_, bf16[128,160]{1,0:T(8,128)(2,1)S(1)} %get-tuple-element.714.refs_5_.refs_2_, f32[16,80]{1,0:T(8,128)S(1)} %get-tuple-element.744.refs_3_, ...), custom_call_target="tpu_custom_call" | custom-call | flops 2252800 | bytes 3363904 | tf_op jit(solution)/shard_map/pallas_call | solution.py:450
  57.3 10.2 %all_to_all.112 = f32[32,1,128]{2,1,0:T(1,128)S(1)} all-to-all(f32[32,1,128]{2,1,0:T(1,128)S(1)} %broadcast_in_dim.83), channel_id=1, replica_groups=mesh['span'=8,'plane'=4] {'span','plane'}, dimensions={0} | all-to-all | bytes 32768 | tf_op jit(solution)/shard_map/all_to_all | solution.py:464
  67.5 0.8 %shard_map.103 = (f32[16,80]{1,0:T(8,128)}, f32[16,80]{1,0:T(8,128)}, f32[1,128]{1,0:T(1,128)S(1)}) custom-call(f32[32,128]{1,0:T(8,128)S(1)} %bitcast.558, f32[16,80]{1,0:T(8,128)S(1)} %get-tuple-element.703._.refs_9_.refs_0_, f32[16,80]{1,0:T(8,128)S(1)} %get-tuple-element.721._.refs_9_.refs_10_.refs_1_, ...), custom_call_target="tpu_custom_call" | custom-call | bytes 52224 | tf_op jit(solution)/shard_map/pallas_call | solution.py:450
  (59 shorter events, 10.1 us)
Async XLA Ops:
  1.5 5.4 %collective-permute-start.16 = (f32[4,80]{1,0:T(4,128)S(1)}, f32[4,80]{1,0:T(4,128)S(1)}, u32[]{:S(2)}, u32[]{:S(2)}) collective-permute-start(f32[4,80]{1,0:T(4,128)S(1)} %get-tuple-element.699), channel_id=1, source_target_pairs={{0,3},{1,2},{2,1},{3,0},{4,7},{5,6},{6,5},{7,4},{8,11},{9,10},{10,... | collective-permute-start | bytes 3848 | tf_op jit(solution)/shard_map/ppermute | solution.py:153
  4.0 3.6 %collective-permute-start.17 = (f32[4,80]{1,0:T(4,128)S(1)}, f32[4,80]{1,0:T(4,128)S(1)}, u32[]{:S(2)}, u32[]{:S(2)}) collective-permute-start(f32[4,80]{1,0:T(4,128)S(1)} %get-tuple-element.700), channel_id=1, source_target_pairs={{0,2},{1,3},{2,0},{3,1},{4,6},{5,7},{6,4},{7,5},{8,10},{9,11},{10,... | collective-permute-start | bytes 3848 | tf_op jit(solution)/shard_map/ppermute | solution.py:153
  4.6 2.9 %collective-permute-start.18 = (f32[4,80]{1,0:T(4,128)S(1)}, f32[4,80]{1,0:T(4,128)S(1)}, u32[]{:S(2)}, u32[]{:S(2)}) collective-permute-start(f32[4,80]{1,0:T(4,128)S(1)} %get-tuple-element.701), channel_id=1, source_target_pairs={{0,1},{1,0},{2,3},{3,2},{4,5},{5,4},{6,7},{7,6},{8,9},{9,8},{10,11... | collective-permute-start | bytes 3848 | tf_op jit(solution)/shard_map/ppermute | solution.py:153
  8.8 3.1 %collective-permute-start.19 = (f32[4,80]{1,0:T(4,128)S(1)}, f32[4,80]{1,0:T(4,128)S(1)}, u32[]{:S(2)}, u32[]{:S(2)}) collective-permute-start(f32[4,80]{1,0:T(4,128)S(1)} %get-tuple-element.711), channel_id=1, source_target_pairs={{0,3},{1,2},{2,1},{3,0},{4,7},{5,6},{6,5},{7,4},{8,11},{9,10},{10,... | collective-permute-start | bytes 3848 | tf_op jit(solution)/shard_map/ppermute | solution.py:153
  9.7 3.6 %collective-permute-start.20 = (f32[4,80]{1,0:T(4,128)S(1)}, f32[4,80]{1,0:T(4,128)S(1)}, u32[]{:S(2)}, u32[]{:S(2)}) collective-permute-start(f32[4,80]{1,0:T(4,128)S(1)} %get-tuple-element.712), channel_id=1, source_target_pairs={{0,2},{1,3},{2,0},{3,1},{4,6},{5,7},{6,4},{7,5},{8,10},{9,11},{10,... | collective-permute-start | bytes 3848 | tf_op jit(solution)/shard_map/ppermute | solution.py:153
  10.4 2.9 %collective-permute-start.21 = (f32[4,80]{1,0:T(4,128)S(1)}, f32[4,80]{1,0:T(4,128)S(1)}, u32[]{:S(2)}, u32[]{:S(2)}) collective-permute-start(f32[4,80]{1,0:T(4,128)S(1)} %get-tuple-element.713), channel_id=1, source_target_pairs={{0,1},{1,0},{2,3},{3,2},{4,5},{5,4},{6,7},{7,6},{8,9},{9,8},{10,11... | collective-permute-start | bytes 3848 | tf_op jit(solution)/shard_map/ppermute | solution.py:153
  13.5 5.5 %collective-permute-start.22 = (f32[16,80]{1,0:T(8,128)S(1)}, f32[16,80]{1,0:T(8,128)S(1)}, u32[]{:S(2)}, u32[]{:S(2)}) collective-permute-start(f32[16,80]{1,0:T(8,128)S(1)} %shard_map.90.refs_0_.refs_4_), channel_id=1, source_target_pairs={{0,4},{4,0},{8,12},{12,8},{16,20},{20,16},{24,28},{28,24},{1,5},{5... | collective-permute-start | bytes 15368 | tf_op jit(solution)/shard_map/ppermute | solution.py:527
  15.0 4.1 %collective-permute-start.23 = (f32[16,80]{1,0:T(8,128)S(1)}, f32[16,80]{1,0:T(8,128)S(1)}, u32[]{:S(2)}, u32[]{:S(2)}) collective-permute-start(f32[16,80]{1,0:T(8,128)S(1)} %shard_map.90.refs_0_.refs_4_), channel_id=1, source_target_pairs={{0,1},{1,0},{2,3},{3,2},{4,5},{5,4},{6,7},{7,6},{8,9},{9,8},{10,11... | collective-permute-start | bytes 15368 | tf_op jit(solution)/shard_map/ppermute | solution.py:527
  15.0 6.5 %collective-permute-start.24 = (f32[16,80]{1,0:T(8,128)S(1)}, f32[16,80]{1,0:T(8,128)S(1)}, u32[]{:S(2)}, u32[]{:S(2)}) collective-permute-start(f32[16,80]{1,0:T(8,128)S(1)} %shard_map.90.refs_0_.refs_4_), channel_id=1, source_target_pairs={{0,28},{4,8},{8,4},{12,16},{16,12},{20,24},{24,20},{28,0},{1,29},{... | collective-permute-start | bytes 15368 | tf_op jit(solution)/shard_map/ppermute | solution.py:526
  18.5 3.1 %collective-permute-start.25 = (f32[16,80]{1,0:T(8,128)S(1)}, f32[16,80]{1,0:T(8,128)S(1)}, u32[]{:S(2)}, u32[]{:S(2)}) collective-permute-start(f32[16,80]{1,0:T(8,128)S(1)} %shard_map.90.refs_0_.refs_4_), channel_id=1, source_target_pairs={{0,3},{1,2},{2,1},{3,0},{4,7},{5,6},{6,5},{7,4},{8,11},{9,10},{10,... | collective-permute-start | bytes 15368 | tf_op jit(solution)/shard_map/ppermute | solution.py:528
  22.5 4.0 %collective-permute-start.26 = (f32[4,80]{1,0:T(4,128)S(1)}, f32[4,80]{1,0:T(4,128)S(1)}, u32[]{:S(2)}, u32[]{:S(2)}) collective-permute-start(f32[4,80]{1,0:T(4,128)S(1)} %get-tuple-element.717), channel_id=1, source_target_pairs={{0,3},{1,2},{2,1},{3,0},{4,7},{5,6},{6,5},{7,4},{8,11},{9,10},{10,... | collective-permute-start | bytes 3848 | tf_op jit(solution)/shard_map/ppermute | solution.py:153
  23.7 3.6 %collective-permute-start.27 = (f32[4,80]{1,0:T(4,128)S(1)}, f32[4,80]{1,0:T(4,128)S(1)}, u32[]{:S(2)}, u32[]{:S(2)}) collective-permute-start(f32[4,80]{1,0:T(4,128)S(1)} %get-tuple-element.718), channel_id=1, source_target_pairs={{0,2},{1,3},{2,0},{3,1},{4,6},{5,7},{6,4},{7,5},{8,10},{9,11},{10,... | collective-permute-start | bytes 3848 | tf_op jit(solution)/shard_map/ppermute | solution.py:153
  24.4 2.9 %collective-permute-start.28 = (f32[4,80]{1,0:T(4,128)S(1)}, f32[4,80]{1,0:T(4,128)S(1)}, u32[]{:S(2)}, u32[]{:S(2)}) collective-permute-start(f32[4,80]{1,0:T(4,128)S(1)} %get-tuple-element.719), channel_id=1, source_target_pairs={{0,1},{1,0},{2,3},{3,2},{4,5},{5,4},{6,7},{7,6},{8,9},{9,8},{10,11... | collective-permute-start | bytes 3848 | tf_op jit(solution)/shard_map/ppermute | solution.py:153
  28.5 3.1 %collective-permute-start.29 = (f32[4,80]{1,0:T(4,128)S(1)}, f32[4,80]{1,0:T(4,128)S(1)}, u32[]{:S(2)}, u32[]{:S(2)}) collective-permute-start(f32[4,80]{1,0:T(4,128)S(1)} %get-tuple-element.725), channel_id=1, source_target_pairs={{0,3},{1,2},{2,1},{3,0},{4,7},{5,6},{6,5},{7,4},{8,11},{9,10},{10,... | collective-permute-start | bytes 3848 | tf_op jit(solution)/shard_map/ppermute | solution.py:153
  29.2 3.6 %collective-permute-start.30 = (f32[4,80]{1,0:T(4,128)S(1)}, f32[4,80]{1,0:T(4,128)S(1)}, u32[]{:S(2)}, u32[]{:S(2)}) collective-permute-start(f32[4,80]{1,0:T(4,128)S(1)} %get-tuple-element.726), channel_id=1, source_target_pairs={{0,2},{1,3},{2,0},{3,1},{4,6},{5,7},{6,4},{7,5},{8,10},{9,11},{10,... | collective-permute-start | bytes 3848 | tf_op jit(solution)/shard_map/ppermute | solution.py:153
  29.9 2.9 %collective-permute-start.31 = (f32[4,80]{1,0:T(4,128)S(1)}, f32[4,80]{1,0:T(4,128)S(1)}, u32[]{:S(2)}, u32[]{:S(2)}) collective-permute-start(f32[4,80]{1,0:T(4,128)S(1)} %get-tuple-element.727), channel_id=1, source_target_pairs={{0,1},{1,0},{2,3},{3,2},{4,5},{5,4},{6,7},{7,6},{8,9},{9,8},{10,11... | collective-permute-start | bytes 3848 | tf_op jit(solution)/shard_map/ppermute | solution.py:153
  33.0 3.7 %collective-permute-start.32 = (f32[16,80]{1,0:T(8,128)S(1)}, f32[16,80]{1,0:T(8,128)S(1)}, u32[]{:S(2)}, u32[]{:S(2)}) collective-permute-start(f32[16,80]{1,0:T(8,128)S(1)} %shard_map.95.refs_0_.refs_4_.refs_5_), channel_id=1, source_target_pairs={{0,4},{4,0},{8,12},{12,8},{16,20},{20,16},{24,28},{28,24},{1,5},{5... | collective-permute-start | bytes 15368 | tf_op jit(solution)/shard_map/ppermute | solution.py:527
  33.0 3.7 %collective-permute-start.33 = (f32[16,80]{1,0:T(8,128)S(1)}, f32[16,80]{1,0:T(8,128)S(1)}, u32[]{:S(2)}, u32[]{:S(2)}) collective-permute-start(f32[16,80]{1,0:T(8,128)S(1)} %shard_map.95.refs_0_.refs_4_.refs_5_), channel_id=1, source_target_pairs={{0,1},{1,0},{2,3},{3,2},{4,5},{5,4},{6,7},{7,6},{8,9},{9,8},{10,11... | collective-permute-start | bytes 15368 | tf_op jit(solution)/shard_map/ppermute | solution.py:527
  33.0 6.4 %collective-permute-start.34 = (f32[16,80]{1,0:T(8,128)S(1)}, f32[16,80]{1,0:T(8,128)S(1)}, u32[]{:S(2)}, u32[]{:S(2)}) collective-permute-start(f32[16,80]{1,0:T(8,128)S(1)} %shard_map.95.refs_0_.refs_4_.refs_5_), channel_id=1, source_target_pairs={{0,28},{4,8},{8,4},{12,16},{16,12},{20,24},{24,20},{28,0},{1,29},{... | collective-permute-start | bytes 15368 | tf_op jit(solution)/shard_map/ppermute | solution.py:526
  35.3 4.2 %collective-permute-start.35 = (f32[16,80]{1,0:T(8,128)S(1)}, f32[16,80]{1,0:T(8,128)S(1)}, u32[]{:S(2)}, u32[]{:S(2)}) collective-permute-start(f32[16,80]{1,0:T(8,128)S(1)} %shard_map.95.refs_0_.refs_4_.refs_5_), channel_id=1, source_target_pairs={{0,3},{1,2},{2,1},{3,0},{4,7},{5,6},{6,5},{7,4},{8,11},{9,10},{10,... | collective-permute-start | bytes 15368 | tf_op jit(solution)/shard_map/ppermute | solution.py:528
  39.4 28.9 %copy-start.2 = (f32[80,16]{0,1:T(8,128)S(1)}, f32[80,16]{0,1:T(8,128)}, u32[]{:S(2)}) copy-start(f32[80,16]{0,1:T(8,128)} %param.25) | copy-start | bytes 15364
  39.4 28.9 %copy-start.3 = (s32[11,16]{1,0:T(8,128)S(1)}, s32[11,16]{1,0:T(8,128)}, u32[]{:S(2)}) copy-start(s32[11,16]{1,0:T(8,128)} %columns_ref) | copy-start | bytes 2116
  40.3 4.0 %collective-permute-start.36 = (f32[4,80]{1,0:T(4,128)S(1)}, f32[4,80]{1,0:T(4,128)S(1)}, u32[]{:S(2)}, u32[]{:S(2)}) collective-permute-start(f32[4,80]{1,0:T(4,128)S(1)} %get-tuple-element.731), channel_id=1, source_target_pairs={{0,3},{1,2},{2,1},{3,0},{4,7},{5,6},{6,5},{7,4},{8,11},{9,10},{10,... | collective-permute-start | bytes 3848 | tf_op jit(solution)/shard_map/ppermute | solution.py:153
  40.6 3.7 %collective-permute-start.37 = (f32[4,80]{1,0:T(4,128)S(1)}, f32[4,80]{1,0:T(4,128)S(1)}, u32[]{:S(2)}, u32[]{:S(2)}) collective-permute-start(f32[4,80]{1,0:T(4,128)S(1)} %get-tuple-element.732), channel_id=1, source_target_pairs={{0,2},{1,3},{2,0},{3,1},{4,6},{5,7},{6,4},{7,5},{8,10},{9,11},{10,... | collective-permute-start | bytes 3848 | tf_op jit(solution)/shard_map/ppermute | solution.py:153
  41.7 2.6 %collective-permute-start.38 = (f32[4,80]{1,0:T(4,128)S(1)}, f32[4,80]{1,0:T(4,128)S(1)}, u32[]{:S(2)}, u32[]{:S(2)}) collective-permute-start(f32[4,80]{1,0:T(4,128)S(1)} %get-tuple-element.733), channel_id=1, source_target_pairs={{0,1},{1,0},{2,3},{3,2},{4,5},{5,4},{6,7},{7,6},{8,9},{9,8},{10,11... | collective-permute-start | bytes 3848 | tf_op jit(solution)/shard_map/ppermute | solution.py:153
  45.5 3.1 %collective-permute-start.39 = (f32[4,80]{1,0:T(4,128)S(1)}, f32[4,80]{1,0:T(4,128)S(1)}, u32[]{:S(2)}, u32[]{:S(2)}) collective-permute-start(f32[4,80]{1,0:T(4,128)S(1)} %get-tuple-element.739), channel_id=1, source_target_pairs={{0,3},{1,2},{2,1},{3,0},{4,7},{5,6},{6,5},{7,4},{8,11},{9,10},{10,... | collective-permute-start | bytes 3848 | tf_op jit(solution)/shard_map/ppermute | solution.py:153
  46.1 3.6 %collective-permute-start.40 = (f32[4,80]{1,0:T(4,128)S(1)}, f32[4,80]{1,0:T(4,128)S(1)}, u32[]{:S(2)}, u32[]{:S(2)}) collective-permute-start(f32[4,80]{1,0:T(4,128)S(1)} %get-tuple-element.740), channel_id=1, source_target_pairs={{0,2},{1,3},{2,0},{3,1},{4,6},{5,7},{6,4},{7,5},{8,10},{9,11},{10,... | collective-permute-start | bytes 3848 | tf_op jit(solution)/shard_map/ppermute | solution.py:153
  47.3 2.5 %collective-permute-start.41 = (f32[4,80]{1,0:T(4,128)S(1)}, f32[4,80]{1,0:T(4,128)S(1)}, u32[]{:S(2)}, u32[]{:S(2)}) collective-permute-start(f32[4,80]{1,0:T(4,128)S(1)} %get-tuple-element.741), channel_id=1, source_target_pairs={{0,1},{1,0},{2,3},{3,2},{4,5},{5,4},{6,7},{7,6},{8,9},{9,8},{10,11... | collective-permute-start | bytes 3848 | tf_op jit(solution)/shard_map/ppermute | solution.py:153
  49.9 3.7 %collective-permute-start.42 = (f32[16,80]{1,0:T(8,128)S(1)}, f32[16,80]{1,0:T(8,128)S(1)}, u32[]{:S(2)}, u32[]{:S(2)}) collective-permute-start(f32[16,80]{1,0:T(8,128)S(1)} %shard_map.100.refs_0_.refs_4_.refs_6_), channel_id=1, source_target_pairs={{0,4},{4,0},{8,12},{12,8},{16,20},{20,16},{24,28},{28,24},{1,5},{5... | collective-permute-start | bytes 15368 | tf_op jit(solution)/shard_map/ppermute | solution.py:527
  49.9 3.6 %collective-permute-start.43 = (f32[16,80]{1,0:T(8,128)S(1)}, f32[16,80]{1,0:T(8,128)S(1)}, u32[]{:S(2)}, u32[]{:S(2)}) collective-permute-start(f32[16,80]{1,0:T(8,128)S(1)} %shard_map.100.refs_0_.refs_4_.refs_6_), channel_id=1, source_target_pairs={{0,1},{1,0},{2,3},{3,2},{4,5},{5,4},{6,7},{7,6},{8,9},{9,8},{10,11... | collective-permute-start | bytes 15368 | tf_op jit(solution)/shard_map/ppermute | solution.py:527
  49.9 6.4 %collective-permute-start.44 = (f32[16,80]{1,0:T(8,128)S(1)}, f32[16,80]{1,0:T(8,128)S(1)}, u32[]{:S(2)}, u32[]{:S(2)}) collective-permute-start(f32[16,80]{1,0:T(8,128)S(1)} %shard_map.100.refs_0_.refs_4_.refs_6_), channel_id=1, source_target_pairs={{0,28},{4,8},{8,4},{12,16},{16,12},{20,24},{24,20},{28,0},{1,29},{... | collective-permute-start | bytes 15368 | tf_op jit(solution)/shard_map/ppermute | solution.py:526
  52.5 3.8 %collective-permute-start.45 = (f32[16,80]{1,0:T(8,128)S(1)}, f32[16,80]{1,0:T(8,128)S(1)}, u32[]{:S(2)}, u32[]{:S(2)}) collective-permute-start(f32[16,80]{1,0:T(8,128)S(1)} %shard_map.100.refs_0_.refs_4_.refs_6_), channel_id=1, source_target_pairs={{0,3},{1,2},{2,1},{3,0},{4,7},{5,6},{6,5},{7,4},{8,11},{9,10},{10,... | collective-permute-start | bytes 15368 | tf_op jit(solution)/shard_map/ppermute | solution.py:528
  (3 other events, 68.5 us)

commit v8 on v7

--- a/solution.py
+++ b/solution.py
@@ -181,24 +181,63 @@
     choose_ref[...] = choose
 
 
-def square_kernel(length, low, upp, piv, _, low_out, upp_out, piv_out, low_scr, upp_scr, piv_scr, sems):
-    nrows, width = low.shape[0], low_out.shape[1]
+def to_squares(src, dst):
+    nrows, width = src.shape[0], dst.shape[1]
     chunk = math.lcm(width, 128)
-    work = ((low, low_scr, low_out), (piv, piv_scr, piv_out), (upp, upp_scr, upp_out))
-    fetches = [pltpu.make_async_copy(src, scr, sems.at[n]) for n, (src, scr, _) in enumerate(work)]
-    for fetch in fetches:
-        fetch.start()
-    for fetch, (src, scr, dst) in zip(fetches, work):
+    for c in range(width * width // chunk):
+        piece = src[:, c * chunk : (c + 1) * chunk]
+        for r in range(chunk // width):
+            a = c * (chunk // width) + r
+            dst[pl.ds(a, nrows, stride=width), :] = piece[:, r * width : (r + 1) * width]
+
+
+def turn_some(squares, length, parity):
+    width = squares.shape[1]
+    for at in range(squares.shape[0] // width):
+        if at % length % 2 == parity and at % length:
+            here = slice(at * width, (at + 1) * width)
+            squares[here, :] = squares[here, :].T
+
+
+def first_squares_kernel(length, low, piv, upp, _, low_out, piv_out, fold_out, low_scr, piv_scr, upp_scr, upp_sq, sems):
+    width = low_out.shape[1]
+    fetches = []
+    for n, (src, scr) in enumerate(((low, low_scr), (piv, piv_scr), (upp, upp_scr))):
+        fetches.append(pltpu.make_async_copy(src, scr, sems.at[n]))
+        fetches[-1].start()
+    for fetch, scr, dst in zip(fetches, (low_scr, piv_scr, upp_scr), (low_out, piv_out, upp_sq)):
         fetch.wait()
-        for c in range(width * width // chunk):
-            piece = scr[:, c * chunk : (c + 1) * chunk]
-            for r in range(chunk // width):
-                a = c * (chunk // width) + r
-                dst[pl.ds(a, nrows, stride=width), :] = piece[:, r * width : (r + 1) * width]
-        for at in range(nrows):
-            here = slice(at * width, (at + 1) * width)
-            if src is piv or (src is low and at % length % 2 == 0 and at % length):
-                dst[here, :] = dst[here, :].T
+        to_squares(scr, dst)
+    for at in range(low.shape[0]):
+        here = slice(at * width, (at + 1) * width)
+        if at % length == length - 1:
+            fold_out[here, :] = jnp.zeros((width, width), F32)
+            continue
+        (ph, pl_), (uh, ul) = [
+            (x.astype(BF16), (x - x.astype(BF16).astype(F32)).astype(BF16)) for x in (piv_out[here, :], upp_sq[here, :])
+        ]
+        fold = sum(jnp.dot(x, y, preferred_element_type=F32) for x, y in ((pl_, uh), (ph, ul), (ph, uh)))
+        fold_out[here, :] = fold.T if at % length % 2 else fold
+    turn_some(low_out, length, 0)
+    turn_some(piv_out, length, 1)
+
+
+def next_squares_kernel(length, low, piv, fold, _, low_out, piv_out, fold_out, low_scr, piv_scr, sems):
+    fetches = []
+    for n, (src, scr) in enumerate(((low, low_scr), (piv, piv_scr), (fold, fold_out))):
+        fetches.append(pltpu.make_async_copy(src, scr, sems.at[n]))
+        fetches[-1].start()
+    for fetch, scr, dst, parity in zip(fetches, (low_scr, piv_scr), (low_out, piv_out), (0, 1)):
+        fetch.wait()
+        to_squares(scr, dst)
+        turn_some(dst, length, parity)
+    fetches[2].wait()
+
+
+def store_kernel(x, _, out, sem):
+    copy = pltpu.make_async_copy(x, out, sem)
+    copy.start()
+    copy.wait()
 
 
 def parities():
@@ -232,7 +271,7 @@
 
 
 def line_kernel(nplane, nlines, *refs):
-    msgs, (low, upp, piv_t), outs, (r_scr, z_scr) = refs[:nplane], refs[nplane:-nplane-2], refs[-nplane-2:-2], refs[-2:]
+    msgs, (low, piv, fold), outs, (r_scr, z_scr) = refs[:nplane], refs[nplane:-nplane-2], refs[-nplane-2:-2], refs[-2:]
     _, length, width = r_scr.shape
     me = lax.axis_index("plane")
     for k, msg in zip(far_first(nplane), msgs):
@@ -246,7 +285,7 @@
         return jnp.sum(jnp.where(eye, row, 0.0), axis=1, keepdims=True)
 
     rows = [[r_scr[m, pl.ds(j, 1), :] for m in range(nlines)] for j in range(length)]
-    y_cols = [[None] * nlines for _ in range(length)]
+    scaled = [[None] * nlines for _ in range(length)]
     carry = [None] * nlines
     for j in range(length):
         for m in range(nlines):
@@ -257,16 +296,17 @@
                 carry[m] = column(rows[j][m]) - jnp.sum(low[at] * carry[m], axis=1, keepdims=True)
             else:
                 carry[m] = rows[j][m] - jnp.sum(low[at] * carry[m], axis=0, keepdims=True)
-            y_cols[j][m] = carry[m] if j % 2 else column(carry[m])
+            scaled[j][m] = jnp.sum(piv[at] * carry[m], axis=0 if j % 2 else 1, keepdims=True)
     after = [None] * nlines
     for j in reversed(range(length)):
         for m in range(nlines):
             at = m * length + j
-            inner = y_cols[j][m]
+            value = scaled[j][m]
             if j < length - 1:
-                inner = inner - jnp.sum(upp[at] * after[m], axis=1, keepdims=True)
-            after[m] = jnp.sum(piv_t[at] * inner, axis=0, keepdims=True)
-            z_scr[m, pl.ds(j, 1), :] = after[m]
+                value = value - jnp.sum(fold[at] * after[m], axis=0 if j % 2 else 1, keepdims=True)
+            after[m] = value
+            row = value if j % 2 else jnp.sum(jnp.where(eye, value, 0.0), axis=0, keepdims=True)
+            z_scr[m, pl.ds(j, 1), :] = row
     for k in range(nplane):
         to, _ = partner(me, k, nplane)
         for m in range(nlines):
@@ -493,24 +533,44 @@
     zs = []
     picks = None
     for step in range(ITERS):
-        factors = call(
-            functools.partial(square_kernel, length),
-            [line_lower, line_upper, pivot_inv, us[-1]],
-            [(nfaces * width, width)] * 3,
-            [pl.ANY] * 4,
-            [pltpu.VMEM((nfaces, area), F32)] * 3 + [pltpu.SemaphoreType.DMA((3,))],
-            flops=nfaces * area,
-        )
-        factors = [x.reshape(nfaces, width, width) for x in factors]
+        flat = pltpu.VMEM((nfaces, area), F32)
+        squares = [(nfaces * width, width)] * 3
+        if step == 0:
+            factors = call(
+                functools.partial(first_squares_kernel, length),
+                [line_lower, pivot_inv, line_upper, us[-1]],
+                squares,
+                [pl.ANY] * 4,
+                [flat] * 3 + [pltpu.VMEM(squares[0], F32), pltpu.SemaphoreType.DMA((3,))],
+                flops=nfaces * area * width,
+            )
+        else:
+            factors = call(
+                functools.partial(next_squares_kernel, length),
+                [line_lower, pivot_inv, fold, us[-1]],
+                squares,
+                [pl.ANY] * 4,
+                [flat] * 2 + [pltpu.SemaphoreType.DMA((3,))],
+                flops=nfaces * area,
+            )
+        shaped = [x.reshape(nfaces, width, width) for x in factors]
         got = [exchange(send[k], "plane", k) if k else send[0] for k in far_first(nplane)]
         solved = call(
             functools.partial(line_kernel, nplane, owned),
-            [*got, *factors],
+            [*got, *shaped],
             [(per, width)] * nplane,
             scratch=[pltpu.VMEM((owned, length, width), F32)] * 2,
             flops=6 * nfaces * area,
         )
         if step == 0:
+            fold = pl.pallas_call(
+                store_kernel,
+                out_shape=pltpu.HBM(squares[0], F32),
+                in_specs=[pl.BlockSpec(memory_space=pl.ANY)] * 2,
+                out_specs=pl.BlockSpec(memory_space=pl.ANY),
+                scratch_shapes=[pltpu.SemaphoreType.DMA],
+                cost_estimate=pl.CostEstimate(flops=0, bytes_accessed=4 * nfaces * area, transcendentals=0),
+            )(pltpu.with_memory_space_constraint(factors[2], pltpu.VMEM), solved[0])
             picks = call(
                 functools.partial(pick_kernel, nspan, nplane),
                 [lax.optimization_barrier((columns, solved[0]))[0]],
@@ -519,7 +579,7 @@
                 kind=BF16,
             )
         pieces = [exchange(solved[k], "plane", k) if k else solved[0] for k in far_first(nplane)]
-        args = [choose, *pieces, *(picks if step == 0 else ())]
+        args = [choose, *pieces, *((*picks, fold) if step == 0 else ())]
         spaces = [pltpu.VMEM] * (nplane + 1) + [pl.ANY] * (len(args) - nplane - 1)
         (mine,) = call(functools.partial(faces_kernel, nplane), args, [shape], spaces)
         zs.append(mine)

time: 69.1 us -> 69.9 us (1.012)
  local copies, waits for them, and re-layouts: 0.03 us -> 2.39 us
  Pallas kernels: 23 us -> 22.1 us
    unnamed x10 -> x20, local copies, waits for them, and re-layouts: 0.02 us -> 2.38 us
    pallas_call x18, Pallas kernels: 23 us -> 21.2 us  [call(): pl.pallas_call(kernel, out_shape=[pltpu.VMEM(shape, kind) if pinned else...]
    pallas_call x0 -> x1, Pallas kernels: none -> 0.87 us  [on_device(): pl.pallas_call(store_kernel, out_shape=pltpu.HBM(squares[0], F32), in_spe...]
where the time goes in v8:
time: 69.9 us; the launch traced here: 69.6 us
  starting transfers between devices  25 us (36%)
  Pallas kernels  22.1 us (32%)
  blocking collectives  10.2 us (15%)
  waiting for transfers between devices  8.62 us (12%)
  local copies, waits for them, and re-layouts  2.39 us (3%)
  between operations  1.09 us (2%)
    pallas_call x18, Pallas kernels, call(): pl.pallas_call(kernel, out_shape=[pltpu.VMEM(shape, kind) if pinned else...  21.2 us
    ppermute x18, starting transfers between devices, exchange(): lax.ppermute(x, axis, [(i, partner(i, k, size)[0]) for i in range(size)])  12.7 us
    all_to_all x1, blocking collectives, add_up(): lax.all_to_all(rows, ('span', 'plane'), split_axis=0, concat_axis=0, tile...  10.2 us
    ppermute x3, starting transfers between devices, on_device(): other = lax.ppermute(mine, 'span', span_others)  9.01 us
    ppermute x18, waiting for transfers between devices, exchange(): lax.ppermute(x, axis, [(i, partner(i, k, size)[0]) for i in range(size)])  7.27 us
    unnamed x20, local copies, waits for them, and re-layouts  2.38 us
    ppermute x3, starting transfers between devices, on_device(): far = [other, lax.ppermute(mine, 'plane', plane_others)]  1.67 us
    ppermute x3, starting transfers between devices, on_device(): lax.ppermute(mine, 'span', span_pairs)  1.62 us
  transfers between devices with their start and end apart: 30, of which 13 were waited for; matrix products, arithmetic and copies ran while one was open for 0% of the time, Pallas kernels for 21%

profile of v8, /device:TPU:0, one launch (start us, length us, event | category | flops | bytes accessed | tf_op | source)
XLA Modules:
  0.0 69.6 jit_solution(12272907099564121179)
XLA Ops:
  1.5 2.5 %collective-permute-start.16 = (f32[4,80]{1,0:T(4,128)S(1)}, f32[4,80]{1,0:T(4,128)S(1)}, u32[]{:S(2)}, u32[]{:S(2)}) collective-permute-start(f32[4,80]{1,0:T(4,128)S(1)} %get-tuple-element.699), channel_id=1, source_target_pairs={{0,3},{1,2},{2,1},{3,0},{4,7},{5,6},{6,5},{7,4},{8,11},{9,10},{10,... | collective-permute-start | bytes 3848 | tf_op jit(solution)/shard_map/ppermute | solution.py:153
  4.7 2.5 %shard_map.87 = (f32[1280,80]{1,0:T(8,128)S(1)}, f32[1280,80]{1,0:T(8,128)S(1)}, f32[1280,80]{1,0:T(8,128)S(1)}) custom-call(f32[16,6400]{1,0:T(8,128)} %low.5, f32[16,6400]{1,0:T(8,128)} %piv.5, f32[16,6400]{1,0:T(8,128)} %upp.1, f32[16,80]{1,0:T(8,128)S(1)} %get-tuple-element.703._.refs_9_.refs_0_), custom_call_target="tpu_custom_call" | custom-call | flops 8192000 | bytes 1233920 | tf_op jit(solution)/shard_map/pallas_call | solution.py:490
  7.6 0.9 %shard_map.88 = (f32[4,80]{1,0:T(4,128)S(1)}, f32[4,80]{1,0:T(4,128)S(1)}, f32[4,80]{1,0:T(4,128)S(1)}, f32[4,80]{1,0:T(4,128)S(1)}) custom-call(f32[4,80]{1,0:T(4,128)S(1)} %collective-permute-done.16.refs_0_, f32[4,80]{1,0:T(4,128)S(1)} %collective-permute-done.17.refs_1_, f32[4,80]{1,0:T(4,128)S(1)} %collective-permute-done.18.refs_2_, ...), custom_call_target="tpu_custom_call" | custom-call | flops 614400 | bytes 1233920 | tf_op jit(solution)/shard_map/pallas_call | solution.py:490
  9.1 1.1 %collective-permute-start.19 = (f32[4,80]{1,0:T(4,128)S(1)}, f32[4,80]{1,0:T(4,128)S(1)}, u32[]{:S(2)}, u32[]{:S(2)}) collective-permute-start(f32[4,80]{1,0:T(4,128)S(1)} %get-tuple-element.711), channel_id=1, source_target_pairs={{0,3},{1,2},{2,1},{3,0},{4,7},{5,6},{6,5},{7,4},{8,11},{9,10},{10,... | collective-permute-start | bytes 3848 | tf_op jit(solution)/shard_map/ppermute | solution.py:153
  10.9 0.9 %shard_map.90.refs_6_.fold = f32[1280,80]{1,0:T(8,128)} custom-call(f32[1280,80]{1,0:T(8,128)S(1)} %get-tuple-element.706.x, f32[4,80]{1,0:T(4,128)} %copy-done.2), custom_call_target="tpu_custom_call" | custom-call | bytes 409600 | tf_op jit(solution)/shard_map/pallas_call | solution.py:566
  11.8 0.8 %shard_map.89 = (bf16[48,96]{1,0:T(8,128)(2,1)S(1)}, bf16[128,160]{1,0:T(8,128)(2,1)S(1)}) custom-call(s32[11,16]{1,0:T(8,128)} %columns_ref), custom_call_target="tpu_custom_call" | custom-call | bytes 704 | tf_op jit(solution)/shard_map/pallas_call | solution.py:490
  12.7 1.1 %collective-permute-done.20.refs_1_ = f32[4,80]{1,0:T(4,128)S(1)} collective-permute-done((f32[4,80]{1,0:T(4,128)S(1)}, f32[4,80]{1,0:T(4,128)S(1)}, u32[]{:S(2)}, u32[]{:S(2)}) %collective-permute-start.20) | collective-permute-done | bytes 1312 | tf_op jit(solution)/shard_map/ppermute | solution.py:153
  13.8 1.1 %copy-done = f32[1280,80]{1,0:T(8,128)S(1)} copy-done((f32[1280,80]{1,0:T(8,128)S(1)}, f32[1280,80]{1,0:T(8,128)}, u32[]{:S(2)}) %copy-start) | copy-done | bytes 409624
  15.7 1.5 %collective-permute-start.22 = (f32[16,80]{1,0:T(8,128)S(1)}, f32[16,80]{1,0:T(8,128)S(1)}, u32[]{:S(2)}, u32[]{:S(2)}) collective-permute-start(f32[16,80]{1,0:T(8,128)S(1)} %shard_map.91.refs_0_.refs_4_), channel_id=1, source_target_pairs={{0,4},{4,0},{8,12},{12,8},{16,20},{20,16},{24,28},{28,24},{1,5},{5... | collective-permute-start | bytes 15368 | tf_op jit(solution)/shard_map/ppermute | solution.py:587
  17.2 3.6 %collective-permute-start.24 = (f32[16,80]{1,0:T(8,128)S(1)}, f32[16,80]{1,0:T(8,128)S(1)}, u32[]{:S(2)}, u32[]{:S(2)}) collective-permute-start(f32[16,80]{1,0:T(8,128)S(1)} %shard_map.91.refs_0_.refs_4_), channel_id=1, source_target_pairs={{0,28},{4,8},{8,4},{12,16},{16,12},{20,24},{24,20},{28,0},{1,29},{... | collective-permute-start | bytes 15368 | tf_op jit(solution)/shard_map/ppermute | solution.py:586
  21.2 2.5 %shard_map.92 = (f32[16,80]{1,0:T(8,128)S(1)}, f32[16,51200]{1,0:T(8,128)S(1)}) custom-call(f32[16,70400]{1,0:T(8,128)} %blocks.5, bf16[48,96]{1,0:T(8,128)(2,1)S(1)} %get-tuple-element.709.refs_4_.pick, f32[16,80]{1,0:T(8,128)S(1)} %shard_map.91.refs_0_.refs_4_, f32[16,80]{1,0:T(8,128)S(1)} %collective-permute-done.22.refs_1_.refs_5_, ...), custom_call_target="tpu_custom_call" | custom-call | flops 614400 | bytes 4530176 | tf_op jit(solution)/shard_map/pallas_call | solution.py:490
  23.8 0.8 %shard_map.93 = (f32[16,80]{1,0:T(8,128)S(1)}, f32[4,80]{1,0:T(4,128)S(1)}, f32[4,80]{1,0:T(4,128)S(1)}, f32[4,80]{1,0:T(4,128)S(1)}, f32[4,80]{1,0:T(4,128)S(1)}) custom-call(s32[1,16]{1,0:T(1,128)S(1)} %copy-done.11, f32[16,51200]{1,0:T(8,128)S(1)} %get-tuple-element.715.refs_1_, bf16[128,160]{1,0:T(8,128)(2,1)S(1)} %get-tuple-element.714.refs_5_.refs_2_, ...), custom_call_target="tpu_custom_call" | custom-call | flops 2252800 | bytes 3353664 | tf_op jit(solution)/shard_map/pallas_call | solution.py:490
  24.7 1.2 %collective-permute-start.26 = (f32[4,80]{1,0:T(4,128)S(1)}, f32[4,80]{1,0:T(4,128)S(1)}, u32[]{:S(2)}, u32[]{:S(2)}) collective-permute-start(f32[4,80]{1,0:T(4,128)S(1)} %get-tuple-element.717), channel_id=1, source_target_pairs={{0,3},{1,2},{2,1},{3,0},{4,7},{5,6},{6,5},{7,4},{8,11},{9,10},{10,... | collective-permute-start | bytes 3848 | tf_op jit(solution)/shard_map/ppermute | solution.py:153
  26.6 1.5 %shard_map.94 = (f32[1280,80]{1,0:T(8,128)S(1)}, f32[1280,80]{1,0:T(8,128)S(1)}, f32[1280,80]{1,0:T(8,128)S(1)}) custom-call(f32[16,6400]{1,0:T(8,128)S(1)} %copy-done.4, f32[16,6400]{1,0:T(8,128)S(1)} %copy-done.5, f32[1280,80]{1,0:T(8,128)S(1)} %copy-done.1, f32[16,80]{1,0:T(8,128)S(1)} %get-tuple-element.721._.refs_9_.refs_10_.refs_1_), custom_call_target="tpu_custom_call" | custom-call | flops 102400 | bytes 1233920 | tf_op jit(solution)/shard_map/pallas_call | solution.py:490
  28.2 1.3 %collective-permute-done.27.refs_1_ = f32[4,80]{1,0:T(4,128)S(1)} collective-permute-done((f32[4,80]{1,0:T(4,128)S(1)}, f32[4,80]{1,0:T(4,128)S(1)}, u32[]{:S(2)}, u32[]{:S(2)}) %collective-permute-start.27) | collective-permute-done | bytes 1312 | tf_op jit(solution)/shard_map/ppermute | solution.py:153
  29.5 0.9 %shard_map.95 = (f32[4,80]{1,0:T(4,128)S(1)}, f32[4,80]{1,0:T(4,128)S(1)}, f32[4,80]{1,0:T(4,128)S(1)}, f32[4,80]{1,0:T(4,128)S(1)}) custom-call(f32[4,80]{1,0:T(4,128)S(1)} %collective-permute-done.26.refs_0_, f32[4,80]{1,0:T(4,128)S(1)} %collective-permute-done.27.refs_1_, f32[4,80]{1,0:T(4,128)S(1)} %collective-permute-done.28.refs_2_, ...), custom_call_target="tpu_custom_call" | custom-call | flops 614400 | bytes 1233920 | tf_op jit(solution)/shard_map/pallas_call | solution.py:490
  31.3 1.1 %collective-permute-start.31 = (f32[4,80]{1,0:T(4,128)S(1)}, f32[4,80]{1,0:T(4,128)S(1)}, u32[]{:S(2)}, u32[]{:S(2)}) collective-permute-start(f32[4,80]{1,0:T(4,128)S(1)} %get-tuple-element.727), channel_id=1, source_target_pairs={{0,1},{1,0},{2,3},{3,2},{4,5},{5,4},{6,7},{7,6},{8,9},{9,8},{10,11... | collective-permute-start | bytes 3848 | tf_op jit(solution)/shard_map/ppermute | solution.py:153
  32.3 1.1 %collective-permute-done.29.refs_0_ = f32[4,80]{1,0:T(4,128)S(1)} collective-permute-done((f32[4,80]{1,0:T(4,128)S(1)}, f32[4,80]{1,0:T(4,128)S(1)}, u32[]{:S(2)}, u32[]{:S(2)}) %collective-permute-start.29) | collective-permute-done | bytes 1312 | tf_op jit(solution)/shard_map/ppermute | solution.py:153
  34.4 2.7 %collective-permute-start.34 = (f32[16,80]{1,0:T(8,128)S(1)}, f32[16,80]{1,0:T(8,128)S(1)}, u32[]{:S(2)}, u32[]{:S(2)}) collective-permute-start(f32[16,80]{1,0:T(8,128)S(1)} %shard_map.96.refs_0_.refs_4_.refs_5_), channel_id=1, source_target_pairs={{0,28},{4,8},{8,4},{12,16},{16,12},{20,24},{24,20},{28,0},{1,29},{... | collective-permute-start | bytes 15368 | tf_op jit(solution)/shard_map/ppermute | solution.py:586
  38.0 2.5 %shard_map.97 = (f32[16,80]{1,0:T(8,128)S(1)}, f32[16,51200]{1,0:T(8,128)S(1)}) custom-call(f32[16,70400]{1,0:T(8,128)} %blocks.5, bf16[48,96]{1,0:T(8,128)(2,1)S(1)} %get-tuple-element.709.refs_4_.pick, f32[16,80]{1,0:T(8,128)S(1)} %shard_map.96.refs_0_.refs_4_.refs_5_, f32[16,80]{1,0:T(8,128)S(1)} %collective-permute-done.32.refs_1_.refs_5_, ...), custom_call_target="tpu_custom_call" | custom-call | flops 614400 | bytes 4530176 | tf_op jit(solution)/shard_map/pallas_call | solution.py:490
  40.8 0.9 %shard_map.98 = (f32[16,80]{1,0:T(8,128)S(1)}, f32[4,80]{1,0:T(4,128)S(1)}, f32[4,80]{1,0:T(4,128)S(1)}, f32[4,80]{1,0:T(4,128)S(1)}, f32[4,80]{1,0:T(4,128)S(1)}) custom-call(s32[1,16]{1,0:T(1,128)S(1)} %copy-done.11, f32[16,51200]{1,0:T(8,128)S(1)} %get-tuple-element.729.refs_1_, bf16[128,160]{1,0:T(8,128)(2,1)S(1)} %get-tuple-element.714.refs_5_.refs_2_, ...), custom_call_target="tpu_custom_call" | custom-call | flops 2252800 | bytes 3353664 | tf_op jit(solution)/shard_map/pallas_call | solution.py:490
  42.3 0.9 %collective-permute-start.37 = (f32[4,80]{1,0:T(4,128)S(1)}, f32[4,80]{1,0:T(4,128)S(1)}, u32[]{:S(2)}, u32[]{:S(2)}) collective-permute-start(f32[4,80]{1,0:T(4,128)S(1)} %get-tuple-element.732), channel_id=1, source_target_pairs={{0,2},{1,3},{2,0},{3,1},{4,6},{5,7},{6,4},{7,5},{8,10},{9,11},{10,... | collective-permute-start | bytes 3848 | tf_op jit(solution)/shard_map/ppermute | solution.py:153
  43.6 1.5 %shard_map.99 = (f32[1280,80]{1,0:T(8,128)S(1)}, f32[1280,80]{1,0:T(8,128)S(1)}, f32[1280,80]{1,0:T(8,128)S(1)}) custom-call(f32[16,6400]{1,0:T(8,128)S(1)} %copy-done.4, f32[16,6400]{1,0:T(8,128)S(1)} %copy-done.5, f32[1280,80]{1,0:T(8,128)S(1)} %copy-done.1, f32[16,80]{1,0:T(8,128)S(1)} %get-tuple-element.735._.refs_11_.refs_2_), custom_call_target="tpu_custom_call" | custom-call | flops 102400 | bytes 1233920 | tf_op jit(solution)/shard_map/pallas_call | solution.py:490
  45.9 0.9 %shard_map.100 = (f32[4,80]{1,0:T(4,128)S(1)}, f32[4,80]{1,0:T(4,128)S(1)}, f32[4,80]{1,0:T(4,128)S(1)}, f32[4,80]{1,0:T(4,128)S(1)}) custom-call(f32[4,80]{1,0:T(4,128)S(1)} %collective-permute-done.36.refs_0_, f32[4,80]{1,0:T(4,128)S(1)} %collective-permute-done.37.refs_1_, f32[4,80]{1,0:T(4,128)S(1)} %collective-permute-done.38.refs_2_, ...), custom_call_target="tpu_custom_call" | custom-call | flops 614400 | bytes 1233920 | tf_op jit(solution)/shard_map/pallas_call | solution.py:490
  47.0 0.9 %collective-permute-start.40 = (f32[4,80]{1,0:T(4,128)S(1)}, f32[4,80]{1,0:T(4,128)S(1)}, u32[]{:S(2)}, u32[]{:S(2)}) collective-permute-start(f32[4,80]{1,0:T(4,128)S(1)} %get-tuple-element.740), channel_id=1, source_target_pairs={{0,2},{1,3},{2,0},{3,1},{4,6},{5,7},{6,4},{7,5},{8,10},{9,11},{10,... | collective-permute-start | bytes 3848 | tf_op jit(solution)/shard_map/ppermute | solution.py:153
  47.9 0.9 %collective-permute-start.41 = (f32[4,80]{1,0:T(4,128)S(1)}, f32[4,80]{1,0:T(4,128)S(1)}, u32[]{:S(2)}, u32[]{:S(2)}) collective-permute-start(f32[4,80]{1,0:T(4,128)S(1)} %get-tuple-element.741), channel_id=1, source_target_pairs={{0,1},{1,0},{2,3},{3,2},{4,5},{5,4},{6,7},{7,6},{8,9},{9,8},{10,11... | collective-permute-start | bytes 3848 | tf_op jit(solution)/shard_map/ppermute | solution.py:153
  48.7 1.1 %collective-permute-done.39.refs_0_ = f32[4,80]{1,0:T(4,128)S(1)} collective-permute-done((f32[4,80]{1,0:T(4,128)S(1)}, f32[4,80]{1,0:T(4,128)S(1)}, u32[]{:S(2)}, u32[]{:S(2)}) %collective-permute-start.39) | collective-permute-done | bytes 1312 | tf_op jit(solution)/shard_map/ppermute | solution.py:153
  50.8 2.7 %collective-permute-start.44 = (f32[16,80]{1,0:T(8,128)S(1)}, f32[16,80]{1,0:T(8,128)S(1)}, u32[]{:S(2)}, u32[]{:S(2)}) collective-permute-start(f32[16,80]{1,0:T(8,128)S(1)} %shard_map.101.refs_0_.refs_4_.refs_6_), channel_id=1, source_target_pairs={{0,28},{4,8},{8,4},{12,16},{16,12},{20,24},{24,20},{28,0},{1,29},{... | collective-permute-start | bytes 15368 | tf_op jit(solution)/shard_map/ppermute | solution.py:586
  54.4 2.5 %shard_map.102 = (f32[16,80]{1,0:T(8,128)S(1)}, f32[16,51200]{1,0:T(8,128)S(1)}) custom-call(f32[16,70400]{1,0:T(8,128)} %blocks.5, bf16[48,96]{1,0:T(8,128)(2,1)S(1)} %get-tuple-element.709.refs_4_.pick, f32[16,80]{1,0:T(8,128)S(1)} %shard_map.101.refs_0_.refs_4_.refs_6_, f32[16,80]{1,0:T(8,128)S(1)} %collective-permute-done.42.refs_1_.refs_5_, ...), custom_call_target="tpu_custom_call" | custom-call | flops 614400 | bytes 4530176 | tf_op jit(solution)/shard_map/pallas_call | solution.py:490
  57.2 0.9 %shard_map.103 = (f32[16,80]{1,0:T(8,128)S(1)}, f32[1,128]{1,0:T(1,128)S(1)}) custom-call(s32[1,16]{1,0:T(1,128)S(1)} %copy-done.11, f32[16,51200]{1,0:T(8,128)S(1)} %get-tuple-element.743.refs_1_, bf16[128,160]{1,0:T(8,128)(2,1)S(1)} %get-tuple-element.714.refs_5_.refs_2_, f32[16,80]{1,0:T(8,128)S(1)} %get-tuple-element.744.refs_3_, ...), custom_call_target="tpu_custom_call" | custom-call | flops 2252800 | bytes 3363904 | tf_op jit(solution)/shard_map/pallas_call | solution.py:490
  58.1 10.2 %all_to_all.112 = f32[32,1,128]{2,1,0:T(1,128)S(1)} all-to-all(f32[32,1,128]{2,1,0:T(1,128)S(1)} %broadcast_in_dim.83), channel_id=1, replica_groups=mesh['span'=8,'plane'=4] {'span','plane'}, dimensions={0} | all-to-all | bytes 32768 | tf_op jit(solution)/shard_map/all_to_all | solution.py:504
  68.3 0.8 %shard_map.104 = (f32[16,80]{1,0:T(8,128)}, f32[16,80]{1,0:T(8,128)}, f32[1,128]{1,0:T(1,128)S(1)}) custom-call(f32[32,128]{1,0:T(8,128)S(1)} %bitcast.558, f32[16,80]{1,0:T(8,128)S(1)} %get-tuple-element.703._.refs_9_.refs_0_, f32[16,80]{1,0:T(8,128)S(1)} %get-tuple-element.721._.refs_9_.refs_10_.refs_1_, ...), custom_call_target="tpu_custom_call" | custom-call | bytes 52224 | tf_op jit(solution)/shard_map/pallas_call | solution.py:490
  (70 shorter events, 12.6 us)
Async XLA Ops:
  1.5 5.7 %collective-permute-start.16 = (f32[4,80]{1,0:T(4,128)S(1)}, f32[4,80]{1,0:T(4,128)S(1)}, u32[]{:S(2)}, u32[]{:S(2)}) collective-permute-start(f32[4,80]{1,0:T(4,128)S(1)} %get-tuple-element.699), channel_id=1, source_target_pairs={{0,3},{1,2},{2,1},{3,0},{4,7},{5,6},{6,5},{7,4},{8,11},{9,10},{10,... | collective-permute-start | bytes 3848 | tf_op jit(solution)/shard_map/ppermute | solution.py:153
  4.0 3.6 %collective-permute-start.17 = (f32[4,80]{1,0:T(4,128)S(1)}, f32[4,80]{1,0:T(4,128)S(1)}, u32[]{:S(2)}, u32[]{:S(2)}) collective-permute-start(f32[4,80]{1,0:T(4,128)S(1)} %get-tuple-element.700), channel_id=1, source_target_pairs={{0,2},{1,3},{2,0},{3,1},{4,6},{5,7},{6,4},{7,5},{8,10},{9,11},{10,... | collective-permute-start | bytes 3848 | tf_op jit(solution)/shard_map/ppermute | solution.py:153
  4.6 2.9 %collective-permute-start.18 = (f32[4,80]{1,0:T(4,128)S(1)}, f32[4,80]{1,0:T(4,128)S(1)}, u32[]{:S(2)}, u32[]{:S(2)}) collective-permute-start(f32[4,80]{1,0:T(4,128)S(1)} %get-tuple-element.701), channel_id=1, source_target_pairs={{0,1},{1,0},{2,3},{3,2},{4,5},{5,4},{6,7},{7,6},{8,9},{9,8},{10,11... | collective-permute-start | bytes 3848 | tf_op jit(solution)/shard_map/ppermute | solution.py:153
  9.1 3.6 %collective-permute-start.19 = (f32[4,80]{1,0:T(4,128)S(1)}, f32[4,80]{1,0:T(4,128)S(1)}, u32[]{:S(2)}, u32[]{:S(2)}) collective-permute-start(f32[4,80]{1,0:T(4,128)S(1)} %get-tuple-element.711), channel_id=1, source_target_pairs={{0,3},{1,2},{2,1},{3,0},{4,7},{5,6},{6,5},{7,4},{8,11},{9,10},{10,... | collective-permute-start | bytes 3848 | tf_op jit(solution)/shard_map/ppermute | solution.py:153
  10.2 3.6 %collective-permute-start.20 = (f32[4,80]{1,0:T(4,128)S(1)}, f32[4,80]{1,0:T(4,128)S(1)}, u32[]{:S(2)}, u32[]{:S(2)}) collective-permute-start(f32[4,80]{1,0:T(4,128)S(1)} %get-tuple-element.712), channel_id=1, source_target_pairs={{0,2},{1,3},{2,0},{3,1},{4,6},{5,7},{6,4},{7,5},{8,10},{9,11},{10,... | collective-permute-start | bytes 3848 | tf_op jit(solution)/shard_map/ppermute | solution.py:153
  10.9 2.9 %collective-permute-start.21 = (f32[4,80]{1,0:T(4,128)S(1)}, f32[4,80]{1,0:T(4,128)S(1)}, u32[]{:S(2)}, u32[]{:S(2)}) collective-permute-start(f32[4,80]{1,0:T(4,128)S(1)} %get-tuple-element.713), channel_id=1, source_target_pairs={{0,1},{1,0},{2,3},{3,2},{4,5},{5,4},{6,7},{7,6},{8,9},{9,8},{10,11... | collective-permute-start | bytes 3848 | tf_op jit(solution)/shard_map/ppermute | solution.py:153
  15.7 5.6 %collective-permute-start.22 = (f32[16,80]{1,0:T(8,128)S(1)}, f32[16,80]{1,0:T(8,128)S(1)}, u32[]{:S(2)}, u32[]{:S(2)}) collective-permute-start(f32[16,80]{1,0:T(8,128)S(1)} %shard_map.91.refs_0_.refs_4_), channel_id=1, source_target_pairs={{0,4},{4,0},{8,12},{12,8},{16,20},{20,16},{24,28},{28,24},{1,5},{5... | collective-permute-start | bytes 15368 | tf_op jit(solution)/shard_map/ppermute | solution.py:587
  17.2 4.1 %collective-permute-start.23 = (f32[16,80]{1,0:T(8,128)S(1)}, f32[16,80]{1,0:T(8,128)S(1)}, u32[]{:S(2)}, u32[]{:S(2)}) collective-permute-start(f32[16,80]{1,0:T(8,128)S(1)} %shard_map.91.refs_0_.refs_4_), channel_id=1, source_target_pairs={{0,1},{1,0},{2,3},{3,2},{4,5},{5,4},{6,7},{7,6},{8,9},{9,8},{10,11... | collective-permute-start | bytes 15368 | tf_op jit(solution)/shard_map/ppermute | solution.py:587
  17.2 6.5 %collective-permute-start.24 = (f32[16,80]{1,0:T(8,128)S(1)}, f32[16,80]{1,0:T(8,128)S(1)}, u32[]{:S(2)}, u32[]{:S(2)}) collective-permute-start(f32[16,80]{1,0:T(8,128)S(1)} %shard_map.91.refs_0_.refs_4_), channel_id=1, source_target_pairs={{0,28},{4,8},{8,4},{12,16},{16,12},{20,24},{24,20},{28,0},{1,29},{... | collective-permute-start | bytes 15368 | tf_op jit(solution)/shard_map/ppermute | solution.py:586
  20.7 3.1 %collective-permute-start.25 = (f32[16,80]{1,0:T(8,128)S(1)}, f32[16,80]{1,0:T(8,128)S(1)}, u32[]{:S(2)}, u32[]{:S(2)}) collective-permute-start(f32[16,80]{1,0:T(8,128)S(1)} %shard_map.91.refs_0_.refs_4_), channel_id=1, source_target_pairs={{0,3},{1,2},{2,1},{3,0},{4,7},{5,6},{6,5},{7,4},{8,11},{9,10},{10,... | collective-permute-start | bytes 15368 | tf_op jit(solution)/shard_map/ppermute | solution.py:588
  24.7 3.5 %collective-permute-start.26 = (f32[4,80]{1,0:T(4,128)S(1)}, f32[4,80]{1,0:T(4,128)S(1)}, u32[]{:S(2)}, u32[]{:S(2)}) collective-permute-start(f32[4,80]{1,0:T(4,128)S(1)} %get-tuple-element.717), channel_id=1, source_target_pairs={{0,3},{1,2},{2,1},{3,0},{4,7},{5,6},{6,5},{7,4},{8,11},{9,10},{10,... | collective-permute-start | bytes 3848 | tf_op jit(solution)/shard_map/ppermute | solution.py:153
  25.9 3.6 %collective-permute-start.27 = (f32[4,80]{1,0:T(4,128)S(1)}, f32[4,80]{1,0:T(4,128)S(1)}, u32[]{:S(2)}, u32[]{:S(2)}) collective-permute-start(f32[4,80]{1,0:T(4,128)S(1)} %get-tuple-element.718), channel_id=1, source_target_pairs={{0,2},{1,3},{2,0},{3,1},{4,6},{5,7},{6,4},{7,5},{8,10},{9,11},{10,... | collective-permute-start | bytes 3848 | tf_op jit(solution)/shard_map/ppermute | solution.py:153
  26.6 2.9 %collective-permute-start.28 = (f32[4,80]{1,0:T(4,128)S(1)}, f32[4,80]{1,0:T(4,128)S(1)}, u32[]{:S(2)}, u32[]{:S(2)}) collective-permute-start(f32[4,80]{1,0:T(4,128)S(1)} %get-tuple-element.719), channel_id=1, source_target_pairs={{0,1},{1,0},{2,3},{3,2},{4,5},{5,4},{6,7},{7,6},{8,9},{9,8},{10,11... | collective-permute-start | bytes 3848 | tf_op jit(solution)/shard_map/ppermute | solution.py:153
  30.4 3.1 %collective-permute-start.29 = (f32[4,80]{1,0:T(4,128)S(1)}, f32[4,80]{1,0:T(4,128)S(1)}, u32[]{:S(2)}, u32[]{:S(2)}) collective-permute-start(f32[4,80]{1,0:T(4,128)S(1)} %get-tuple-element.725), channel_id=1, source_target_pairs={{0,3},{1,2},{2,1},{3,0},{4,7},{5,6},{6,5},{7,4},{8,11},{9,10},{10,... | collective-permute-start | bytes 3848 | tf_op jit(solution)/shard_map/ppermute | solution.py:153
  30.6 3.6 %collective-permute-start.30 = (f32[4,80]{1,0:T(4,128)S(1)}, f32[4,80]{1,0:T(4,128)S(1)}, u32[]{:S(2)}, u32[]{:S(2)}) collective-permute-start(f32[4,80]{1,0:T(4,128)S(1)} %get-tuple-element.726), channel_id=1, source_target_pairs={{0,2},{1,3},{2,0},{3,1},{4,6},{5,7},{6,4},{7,5},{8,10},{9,11},{10,... | collective-permute-start | bytes 3848 | tf_op jit(solution)/shard_map/ppermute | solution.py:153
  31.3 2.9 %collective-permute-start.31 = (f32[4,80]{1,0:T(4,128)S(1)}, f32[4,80]{1,0:T(4,128)S(1)}, u32[]{:S(2)}, u32[]{:S(2)}) collective-permute-start(f32[4,80]{1,0:T(4,128)S(1)} %get-tuple-element.727), channel_id=1, source_target_pairs={{0,1},{1,0},{2,3},{3,2},{4,5},{5,4},{6,7},{7,6},{8,9},{9,8},{10,11... | collective-permute-start | bytes 3848 | tf_op jit(solution)/shard_map/ppermute | solution.py:153
  34.3 3.7 %collective-permute-start.32 = (f32[16,80]{1,0:T(8,128)S(1)}, f32[16,80]{1,0:T(8,128)S(1)}, u32[]{:S(2)}, u32[]{:S(2)}) collective-permute-start(f32[16,80]{1,0:T(8,128)S(1)} %shard_map.96.refs_0_.refs_4_.refs_5_), channel_id=1, source_target_pairs={{0,4},{4,0},{8,12},{12,8},{16,20},{20,16},{24,28},{28,24},{1,5},{5... | collective-permute-start | bytes 15368 | tf_op jit(solution)/shard_map/ppermute | solution.py:587
  34.3 3.7 %collective-permute-start.33 = (f32[16,80]{1,0:T(8,128)S(1)}, f32[16,80]{1,0:T(8,128)S(1)}, u32[]{:S(2)}, u32[]{:S(2)}) collective-permute-start(f32[16,80]{1,0:T(8,128)S(1)} %shard_map.96.refs_0_.refs_4_.refs_5_), channel_id=1, source_target_pairs={{0,1},{1,0},{2,3},{3,2},{4,5},{5,4},{6,7},{7,6},{8,9},{9,8},{10,11... | collective-permute-start | bytes 15368 | tf_op jit(solution)/shard_map/ppermute | solution.py:587
  34.4 6.4 %collective-permute-start.34 = (f32[16,80]{1,0:T(8,128)S(1)}, f32[16,80]{1,0:T(8,128)S(1)}, u32[]{:S(2)}, u32[]{:S(2)}) collective-permute-start(f32[16,80]{1,0:T(8,128)S(1)} %shard_map.96.refs_0_.refs_4_.refs_5_), channel_id=1, source_target_pairs={{0,28},{4,8},{8,4},{12,16},{16,12},{20,24},{24,20},{28,0},{1,29},{... | collective-permute-start | bytes 15368 | tf_op jit(solution)/shard_map/ppermute | solution.py:586
  37.1 3.7 %collective-permute-start.35 = (f32[16,80]{1,0:T(8,128)S(1)}, f32[16,80]{1,0:T(8,128)S(1)}, u32[]{:S(2)}, u32[]{:S(2)}) collective-permute-start(f32[16,80]{1,0:T(8,128)S(1)} %shard_map.96.refs_0_.refs_4_.refs_5_), channel_id=1, source_target_pairs={{0,3},{1,2},{2,1},{3,0},{4,7},{5,6},{6,5},{7,4},{8,11},{9,10},{10,... | collective-permute-start | bytes 15368 | tf_op jit(solution)/shard_map/ppermute | solution.py:588
  40.8 28.4 %copy-start.8 = (f32[80,16]{0,1:T(8,128)S(1)}, f32[80,16]{0,1:T(8,128)}, u32[]{:S(2)}) copy-start(f32[80,16]{0,1:T(8,128)} %param.25) | copy-start | bytes 15364
  40.8 28.4 %copy-start.9 = (s32[11,16]{1,0:T(8,128)S(1)}, s32[11,16]{1,0:T(8,128)}, u32[]{:S(2)}) copy-start(s32[11,16]{1,0:T(8,128)} %columns_ref) | copy-start | bytes 2116
  41.7 3.5 %collective-permute-start.36 = (f32[4,80]{1,0:T(4,128)S(1)}, f32[4,80]{1,0:T(4,128)S(1)}, u32[]{:S(2)}, u32[]{:S(2)}) collective-permute-start(f32[4,80]{1,0:T(4,128)S(1)} %get-tuple-element.731), channel_id=1, source_target_pairs={{0,3},{1,2},{2,1},{3,0},{4,7},{5,6},{6,5},{7,4},{8,11},{9,10},{10,... | collective-permute-start | bytes 3848 | tf_op jit(solution)/shard_map/ppermute | solution.py:153
  42.3 3.6 %collective-permute-start.37 = (f32[4,80]{1,0:T(4,128)S(1)}, f32[4,80]{1,0:T(4,128)S(1)}, u32[]{:S(2)}, u32[]{:S(2)}) collective-permute-start(f32[4,80]{1,0:T(4,128)S(1)} %get-tuple-element.732), channel_id=1, source_target_pairs={{0,2},{1,3},{2,0},{3,1},{4,6},{5,7},{6,4},{7,5},{8,10},{9,11},{10,... | collective-permute-start | bytes 3848 | tf_op jit(solution)/shard_map/ppermute | solution.py:153
  43.2 2.7 %collective-permute-start.38 = (f32[4,80]{1,0:T(4,128)S(1)}, f32[4,80]{1,0:T(4,128)S(1)}, u32[]{:S(2)}, u32[]{:S(2)}) collective-permute-start(f32[4,80]{1,0:T(4,128)S(1)} %get-tuple-element.733), channel_id=1, source_target_pairs={{0,1},{1,0},{2,3},{3,2},{4,5},{5,4},{6,7},{7,6},{8,9},{9,8},{10,11... | collective-permute-start | bytes 3848 | tf_op jit(solution)/shard_map/ppermute | solution.py:153
  46.8 3.1 %collective-permute-start.39 = (f32[4,80]{1,0:T(4,128)S(1)}, f32[4,80]{1,0:T(4,128)S(1)}, u32[]{:S(2)}, u32[]{:S(2)}) collective-permute-start(f32[4,80]{1,0:T(4,128)S(1)} %get-tuple-element.739), channel_id=1, source_target_pairs={{0,3},{1,2},{2,1},{3,0},{4,7},{5,6},{6,5},{7,4},{8,11},{9,10},{10,... | collective-permute-start | bytes 3848 | tf_op jit(solution)/shard_map/ppermute | solution.py:153
  47.0 3.6 %collective-permute-start.40 = (f32[4,80]{1,0:T(4,128)S(1)}, f32[4,80]{1,0:T(4,128)S(1)}, u32[]{:S(2)}, u32[]{:S(2)}) collective-permute-start(f32[4,80]{1,0:T(4,128)S(1)} %get-tuple-element.740), channel_id=1, source_target_pairs={{0,2},{1,3},{2,0},{3,1},{4,6},{5,7},{6,4},{7,5},{8,10},{9,11},{10,... | collective-permute-start | bytes 3848 | tf_op jit(solution)/shard_map/ppermute | solution.py:153
  47.9 2.7 %collective-permute-start.41 = (f32[4,80]{1,0:T(4,128)S(1)}, f32[4,80]{1,0:T(4,128)S(1)}, u32[]{:S(2)}, u32[]{:S(2)}) collective-permute-start(f32[4,80]{1,0:T(4,128)S(1)} %get-tuple-element.741), channel_id=1, source_target_pairs={{0,1},{1,0},{2,3},{3,2},{4,5},{5,4},{6,7},{7,6},{8,9},{9,8},{10,11... | collective-permute-start | bytes 3848 | tf_op jit(solution)/shard_map/ppermute | solution.py:153
  50.7 3.7 %collective-permute-start.42 = (f32[16,80]{1,0:T(8,128)S(1)}, f32[16,80]{1,0:T(8,128)S(1)}, u32[]{:S(2)}, u32[]{:S(2)}) collective-permute-start(f32[16,80]{1,0:T(8,128)S(1)} %shard_map.101.refs_0_.refs_4_.refs_6_), channel_id=1, source_target_pairs={{0,4},{4,0},{8,12},{12,8},{16,20},{20,16},{24,28},{28,24},{1,5},{5... | collective-permute-start | bytes 15368 | tf_op jit(solution)/shard_map/ppermute | solution.py:587
  50.8 3.5 %collective-permute-start.43 = (f32[16,80]{1,0:T(8,128)S(1)}, f32[16,80]{1,0:T(8,128)S(1)}, u32[]{:S(2)}, u32[]{:S(2)}) collective-permute-start(f32[16,80]{1,0:T(8,128)S(1)} %shard_map.101.refs_0_.refs_4_.refs_6_), channel_id=1, source_target_pairs={{0,1},{1,0},{2,3},{3,2},{4,5},{5,4},{6,7},{7,6},{8,9},{9,8},{10,11... | collective-permute-start | bytes 15368 | tf_op jit(solution)/shard_map/ppermute | solution.py:587
  50.8 6.3 %collective-permute-start.44 = (f32[16,80]{1,0:T(8,128)S(1)}, f32[16,80]{1,0:T(8,128)S(1)}, u32[]{:S(2)}, u32[]{:S(2)}) collective-permute-start(f32[16,80]{1,0:T(8,128)S(1)} %shard_map.101.refs_0_.refs_4_.refs_6_), channel_id=1, source_target_pairs={{0,28},{4,8},{8,4},{12,16},{16,12},{20,24},{24,20},{28,0},{1,29},{... | collective-permute-start | bytes 15368 | tf_op jit(solution)/shard_map/ppermute | solution.py:586
  53.5 3.7 %collective-permute-start.45 = (f32[16,80]{1,0:T(8,128)S(1)}, f32[16,80]{1,0:T(8,128)S(1)}, u32[]{:S(2)}, u32[]{:S(2)}) collective-permute-start(f32[16,80]{1,0:T(8,128)S(1)} %shard_map.101.refs_0_.refs_4_.refs_6_), channel_id=1, source_target_pairs={{0,3},{1,2},{2,1},{3,0},{4,7},{5,6},{6,5},{7,4},{8,11},{9,10},{10,... | collective-permute-start | bytes 15368 | tf_op jit(solution)/shard_map/ppermute | solution.py:588
  (8 other events, 117.0 us)

commit v9 on v8

--- a/solution.py
+++ b/solution.py
@@ -234,12 +234,6 @@
     fetches[2].wait()
 
 
-def store_kernel(x, _, out, sem):
-    copy = pltpu.make_async_copy(x, out, sem)
-    copy.start()
-    copy.wait()
-
-
 def parities():
     return [1 if lax.axis_size(a) % 2 else lax.axis_index(a) % 2 for a in ("span", "plane")]
 
@@ -249,7 +243,9 @@
     return (1 + span_odd, 3 + plane_odd), (2 - span_odd, 4 - plane_odd)
 
 
-def pick_kernel(nspan, nplane, columns_ref, early_ref, late_ref):
+def pick_kernel(nspan, nplane, columns_ref, fold_ref, early_ref, late_ref, store_ref, sem):
+    store = pltpu.make_async_copy(fold_ref, store_ref, sem)
+    store.start()
     nblocks, nfaces = columns_ref.shape
     span, plane = lax.axis_index("span"), lax.axis_index("plane")
     position = table_positions(columns_ref[...], nfaces, span, plane, nspan, nplane)
@@ -268,6 +264,7 @@
         for n, row in enumerate(rows):
             column = jnp.sum(jnp.where(eye, row, 0.0), axis=1, keepdims=True).astype(jnp.int32)
             ref[n * nfaces : (n + 1) * nfaces, :] = jnp.where(lane == column, 1.0, 0.0).astype(BF16)
+    store.wait()
 
 
 def line_kernel(nplane, nlines, *refs):
@@ -482,14 +479,14 @@
     ok_ref[...] = jnp.where(ok, 1.0, 0.0)
 
 
-def call(kernel, args, outs, spaces=None, scratch=(), flops=0, pinned=True, ready=True, kind=F32):
+def call(kernel, args, outs, spaces=None, scratch=(), flops=0, pinned=True, ready=True):
     spaces = [pltpu.VMEM] * len(args) if spaces is None else spaces
     if ready:
         args = [pltpu.with_memory_space_constraint(x, s) if s is pltpu.VMEM else x for x, s in zip(args, spaces)]
     size = sum(x.dtype.itemsize * math.prod(x.shape) for x in args)
     return pl.pallas_call(
         kernel,
-        out_shape=[pltpu.VMEM(shape, kind) if pinned else jax.ShapeDtypeStruct(shape, kind) for shape in outs],
+        out_shape=[pltpu.VMEM(shape, F32) if pinned else jax.ShapeDtypeStruct(shape, F32) for shape in outs],
         in_specs=[pl.BlockSpec(memory_space=s) for s in spaces],
         out_specs=[pl.BlockSpec(memory_space=pltpu.VMEM) for _ in outs],
         scratch_shapes=scratch,
@@ -563,23 +560,24 @@
             flops=6 * nfaces * area,
         )
         if step == 0:
-            fold = pl.pallas_call(
-                store_kernel,
-                out_shape=pltpu.HBM(squares[0], F32),
-                in_specs=[pl.BlockSpec(memory_space=pl.ANY)] * 2,
-                out_specs=pl.BlockSpec(memory_space=pl.ANY),
+            *picks, fold = pl.pallas_call(
+                functools.partial(pick_kernel, nspan, nplane),
+                out_shape=[
+                    pltpu.VMEM((3 * nfaces, 6 * nfaces), BF16),
+                    pltpu.VMEM(((nblocks - 3) * nfaces, 10 * nfaces), BF16),
+                    pltpu.HBM(squares[0], F32),
+                ],
+                in_specs=[pl.BlockSpec(memory_space=pltpu.VMEM)] * 2,
+                out_specs=[pl.BlockSpec(memory_space=pltpu.VMEM)] * 2 + [pl.BlockSpec(memory_space=pl.ANY)],
                 scratch_shapes=[pltpu.SemaphoreType.DMA],
+                compiler_params=pltpu.CompilerParams(vmem_limit_bytes=VMEM_LIMIT),
                 cost_estimate=pl.CostEstimate(flops=0, bytes_accessed=4 * nfaces * area, transcendentals=0),
-            )(pltpu.with_memory_space_constraint(factors[2], pltpu.VMEM), solved[0])
-            picks = call(
-                functools.partial(pick_kernel, nspan, nplane),
-                [lax.optimization_barrier((columns, solved[0]))[0]],
-                [(3 * nfaces, 6 * nfaces), ((nblocks - 3) * nfaces, 10 * nfaces)],
-                ready=False,
-                kind=BF16,
+            )(
+                lax.optimization_barrier((columns, solved[0]))[0],
+                pltpu.with_memory_space_constraint(factors[2], pltpu.VMEM),
             )
         pieces = [exchange(solved[k], "plane", k) if k else solved[0] for k in far_first(nplane)]
-        args = [choose, *pieces, *((*picks, fold) if step == 0 else ())]
+        args = [choose, *pieces, *(picks if step == 0 else ())]
         spaces = [pltpu.VMEM] * (nplane + 1) + [pl.ANY] * (len(args) - nplane - 1)
         (mine,) = call(functools.partial(faces_kernel, nplane), args, [shape], spaces)
         zs.append(mine)

time: 69.9 us -> 67.6 us (0.967)
  local copies, waits for them, and re-layouts: 2.39 us -> 0.04 us
    unnamed x20 -> x14, local copies, waits for them, and re-layouts: 2.38 us -> 0.03 us
    pallas_call x19 -> x18, Pallas kernels: 22.1 us -> 21.9 us  [the longest x17 20.3 us: call(): pl.pallas_call(kernel, out_shape=[pltpu.VMEM(shape, F32) if pinned else j...]
  transfers between devices with their start and end apart: 30 -> 30, of which waited for: 13 -> 13; matrix products, arithmetic and copies ran while one was open for 0% -> 0% of each run, Pallas kernels for 21% -> 22%
where the time goes in v9:
time: 67.6 us; the launch traced here: 67.3 us
  starting transfers between devices  25.1 us (37%)
  Pallas kernels  21.9 us (32%)
  blocking collectives  10.2 us (15%)
  waiting for transfers between devices  8.75 us (13%)
  between operations  1.08 us (2%)
    pallas_call x17, Pallas kernels, call(): pl.pallas_call(kernel, out_shape=[pltpu.VMEM(shape, F32) if pinned else j...  20.3 us
    ppermute x18, starting transfers between devices, exchange(): lax.ppermute(x, axis, [(i, partner(i, k, size)[0]) for i in range(size)])  12.8 us
    all_to_all x1, blocking collectives, add_up(): lax.all_to_all(rows, ('span', 'plane'), split_axis=0, concat_axis=0, tile...  10.2 us
    ppermute x3, starting transfers between devices, on_device(): other = lax.ppermute(mine, 'span', span_others)  9.03 us
    ppermute x18, waiting for transfers between devices, exchange(): lax.ppermute(x, axis, [(i, partner(i, k, size)[0]) for i in range(size)])  7.41 us
    ppermute x3, starting transfers between devices, on_device(): far = [other, lax.ppermute(mine, 'plane', plane_others)]  1.66 us
    ppermute x3, starting transfers between devices, on_device(): lax.ppermute(mine, 'span', span_pairs)  1.61 us
    pallas_call x1, Pallas kernels, on_device(): pl.pallas_call(functools.partial(pick_kernel, nspan, nplane), out_shape=[...  1.58 us
  transfers between devices with their start and end apart: 30, of which 13 were waited for; matrix products, arithmetic and copies ran while one was open for 0% of the time, Pallas kernels for 22%

profile of v9, /device:TPU:0, one launch (start us, length us, event | category | flops | bytes accessed | tf_op | source)
XLA Modules:
  0.0 67.3 jit_solution(7635131512871213268)
XLA Ops:
  0.7 0.8 %shard_map.86 = (f32[16,80]{1,0:T(8,128)S(1)}, f32[16,48]{1,0:T(8,128)S(1)}, f32[4,80]{1,0:T(4,128)S(1)}, f32[4,80]{1,0:T(4,128)S(1)}, f32[4,80]{1,0:T(4,128)S(1)}, /*index=5*/f32[4,80]{1,0:T(4,128)S(1)}) custom-call(s32[1,16]{1,0:T(1,128)} %refs_0_.5, f32[16,80]{1,0:T(8,128)} %bitcast.571), custom_call_target="tpu_custom_call" | custom-call | bytes 5184 | tf_op jit(solution)/shard_map/pallas_call | solution.py:487
  1.5 2.5 %collective-permute-start.16 = (f32[4,80]{1,0:T(4,128)S(1)}, f32[4,80]{1,0:T(4,128)S(1)}, u32[]{:S(2)}, u32[]{:S(2)}) collective-permute-start(f32[4,80]{1,0:T(4,128)S(1)} %get-tuple-element.700), channel_id=1, source_target_pairs={{0,3},{1,2},{2,1},{3,0},{4,7},{5,6},{6,5},{7,4},{8,11},{9,10},{10,... | collective-permute-start | bytes 3848 | tf_op jit(solution)/shard_map/ppermute | solution.py:153
  4.7 2.5 %shard_map.87 = (f32[1280,80]{1,0:T(8,128)S(1)}, f32[1280,80]{1,0:T(8,128)S(1)}, f32[1280,80]{1,0:T(8,128)S(1)}) custom-call(f32[16,6400]{1,0:T(8,128)} %low.5, f32[16,6400]{1,0:T(8,128)} %piv.5, f32[16,6400]{1,0:T(8,128)} %upp.1, f32[16,80]{1,0:T(8,128)S(1)} %get-tuple-element.704._.refs_9_.refs_0_), custom_call_target="tpu_custom_call" | custom-call | flops 8192000 | bytes 1233920 | tf_op jit(solution)/shard_map/pallas_call | solution.py:487
  7.6 0.9 %shard_map.88 = (f32[4,80]{1,0:T(4,128)S(1)}, f32[4,80]{1,0:T(4,128)S(1)}, f32[4,80]{1,0:T(4,128)S(1)}, f32[4,80]{1,0:T(4,128)S(1)}) custom-call(f32[4,80]{1,0:T(4,128)S(1)} %collective-permute-done.16.refs_0_, f32[4,80]{1,0:T(4,128)S(1)} %collective-permute-done.17.refs_1_, f32[4,80]{1,0:T(4,128)S(1)} %collective-permute-done.18.refs_2_, ...), custom_call_target="tpu_custom_call" | custom-call | flops 614400 | bytes 1233920 | tf_op jit(solution)/shard_map/pallas_call | solution.py:487
  8.5 1.2 %collective-permute-start.19 = (f32[4,80]{1,0:T(4,128)S(1)}, f32[4,80]{1,0:T(4,128)S(1)}, u32[]{:S(2)}, u32[]{:S(2)}) collective-permute-start(f32[4,80]{1,0:T(4,128)S(1)} %get-tuple-element.712), channel_id=1, source_target_pairs={{0,3},{1,2},{2,1},{3,0},{4,7},{5,6},{6,5},{7,4},{8,11},{9,10},{10,... | collective-permute-start | bytes 3848 | tf_op jit(solution)/shard_map/ppermute | solution.py:153
  10.4 1.6 %shard_map.89 = (bf16[48,96]{1,0:T(8,128)(2,1)S(1)}, bf16[128,160]{1,0:T(8,128)(2,1)S(1)}, f32[1280,80]{1,0:T(8,128)}) custom-call(s32[11,16]{1,0:T(8,128)} %columns_ref, f32[1280,80]{1,0:T(8,128)S(1)} %get-tuple-element.707.fold_ref), custom_call_target="tpu_custom_call" | custom-call | bytes 409600 | tf_op jit(solution)/shard_map/pallas_call | solution.py:563
  12.0 1.2 %collective-permute-done.20.refs_1_ = f32[4,80]{1,0:T(4,128)S(1)} collective-permute-done((f32[4,80]{1,0:T(4,128)S(1)}, f32[4,80]{1,0:T(4,128)S(1)}, u32[]{:S(2)}, u32[]{:S(2)}) %collective-permute-start.20) | collective-permute-done | bytes 1312 | tf_op jit(solution)/shard_map/ppermute | solution.py:153
  13.4 1.5 %collective-permute-start.22 = (f32[16,80]{1,0:T(8,128)S(1)}, f32[16,80]{1,0:T(8,128)S(1)}, u32[]{:S(2)}, u32[]{:S(2)}) collective-permute-start(f32[16,80]{1,0:T(8,128)S(1)} %shard_map.90.refs_0_.refs_4_), channel_id=1, source_target_pairs={{0,4},{4,0},{8,12},{12,8},{16,20},{20,16},{24,28},{28,24},{1,5},{5... | collective-permute-start | bytes 15368 | tf_op jit(solution)/shard_map/ppermute | solution.py:585
  14.9 3.6 %collective-permute-start.24 = (f32[16,80]{1,0:T(8,128)S(1)}, f32[16,80]{1,0:T(8,128)S(1)}, u32[]{:S(2)}, u32[]{:S(2)}) collective-permute-start(f32[16,80]{1,0:T(8,128)S(1)} %shard_map.90.refs_0_.refs_4_), channel_id=1, source_target_pairs={{0,28},{4,8},{8,4},{12,16},{16,12},{20,24},{24,20},{28,0},{1,29},{... | collective-permute-start | bytes 15368 | tf_op jit(solution)/shard_map/ppermute | solution.py:584
  19.0 2.5 %shard_map.91 = (f32[16,80]{1,0:T(8,128)S(1)}, f32[16,51200]{1,0:T(8,128)S(1)}) custom-call(f32[16,70400]{1,0:T(8,128)} %blocks.5, bf16[48,96]{1,0:T(8,128)(2,1)S(1)} %get-tuple-element.710.refs_4_.pick, f32[16,80]{1,0:T(8,128)S(1)} %shard_map.90.refs_0_.refs_4_, f32[16,80]{1,0:T(8,128)S(1)} %collective-permute-done.22.refs_1_.refs_5_, ...), custom_call_target="tpu_custom_call" | custom-call | flops 614400 | bytes 4530176 | tf_op jit(solution)/shard_map/pallas_call | solution.py:487
  21.5 0.8 %shard_map.92 = (f32[16,80]{1,0:T(8,128)S(1)}, f32[4,80]{1,0:T(4,128)S(1)}, f32[4,80]{1,0:T(4,128)S(1)}, f32[4,80]{1,0:T(4,128)S(1)}, f32[4,80]{1,0:T(4,128)S(1)}) custom-call(s32[1,16]{1,0:T(1,128)S(1)} %copy-done.8, f32[16,51200]{1,0:T(8,128)S(1)} %get-tuple-element.716.refs_1_, bf16[128,160]{1,0:T(8,128)(2,1)S(1)} %get-tuple-element.715.refs_5_.refs_2_, ...), custom_call_target="tpu_custom_call" | custom-call | flops 2252800 | bytes 3353664 | tf_op jit(solution)/shard_map/pallas_call | solution.py:487
  22.4 1.2 %collective-permute-start.26 = (f32[4,80]{1,0:T(4,128)S(1)}, f32[4,80]{1,0:T(4,128)S(1)}, u32[]{:S(2)}, u32[]{:S(2)}) collective-permute-start(f32[4,80]{1,0:T(4,128)S(1)} %get-tuple-element.718), channel_id=1, source_target_pairs={{0,3},{1,2},{2,1},{3,0},{4,7},{5,6},{6,5},{7,4},{8,11},{9,10},{10,... | collective-permute-start | bytes 3848 | tf_op jit(solution)/shard_map/ppermute | solution.py:153
  24.3 1.5 %shard_map.93 = (f32[1280,80]{1,0:T(8,128)S(1)}, f32[1280,80]{1,0:T(8,128)S(1)}, f32[1280,80]{1,0:T(8,128)S(1)}) custom-call(f32[16,6400]{1,0:T(8,128)S(1)} %copy-done.1, f32[16,6400]{1,0:T(8,128)S(1)} %copy-done.2, f32[1280,80]{1,0:T(8,128)S(1)} %copy-done, f32[16,80]{1,0:T(8,128)S(1)} %get-tuple-element.723._.refs_9_.refs_10_.refs_1_), custom_call_target="tpu_custom_call" | custom-call | flops 102400 | bytes 1233920 | tf_op jit(solution)/shard_map/pallas_call | solution.py:487
  25.9 1.3 %collective-permute-done.27.refs_1_ = f32[4,80]{1,0:T(4,128)S(1)} collective-permute-done((f32[4,80]{1,0:T(4,128)S(1)}, f32[4,80]{1,0:T(4,128)S(1)}, u32[]{:S(2)}, u32[]{:S(2)}) %collective-permute-start.27) | collective-permute-done | bytes 1312 | tf_op jit(solution)/shard_map/ppermute | solution.py:153
  27.2 0.9 %shard_map.94 = (f32[4,80]{1,0:T(4,128)S(1)}, f32[4,80]{1,0:T(4,128)S(1)}, f32[4,80]{1,0:T(4,128)S(1)}, f32[4,80]{1,0:T(4,128)S(1)}) custom-call(f32[4,80]{1,0:T(4,128)S(1)} %collective-permute-done.26.refs_0_, f32[4,80]{1,0:T(4,128)S(1)} %collective-permute-done.27.refs_1_, f32[4,80]{1,0:T(4,128)S(1)} %collective-permute-done.28.refs_2_, ...), custom_call_target="tpu_custom_call" | custom-call | flops 614400 | bytes 1233920 | tf_op jit(solution)/shard_map/pallas_call | solution.py:487
  29.0 1.0 %collective-permute-start.31 = (f32[4,80]{1,0:T(4,128)S(1)}, f32[4,80]{1,0:T(4,128)S(1)}, u32[]{:S(2)}, u32[]{:S(2)}) collective-permute-start(f32[4,80]{1,0:T(4,128)S(1)} %get-tuple-element.729), channel_id=1, source_target_pairs={{0,1},{1,0},{2,3},{3,2},{4,5},{5,4},{6,7},{7,6},{8,9},{9,8},{10,11... | collective-permute-start | bytes 3848 | tf_op jit(solution)/shard_map/ppermute | solution.py:153
  30.0 1.1 %collective-permute-done.29.refs_0_ = f32[4,80]{1,0:T(4,128)S(1)} collective-permute-done((f32[4,80]{1,0:T(4,128)S(1)}, f32[4,80]{1,0:T(4,128)S(1)}, u32[]{:S(2)}, u32[]{:S(2)}) %collective-permute-start.29) | collective-permute-done | bytes 1312 | tf_op jit(solution)/shard_map/ppermute | solution.py:153
  32.1 2.8 %collective-permute-start.34 = (f32[16,80]{1,0:T(8,128)S(1)}, f32[16,80]{1,0:T(8,128)S(1)}, u32[]{:S(2)}, u32[]{:S(2)}) collective-permute-start(f32[16,80]{1,0:T(8,128)S(1)} %shard_map.95.refs_0_.refs_4_.refs_5_), channel_id=1, source_target_pairs={{0,28},{4,8},{8,4},{12,16},{16,12},{20,24},{24,20},{28,0},{1,29},{... | collective-permute-start | bytes 15368 | tf_op jit(solution)/shard_map/ppermute | solution.py:584
  35.7 2.5 %shard_map.96 = (f32[16,80]{1,0:T(8,128)S(1)}, f32[16,51200]{1,0:T(8,128)S(1)}) custom-call(f32[16,70400]{1,0:T(8,128)} %blocks.5, bf16[48,96]{1,0:T(8,128)(2,1)S(1)} %get-tuple-element.710.refs_4_.pick, f32[16,80]{1,0:T(8,128)S(1)} %shard_map.95.refs_0_.refs_4_.refs_5_, f32[16,80]{1,0:T(8,128)S(1)} %collective-permute-done.32.refs_1_.refs_5_, ...), custom_call_target="tpu_custom_call" | custom-call | flops 614400 | bytes 4530176 | tf_op jit(solution)/shard_map/pallas_call | solution.py:487
  38.5 0.8 %shard_map.97 = (f32[16,80]{1,0:T(8,128)S(1)}, f32[4,80]{1,0:T(4,128)S(1)}, f32[4,80]{1,0:T(4,128)S(1)}, f32[4,80]{1,0:T(4,128)S(1)}, f32[4,80]{1,0:T(4,128)S(1)}) custom-call(s32[1,16]{1,0:T(1,128)S(1)} %copy-done.8, f32[16,51200]{1,0:T(8,128)S(1)} %get-tuple-element.731.refs_1_, bf16[128,160]{1,0:T(8,128)(2,1)S(1)} %get-tuple-element.715.refs_5_.refs_2_, ...), custom_call_target="tpu_custom_call" | custom-call | flops 2252800 | bytes 3353664 | tf_op jit(solution)/shard_map/pallas_call | solution.py:487
  40.0 0.9 %collective-permute-start.37 = (f32[4,80]{1,0:T(4,128)S(1)}, f32[4,80]{1,0:T(4,128)S(1)}, u32[]{:S(2)}, u32[]{:S(2)}) collective-permute-start(f32[4,80]{1,0:T(4,128)S(1)} %get-tuple-element.734), channel_id=1, source_target_pairs={{0,2},{1,3},{2,0},{3,1},{4,6},{5,7},{6,4},{7,5},{8,10},{9,11},{10,... | collective-permute-start | bytes 3848 | tf_op jit(solution)/shard_map/ppermute | solution.py:153
  41.3 1.5 %shard_map.98 = (f32[1280,80]{1,0:T(8,128)S(1)}, f32[1280,80]{1,0:T(8,128)S(1)}, f32[1280,80]{1,0:T(8,128)S(1)}) custom-call(f32[16,6400]{1,0:T(8,128)S(1)} %copy-done.1, f32[16,6400]{1,0:T(8,128)S(1)} %copy-done.2, f32[1280,80]{1,0:T(8,128)S(1)} %copy-done, f32[16,80]{1,0:T(8,128)S(1)} %get-tuple-element.737._.refs_11_.refs_2_), custom_call_target="tpu_custom_call" | custom-call | flops 102400 | bytes 1233920 | tf_op jit(solution)/shard_map/pallas_call | solution.py:487
  42.8 0.8 %collective-permute-done.37.refs_1_ = f32[4,80]{1,0:T(4,128)S(1)} collective-permute-done((f32[4,80]{1,0:T(4,128)S(1)}, f32[4,80]{1,0:T(4,128)S(1)}, u32[]{:S(2)}, u32[]{:S(2)}) %collective-permute-start.37) | collective-permute-done | bytes 1312 | tf_op jit(solution)/shard_map/ppermute | solution.py:153
  43.6 0.9 %shard_map.99 = (f32[4,80]{1,0:T(4,128)S(1)}, f32[4,80]{1,0:T(4,128)S(1)}, f32[4,80]{1,0:T(4,128)S(1)}, f32[4,80]{1,0:T(4,128)S(1)}) custom-call(f32[4,80]{1,0:T(4,128)S(1)} %collective-permute-done.36.refs_0_, f32[4,80]{1,0:T(4,128)S(1)} %collective-permute-done.37.refs_1_, f32[4,80]{1,0:T(4,128)S(1)} %collective-permute-done.38.refs_2_, ...), custom_call_target="tpu_custom_call" | custom-call | flops 614400 | bytes 1233920 | tf_op jit(solution)/shard_map/pallas_call | solution.py:487
  44.7 0.9 %collective-permute-start.40 = (f32[4,80]{1,0:T(4,128)S(1)}, f32[4,80]{1,0:T(4,128)S(1)}, u32[]{:S(2)}, u32[]{:S(2)}) collective-permute-start(f32[4,80]{1,0:T(4,128)S(1)} %get-tuple-element.742), channel_id=1, source_target_pairs={{0,2},{1,3},{2,0},{3,1},{4,6},{5,7},{6,4},{7,5},{8,10},{9,11},{10,... | collective-permute-start | bytes 3848 | tf_op jit(solution)/shard_map/ppermute | solution.py:153
  45.6 0.9 %collective-permute-start.41 = (f32[4,80]{1,0:T(4,128)S(1)}, f32[4,80]{1,0:T(4,128)S(1)}, u32[]{:S(2)}, u32[]{:S(2)}) collective-permute-start(f32[4,80]{1,0:T(4,128)S(1)} %get-tuple-element.743), channel_id=1, source_target_pairs={{0,1},{1,0},{2,3},{3,2},{4,5},{5,4},{6,7},{7,6},{8,9},{9,8},{10,11... | collective-permute-start | bytes 3848 | tf_op jit(solution)/shard_map/ppermute | solution.py:153
  46.5 1.1 %collective-permute-done.39.refs_0_ = f32[4,80]{1,0:T(4,128)S(1)} collective-permute-done((f32[4,80]{1,0:T(4,128)S(1)}, f32[4,80]{1,0:T(4,128)S(1)}, u32[]{:S(2)}, u32[]{:S(2)}) %collective-permute-start.39) | collective-permute-done | bytes 1312 | tf_op jit(solution)/shard_map/ppermute | solution.py:153
  48.5 2.7 %collective-permute-start.44 = (f32[16,80]{1,0:T(8,128)S(1)}, f32[16,80]{1,0:T(8,128)S(1)}, u32[]{:S(2)}, u32[]{:S(2)}) collective-permute-start(f32[16,80]{1,0:T(8,128)S(1)} %shard_map.100.refs_0_.refs_4_.refs_6_), channel_id=1, source_target_pairs={{0,28},{4,8},{8,4},{12,16},{16,12},{20,24},{24,20},{28,0},{1,29},{... | collective-permute-start | bytes 15368 | tf_op jit(solution)/shard_map/ppermute | solution.py:584
  52.1 2.5 %shard_map.101 = (f32[16,80]{1,0:T(8,128)S(1)}, f32[16,51200]{1,0:T(8,128)S(1)}) custom-call(f32[16,70400]{1,0:T(8,128)} %blocks.5, bf16[48,96]{1,0:T(8,128)(2,1)S(1)} %get-tuple-element.710.refs_4_.pick, f32[16,80]{1,0:T(8,128)S(1)} %shard_map.100.refs_0_.refs_4_.refs_6_, f32[16,80]{1,0:T(8,128)S(1)} %collective-permute-done.42.refs_1_.refs_5_, ...), custom_call_target="tpu_custom_call" | custom-call | flops 614400 | bytes 4530176 | tf_op jit(solution)/shard_map/pallas_call | solution.py:487
  54.9 0.9 %shard_map.102 = (f32[16,80]{1,0:T(8,128)S(1)}, f32[1,128]{1,0:T(1,128)S(1)}) custom-call(s32[1,16]{1,0:T(1,128)S(1)} %copy-done.8, f32[16,51200]{1,0:T(8,128)S(1)} %get-tuple-element.745.refs_1_, bf16[128,160]{1,0:T(8,128)(2,1)S(1)} %get-tuple-element.715.refs_5_.refs_2_, f32[16,80]{1,0:T(8,128)S(1)} %get-tuple-element.746.refs_3_, ...), custom_call_target="tpu_custom_call" | custom-call | flops 2252800 | bytes 3363904 | tf_op jit(solution)/shard_map/pallas_call | solution.py:487
  55.8 10.2 %all_to_all.112 = f32[32,1,128]{2,1,0:T(1,128)S(1)} all-to-all(f32[32,1,128]{2,1,0:T(1,128)S(1)} %broadcast_in_dim.83), channel_id=1, replica_groups=mesh['span'=8,'plane'=4] {'span','plane'}, dimensions={0} | all-to-all | bytes 32768 | tf_op jit(solution)/shard_map/all_to_all | solution.py:501
  66.0 0.8 %shard_map.103 = (f32[16,80]{1,0:T(8,128)}, f32[16,80]{1,0:T(8,128)}, f32[1,128]{1,0:T(1,128)S(1)}) custom-call(f32[32,128]{1,0:T(8,128)S(1)} %bitcast.558, f32[16,80]{1,0:T(8,128)S(1)} %get-tuple-element.704._.refs_9_.refs_0_, f32[16,80]{1,0:T(8,128)S(1)} %get-tuple-element.723._.refs_9_.refs_10_.refs_1_, ...), custom_call_target="tpu_custom_call" | custom-call | bytes 52224 | tf_op jit(solution)/shard_map/pallas_call | solution.py:487
  (63 shorter events, 9.8 us)
Async XLA Ops:
  1.5 5.7 %collective-permute-start.16 = (f32[4,80]{1,0:T(4,128)S(1)}, f32[4,80]{1,0:T(4,128)S(1)}, u32[]{:S(2)}, u32[]{:S(2)}) collective-permute-start(f32[4,80]{1,0:T(4,128)S(1)} %get-tuple-element.700), channel_id=1, source_target_pairs={{0,3},{1,2},{2,1},{3,0},{4,7},{5,6},{6,5},{7,4},{8,11},{9,10},{10,... | collective-permute-start | bytes 3848 | tf_op jit(solution)/shard_map/ppermute | solution.py:153
  4.0 3.6 %collective-permute-start.17 = (f32[4,80]{1,0:T(4,128)S(1)}, f32[4,80]{1,0:T(4,128)S(1)}, u32[]{:S(2)}, u32[]{:S(2)}) collective-permute-start(f32[4,80]{1,0:T(4,128)S(1)} %get-tuple-element.701), channel_id=1, source_target_pairs={{0,2},{1,3},{2,0},{3,1},{4,6},{5,7},{6,4},{7,5},{8,10},{9,11},{10,... | collective-permute-start | bytes 3848 | tf_op jit(solution)/shard_map/ppermute | solution.py:153
  4.6 2.9 %collective-permute-start.18 = (f32[4,80]{1,0:T(4,128)S(1)}, f32[4,80]{1,0:T(4,128)S(1)}, u32[]{:S(2)}, u32[]{:S(2)}) collective-permute-start(f32[4,80]{1,0:T(4,128)S(1)} %get-tuple-element.702), channel_id=1, source_target_pairs={{0,1},{1,0},{2,3},{3,2},{4,5},{5,4},{6,7},{7,6},{8,9},{9,8},{10,11... | collective-permute-start | bytes 3848 | tf_op jit(solution)/shard_map/ppermute | solution.py:153
  8.5 3.5 %collective-permute-start.19 = (f32[4,80]{1,0:T(4,128)S(1)}, f32[4,80]{1,0:T(4,128)S(1)}, u32[]{:S(2)}, u32[]{:S(2)}) collective-permute-start(f32[4,80]{1,0:T(4,128)S(1)} %get-tuple-element.712), channel_id=1, source_target_pairs={{0,3},{1,2},{2,1},{3,0},{4,7},{5,6},{6,5},{7,4},{8,11},{9,10},{10,... | collective-permute-start | bytes 3848 | tf_op jit(solution)/shard_map/ppermute | solution.py:153
  9.7 3.6 %collective-permute-start.20 = (f32[4,80]{1,0:T(4,128)S(1)}, f32[4,80]{1,0:T(4,128)S(1)}, u32[]{:S(2)}, u32[]{:S(2)}) collective-permute-start(f32[4,80]{1,0:T(4,128)S(1)} %get-tuple-element.713), channel_id=1, source_target_pairs={{0,2},{1,3},{2,0},{3,1},{4,6},{5,7},{6,4},{7,5},{8,10},{9,11},{10,... | collective-permute-start | bytes 3848 | tf_op jit(solution)/shard_map/ppermute | solution.py:153
  10.3 2.9 %collective-permute-start.21 = (f32[4,80]{1,0:T(4,128)S(1)}, f32[4,80]{1,0:T(4,128)S(1)}, u32[]{:S(2)}, u32[]{:S(2)}) collective-permute-start(f32[4,80]{1,0:T(4,128)S(1)} %get-tuple-element.714), channel_id=1, source_target_pairs={{0,1},{1,0},{2,3},{3,2},{4,5},{5,4},{6,7},{7,6},{8,9},{9,8},{10,11... | collective-permute-start | bytes 3848 | tf_op jit(solution)/shard_map/ppermute | solution.py:153
  13.4 5.6 %collective-permute-start.22 = (f32[16,80]{1,0:T(8,128)S(1)}, f32[16,80]{1,0:T(8,128)S(1)}, u32[]{:S(2)}, u32[]{:S(2)}) collective-permute-start(f32[16,80]{1,0:T(8,128)S(1)} %shard_map.90.refs_0_.refs_4_), channel_id=1, source_target_pairs={{0,4},{4,0},{8,12},{12,8},{16,20},{20,16},{24,28},{28,24},{1,5},{5... | collective-permute-start | bytes 15368 | tf_op jit(solution)/shard_map/ppermute | solution.py:585
  14.9 4.1 %collective-permute-start.23 = (f32[16,80]{1,0:T(8,128)S(1)}, f32[16,80]{1,0:T(8,128)S(1)}, u32[]{:S(2)}, u32[]{:S(2)}) collective-permute-start(f32[16,80]{1,0:T(8,128)S(1)} %shard_map.90.refs_0_.refs_4_), channel_id=1, source_target_pairs={{0,1},{1,0},{2,3},{3,2},{4,5},{5,4},{6,7},{7,6},{8,9},{9,8},{10,11... | collective-permute-start | bytes 15368 | tf_op jit(solution)/shard_map/ppermute | solution.py:585
  14.9 6.5 %collective-permute-start.24 = (f32[16,80]{1,0:T(8,128)S(1)}, f32[16,80]{1,0:T(8,128)S(1)}, u32[]{:S(2)}, u32[]{:S(2)}) collective-permute-start(f32[16,80]{1,0:T(8,128)S(1)} %shard_map.90.refs_0_.refs_4_), channel_id=1, source_target_pairs={{0,28},{4,8},{8,4},{12,16},{16,12},{20,24},{24,20},{28,0},{1,29},{... | collective-permute-start | bytes 15368 | tf_op jit(solution)/shard_map/ppermute | solution.py:584
  18.5 3.1 %collective-permute-start.25 = (f32[16,80]{1,0:T(8,128)S(1)}, f32[16,80]{1,0:T(8,128)S(1)}, u32[]{:S(2)}, u32[]{:S(2)}) collective-permute-start(f32[16,80]{1,0:T(8,128)S(1)} %shard_map.90.refs_0_.refs_4_), channel_id=1, source_target_pairs={{0,3},{1,2},{2,1},{3,0},{4,7},{5,6},{6,5},{7,4},{8,11},{9,10},{10,... | collective-permute-start | bytes 15368 | tf_op jit(solution)/shard_map/ppermute | solution.py:586
  22.4 3.5 %collective-permute-start.26 = (f32[4,80]{1,0:T(4,128)S(1)}, f32[4,80]{1,0:T(4,128)S(1)}, u32[]{:S(2)}, u32[]{:S(2)}) collective-permute-start(f32[4,80]{1,0:T(4,128)S(1)} %get-tuple-element.718), channel_id=1, source_target_pairs={{0,3},{1,2},{2,1},{3,0},{4,7},{5,6},{6,5},{7,4},{8,11},{9,10},{10,... | collective-permute-start | bytes 3848 | tf_op jit(solution)/shard_map/ppermute | solution.py:153
  23.6 3.6 %collective-permute-start.27 = (f32[4,80]{1,0:T(4,128)S(1)}, f32[4,80]{1,0:T(4,128)S(1)}, u32[]{:S(2)}, u32[]{:S(2)}) collective-permute-start(f32[4,80]{1,0:T(4,128)S(1)} %get-tuple-element.719), channel_id=1, source_target_pairs={{0,2},{1,3},{2,0},{3,1},{4,6},{5,7},{6,4},{7,5},{8,10},{9,11},{10,... | collective-permute-start | bytes 3848 | tf_op jit(solution)/shard_map/ppermute | solution.py:153
  24.3 2.9 %collective-permute-start.28 = (f32[4,80]{1,0:T(4,128)S(1)}, f32[4,80]{1,0:T(4,128)S(1)}, u32[]{:S(2)}, u32[]{:S(2)}) collective-permute-start(f32[4,80]{1,0:T(4,128)S(1)} %get-tuple-element.720), channel_id=1, source_target_pairs={{0,1},{1,0},{2,3},{3,2},{4,5},{5,4},{6,7},{7,6},{8,9},{9,8},{10,11... | collective-permute-start | bytes 3848 | tf_op jit(solution)/shard_map/ppermute | solution.py:153
  28.1 3.1 %collective-permute-start.29 = (f32[4,80]{1,0:T(4,128)S(1)}, f32[4,80]{1,0:T(4,128)S(1)}, u32[]{:S(2)}, u32[]{:S(2)}) collective-permute-start(f32[4,80]{1,0:T(4,128)S(1)} %get-tuple-element.727), channel_id=1, source_target_pairs={{0,3},{1,2},{2,1},{3,0},{4,7},{5,6},{6,5},{7,4},{8,11},{9,10},{10,... | collective-permute-start | bytes 3848 | tf_op jit(solution)/shard_map/ppermute | solution.py:153
  28.3 3.6 %collective-permute-start.30 = (f32[4,80]{1,0:T(4,128)S(1)}, f32[4,80]{1,0:T(4,128)S(1)}, u32[]{:S(2)}, u32[]{:S(2)}) collective-permute-start(f32[4,80]{1,0:T(4,128)S(1)} %get-tuple-element.728), channel_id=1, source_target_pairs={{0,2},{1,3},{2,0},{3,1},{4,6},{5,7},{6,4},{7,5},{8,10},{9,11},{10,... | collective-permute-start | bytes 3848 | tf_op jit(solution)/shard_map/ppermute | solution.py:153
  29.0 2.9 %collective-permute-start.31 = (f32[4,80]{1,0:T(4,128)S(1)}, f32[4,80]{1,0:T(4,128)S(1)}, u32[]{:S(2)}, u32[]{:S(2)}) collective-permute-start(f32[4,80]{1,0:T(4,128)S(1)} %get-tuple-element.729), channel_id=1, source_target_pairs={{0,1},{1,0},{2,3},{3,2},{4,5},{5,4},{6,7},{7,6},{8,9},{9,8},{10,11... | collective-permute-start | bytes 3848 | tf_op jit(solution)/shard_map/ppermute | solution.py:153
  32.0 3.7 %collective-permute-start.32 = (f32[16,80]{1,0:T(8,128)S(1)}, f32[16,80]{1,0:T(8,128)S(1)}, u32[]{:S(2)}, u32[]{:S(2)}) collective-permute-start(f32[16,80]{1,0:T(8,128)S(1)} %shard_map.95.refs_0_.refs_4_.refs_5_), channel_id=1, source_target_pairs={{0,4},{4,0},{8,12},{12,8},{16,20},{20,16},{24,28},{28,24},{1,5},{5... | collective-permute-start | bytes 15368 | tf_op jit(solution)/shard_map/ppermute | solution.py:585
  32.0 3.7 %collective-permute-start.33 = (f32[16,80]{1,0:T(8,128)S(1)}, f32[16,80]{1,0:T(8,128)S(1)}, u32[]{:S(2)}, u32[]{:S(2)}) collective-permute-start(f32[16,80]{1,0:T(8,128)S(1)} %shard_map.95.refs_0_.refs_4_.refs_5_), channel_id=1, source_target_pairs={{0,1},{1,0},{2,3},{3,2},{4,5},{5,4},{6,7},{7,6},{8,9},{9,8},{10,11... | collective-permute-start | bytes 15368 | tf_op jit(solution)/shard_map/ppermute | solution.py:585
  32.1 6.4 %collective-permute-start.34 = (f32[16,80]{1,0:T(8,128)S(1)}, f32[16,80]{1,0:T(8,128)S(1)}, u32[]{:S(2)}, u32[]{:S(2)}) collective-permute-start(f32[16,80]{1,0:T(8,128)S(1)} %shard_map.95.refs_0_.refs_4_.refs_5_), channel_id=1, source_target_pairs={{0,28},{4,8},{8,4},{12,16},{16,12},{20,24},{24,20},{28,0},{1,29},{... | collective-permute-start | bytes 15368 | tf_op jit(solution)/shard_map/ppermute | solution.py:584
  34.8 3.7 %collective-permute-start.35 = (f32[16,80]{1,0:T(8,128)S(1)}, f32[16,80]{1,0:T(8,128)S(1)}, u32[]{:S(2)}, u32[]{:S(2)}) collective-permute-start(f32[16,80]{1,0:T(8,128)S(1)} %shard_map.95.refs_0_.refs_4_.refs_5_), channel_id=1, source_target_pairs={{0,3},{1,2},{2,1},{3,0},{4,7},{5,6},{6,5},{7,4},{8,11},{9,10},{10,... | collective-permute-start | bytes 15368 | tf_op jit(solution)/shard_map/ppermute | solution.py:586
  38.5 28.5 %copy-start.5 = (f32[80,16]{0,1:T(8,128)S(1)}, f32[80,16]{0,1:T(8,128)}, u32[]{:S(2)}) copy-start(f32[80,16]{0,1:T(8,128)} %param.25) | copy-start | bytes 15364
  38.5 28.5 %copy-start.6 = (s32[11,16]{1,0:T(8,128)S(1)}, s32[11,16]{1,0:T(8,128)}, u32[]{:S(2)}) copy-start(s32[11,16]{1,0:T(8,128)} %columns_ref) | copy-start | bytes 2116
  39.4 3.5 %collective-permute-start.36 = (f32[4,80]{1,0:T(4,128)S(1)}, f32[4,80]{1,0:T(4,128)S(1)}, u32[]{:S(2)}, u32[]{:S(2)}) collective-permute-start(f32[4,80]{1,0:T(4,128)S(1)} %get-tuple-element.733), channel_id=1, source_target_pairs={{0,3},{1,2},{2,1},{3,0},{4,7},{5,6},{6,5},{7,4},{8,11},{9,10},{10,... | collective-permute-start | bytes 3848 | tf_op jit(solution)/shard_map/ppermute | solution.py:153
  40.0 3.6 %collective-permute-start.37 = (f32[4,80]{1,0:T(4,128)S(1)}, f32[4,80]{1,0:T(4,128)S(1)}, u32[]{:S(2)}, u32[]{:S(2)}) collective-permute-start(f32[4,80]{1,0:T(4,128)S(1)} %get-tuple-element.734), channel_id=1, source_target_pairs={{0,2},{1,3},{2,0},{3,1},{4,6},{5,7},{6,4},{7,5},{8,10},{9,11},{10,... | collective-permute-start | bytes 3848 | tf_op jit(solution)/shard_map/ppermute | solution.py:153
  40.9 2.7 %collective-permute-start.38 = (f32[4,80]{1,0:T(4,128)S(1)}, f32[4,80]{1,0:T(4,128)S(1)}, u32[]{:S(2)}, u32[]{:S(2)}) collective-permute-start(f32[4,80]{1,0:T(4,128)S(1)} %get-tuple-element.735), channel_id=1, source_target_pairs={{0,1},{1,0},{2,3},{3,2},{4,5},{5,4},{6,7},{7,6},{8,9},{9,8},{10,11... | collective-permute-start | bytes 3848 | tf_op jit(solution)/shard_map/ppermute | solution.py:153
  44.5 3.1 %collective-permute-start.39 = (f32[4,80]{1,0:T(4,128)S(1)}, f32[4,80]{1,0:T(4,128)S(1)}, u32[]{:S(2)}, u32[]{:S(2)}) collective-permute-start(f32[4,80]{1,0:T(4,128)S(1)} %get-tuple-element.741), channel_id=1, source_target_pairs={{0,3},{1,2},{2,1},{3,0},{4,7},{5,6},{6,5},{7,4},{8,11},{9,10},{10,... | collective-permute-start | bytes 3848 | tf_op jit(solution)/shard_map/ppermute | solution.py:153
  44.7 3.6 %collective-permute-start.40 = (f32[4,80]{1,0:T(4,128)S(1)}, f32[4,80]{1,0:T(4,128)S(1)}, u32[]{:S(2)}, u32[]{:S(2)}) collective-permute-start(f32[4,80]{1,0:T(4,128)S(1)} %get-tuple-element.742), channel_id=1, source_target_pairs={{0,2},{1,3},{2,0},{3,1},{4,6},{5,7},{6,4},{7,5},{8,10},{9,11},{10,... | collective-permute-start | bytes 3848 | tf_op jit(solution)/shard_map/ppermute | solution.py:153
  45.6 2.7 %collective-permute-start.41 = (f32[4,80]{1,0:T(4,128)S(1)}, f32[4,80]{1,0:T(4,128)S(1)}, u32[]{:S(2)}, u32[]{:S(2)}) collective-permute-start(f32[4,80]{1,0:T(4,128)S(1)} %get-tuple-element.743), channel_id=1, source_target_pairs={{0,1},{1,0},{2,3},{3,2},{4,5},{5,4},{6,7},{7,6},{8,9},{9,8},{10,11... | collective-permute-start | bytes 3848 | tf_op jit(solution)/shard_map/ppermute | solution.py:153
  48.4 3.7 %collective-permute-start.42 = (f32[16,80]{1,0:T(8,128)S(1)}, f32[16,80]{1,0:T(8,128)S(1)}, u32[]{:S(2)}, u32[]{:S(2)}) collective-permute-start(f32[16,80]{1,0:T(8,128)S(1)} %shard_map.100.refs_0_.refs_4_.refs_6_), channel_id=1, source_target_pairs={{0,4},{4,0},{8,12},{12,8},{16,20},{20,16},{24,28},{28,24},{1,5},{5... | collective-permute-start | bytes 15368 | tf_op jit(solution)/shard_map/ppermute | solution.py:585
  48.5 3.5 %collective-permute-start.43 = (f32[16,80]{1,0:T(8,128)S(1)}, f32[16,80]{1,0:T(8,128)S(1)}, u32[]{:S(2)}, u32[]{:S(2)}) collective-permute-start(f32[16,80]{1,0:T(8,128)S(1)} %shard_map.100.refs_0_.refs_4_.refs_6_), channel_id=1, source_target_pairs={{0,1},{1,0},{2,3},{3,2},{4,5},{5,4},{6,7},{7,6},{8,9},{9,8},{10,11... | collective-permute-start | bytes 15368 | tf_op jit(solution)/shard_map/ppermute | solution.py:585
  48.5 6.3 %collective-permute-start.44 = (f32[16,80]{1,0:T(8,128)S(1)}, f32[16,80]{1,0:T(8,128)S(1)}, u32[]{:S(2)}, u32[]{:S(2)}) collective-permute-start(f32[16,80]{1,0:T(8,128)S(1)} %shard_map.100.refs_0_.refs_4_.refs_6_), channel_id=1, source_target_pairs={{0,28},{4,8},{8,4},{12,16},{16,12},{20,24},{24,20},{28,0},{1,29},{... | collective-permute-start | bytes 15368 | tf_op jit(solution)/shard_map/ppermute | solution.py:584
  51.2 3.7 %collective-permute-start.45 = (f32[16,80]{1,0:T(8,128)S(1)}, f32[16,80]{1,0:T(8,128)S(1)}, u32[]{:S(2)}, u32[]{:S(2)}) collective-permute-start(f32[16,80]{1,0:T(8,128)S(1)} %shard_map.100.refs_0_.refs_4_.refs_6_), channel_id=1, source_target_pairs={{0,3},{1,2},{2,1},{3,0},{4,7},{5,6},{6,5},{7,4},{8,11},{9,10},{10,... | collective-permute-start | bytes 15368 | tf_op jit(solution)/shard_map/ppermute | solution.py:586
  (5 other events, 109.0 us)

commit v10 on v9

--- a/solution.py
+++ b/solution.py
@@ -243,9 +243,13 @@
     return (1 + span_odd, 3 + plane_odd), (2 - span_odd, 4 - plane_odd)
 
 
-def pick_kernel(nspan, nplane, columns_ref, fold_ref, early_ref, late_ref, store_ref, sem):
+def pick_kernel(nspan, nplane, width, columns_ref, fold_ref, early_ref, late_ref, seg_ref, store_ref, sem):
     store = pltpu.make_async_copy(fold_ref, store_ref, sem)
     store.start()
+    copies = seg_ref.shape[0] // width
+    lane = lax.broadcasted_iota(jnp.int32, (width, 128), 1) % copies
+    for r in range(copies):
+        seg_ref[r * width : (r + 1) * width, :] = jnp.where(lane == r, 1.0, 0.0).astype(BF16)
     nblocks, nfaces = columns_ref.shape
     span, plane = lax.axis_index("span"), lax.axis_index("plane")
     position = table_positions(columns_ref[...], nfaces, span, plane, nspan, nplane)
@@ -260,7 +264,7 @@
     third, fourth = jnp.where(plane_odd, at[4:5], at[3:4]), jnp.where(plane_odd, at[3:4], at[4:5])
     rest = [at[k : k + 1] for k in range(5, nblocks)]
     for ref, rows in ((early_ref, [at[0:1], first, third]), (late_ref, [second, fourth, *rest])):
-        lane = lax.broadcasted_iota(jnp.int32, (nfaces, ref.shape[1]), 1) % (ref.shape[1] // 2)
+        lane = lax.broadcasted_iota(jnp.int32, (nfaces, ref.shape[1]), 1) % (ref.shape[1] // 3)
         for n, row in enumerate(rows):
             column = jnp.sum(jnp.where(eye, row, 0.0), axis=1, keepdims=True).astype(jnp.int32)
             ref[n * nfaces : (n + 1) * nfaces, :] = jnp.where(lane == column, 1.0, 0.0).astype(BF16)
@@ -318,18 +322,16 @@
 
 
 def repeat_faces(faces, pick, copies):
-    both = split(jnp.concatenate([f[...] for f in faces], axis=0), 2).astype(BF16)
-    picked = jnp.dot(pick[...], both, preferred_element_type=F32)
+    table = split(jnp.concatenate([f[...] for f in faces], axis=0), 3).astype(BF16)
+    picked = jnp.dot(pick[...], table, preferred_element_type=F32)
     return jnp.concatenate([picked] * copies, axis=1)
 
 
-def add_products(work, x_scr, acc_scr, parts, width):
+def add_products(work, x_scr, acc_scr, parts, seg, width):
     nfaces, area = acc_scr.shape
     chunk = x_scr.shape[1]
     copies, count = chunk // width, area // chunk
     lane = lax.broadcasted_iota(jnp.int32, (1, 128), 1)
-    seg = [jnp.broadcast_to(jnp.where(lane % copies == r, 1.0, 0.0), (width, 128)) for r in range(copies)]
-    seg = jnp.concatenate(seg, axis=0).astype(BF16)
     total = jnp.zeros((nfaces, 128), F32)
     done = 0
     for n, (places, fetch) in enumerate(work):
@@ -349,22 +351,24 @@
                     if not last:
                         acc_scr[:, at : at + 128] = value
                         continue
-                    high = value.astype(BF16)
-                    row = 2 * c * nfaces
-                    parts[row : row + nfaces, v : v + 128] = high
-                    parts[row + nfaces : row + 2 * nfaces, v : v + 128] = (value - high.astype(F32)).astype(BF16)
+                    for n_part in range(3):
+                        part = value.astype(BF16)
+                        row = (3 * c + n_part) * nfaces
+                        parts[row : row + nfaces, v : v + 128] = part
+                        value = value - part.astype(F32)
             if last:
-                base = 2 * half[0] * nfaces
-                sums = jnp.dot(parts[base : 2 * half[1] * nfaces, :], seg, preferred_element_type=F32)
+                base = 3 * half[0] * nfaces
+                sums = jnp.dot(parts[base : 3 * half[1] * nfaces, :], seg[...], preferred_element_type=F32)
                 for c in range(*half):
-                    at = 2 * c * nfaces - base
-                    pair = sums[at : at + nfaces] + sums[at + nfaces : at + 2 * nfaces]
-                    total = total + jnp.where(lane // copies == c, pair, 0.0)
+                    high, middle, low = [
+                        sums[at : at + nfaces] for at in range(3 * c * nfaces - base, 3 * (c + 1) * nfaces - base, nfaces)
+                    ]
+                    total = total + jnp.where(lane // copies == c, high + (middle + low), 0.0)
         done += len(places)
     return total[:, :width]
 
 
-def early_kernel(nblocks, blocks, pick, *refs):
+def early_kernel(nblocks, blocks, pick, seg, *refs):
     faces, (sum_ref, held, buf, x_scr, acc_scr, parts, sems) = refs[:3], refs[3:]
     width = faces[0].shape[1]
     area = width * width
@@ -383,13 +387,13 @@
         copy.start()
     x_scr[...] = repeat_faces(faces, pick, x_scr.shape[1] // width)
     work = [([(buf, n * area)], copy) for n, copy in enumerate(mine)]
-    sum_ref[...] = add_products(work, x_scr, acc_scr, parts, width)
+    sum_ref[...] = add_products(work, x_scr, acc_scr, parts, seg, width)
     for copy in kept:
         copy.wait()
 
 
 def late_kernel(nplane, last, *refs):
-    (slot, held, pick, early_sum), faces, refs = refs[:4], refs[4:9], refs[9:]
+    (slot, held, pick, seg, early_sum), faces, refs = refs[:5], refs[5:10], refs[10:]
     nold = ITERS if last else 1
     olds, refs = refs[:nold], refs[nold:]
     next_ref, outs, (x_scr, acc_scr, parts, slot_scr, slot_sem) = refs[0], refs[1:-5], refs[-5:]
@@ -400,7 +404,7 @@
         slots.start()
     x_scr[...] = repeat_faces(faces, pick, x_scr.shape[1] // width)
     work = [([(held, column) for column in range(0, held.shape[1], area)], None)]
-    u_next = early_sum[...] + add_products(work, x_scr, acc_scr, parts, width) - SHIFT * olds[-1][...]
+    u_next = early_sum[...] + add_products(work, x_scr, acc_scr, parts, seg, width) - SHIFT * olds[-1][...]
     next_ref[...] = u_next
     if last:
         gram_ref = outs[0]
@@ -561,14 +565,15 @@
         )
         if step == 0:
             *picks, fold = pl.pallas_call(
-                functools.partial(pick_kernel, nspan, nplane),
+                functools.partial(pick_kernel, nspan, nplane, width),
                 out_shape=[
-                    pltpu.VMEM((3 * nfaces, 6 * nfaces), BF16),
-                    pltpu.VMEM(((nblocks - 3) * nfaces, 10 * nfaces), BF16),
+                    pltpu.VMEM((3 * nfaces, 9 * nfaces), BF16),
+                    pltpu.VMEM(((nblocks - 3) * nfaces, 15 * nfaces), BF16),
+                    pltpu.VMEM((math.lcm(width, 128), 128), BF16),
                     pltpu.HBM(squares[0], F32),
                 ],
                 in_specs=[pl.BlockSpec(memory_space=pltpu.VMEM)] * 2,
-                out_specs=[pl.BlockSpec(memory_space=pltpu.VMEM)] * 2 + [pl.BlockSpec(memory_space=pl.ANY)],
+                out_specs=[pl.BlockSpec(memory_space=pltpu.VMEM)] * 3 + [pl.BlockSpec(memory_space=pl.ANY)],
                 scratch_shapes=[pltpu.SemaphoreType.DMA],
                 compiler_params=pltpu.CompilerParams(vmem_limit_bytes=VMEM_LIMIT),
                 cost_estimate=pl.CostEstimate(flops=0, bytes_accessed=4 * nfaces * area, transcendentals=0),
@@ -590,19 +595,19 @@
             return [
                 pltpu.VMEM((count * nfaces, chunk), F32),
                 pltpu.VMEM((nfaces, area), F32),
-                pltpu.VMEM((2 * nfaces * area // chunk, chunk), BF16),
+                pltpu.VMEM((3 * nfaces * area // chunk, chunk), BF16),
             ]
 
         early_sum, held = call(
             functools.partial(early_kernel, nblocks),
-            [blocks, picks[0], *near],
+            [blocks, picks[0], picks[2], *near],
             [shape, (nfaces, (nblocks - 3) * area)],
-            [pl.ANY] + [pltpu.VMEM] * 4,
+            [pl.ANY] + [pltpu.VMEM] * 5,
             [pltpu.VMEM((nfaces, 3 * area), F32)] + scratch(3) + [pltpu.SemaphoreType.DMA((6,))],
             flops=6 * nfaces * area,
         )
         last = step == ITERS - 1
-        args = [line_slot, held, picks[1], early_sum, *near, *far, *(us if last else us[-1:])]
+        args = [line_slot, held, picks[1], picks[2], early_sum, *near, *far, *(us if last else us[-1:])]
         out = call(
             functools.partial(late_kernel, nplane, last),
             args,

time: 67.6 us -> 67.9 us (level)
  transfers between devices with their start and end apart: 30 -> 30, of which waited for: 13 -> 13; matrix products, arithmetic and copies ran while one was open for 0% -> 0% of each run, Pallas kernels for 22% -> 21%
where the time goes in v10:
time: 67.9 us; the launch traced here: 67.6 us
  starting transfers between devices  25.1 us (37%)
  Pallas kernels  22.2 us (33%)
  blocking collectives  10.2 us (15%)
  waiting for transfers between devices  8.77 us (13%)
  between operations  1.08 us (2%)
    pallas_call x17, Pallas kernels, call(): pl.pallas_call(kernel, out_shape=[pltpu.VMEM(shape, F32) if pinned else j...  20.7 us
    ppermute x18, starting transfers between devices, exchange(): lax.ppermute(x, axis, [(i, partner(i, k, size)[0]) for i in range(size)])  12.8 us
    all_to_all x1, blocking collectives, add_up(): lax.all_to_all(rows, ('span', 'plane'), split_axis=0, concat_axis=0, tile...  10.2 us
    ppermute x3, starting transfers between devices, on_device(): other = lax.ppermute(mine, 'span', span_others)  9.01 us
    ppermute x18, waiting for transfers between devices, exchange(): lax.ppermute(x, axis, [(i, partner(i, k, size)[0]) for i in range(size)])  7.43 us
    ppermute x3, starting transfers between devices, on_device(): far = [other, lax.ppermute(mine, 'plane', plane_others)]  1.66 us
    ppermute x3, starting transfers between devices, on_device(): lax.ppermute(mine, 'span', span_pairs)  1.61 us
    pallas_call x1, Pallas kernels, on_device(): pl.pallas_call(functools.partial(pick_kernel, nspan, nplane, width), out_...  1.57 us
  transfers between devices with their start and end apart: 30, of which 13 were waited for; matrix products, arithmetic and copies ran while one was open for 0% of the time, Pallas kernels for 21%

profile of v10, /device:TPU:0, one launch (start us, length us, event | category | flops | bytes accessed | tf_op | source)
XLA Modules:
  0.0 67.6 jit_solution(16582221679955479072)
XLA Ops:
  0.7 0.8 %shard_map.86 = (f32[16,80]{1,0:T(8,128)S(1)}, f32[16,48]{1,0:T(8,128)S(1)}, f32[4,80]{1,0:T(4,128)S(1)}, f32[4,80]{1,0:T(4,128)S(1)}, f32[4,80]{1,0:T(4,128)S(1)}, /*index=5*/f32[4,80]{1,0:T(4,128)S(1)}) custom-call(s32[1,16]{1,0:T(1,128)} %refs_0_.5, f32[16,80]{1,0:T(8,128)} %bitcast.571), custom_call_target="tpu_custom_call" | custom-call | bytes 5184 | tf_op jit(solution)/shard_map/pallas_call | solution.py:491
  1.5 2.5 %collective-permute-start.16 = (f32[4,80]{1,0:T(4,128)S(1)}, f32[4,80]{1,0:T(4,128)S(1)}, u32[]{:S(2)}, u32[]{:S(2)}) collective-permute-start(f32[4,80]{1,0:T(4,128)S(1)} %get-tuple-element.701), channel_id=1, source_target_pairs={{0,3},{1,2},{2,1},{3,0},{4,7},{5,6},{6,5},{7,4},{8,11},{9,10},{10,... | collective-permute-start | bytes 3848 | tf_op jit(solution)/shard_map/ppermute | solution.py:153
  4.7 2.5 %shard_map.87 = (f32[1280,80]{1,0:T(8,128)S(1)}, f32[1280,80]{1,0:T(8,128)S(1)}, f32[1280,80]{1,0:T(8,128)S(1)}) custom-call(f32[16,6400]{1,0:T(8,128)} %low.5, f32[16,6400]{1,0:T(8,128)} %piv.5, f32[16,6400]{1,0:T(8,128)} %upp.1, f32[16,80]{1,0:T(8,128)S(1)} %get-tuple-element.705._.refs_10_.refs_0_), custom_call_target="tpu_custom_call" | custom-call | flops 8192000 | bytes 1233920 | tf_op jit(solution)/shard_map/pallas_call | solution.py:491
  7.6 0.9 %shard_map.88 = (f32[4,80]{1,0:T(4,128)S(1)}, f32[4,80]{1,0:T(4,128)S(1)}, f32[4,80]{1,0:T(4,128)S(1)}, f32[4,80]{1,0:T(4,128)S(1)}) custom-call(f32[4,80]{1,0:T(4,128)S(1)} %collective-permute-done.16.refs_0_, f32[4,80]{1,0:T(4,128)S(1)} %collective-permute-done.17.refs_1_, f32[4,80]{1,0:T(4,128)S(1)} %collective-permute-done.18.refs_2_, ...), custom_call_target="tpu_custom_call" | custom-call | flops 614400 | bytes 1233920 | tf_op jit(solution)/shard_map/pallas_call | solution.py:491
  8.5 1.2 %collective-permute-start.19 = (f32[4,80]{1,0:T(4,128)S(1)}, f32[4,80]{1,0:T(4,128)S(1)}, u32[]{:S(2)}, u32[]{:S(2)}) collective-permute-start(f32[4,80]{1,0:T(4,128)S(1)} %get-tuple-element.714), channel_id=1, source_target_pairs={{0,3},{1,2},{2,1},{3,0},{4,7},{5,6},{6,5},{7,4},{8,11},{9,10},{10,... | collective-permute-start | bytes 3848 | tf_op jit(solution)/shard_map/ppermute | solution.py:153
  10.4 1.6 %shard_map.89 = (bf16[48,144]{1,0:T(8,128)(2,1)S(1)}, bf16[128,240]{1,0:T(8,128)(2,1)S(1)}, bf16[640,128]{1,0:T(8,128)(2,1)S(1)}, f32[1280,80]{1,0:T(8,128)}) custom-call(s32[11,16]{1,0:T(8,128)} %columns_ref, f32[1280,80]{1,0:T(8,128)S(1)} %get-tuple-element.708.fold_ref), custom_call_target="tpu_custom_call" | custom-call | bytes 409600 | tf_op jit(solution)/shard_map/pallas_call | solution.py:567
  12.0 1.2 %collective-permute-done.20.refs_1_ = f32[4,80]{1,0:T(4,128)S(1)} collective-permute-done((f32[4,80]{1,0:T(4,128)S(1)}, f32[4,80]{1,0:T(4,128)S(1)}, u32[]{:S(2)}, u32[]{:S(2)}) %collective-permute-start.20) | collective-permute-done | bytes 1312 | tf_op jit(solution)/shard_map/ppermute | solution.py:153
  13.4 1.5 %collective-permute-start.22 = (f32[16,80]{1,0:T(8,128)S(1)}, f32[16,80]{1,0:T(8,128)S(1)}, u32[]{:S(2)}, u32[]{:S(2)}) collective-permute-start(f32[16,80]{1,0:T(8,128)S(1)} %shard_map.90.refs_0_.refs_5_.refs_4_), channel_id=1, source_target_pairs={{0,4},{4,0},{8,12},{12,8},{16,20},{20,16},{24,28},{28,24},{1,5},{5... | collective-permute-start | bytes 15368 | tf_op jit(solution)/shard_map/ppermute | solution.py:590
  14.9 3.6 %collective-permute-start.24 = (f32[16,80]{1,0:T(8,128)S(1)}, f32[16,80]{1,0:T(8,128)S(1)}, u32[]{:S(2)}, u32[]{:S(2)}) collective-permute-start(f32[16,80]{1,0:T(8,128)S(1)} %shard_map.90.refs_0_.refs_5_.refs_4_), channel_id=1, source_target_pairs={{0,28},{4,8},{8,4},{12,16},{16,12},{20,24},{24,20},{28,0},{1,29},{... | collective-permute-start | bytes 15368 | tf_op jit(solution)/shard_map/ppermute | solution.py:589
  19.0 2.5 %shard_map.91 = (f32[16,80]{1,0:T(8,128)S(1)}, f32[16,51200]{1,0:T(8,128)S(1)}) custom-call(f32[16,70400]{1,0:T(8,128)} %blocks.5, bf16[48,144]{1,0:T(8,128)(2,1)S(1)} %get-tuple-element.711.refs_4_.pick, bf16[640,128]{1,0:T(8,128)(2,1)S(1)} %get-tuple-element.712.refs_6_.seg.refs_3_, f32[16,80]{1,0:T(8,128)S(1)} %shard_map.90.refs_0_.refs_5_.refs_4_, ...), custom_call_target="tpu_custom_call" | custom-call | flops 614400 | bytes 4698624 | tf_op jit(solution)/shard_map/pallas_call | solution.py:491
  21.5 1.0 %shard_map.92 = (f32[16,80]{1,0:T(8,128)S(1)}, f32[4,80]{1,0:T(4,128)S(1)}, f32[4,80]{1,0:T(4,128)S(1)}, f32[4,80]{1,0:T(4,128)S(1)}, f32[4,80]{1,0:T(4,128)S(1)}) custom-call(s32[1,16]{1,0:T(1,128)S(1)} %copy-done.8, f32[16,51200]{1,0:T(8,128)S(1)} %get-tuple-element.718.refs_1_, bf16[128,240]{1,0:T(8,128)(2,1)S(1)} %get-tuple-element.717.refs_5_.refs_2_, ...), custom_call_target="tpu_custom_call" | custom-call | flops 2252800 | bytes 3537984 | tf_op jit(solution)/shard_map/pallas_call | solution.py:491
  22.5 1.2 %collective-permute-start.26 = (f32[4,80]{1,0:T(4,128)S(1)}, f32[4,80]{1,0:T(4,128)S(1)}, u32[]{:S(2)}, u32[]{:S(2)}) collective-permute-start(f32[4,80]{1,0:T(4,128)S(1)} %get-tuple-element.720), channel_id=1, source_target_pairs={{0,3},{1,2},{2,1},{3,0},{4,7},{5,6},{6,5},{7,4},{8,11},{9,10},{10,... | collective-permute-start | bytes 3848 | tf_op jit(solution)/shard_map/ppermute | solution.py:153
  24.4 1.5 %shard_map.93 = (f32[1280,80]{1,0:T(8,128)S(1)}, f32[1280,80]{1,0:T(8,128)S(1)}, f32[1280,80]{1,0:T(8,128)S(1)}) custom-call(f32[16,6400]{1,0:T(8,128)S(1)} %copy-done.1, f32[16,6400]{1,0:T(8,128)S(1)} %copy-done.2, f32[1280,80]{1,0:T(8,128)S(1)} %copy-done, f32[16,80]{1,0:T(8,128)S(1)} %get-tuple-element.725._.refs_10_.refs_11_.refs_1_), custom_call_target="tpu_custom_call" | custom-call | flops 102400 | bytes 1233920 | tf_op jit(solution)/shard_map/pallas_call | solution.py:491
  26.0 1.3 %collective-permute-done.27.refs_1_ = f32[4,80]{1,0:T(4,128)S(1)} collective-permute-done((f32[4,80]{1,0:T(4,128)S(1)}, f32[4,80]{1,0:T(4,128)S(1)}, u32[]{:S(2)}, u32[]{:S(2)}) %collective-permute-start.27) | collective-permute-done | bytes 1312 | tf_op jit(solution)/shard_map/ppermute | solution.py:153
  27.3 0.9 %shard_map.94 = (f32[4,80]{1,0:T(4,128)S(1)}, f32[4,80]{1,0:T(4,128)S(1)}, f32[4,80]{1,0:T(4,128)S(1)}, f32[4,80]{1,0:T(4,128)S(1)}) custom-call(f32[4,80]{1,0:T(4,128)S(1)} %collective-permute-done.26.refs_0_, f32[4,80]{1,0:T(4,128)S(1)} %collective-permute-done.27.refs_1_, f32[4,80]{1,0:T(4,128)S(1)} %collective-permute-done.28.refs_2_, ...), custom_call_target="tpu_custom_call" | custom-call | flops 614400 | bytes 1233920 | tf_op jit(solution)/shard_map/pallas_call | solution.py:491
  29.1 1.1 %collective-permute-start.31 = (f32[4,80]{1,0:T(4,128)S(1)}, f32[4,80]{1,0:T(4,128)S(1)}, u32[]{:S(2)}, u32[]{:S(2)}) collective-permute-start(f32[4,80]{1,0:T(4,128)S(1)} %get-tuple-element.731), channel_id=1, source_target_pairs={{0,1},{1,0},{2,3},{3,2},{4,5},{5,4},{6,7},{7,6},{8,9},{9,8},{10,11... | collective-permute-start | bytes 3848 | tf_op jit(solution)/shard_map/ppermute | solution.py:153
  30.2 1.1 %collective-permute-done.29.refs_0_ = f32[4,80]{1,0:T(4,128)S(1)} collective-permute-done((f32[4,80]{1,0:T(4,128)S(1)}, f32[4,80]{1,0:T(4,128)S(1)}, u32[]{:S(2)}, u32[]{:S(2)}) %collective-permute-start.29) | collective-permute-done | bytes 1312 | tf_op jit(solution)/shard_map/ppermute | solution.py:153
  32.2 2.7 %collective-permute-start.34 = (f32[16,80]{1,0:T(8,128)S(1)}, f32[16,80]{1,0:T(8,128)S(1)}, u32[]{:S(2)}, u32[]{:S(2)}) collective-permute-start(f32[16,80]{1,0:T(8,128)S(1)} %shard_map.95.refs_0_.refs_5_), channel_id=1, source_target_pairs={{0,28},{4,8},{8,4},{12,16},{16,12},{20,24},{24,20},{28,0},{1,29},{... | collective-permute-start | bytes 15368 | tf_op jit(solution)/shard_map/ppermute | solution.py:589
  35.8 2.5 %shard_map.96 = (f32[16,80]{1,0:T(8,128)S(1)}, f32[16,51200]{1,0:T(8,128)S(1)}) custom-call(f32[16,70400]{1,0:T(8,128)} %blocks.5, bf16[48,144]{1,0:T(8,128)(2,1)S(1)} %get-tuple-element.711.refs_4_.pick, bf16[640,128]{1,0:T(8,128)(2,1)S(1)} %get-tuple-element.712.refs_6_.seg.refs_3_, f32[16,80]{1,0:T(8,128)S(1)} %shard_map.95.refs_0_.refs_5_, ...), custom_call_target="tpu_custom_call" | custom-call | flops 614400 | bytes 4698624 | tf_op jit(solution)/shard_map/pallas_call | solution.py:491
  38.6 1.0 %shard_map.97 = (f32[16,80]{1,0:T(8,128)S(1)}, f32[4,80]{1,0:T(4,128)S(1)}, f32[4,80]{1,0:T(4,128)S(1)}, f32[4,80]{1,0:T(4,128)S(1)}, f32[4,80]{1,0:T(4,128)S(1)}) custom-call(s32[1,16]{1,0:T(1,128)S(1)} %copy-done.8, f32[16,51200]{1,0:T(8,128)S(1)} %get-tuple-element.733.refs_1_, bf16[128,240]{1,0:T(8,128)(2,1)S(1)} %get-tuple-element.717.refs_5_.refs_2_, ...), custom_call_target="tpu_custom_call" | custom-call | flops 2252800 | bytes 3537984 | tf_op jit(solution)/shard_map/pallas_call | solution.py:491
  40.2 0.9 %collective-permute-start.37 = (f32[4,80]{1,0:T(4,128)S(1)}, f32[4,80]{1,0:T(4,128)S(1)}, u32[]{:S(2)}, u32[]{:S(2)}) collective-permute-start(f32[4,80]{1,0:T(4,128)S(1)} %get-tuple-element.736), channel_id=1, source_target_pairs={{0,2},{1,3},{2,0},{3,1},{4,6},{5,7},{6,4},{7,5},{8,10},{9,11},{10,... | collective-permute-start | bytes 3848 | tf_op jit(solution)/shard_map/ppermute | solution.py:153
  41.5 1.5 %shard_map.98 = (f32[1280,80]{1,0:T(8,128)S(1)}, f32[1280,80]{1,0:T(8,128)S(1)}, f32[1280,80]{1,0:T(8,128)S(1)}) custom-call(f32[16,6400]{1,0:T(8,128)S(1)} %copy-done.1, f32[16,6400]{1,0:T(8,128)S(1)} %copy-done.2, f32[1280,80]{1,0:T(8,128)S(1)} %copy-done, f32[16,80]{1,0:T(8,128)S(1)} %get-tuple-element.739._.refs_12_.refs_2_), custom_call_target="tpu_custom_call" | custom-call | flops 102400 | bytes 1233920 | tf_op jit(solution)/shard_map/pallas_call | solution.py:491
  43.0 0.8 %collective-permute-done.37.refs_1_ = f32[4,80]{1,0:T(4,128)S(1)} collective-permute-done((f32[4,80]{1,0:T(4,128)S(1)}, f32[4,80]{1,0:T(4,128)S(1)}, u32[]{:S(2)}, u32[]{:S(2)}) %collective-permute-start.37) | collective-permute-done | bytes 1312 | tf_op jit(solution)/shard_map/ppermute | solution.py:153
  43.8 0.9 %shard_map.99 = (f32[4,80]{1,0:T(4,128)S(1)}, f32[4,80]{1,0:T(4,128)S(1)}, f32[4,80]{1,0:T(4,128)S(1)}, f32[4,80]{1,0:T(4,128)S(1)}) custom-call(f32[4,80]{1,0:T(4,128)S(1)} %collective-permute-done.36.refs_0_, f32[4,80]{1,0:T(4,128)S(1)} %collective-permute-done.37.refs_1_, f32[4,80]{1,0:T(4,128)S(1)} %collective-permute-done.38.refs_2_, ...), custom_call_target="tpu_custom_call" | custom-call | flops 614400 | bytes 1233920 | tf_op jit(solution)/shard_map/pallas_call | solution.py:491
  44.9 0.9 %collective-permute-start.40 = (f32[4,80]{1,0:T(4,128)S(1)}, f32[4,80]{1,0:T(4,128)S(1)}, u32[]{:S(2)}, u32[]{:S(2)}) collective-permute-start(f32[4,80]{1,0:T(4,128)S(1)} %get-tuple-element.744), channel_id=1, source_target_pairs={{0,2},{1,3},{2,0},{3,1},{4,6},{5,7},{6,4},{7,5},{8,10},{9,11},{10,... | collective-permute-start | bytes 3848 | tf_op jit(solution)/shard_map/ppermute | solution.py:153
  45.8 0.9 %collective-permute-start.41 = (f32[4,80]{1,0:T(4,128)S(1)}, f32[4,80]{1,0:T(4,128)S(1)}, u32[]{:S(2)}, u32[]{:S(2)}) collective-permute-start(f32[4,80]{1,0:T(4,128)S(1)} %get-tuple-element.745), channel_id=1, source_target_pairs={{0,1},{1,0},{2,3},{3,2},{4,5},{5,4},{6,7},{7,6},{8,9},{9,8},{10,11... | collective-permute-start | bytes 3848 | tf_op jit(solution)/shard_map/ppermute | solution.py:153
  46.7 1.1 %collective-permute-done.39.refs_0_ = f32[4,80]{1,0:T(4,128)S(1)} collective-permute-done((f32[4,80]{1,0:T(4,128)S(1)}, f32[4,80]{1,0:T(4,128)S(1)}, u32[]{:S(2)}, u32[]{:S(2)}) %collective-permute-start.39) | collective-permute-done | bytes 1312 | tf_op jit(solution)/shard_map/ppermute | solution.py:153
  48.8 2.7 %collective-permute-start.44 = (f32[16,80]{1,0:T(8,128)S(1)}, f32[16,80]{1,0:T(8,128)S(1)}, u32[]{:S(2)}, u32[]{:S(2)}) collective-permute-start(f32[16,80]{1,0:T(8,128)S(1)} %shard_map.100.refs_0_.refs_5_.refs_6_), channel_id=1, source_target_pairs={{0,28},{4,8},{8,4},{12,16},{16,12},{20,24},{24,20},{28,0},{1,29},{... | collective-permute-start | bytes 15368 | tf_op jit(solution)/shard_map/ppermute | solution.py:589
  52.3 2.5 %shard_map.101 = (f32[16,80]{1,0:T(8,128)S(1)}, f32[16,51200]{1,0:T(8,128)S(1)}) custom-call(f32[16,70400]{1,0:T(8,128)} %blocks.5, bf16[48,144]{1,0:T(8,128)(2,1)S(1)} %get-tuple-element.711.refs_4_.pick, bf16[640,128]{1,0:T(8,128)(2,1)S(1)} %get-tuple-element.712.refs_6_.seg.refs_3_, f32[16,80]{1,0:T(8,128)S(1)} %shard_map.100.refs_0_.refs_5_.refs_6_, ...), custom_call_target="tpu_custom_call" | custom-call | flops 614400 | bytes 4698624 | tf_op jit(solution)/shard_map/pallas_call | solution.py:491
  55.1 1.0 %shard_map.102 = (f32[16,80]{1,0:T(8,128)S(1)}, f32[1,128]{1,0:T(1,128)S(1)}) custom-call(s32[1,16]{1,0:T(1,128)S(1)} %copy-done.8, f32[16,51200]{1,0:T(8,128)S(1)} %get-tuple-element.747.refs_1_, bf16[128,240]{1,0:T(8,128)(2,1)S(1)} %get-tuple-element.717.refs_5_.refs_2_, bf16[640,128]{1,0:T(8,128)(2,1)S(1)} %get-tuple-element.712.refs_6_.seg.refs_3_, ...), custom_call_target="tpu_custom_call" | custom-call | flops 2252800 | bytes 3548224 | tf_op jit(solution)/shard_map/pallas_call | solution.py:491
  56.2 10.2 %all_to_all.112 = f32[32,1,128]{2,1,0:T(1,128)S(1)} all-to-all(f32[32,1,128]{2,1,0:T(1,128)S(1)} %broadcast_in_dim.83), channel_id=1, replica_groups=mesh['span'=8,'plane'=4] {'span','plane'}, dimensions={0} | all-to-all | bytes 32768 | tf_op jit(solution)/shard_map/all_to_all | solution.py:505
  66.4 0.8 %shard_map.103 = (f32[16,80]{1,0:T(8,128)}, f32[16,80]{1,0:T(8,128)}, f32[1,128]{1,0:T(1,128)S(1)}) custom-call(f32[32,128]{1,0:T(8,128)S(1)} %bitcast.558, f32[16,80]{1,0:T(8,128)S(1)} %get-tuple-element.705._.refs_10_.refs_0_, f32[16,80]{1,0:T(8,128)S(1)} %get-tuple-element.725._.refs_10_.refs_11_.refs_1_, ...), custom_call_target="tpu_custom_call" | custom-call | bytes 52224 | tf_op jit(solution)/shard_map/pallas_call | solution.py:491
  (63 shorter events, 9.7 us)
Async XLA Ops:
  1.5 5.7 %collective-permute-start.16 = (f32[4,80]{1,0:T(4,128)S(1)}, f32[4,80]{1,0:T(4,128)S(1)}, u32[]{:S(2)}, u32[]{:S(2)}) collective-permute-start(f32[4,80]{1,0:T(4,128)S(1)} %get-tuple-element.701), channel_id=1, source_target_pairs={{0,3},{1,2},{2,1},{3,0},{4,7},{5,6},{6,5},{7,4},{8,11},{9,10},{10,... | collective-permute-start | bytes 3848 | tf_op jit(solution)/shard_map/ppermute | solution.py:153
  4.0 3.6 %collective-permute-start.17 = (f32[4,80]{1,0:T(4,128)S(1)}, f32[4,80]{1,0:T(4,128)S(1)}, u32[]{:S(2)}, u32[]{:S(2)}) collective-permute-start(f32[4,80]{1,0:T(4,128)S(1)} %get-tuple-element.702), channel_id=1, source_target_pairs={{0,2},{1,3},{2,0},{3,1},{4,6},{5,7},{6,4},{7,5},{8,10},{9,11},{10,... | collective-permute-start | bytes 3848 | tf_op jit(solution)/shard_map/ppermute | solution.py:153
  4.6 2.9 %collective-permute-start.18 = (f32[4,80]{1,0:T(4,128)S(1)}, f32[4,80]{1,0:T(4,128)S(1)}, u32[]{:S(2)}, u32[]{:S(2)}) collective-permute-start(f32[4,80]{1,0:T(4,128)S(1)} %get-tuple-element.703), channel_id=1, source_target_pairs={{0,1},{1,0},{2,3},{3,2},{4,5},{5,4},{6,7},{7,6},{8,9},{9,8},{10,11... | collective-permute-start | bytes 3848 | tf_op jit(solution)/shard_map/ppermute | solution.py:153
  8.5 3.5 %collective-permute-start.19 = (f32[4,80]{1,0:T(4,128)S(1)}, f32[4,80]{1,0:T(4,128)S(1)}, u32[]{:S(2)}, u32[]{:S(2)}) collective-permute-start(f32[4,80]{1,0:T(4,128)S(1)} %get-tuple-element.714), channel_id=1, source_target_pairs={{0,3},{1,2},{2,1},{3,0},{4,7},{5,6},{6,5},{7,4},{8,11},{9,10},{10,... | collective-permute-start | bytes 3848 | tf_op jit(solution)/shard_map/ppermute | solution.py:153
  9.7 3.6 %collective-permute-start.20 = (f32[4,80]{1,0:T(4,128)S(1)}, f32[4,80]{1,0:T(4,128)S(1)}, u32[]{:S(2)}, u32[]{:S(2)}) collective-permute-start(f32[4,80]{1,0:T(4,128)S(1)} %get-tuple-element.715), channel_id=1, source_target_pairs={{0,2},{1,3},{2,0},{3,1},{4,6},{5,7},{6,4},{7,5},{8,10},{9,11},{10,... | collective-permute-start | bytes 3848 | tf_op jit(solution)/shard_map/ppermute | solution.py:153
  10.3 2.9 %collective-permute-start.21 = (f32[4,80]{1,0:T(4,128)S(1)}, f32[4,80]{1,0:T(4,128)S(1)}, u32[]{:S(2)}, u32[]{:S(2)}) collective-permute-start(f32[4,80]{1,0:T(4,128)S(1)} %get-tuple-element.716), channel_id=1, source_target_pairs={{0,1},{1,0},{2,3},{3,2},{4,5},{5,4},{6,7},{7,6},{8,9},{9,8},{10,11... | collective-permute-start | bytes 3848 | tf_op jit(solution)/shard_map/ppermute | solution.py:153
  13.4 5.6 %collective-permute-start.22 = (f32[16,80]{1,0:T(8,128)S(1)}, f32[16,80]{1,0:T(8,128)S(1)}, u32[]{:S(2)}, u32[]{:S(2)}) collective-permute-start(f32[16,80]{1,0:T(8,128)S(1)} %shard_map.90.refs_0_.refs_5_.refs_4_), channel_id=1, source_target_pairs={{0,4},{4,0},{8,12},{12,8},{16,20},{20,16},{24,28},{28,24},{1,5},{5... | collective-permute-start | bytes 15368 | tf_op jit(solution)/shard_map/ppermute | solution.py:590
  14.9 4.1 %collective-permute-start.23 = (f32[16,80]{1,0:T(8,128)S(1)}, f32[16,80]{1,0:T(8,128)S(1)}, u32[]{:S(2)}, u32[]{:S(2)}) collective-permute-start(f32[16,80]{1,0:T(8,128)S(1)} %shard_map.90.refs_0_.refs_5_.refs_4_), channel_id=1, source_target_pairs={{0,1},{1,0},{2,3},{3,2},{4,5},{5,4},{6,7},{7,6},{8,9},{9,8},{10,11... | collective-permute-start | bytes 15368 | tf_op jit(solution)/shard_map/ppermute | solution.py:590
  14.9 6.6 %collective-permute-start.24 = (f32[16,80]{1,0:T(8,128)S(1)}, f32[16,80]{1,0:T(8,128)S(1)}, u32[]{:S(2)}, u32[]{:S(2)}) collective-permute-start(f32[16,80]{1,0:T(8,128)S(1)} %shard_map.90.refs_0_.refs_5_.refs_4_), channel_id=1, source_target_pairs={{0,28},{4,8},{8,4},{12,16},{16,12},{20,24},{24,20},{28,0},{1,29},{... | collective-permute-start | bytes 15368 | tf_op jit(solution)/shard_map/ppermute | solution.py:589
  18.5 3.1 %collective-permute-start.25 = (f32[16,80]{1,0:T(8,128)S(1)}, f32[16,80]{1,0:T(8,128)S(1)}, u32[]{:S(2)}, u32[]{:S(2)}) collective-permute-start(f32[16,80]{1,0:T(8,128)S(1)} %shard_map.90.refs_0_.refs_5_.refs_4_), channel_id=1, source_target_pairs={{0,3},{1,2},{2,1},{3,0},{4,7},{5,6},{6,5},{7,4},{8,11},{9,10},{10,... | collective-permute-start | bytes 15368 | tf_op jit(solution)/shard_map/ppermute | solution.py:591
  22.5 3.5 %collective-permute-start.26 = (f32[4,80]{1,0:T(4,128)S(1)}, f32[4,80]{1,0:T(4,128)S(1)}, u32[]{:S(2)}, u32[]{:S(2)}) collective-permute-start(f32[4,80]{1,0:T(4,128)S(1)} %get-tuple-element.720), channel_id=1, source_target_pairs={{0,3},{1,2},{2,1},{3,0},{4,7},{5,6},{6,5},{7,4},{8,11},{9,10},{10,... | collective-permute-start | bytes 3848 | tf_op jit(solution)/shard_map/ppermute | solution.py:153
  23.7 3.6 %collective-permute-start.27 = (f32[4,80]{1,0:T(4,128)S(1)}, f32[4,80]{1,0:T(4,128)S(1)}, u32[]{:S(2)}, u32[]{:S(2)}) collective-permute-start(f32[4,80]{1,0:T(4,128)S(1)} %get-tuple-element.721), channel_id=1, source_target_pairs={{0,2},{1,3},{2,0},{3,1},{4,6},{5,7},{6,4},{7,5},{8,10},{9,11},{10,... | collective-permute-start | bytes 3848 | tf_op jit(solution)/shard_map/ppermute | solution.py:153
  24.4 2.9 %collective-permute-start.28 = (f32[4,80]{1,0:T(4,128)S(1)}, f32[4,80]{1,0:T(4,128)S(1)}, u32[]{:S(2)}, u32[]{:S(2)}) collective-permute-start(f32[4,80]{1,0:T(4,128)S(1)} %get-tuple-element.722), channel_id=1, source_target_pairs={{0,1},{1,0},{2,3},{3,2},{4,5},{5,4},{6,7},{7,6},{8,9},{9,8},{10,11... | collective-permute-start | bytes 3848 | tf_op jit(solution)/shard_map/ppermute | solution.py:153
  28.2 3.1 %collective-permute-start.29 = (f32[4,80]{1,0:T(4,128)S(1)}, f32[4,80]{1,0:T(4,128)S(1)}, u32[]{:S(2)}, u32[]{:S(2)}) collective-permute-start(f32[4,80]{1,0:T(4,128)S(1)} %get-tuple-element.729), channel_id=1, source_target_pairs={{0,3},{1,2},{2,1},{3,0},{4,7},{5,6},{6,5},{7,4},{8,11},{9,10},{10,... | collective-permute-start | bytes 3848 | tf_op jit(solution)/shard_map/ppermute | solution.py:153
  28.4 3.6 %collective-permute-start.30 = (f32[4,80]{1,0:T(4,128)S(1)}, f32[4,80]{1,0:T(4,128)S(1)}, u32[]{:S(2)}, u32[]{:S(2)}) collective-permute-start(f32[4,80]{1,0:T(4,128)S(1)} %get-tuple-element.730), channel_id=1, source_target_pairs={{0,2},{1,3},{2,0},{3,1},{4,6},{5,7},{6,4},{7,5},{8,10},{9,11},{10,... | collective-permute-start | bytes 3848 | tf_op jit(solution)/shard_map/ppermute | solution.py:153
  29.1 2.9 %collective-permute-start.31 = (f32[4,80]{1,0:T(4,128)S(1)}, f32[4,80]{1,0:T(4,128)S(1)}, u32[]{:S(2)}, u32[]{:S(2)}) collective-permute-start(f32[4,80]{1,0:T(4,128)S(1)} %get-tuple-element.731), channel_id=1, source_target_pairs={{0,1},{1,0},{2,3},{3,2},{4,5},{5,4},{6,7},{7,6},{8,9},{9,8},{10,11... | collective-permute-start | bytes 3848 | tf_op jit(solution)/shard_map/ppermute | solution.py:153
  32.1 3.7 %collective-permute-start.32 = (f32[16,80]{1,0:T(8,128)S(1)}, f32[16,80]{1,0:T(8,128)S(1)}, u32[]{:S(2)}, u32[]{:S(2)}) collective-permute-start(f32[16,80]{1,0:T(8,128)S(1)} %shard_map.95.refs_0_.refs_5_), channel_id=1, source_target_pairs={{0,4},{4,0},{8,12},{12,8},{16,20},{20,16},{24,28},{28,24},{1,5},{5... | collective-permute-start | bytes 15368 | tf_op jit(solution)/shard_map/ppermute | solution.py:590
  32.1 3.7 %collective-permute-start.33 = (f32[16,80]{1,0:T(8,128)S(1)}, f32[16,80]{1,0:T(8,128)S(1)}, u32[]{:S(2)}, u32[]{:S(2)}) collective-permute-start(f32[16,80]{1,0:T(8,128)S(1)} %shard_map.95.refs_0_.refs_5_), channel_id=1, source_target_pairs={{0,1},{1,0},{2,3},{3,2},{4,5},{5,4},{6,7},{7,6},{8,9},{9,8},{10,11... | collective-permute-start | bytes 15368 | tf_op jit(solution)/shard_map/ppermute | solution.py:590
  32.2 6.4 %collective-permute-start.34 = (f32[16,80]{1,0:T(8,128)S(1)}, f32[16,80]{1,0:T(8,128)S(1)}, u32[]{:S(2)}, u32[]{:S(2)}) collective-permute-start(f32[16,80]{1,0:T(8,128)S(1)} %shard_map.95.refs_0_.refs_5_), channel_id=1, source_target_pairs={{0,28},{4,8},{8,4},{12,16},{16,12},{20,24},{24,20},{28,0},{1,29},{... | collective-permute-start | bytes 15368 | tf_op jit(solution)/shard_map/ppermute | solution.py:589
  34.9 3.7 %collective-permute-start.35 = (f32[16,80]{1,0:T(8,128)S(1)}, f32[16,80]{1,0:T(8,128)S(1)}, u32[]{:S(2)}, u32[]{:S(2)}) collective-permute-start(f32[16,80]{1,0:T(8,128)S(1)} %shard_map.95.refs_0_.refs_5_), channel_id=1, source_target_pairs={{0,3},{1,2},{2,1},{3,0},{4,7},{5,6},{6,5},{7,4},{8,11},{9,10},{10,... | collective-permute-start | bytes 15368 | tf_op jit(solution)/shard_map/ppermute | solution.py:591
  38.6 28.7 %copy-start.5 = (f32[80,16]{0,1:T(8,128)S(1)}, f32[80,16]{0,1:T(8,128)}, u32[]{:S(2)}) copy-start(f32[80,16]{0,1:T(8,128)} %param.25) | copy-start | bytes 15364
  38.6 28.7 %copy-start.6 = (s32[11,16]{1,0:T(8,128)S(1)}, s32[11,16]{1,0:T(8,128)}, u32[]{:S(2)}) copy-start(s32[11,16]{1,0:T(8,128)} %columns_ref) | copy-start | bytes 2116
  39.6 3.5 %collective-permute-start.36 = (f32[4,80]{1,0:T(4,128)S(1)}, f32[4,80]{1,0:T(4,128)S(1)}, u32[]{:S(2)}, u32[]{:S(2)}) collective-permute-start(f32[4,80]{1,0:T(4,128)S(1)} %get-tuple-element.735), channel_id=1, source_target_pairs={{0,3},{1,2},{2,1},{3,0},{4,7},{5,6},{6,5},{7,4},{8,11},{9,10},{10,... | collective-permute-start | bytes 3848 | tf_op jit(solution)/shard_map/ppermute | solution.py:153
  40.2 3.6 %collective-permute-start.37 = (f32[4,80]{1,0:T(4,128)S(1)}, f32[4,80]{1,0:T(4,128)S(1)}, u32[]{:S(2)}, u32[]{:S(2)}) collective-permute-start(f32[4,80]{1,0:T(4,128)S(1)} %get-tuple-element.736), channel_id=1, source_target_pairs={{0,2},{1,3},{2,0},{3,1},{4,6},{5,7},{6,4},{7,5},{8,10},{9,11},{10,... | collective-permute-start | bytes 3848 | tf_op jit(solution)/shard_map/ppermute | solution.py:153
  41.1 2.7 %collective-permute-start.38 = (f32[4,80]{1,0:T(4,128)S(1)}, f32[4,80]{1,0:T(4,128)S(1)}, u32[]{:S(2)}, u32[]{:S(2)}) collective-permute-start(f32[4,80]{1,0:T(4,128)S(1)} %get-tuple-element.737), channel_id=1, source_target_pairs={{0,1},{1,0},{2,3},{3,2},{4,5},{5,4},{6,7},{7,6},{8,9},{9,8},{10,11... | collective-permute-start | bytes 3848 | tf_op jit(solution)/shard_map/ppermute | solution.py:153
  44.8 3.1 %collective-permute-start.39 = (f32[4,80]{1,0:T(4,128)S(1)}, f32[4,80]{1,0:T(4,128)S(1)}, u32[]{:S(2)}, u32[]{:S(2)}) collective-permute-start(f32[4,80]{1,0:T(4,128)S(1)} %get-tuple-element.743), channel_id=1, source_target_pairs={{0,3},{1,2},{2,1},{3,0},{4,7},{5,6},{6,5},{7,4},{8,11},{9,10},{10,... | collective-permute-start | bytes 3848 | tf_op jit(solution)/shard_map/ppermute | solution.py:153
  44.9 3.6 %collective-permute-start.40 = (f32[4,80]{1,0:T(4,128)S(1)}, f32[4,80]{1,0:T(4,128)S(1)}, u32[]{:S(2)}, u32[]{:S(2)}) collective-permute-start(f32[4,80]{1,0:T(4,128)S(1)} %get-tuple-element.744), channel_id=1, source_target_pairs={{0,2},{1,3},{2,0},{3,1},{4,6},{5,7},{6,4},{7,5},{8,10},{9,11},{10,... | collective-permute-start | bytes 3848 | tf_op jit(solution)/shard_map/ppermute | solution.py:153
  45.8 2.7 %collective-permute-start.41 = (f32[4,80]{1,0:T(4,128)S(1)}, f32[4,80]{1,0:T(4,128)S(1)}, u32[]{:S(2)}, u32[]{:S(2)}) collective-permute-start(f32[4,80]{1,0:T(4,128)S(1)} %get-tuple-element.745), channel_id=1, source_target_pairs={{0,1},{1,0},{2,3},{3,2},{4,5},{5,4},{6,7},{7,6},{8,9},{9,8},{10,11... | collective-permute-start | bytes 3848 | tf_op jit(solution)/shard_map/ppermute | solution.py:153
  48.7 3.7 %collective-permute-start.42 = (f32[16,80]{1,0:T(8,128)S(1)}, f32[16,80]{1,0:T(8,128)S(1)}, u32[]{:S(2)}, u32[]{:S(2)}) collective-permute-start(f32[16,80]{1,0:T(8,128)S(1)} %shard_map.100.refs_0_.refs_5_.refs_6_), channel_id=1, source_target_pairs={{0,4},{4,0},{8,12},{12,8},{16,20},{20,16},{24,28},{28,24},{1,5},{5... | collective-permute-start | bytes 15368 | tf_op jit(solution)/shard_map/ppermute | solution.py:590
  48.8 3.5 %collective-permute-start.43 = (f32[16,80]{1,0:T(8,128)S(1)}, f32[16,80]{1,0:T(8,128)S(1)}, u32[]{:S(2)}, u32[]{:S(2)}) collective-permute-start(f32[16,80]{1,0:T(8,128)S(1)} %shard_map.100.refs_0_.refs_5_.refs_6_), channel_id=1, source_target_pairs={{0,1},{1,0},{2,3},{3,2},{4,5},{5,4},{6,7},{7,6},{8,9},{9,8},{10,11... | collective-permute-start | bytes 15368 | tf_op jit(solution)/shard_map/ppermute | solution.py:590
  48.8 6.3 %collective-permute-start.44 = (f32[16,80]{1,0:T(8,128)S(1)}, f32[16,80]{1,0:T(8,128)S(1)}, u32[]{:S(2)}, u32[]{:S(2)}) collective-permute-start(f32[16,80]{1,0:T(8,128)S(1)} %shard_map.100.refs_0_.refs_5_.refs_6_), channel_id=1, source_target_pairs={{0,28},{4,8},{8,4},{12,16},{16,12},{20,24},{24,20},{28,0},{1,29},{... | collective-permute-start | bytes 15368 | tf_op jit(solution)/shard_map/ppermute | solution.py:589
  51.5 3.7 %collective-permute-start.45 = (f32[16,80]{1,0:T(8,128)S(1)}, f32[16,80]{1,0:T(8,128)S(1)}, u32[]{:S(2)}, u32[]{:S(2)}) collective-permute-start(f32[16,80]{1,0:T(8,128)S(1)} %shard_map.100.refs_0_.refs_5_.refs_6_), channel_id=1, source_target_pairs={{0,3},{1,2},{2,1},{3,0},{4,7},{5,6},{6,5},{7,4},{8,11},{9,10},{10,... | collective-permute-start | bytes 15368 | tf_op jit(solution)/shard_map/ppermute | solution.py:591
  (5 other events, 109.6 us)

commit v11 on v10

--- a/solution.py
+++ b/solution.py
@@ -390,6 +390,14 @@
     sum_ref[...] = add_products(work, x_scr, acc_scr, parts, seg, width)
     for copy in kept:
         copy.wait()
+
+
+def early_again_kernel(pick, seg, first, *refs):
+    faces, (sum_ref, x_scr, acc_scr, parts) = refs[:3], refs[3:]
+    width = faces[0].shape[1]
+    x_scr[...] = repeat_faces(faces, pick, x_scr.shape[1] // width)
+    work = [([(first, column) for column in range(0, first.shape[1], width * width)], None)]
+    sum_ref[...] = add_products(work, x_scr, acc_scr, parts, seg, width)
 
 
 def late_kernel(nplane, last, *refs):
@@ -532,7 +540,7 @@
     )
     us = [u_first]
     zs = []
-    picks = None
+    picks = held = first = None
     for step in range(ITERS):
         flat = pltpu.VMEM((nfaces, area), F32)
         squares = [(nfaces * width, width)] * 3
@@ -598,14 +606,19 @@
                 pltpu.VMEM((3 * nfaces * area // chunk, chunk), BF16),
             ]
 
-        early_sum, held = call(
-            functools.partial(early_kernel, nblocks),
-            [blocks, picks[0], picks[2], *near],
-            [shape, (nfaces, (nblocks - 3) * area)],
-            [pl.ANY] + [pltpu.VMEM] * 5,
-            [pltpu.VMEM((nfaces, 3 * area), F32)] + scratch(3) + [pltpu.SemaphoreType.DMA((6,))],
-            flops=6 * nfaces * area,
-        )
+        if step == 0:
+            early_sum, held, first = call(
+                functools.partial(early_kernel, nblocks),
+                [blocks, picks[0], picks[2], *near],
+                [shape, (nfaces, (nblocks - 3) * area), (nfaces, 3 * area)],
+                [pl.ANY] + [pltpu.VMEM] * 5,
+                scratch(3) + [pltpu.SemaphoreType.DMA((6,))],
+                flops=6 * nfaces * area,
+            )
+        else:
+            (early_sum,) = call(
+                early_again_kernel, [picks[0], picks[2], first, *near], [shape], scratch=scratch(3), flops=6 * nfaces * area
+            )
         last = step == ITERS - 1
         args = [line_slot, held, picks[1], picks[2], early_sum, *near, *far, *(us if last else us[-1:])]
         out = call(

time: 67.9 us -> 67.8 us (level)
  Pallas kernels: 22.2 us -> 18.7 us
  waiting for transfers between devices: 8.77 us -> 12.1 us
    ppermute x3, waiting for transfers between devices: 0.68 us -> 4.28 us  [on_device(): other = lax.ppermute(mine, 'span', span_others)]
    pallas_call x17, Pallas kernels: 20.7 us -> 17.1 us  [call(): pl.pallas_call(kernel, out_shape=[pltpu.VMEM(shape, F32) if pinned else j...]
  transfers between devices with their start and end apart: 30 -> 30, of which waited for: 13 -> 13; matrix products, arithmetic and copies ran while one was open for 0% -> 0% of each run, Pallas kernels for 21% -> 16%
where the time goes in v11:
time: 67.8 us; the launch traced here: 67.5 us
  starting transfers between devices  25.2 us (37%)
  Pallas kernels  18.7 us (28%)
  waiting for transfers between devices  12.1 us (18%)
  blocking collectives  10.2 us (15%)
  between operations  1.09 us (2%)
    pallas_call x17, Pallas kernels, call(): pl.pallas_call(kernel, out_shape=[pltpu.VMEM(shape, F32) if pinned else j...  17.1 us
    ppermute x18, starting transfers between devices, exchange(): lax.ppermute(x, axis, [(i, partner(i, k, size)[0]) for i in range(size)])  12.8 us
    all_to_all x1, blocking collectives, add_up(): lax.all_to_all(rows, ('span', 'plane'), split_axis=0, concat_axis=0, tile...  10.2 us
    ppermute x3, starting transfers between devices, on_device(): other = lax.ppermute(mine, 'span', span_others)  9.01 us
    ppermute x18, waiting for transfers between devices, exchange(): lax.ppermute(x, axis, [(i, partner(i, k, size)[0]) for i in range(size)])  7.31 us
    ppermute x3, waiting for transfers between devices, on_device(): other = lax.ppermute(mine, 'span', span_others)  4.28 us
    ppermute x3, starting transfers between devices, on_device(): lax.ppermute(mine, 'span', span_pairs)  1.73 us
    ppermute x3, starting transfers between devices, on_device(): far = [other, lax.ppermute(mine, 'plane', plane_others)]  1.65 us
  transfers between devices with their start and end apart: 30, of which 13 were waited for; matrix products, arithmetic and copies ran while one was open for 0% of the time, Pallas kernels for 16%

profile of v11, /device:TPU:0, one launch (start us, length us, event | category | flops | bytes accessed | tf_op | source)
XLA Modules:
  0.0 67.5 jit_solution(13720731757087184902)
XLA Ops:
  0.7 0.8 %shard_map.86 = (f32[16,80]{1,0:T(8,128)S(1)}, f32[16,48]{1,0:T(8,128)S(1)}, f32[4,80]{1,0:T(4,128)S(1)}, f32[4,80]{1,0:T(4,128)S(1)}, f32[4,80]{1,0:T(4,128)S(1)}, /*index=5*/f32[4,80]{1,0:T(4,128)S(1)}) custom-call(s32[1,16]{1,0:T(1,128)} %refs_0_.5, f32[16,80]{1,0:T(8,128)} %bitcast.571), custom_call_target="tpu_custom_call" | custom-call | bytes 5184 | tf_op jit(solution)/shard_map/pallas_call | solution.py:499
  1.5 2.5 %collective-permute-start.16 = (f32[4,80]{1,0:T(4,128)S(1)}, f32[4,80]{1,0:T(4,128)S(1)}, u32[]{:S(2)}, u32[]{:S(2)}) collective-permute-start(f32[4,80]{1,0:T(4,128)S(1)} %get-tuple-element.698), channel_id=1, source_target_pairs={{0,3},{1,2},{2,1},{3,0},{4,7},{5,6},{6,5},{7,4},{8,11},{9,10},{10,... | collective-permute-start | bytes 3848 | tf_op jit(solution)/shard_map/ppermute | solution.py:153
  4.7 2.5 %shard_map.87 = (f32[1280,80]{1,0:T(8,128)S(1)}, f32[1280,80]{1,0:T(8,128)S(1)}, f32[1280,80]{1,0:T(8,128)S(1)}) custom-call(f32[16,6400]{1,0:T(8,128)} %low.5, f32[16,6400]{1,0:T(8,128)} %piv.5, f32[16,6400]{1,0:T(8,128)} %upp.1, f32[16,80]{1,0:T(8,128)S(1)} %get-tuple-element.702._.refs_10_.refs_0_), custom_call_target="tpu_custom_call" | custom-call | flops 8192000 | bytes 1233920 | tf_op jit(solution)/shard_map/pallas_call | solution.py:499
  7.6 0.9 %shard_map.88 = (f32[4,80]{1,0:T(4,128)S(1)}, f32[4,80]{1,0:T(4,128)S(1)}, f32[4,80]{1,0:T(4,128)S(1)}, f32[4,80]{1,0:T(4,128)S(1)}) custom-call(f32[4,80]{1,0:T(4,128)S(1)} %collective-permute-done.16.refs_0_, f32[4,80]{1,0:T(4,128)S(1)} %collective-permute-done.17.refs_1_, f32[4,80]{1,0:T(4,128)S(1)} %collective-permute-done.18.refs_2_, ...), custom_call_target="tpu_custom_call" | custom-call | flops 614400 | bytes 1233920 | tf_op jit(solution)/shard_map/pallas_call | solution.py:499
  8.5 1.2 %collective-permute-start.19 = (f32[4,80]{1,0:T(4,128)S(1)}, f32[4,80]{1,0:T(4,128)S(1)}, u32[]{:S(2)}, u32[]{:S(2)}) collective-permute-start(f32[4,80]{1,0:T(4,128)S(1)} %get-tuple-element.711), channel_id=1, source_target_pairs={{0,3},{1,2},{2,1},{3,0},{4,7},{5,6},{6,5},{7,4},{8,11},{9,10},{10,... | collective-permute-start | bytes 3848 | tf_op jit(solution)/shard_map/ppermute | solution.py:153
  10.4 1.6 %shard_map.89 = (bf16[48,144]{1,0:T(8,128)(2,1)S(1)}, bf16[128,240]{1,0:T(8,128)(2,1)S(1)}, bf16[640,128]{1,0:T(8,128)(2,1)S(1)}, f32[1280,80]{1,0:T(8,128)}) custom-call(s32[11,16]{1,0:T(8,128)} %columns_ref, f32[1280,80]{1,0:T(8,128)S(1)} %get-tuple-element.705.fold_ref), custom_call_target="tpu_custom_call" | custom-call | bytes 409600 | tf_op jit(solution)/shard_map/pallas_call | solution.py:575
  12.0 1.2 %collective-permute-done.20.refs_1_ = f32[4,80]{1,0:T(4,128)S(1)} collective-permute-done((f32[4,80]{1,0:T(4,128)S(1)}, f32[4,80]{1,0:T(4,128)S(1)}, u32[]{:S(2)}, u32[]{:S(2)}) %collective-permute-start.20) | collective-permute-done | bytes 1312 | tf_op jit(solution)/shard_map/ppermute | solution.py:153
  13.4 1.5 %collective-permute-start.22 = (f32[16,80]{1,0:T(8,128)S(1)}, f32[16,80]{1,0:T(8,128)S(1)}, u32[]{:S(2)}, u32[]{:S(2)}) collective-permute-start(f32[16,80]{1,0:T(8,128)S(1)} %shard_map.90.refs_0_.refs_5_.refs_4_), channel_id=1, source_target_pairs={{0,4},{4,0},{8,12},{12,8},{16,20},{20,16},{24,28},{28,24},{1,5},{5... | collective-permute-start | bytes 15368 | tf_op jit(solution)/shard_map/ppermute | solution.py:598
  14.9 3.6 %collective-permute-start.24 = (f32[16,80]{1,0:T(8,128)S(1)}, f32[16,80]{1,0:T(8,128)S(1)}, u32[]{:S(2)}, u32[]{:S(2)}) collective-permute-start(f32[16,80]{1,0:T(8,128)S(1)} %shard_map.90.refs_0_.refs_5_.refs_4_), channel_id=1, source_target_pairs={{0,28},{4,8},{8,4},{12,16},{16,12},{20,24},{24,20},{28,0},{1,29},{... | collective-permute-start | bytes 15368 | tf_op jit(solution)/shard_map/ppermute | solution.py:597
  19.0 2.5 %shard_map.91 = (f32[16,80]{1,0:T(8,128)S(1)}, f32[16,51200]{1,0:T(8,128)S(1)}, f32[16,19200]{1,0:T(8,128)S(1)}) custom-call(f32[16,70400]{1,0:T(8,128)} %blocks.1, bf16[48,144]{1,0:T(8,128)(2,1)S(1)} %get-tuple-element.708.refs_4_.pick, bf16[640,128]{1,0:T(8,128)(2,1)S(1)} %get-tuple-element.709.refs_6_.seg.refs_3_, ...), custom_call_target="tpu_custom_call" | custom-call | flops 614400 | bytes 4698624 | tf_op jit(solution)/shard_map/pallas_call | solution.py:499
  21.5 0.9 %shard_map.92 = (f32[16,80]{1,0:T(8,128)S(1)}, f32[4,80]{1,0:T(4,128)S(1)}, f32[4,80]{1,0:T(4,128)S(1)}, f32[4,80]{1,0:T(4,128)S(1)}, f32[4,80]{1,0:T(4,128)S(1)}) custom-call(s32[1,16]{1,0:T(1,128)S(1)} %copy-done.8, f32[16,51200]{1,0:T(8,128)S(1)} %get-tuple-element.715.refs_1_, bf16[128,240]{1,0:T(8,128)(2,1)S(1)} %get-tuple-element.714.refs_5_.refs_2_, ...), custom_call_target="tpu_custom_call" | custom-call | flops 2252800 | bytes 3537984 | tf_op jit(solution)/shard_map/pallas_call | solution.py:499
  22.5 1.2 %collective-permute-start.26 = (f32[4,80]{1,0:T(4,128)S(1)}, f32[4,80]{1,0:T(4,128)S(1)}, u32[]{:S(2)}, u32[]{:S(2)}) collective-permute-start(f32[4,80]{1,0:T(4,128)S(1)} %get-tuple-element.718), channel_id=1, source_target_pairs={{0,3},{1,2},{2,1},{3,0},{4,7},{5,6},{6,5},{7,4},{8,11},{9,10},{10,... | collective-permute-start | bytes 3848 | tf_op jit(solution)/shard_map/ppermute | solution.py:153
  24.4 1.5 %shard_map.93 = (f32[1280,80]{1,0:T(8,128)S(1)}, f32[1280,80]{1,0:T(8,128)S(1)}, f32[1280,80]{1,0:T(8,128)S(1)}) custom-call(f32[16,6400]{1,0:T(8,128)S(1)} %copy-done.1, f32[16,6400]{1,0:T(8,128)S(1)} %copy-done.2, f32[1280,80]{1,0:T(8,128)S(1)} %copy-done, f32[16,80]{1,0:T(8,128)S(1)} %get-tuple-element.723._.refs_10_.refs_11_.refs_1_), custom_call_target="tpu_custom_call" | custom-call | flops 102400 | bytes 1233920 | tf_op jit(solution)/shard_map/pallas_call | solution.py:499
  26.0 1.3 %collective-permute-done.27.refs_1_ = f32[4,80]{1,0:T(4,128)S(1)} collective-permute-done((f32[4,80]{1,0:T(4,128)S(1)}, f32[4,80]{1,0:T(4,128)S(1)}, u32[]{:S(2)}, u32[]{:S(2)}) %collective-permute-start.27) | collective-permute-done | bytes 1312 | tf_op jit(solution)/shard_map/ppermute | solution.py:153
  27.3 0.9 %shard_map.94 = (f32[4,80]{1,0:T(4,128)S(1)}, f32[4,80]{1,0:T(4,128)S(1)}, f32[4,80]{1,0:T(4,128)S(1)}, f32[4,80]{1,0:T(4,128)S(1)}) custom-call(f32[4,80]{1,0:T(4,128)S(1)} %collective-permute-done.26.refs_0_, f32[4,80]{1,0:T(4,128)S(1)} %collective-permute-done.27.refs_1_, f32[4,80]{1,0:T(4,128)S(1)} %collective-permute-done.28.refs_2_, ...), custom_call_target="tpu_custom_call" | custom-call | flops 614400 | bytes 1233920 | tf_op jit(solution)/shard_map/pallas_call | solution.py:499
  29.1 1.1 %collective-permute-start.31 = (f32[4,80]{1,0:T(4,128)S(1)}, f32[4,80]{1,0:T(4,128)S(1)}, u32[]{:S(2)}, u32[]{:S(2)}) collective-permute-start(f32[4,80]{1,0:T(4,128)S(1)} %get-tuple-element.729), channel_id=1, source_target_pairs={{0,1},{1,0},{2,3},{3,2},{4,5},{5,4},{6,7},{7,6},{8,9},{9,8},{10,11... | collective-permute-start | bytes 3848 | tf_op jit(solution)/shard_map/ppermute | solution.py:153
  30.2 1.1 %collective-permute-done.29.refs_0_ = f32[4,80]{1,0:T(4,128)S(1)} collective-permute-done((f32[4,80]{1,0:T(4,128)S(1)}, f32[4,80]{1,0:T(4,128)S(1)}, u32[]{:S(2)}, u32[]{:S(2)}) %collective-permute-start.29) | collective-permute-done | bytes 1312 | tf_op jit(solution)/shard_map/ppermute | solution.py:153
  32.2 2.7 %collective-permute-start.34 = (f32[16,80]{1,0:T(8,128)S(1)}, f32[16,80]{1,0:T(8,128)S(1)}, u32[]{:S(2)}, u32[]{:S(2)}) collective-permute-start(f32[16,80]{1,0:T(8,128)S(1)} %shard_map.95.refs_0_.refs_5_), channel_id=1, source_target_pairs={{0,28},{4,8},{8,4},{12,16},{16,12},{20,24},{24,20},{28,0},{1,29},{... | collective-permute-start | bytes 15368 | tf_op jit(solution)/shard_map/ppermute | solution.py:597
  35.8 0.7 %shard_map.96.refs_4_ = f32[16,80]{1,0:T(8,128)S(1)} custom-call(bf16[48,144]{1,0:T(8,128)(2,1)S(1)} %get-tuple-element.708.refs_4_.pick, bf16[640,128]{1,0:T(8,128)(2,1)S(1)} %get-tuple-element.709.refs_6_.seg.refs_3_, f32[16,19200]{1,0:T(8,128)S(1)} %get-tuple-element.716.first, f32[16,80]{1,0:T(8,128)S(1)} %shard_map.95.refs_0_.refs_5_, ...), custom_call_target="tpu_custom_call" | custom-call | flops 614400 | bytes 1421824 | tf_op jit(solution)/shard_map/pallas_call | solution.py:499
  36.5 2.1 %collective-permute-done.34.refs_8_ = f32[16,80]{1,0:T(8,128)S(1)} collective-permute-done((f32[16,80]{1,0:T(8,128)S(1)}, f32[16,80]{1,0:T(8,128)S(1)}, u32[]{:S(2)}, u32[]{:S(2)}) %collective-permute-start.34) | collective-permute-done | bytes 5152 | tf_op jit(solution)/shard_map/ppermute | solution.py:597
  38.6 0.9 %shard_map.97 = (f32[16,80]{1,0:T(8,128)S(1)}, f32[4,80]{1,0:T(4,128)S(1)}, f32[4,80]{1,0:T(4,128)S(1)}, f32[4,80]{1,0:T(4,128)S(1)}, f32[4,80]{1,0:T(4,128)S(1)}) custom-call(s32[1,16]{1,0:T(1,128)S(1)} %copy-done.8, f32[16,51200]{1,0:T(8,128)S(1)} %get-tuple-element.715.refs_1_, bf16[128,240]{1,0:T(8,128)(2,1)S(1)} %get-tuple-element.714.refs_5_.refs_2_, ...), custom_call_target="tpu_custom_call" | custom-call | flops 2252800 | bytes 3537984 | tf_op jit(solution)/shard_map/pallas_call | solution.py:499
  39.9 1.2 %collective-permute-start.37 = (f32[4,80]{1,0:T(4,128)S(1)}, f32[4,80]{1,0:T(4,128)S(1)}, u32[]{:S(2)}, u32[]{:S(2)}) collective-permute-start(f32[4,80]{1,0:T(4,128)S(1)} %get-tuple-element.732), channel_id=1, source_target_pairs={{0,2},{1,3},{2,0},{3,1},{4,6},{5,7},{6,4},{7,5},{8,10},{9,11},{10,... | collective-permute-start | bytes 3848 | tf_op jit(solution)/shard_map/ppermute | solution.py:153
  41.5 1.5 %shard_map.98 = (f32[1280,80]{1,0:T(8,128)S(1)}, f32[1280,80]{1,0:T(8,128)S(1)}, f32[1280,80]{1,0:T(8,128)S(1)}) custom-call(f32[16,6400]{1,0:T(8,128)S(1)} %copy-done.1, f32[16,6400]{1,0:T(8,128)S(1)} %copy-done.2, f32[1280,80]{1,0:T(8,128)S(1)} %copy-done, f32[16,80]{1,0:T(8,128)S(1)} %get-tuple-element.735._.refs_12_.refs_2_), custom_call_target="tpu_custom_call" | custom-call | flops 102400 | bytes 1233920 | tf_op jit(solution)/shard_map/pallas_call | solution.py:499
  43.5 0.9 %shard_map.99 = (f32[4,80]{1,0:T(4,128)S(1)}, f32[4,80]{1,0:T(4,128)S(1)}, f32[4,80]{1,0:T(4,128)S(1)}, f32[4,80]{1,0:T(4,128)S(1)}) custom-call(f32[4,80]{1,0:T(4,128)S(1)} %collective-permute-done.36.refs_0_, f32[4,80]{1,0:T(4,128)S(1)} %collective-permute-done.37.refs_1_, f32[4,80]{1,0:T(4,128)S(1)} %collective-permute-done.38.refs_2_, ...), custom_call_target="tpu_custom_call" | custom-call | flops 614400 | bytes 1233920 | tf_op jit(solution)/shard_map/pallas_call | solution.py:499
  44.8 1.0 %collective-permute-start.40 = (f32[4,80]{1,0:T(4,128)S(1)}, f32[4,80]{1,0:T(4,128)S(1)}, u32[]{:S(2)}, u32[]{:S(2)}) collective-permute-start(f32[4,80]{1,0:T(4,128)S(1)} %get-tuple-element.740), channel_id=1, source_target_pairs={{0,2},{1,3},{2,0},{3,1},{4,6},{5,7},{6,4},{7,5},{8,10},{9,11},{10,... | collective-permute-start | bytes 3848 | tf_op jit(solution)/shard_map/ppermute | solution.py:153
  46.3 1.1 %collective-permute-done.39.refs_0_ = f32[4,80]{1,0:T(4,128)S(1)} collective-permute-done((f32[4,80]{1,0:T(4,128)S(1)}, f32[4,80]{1,0:T(4,128)S(1)}, u32[]{:S(2)}, u32[]{:S(2)}) %collective-permute-start.39) | collective-permute-done | bytes 1312 | tf_op jit(solution)/shard_map/ppermute | solution.py:153
  47.4 0.9 %collective-permute-done.40.refs_1_ = f32[4,80]{1,0:T(4,128)S(1)} collective-permute-done((f32[4,80]{1,0:T(4,128)S(1)}, f32[4,80]{1,0:T(4,128)S(1)}, u32[]{:S(2)}, u32[]{:S(2)}) %collective-permute-start.40) | collective-permute-done | bytes 1312 | tf_op jit(solution)/shard_map/ppermute | solution.py:153
  48.7 2.7 %collective-permute-start.44 = (f32[16,80]{1,0:T(8,128)S(1)}, f32[16,80]{1,0:T(8,128)S(1)}, u32[]{:S(2)}, u32[]{:S(2)}) collective-permute-start(f32[16,80]{1,0:T(8,128)S(1)} %shard_map.100.refs_0_.refs_5_.refs_6_), channel_id=1, source_target_pairs={{0,28},{4,8},{8,4},{12,16},{16,12},{20,24},{24,20},{28,0},{1,29},{... | collective-permute-start | bytes 15368 | tf_op jit(solution)/shard_map/ppermute | solution.py:597
  52.9 2.2 %collective-permute-done.44.refs_8_ = f32[16,80]{1,0:T(8,128)S(1)} collective-permute-done((f32[16,80]{1,0:T(8,128)S(1)}, f32[16,80]{1,0:T(8,128)S(1)}, u32[]{:S(2)}, u32[]{:S(2)}) %collective-permute-start.44) | collective-permute-done | bytes 5152 | tf_op jit(solution)/shard_map/ppermute | solution.py:597
  55.1 1.0 %shard_map.102 = (f32[16,80]{1,0:T(8,128)S(1)}, f32[1,128]{1,0:T(1,128)S(1)}) custom-call(s32[1,16]{1,0:T(1,128)S(1)} %copy-done.8, f32[16,51200]{1,0:T(8,128)S(1)} %get-tuple-element.715.refs_1_, bf16[128,240]{1,0:T(8,128)(2,1)S(1)} %get-tuple-element.714.refs_5_.refs_2_, bf16[640,128]{1,0:T(8,128)(2,1)S(1)} %get-tuple-element.709.refs_6_.seg.refs_3_, ...), custom_call_target="tpu_custom_call" | custom-call | flops 2252800 | bytes 3548224 | tf_op jit(solution)/shard_map/pallas_call | solution.py:499
  56.1 10.2 %all_to_all.112 = f32[32,1,128]{2,1,0:T(1,128)S(1)} all-to-all(f32[32,1,128]{2,1,0:T(1,128)S(1)} %broadcast_in_dim.83), channel_id=1, replica_groups=mesh['span'=8,'plane'=4] {'span','plane'}, dimensions={0} | all-to-all | bytes 32768 | tf_op jit(solution)/shard_map/all_to_all | solution.py:513
  66.3 0.8 %shard_map.103 = (f32[16,80]{1,0:T(8,128)}, f32[16,80]{1,0:T(8,128)}, f32[1,128]{1,0:T(1,128)S(1)}) custom-call(f32[32,128]{1,0:T(8,128)S(1)} %bitcast.558, f32[16,80]{1,0:T(8,128)S(1)} %get-tuple-element.702._.refs_10_.refs_0_, f32[16,80]{1,0:T(8,128)S(1)} %get-tuple-element.723._.refs_10_.refs_11_.refs_1_, ...), custom_call_target="tpu_custom_call" | custom-call | bytes 52224 | tf_op jit(solution)/shard_map/pallas_call | solution.py:499
  (63 shorter events, 9.9 us)
Async XLA Ops:
  1.5 5.7 %collective-permute-start.16 = (f32[4,80]{1,0:T(4,128)S(1)}, f32[4,80]{1,0:T(4,128)S(1)}, u32[]{:S(2)}, u32[]{:S(2)}) collective-permute-start(f32[4,80]{1,0:T(4,128)S(1)} %get-tuple-element.698), channel_id=1, source_target_pairs={{0,3},{1,2},{2,1},{3,0},{4,7},{5,6},{6,5},{7,4},{8,11},{9,10},{10,... | collective-permute-start | bytes 3848 | tf_op jit(solution)/shard_map/ppermute | solution.py:153
  4.0 3.6 %collective-permute-start.17 = (f32[4,80]{1,0:T(4,128)S(1)}, f32[4,80]{1,0:T(4,128)S(1)}, u32[]{:S(2)}, u32[]{:S(2)}) collective-permute-start(f32[4,80]{1,0:T(4,128)S(1)} %get-tuple-element.699), channel_id=1, source_target_pairs={{0,2},{1,3},{2,0},{3,1},{4,6},{5,7},{6,4},{7,5},{8,10},{9,11},{10,... | collective-permute-start | bytes 3848 | tf_op jit(solution)/shard_map/ppermute | solution.py:153
  4.6 2.9 %collective-permute-start.18 = (f32[4,80]{1,0:T(4,128)S(1)}, f32[4,80]{1,0:T(4,128)S(1)}, u32[]{:S(2)}, u32[]{:S(2)}) collective-permute-start(f32[4,80]{1,0:T(4,128)S(1)} %get-tuple-element.700), channel_id=1, source_target_pairs={{0,1},{1,0},{2,3},{3,2},{4,5},{5,4},{6,7},{7,6},{8,9},{9,8},{10,11... | collective-permute-start | bytes 3848 | tf_op jit(solution)/shard_map/ppermute | solution.py:153
  8.5 3.5 %collective-permute-start.19 = (f32[4,80]{1,0:T(4,128)S(1)}, f32[4,80]{1,0:T(4,128)S(1)}, u32[]{:S(2)}, u32[]{:S(2)}) collective-permute-start(f32[4,80]{1,0:T(4,128)S(1)} %get-tuple-element.711), channel_id=1, source_target_pairs={{0,3},{1,2},{2,1},{3,0},{4,7},{5,6},{6,5},{7,4},{8,11},{9,10},{10,... | collective-permute-start | bytes 3848 | tf_op jit(solution)/shard_map/ppermute | solution.py:153
  9.7 3.6 %collective-permute-start.20 = (f32[4,80]{1,0:T(4,128)S(1)}, f32[4,80]{1,0:T(4,128)S(1)}, u32[]{:S(2)}, u32[]{:S(2)}) collective-permute-start(f32[4,80]{1,0:T(4,128)S(1)} %get-tuple-element.712), channel_id=1, source_target_pairs={{0,2},{1,3},{2,0},{3,1},{4,6},{5,7},{6,4},{7,5},{8,10},{9,11},{10,... | collective-permute-start | bytes 3848 | tf_op jit(solution)/shard_map/ppermute | solution.py:153
  10.3 2.9 %collective-permute-start.21 = (f32[4,80]{1,0:T(4,128)S(1)}, f32[4,80]{1,0:T(4,128)S(1)}, u32[]{:S(2)}, u32[]{:S(2)}) collective-permute-start(f32[4,80]{1,0:T(4,128)S(1)} %get-tuple-element.713), channel_id=1, source_target_pairs={{0,1},{1,0},{2,3},{3,2},{4,5},{5,4},{6,7},{7,6},{8,9},{9,8},{10,11... | collective-permute-start | bytes 3848 | tf_op jit(solution)/shard_map/ppermute | solution.py:153
  13.4 5.6 %collective-permute-start.22 = (f32[16,80]{1,0:T(8,128)S(1)}, f32[16,80]{1,0:T(8,128)S(1)}, u32[]{:S(2)}, u32[]{:S(2)}) collective-permute-start(f32[16,80]{1,0:T(8,128)S(1)} %shard_map.90.refs_0_.refs_5_.refs_4_), channel_id=1, source_target_pairs={{0,4},{4,0},{8,12},{12,8},{16,20},{20,16},{24,28},{28,24},{1,5},{5... | collective-permute-start | bytes 15368 | tf_op jit(solution)/shard_map/ppermute | solution.py:598
  14.9 4.1 %collective-permute-start.23 = (f32[16,80]{1,0:T(8,128)S(1)}, f32[16,80]{1,0:T(8,128)S(1)}, u32[]{:S(2)}, u32[]{:S(2)}) collective-permute-start(f32[16,80]{1,0:T(8,128)S(1)} %shard_map.90.refs_0_.refs_5_.refs_4_), channel_id=1, source_target_pairs={{0,1},{1,0},{2,3},{3,2},{4,5},{5,4},{6,7},{7,6},{8,9},{9,8},{10,11... | collective-permute-start | bytes 15368 | tf_op jit(solution)/shard_map/ppermute | solution.py:598
  14.9 6.5 %collective-permute-start.24 = (f32[16,80]{1,0:T(8,128)S(1)}, f32[16,80]{1,0:T(8,128)S(1)}, u32[]{:S(2)}, u32[]{:S(2)}) collective-permute-start(f32[16,80]{1,0:T(8,128)S(1)} %shard_map.90.refs_0_.refs_5_.refs_4_), channel_id=1, source_target_pairs={{0,28},{4,8},{8,4},{12,16},{16,12},{20,24},{24,20},{28,0},{1,29},{... | collective-permute-start | bytes 15368 | tf_op jit(solution)/shard_map/ppermute | solution.py:597
  18.5 3.1 %collective-permute-start.25 = (f32[16,80]{1,0:T(8,128)S(1)}, f32[16,80]{1,0:T(8,128)S(1)}, u32[]{:S(2)}, u32[]{:S(2)}) collective-permute-start(f32[16,80]{1,0:T(8,128)S(1)} %shard_map.90.refs_0_.refs_5_.refs_4_), channel_id=1, source_target_pairs={{0,3},{1,2},{2,1},{3,0},{4,7},{5,6},{6,5},{7,4},{8,11},{9,10},{10,... | collective-permute-start | bytes 15368 | tf_op jit(solution)/shard_map/ppermute | solution.py:599
  22.5 3.5 %collective-permute-start.26 = (f32[4,80]{1,0:T(4,128)S(1)}, f32[4,80]{1,0:T(4,128)S(1)}, u32[]{:S(2)}, u32[]{:S(2)}) collective-permute-start(f32[4,80]{1,0:T(4,128)S(1)} %get-tuple-element.718), channel_id=1, source_target_pairs={{0,3},{1,2},{2,1},{3,0},{4,7},{5,6},{6,5},{7,4},{8,11},{9,10},{10,... | collective-permute-start | bytes 3848 | tf_op jit(solution)/shard_map/ppermute | solution.py:153
  23.7 3.6 %collective-permute-start.27 = (f32[4,80]{1,0:T(4,128)S(1)}, f32[4,80]{1,0:T(4,128)S(1)}, u32[]{:S(2)}, u32[]{:S(2)}) collective-permute-start(f32[4,80]{1,0:T(4,128)S(1)} %get-tuple-element.719), channel_id=1, source_target_pairs={{0,2},{1,3},{2,0},{3,1},{4,6},{5,7},{6,4},{7,5},{8,10},{9,11},{10,... | collective-permute-start | bytes 3848 | tf_op jit(solution)/shard_map/ppermute | solution.py:153
  24.4 2.9 %collective-permute-start.28 = (f32[4,80]{1,0:T(4,128)S(1)}, f32[4,80]{1,0:T(4,128)S(1)}, u32[]{:S(2)}, u32[]{:S(2)}) collective-permute-start(f32[4,80]{1,0:T(4,128)S(1)} %get-tuple-element.720), channel_id=1, source_target_pairs={{0,1},{1,0},{2,3},{3,2},{4,5},{5,4},{6,7},{7,6},{8,9},{9,8},{10,11... | collective-permute-start | bytes 3848 | tf_op jit(solution)/shard_map/ppermute | solution.py:153
  28.2 39.0 %copy-start.3 = (f32[16,6400]{1,0:T(8,128)S(1)}, f32[16,6400]{1,0:T(8,128)}, u32[]{:S(2)}) copy-start(f32[16,6400]{1,0:T(8,128)} %upp.1) | copy-start | bytes 1228804
  28.2 39.0 %copy-start.5 = (f32[80,16]{0,1:T(8,128)S(1)}, f32[80,16]{0,1:T(8,128)}, u32[]{:S(2)}) copy-start(f32[80,16]{0,1:T(8,128)} %param.25) | copy-start | bytes 15364
  28.2 3.1 %collective-permute-start.29 = (f32[4,80]{1,0:T(4,128)S(1)}, f32[4,80]{1,0:T(4,128)S(1)}, u32[]{:S(2)}, u32[]{:S(2)}) collective-permute-start(f32[4,80]{1,0:T(4,128)S(1)} %get-tuple-element.727), channel_id=1, source_target_pairs={{0,3},{1,2},{2,1},{3,0},{4,7},{5,6},{6,5},{7,4},{8,11},{9,10},{10,... | collective-permute-start | bytes 3848 | tf_op jit(solution)/shard_map/ppermute | solution.py:153
  28.4 3.6 %collective-permute-start.30 = (f32[4,80]{1,0:T(4,128)S(1)}, f32[4,80]{1,0:T(4,128)S(1)}, u32[]{:S(2)}, u32[]{:S(2)}) collective-permute-start(f32[4,80]{1,0:T(4,128)S(1)} %get-tuple-element.728), channel_id=1, source_target_pairs={{0,2},{1,3},{2,0},{3,1},{4,6},{5,7},{6,4},{7,5},{8,10},{9,11},{10,... | collective-permute-start | bytes 3848 | tf_op jit(solution)/shard_map/ppermute | solution.py:153
  29.1 2.9 %collective-permute-start.31 = (f32[4,80]{1,0:T(4,128)S(1)}, f32[4,80]{1,0:T(4,128)S(1)}, u32[]{:S(2)}, u32[]{:S(2)}) collective-permute-start(f32[4,80]{1,0:T(4,128)S(1)} %get-tuple-element.729), channel_id=1, source_target_pairs={{0,1},{1,0},{2,3},{3,2},{4,5},{5,4},{6,7},{7,6},{8,9},{9,8},{10,11... | collective-permute-start | bytes 3848 | tf_op jit(solution)/shard_map/ppermute | solution.py:153
  32.1 3.7 %collective-permute-start.32 = (f32[16,80]{1,0:T(8,128)S(1)}, f32[16,80]{1,0:T(8,128)S(1)}, u32[]{:S(2)}, u32[]{:S(2)}) collective-permute-start(f32[16,80]{1,0:T(8,128)S(1)} %shard_map.95.refs_0_.refs_5_), channel_id=1, source_target_pairs={{0,4},{4,0},{8,12},{12,8},{16,20},{20,16},{24,28},{28,24},{1,5},{5... | collective-permute-start | bytes 15368 | tf_op jit(solution)/shard_map/ppermute | solution.py:598
  32.1 3.7 %collective-permute-start.33 = (f32[16,80]{1,0:T(8,128)S(1)}, f32[16,80]{1,0:T(8,128)S(1)}, u32[]{:S(2)}, u32[]{:S(2)}) collective-permute-start(f32[16,80]{1,0:T(8,128)S(1)} %shard_map.95.refs_0_.refs_5_), channel_id=1, source_target_pairs={{0,1},{1,0},{2,3},{3,2},{4,5},{5,4},{6,7},{7,6},{8,9},{9,8},{10,11... | collective-permute-start | bytes 15368 | tf_op jit(solution)/shard_map/ppermute | solution.py:598
  32.2 6.4 %collective-permute-start.34 = (f32[16,80]{1,0:T(8,128)S(1)}, f32[16,80]{1,0:T(8,128)S(1)}, u32[]{:S(2)}, u32[]{:S(2)}) collective-permute-start(f32[16,80]{1,0:T(8,128)S(1)} %shard_map.95.refs_0_.refs_5_), channel_id=1, source_target_pairs={{0,28},{4,8},{8,4},{12,16},{16,12},{20,24},{24,20},{28,0},{1,29},{... | collective-permute-start | bytes 15368 | tf_op jit(solution)/shard_map/ppermute | solution.py:597
  34.9 3.7 %collective-permute-start.35 = (f32[16,80]{1,0:T(8,128)S(1)}, f32[16,80]{1,0:T(8,128)S(1)}, u32[]{:S(2)}, u32[]{:S(2)}) collective-permute-start(f32[16,80]{1,0:T(8,128)S(1)} %shard_map.95.refs_0_.refs_5_), channel_id=1, source_target_pairs={{0,3},{1,2},{2,1},{3,0},{4,7},{5,6},{6,5},{7,4},{8,11},{9,10},{10,... | collective-permute-start | bytes 15368 | tf_op jit(solution)/shard_map/ppermute | solution.py:599
  39.5 3.5 %collective-permute-start.36 = (f32[4,80]{1,0:T(4,128)S(1)}, f32[4,80]{1,0:T(4,128)S(1)}, u32[]{:S(2)}, u32[]{:S(2)}) collective-permute-start(f32[4,80]{1,0:T(4,128)S(1)} %get-tuple-element.731), channel_id=1, source_target_pairs={{0,3},{1,2},{2,1},{3,0},{4,7},{5,6},{6,5},{7,4},{8,11},{9,10},{10,... | collective-permute-start | bytes 3848 | tf_op jit(solution)/shard_map/ppermute | solution.py:153
  39.9 3.6 %collective-permute-start.37 = (f32[4,80]{1,0:T(4,128)S(1)}, f32[4,80]{1,0:T(4,128)S(1)}, u32[]{:S(2)}, u32[]{:S(2)}) collective-permute-start(f32[4,80]{1,0:T(4,128)S(1)} %get-tuple-element.732), channel_id=1, source_target_pairs={{0,2},{1,3},{2,0},{3,1},{4,6},{5,7},{6,4},{7,5},{8,10},{9,11},{10,... | collective-permute-start | bytes 3848 | tf_op jit(solution)/shard_map/ppermute | solution.py:153
  41.1 2.4 %collective-permute-start.38 = (f32[4,80]{1,0:T(4,128)S(1)}, f32[4,80]{1,0:T(4,128)S(1)}, u32[]{:S(2)}, u32[]{:S(2)}) collective-permute-start(f32[4,80]{1,0:T(4,128)S(1)} %get-tuple-element.733), channel_id=1, source_target_pairs={{0,1},{1,0},{2,3},{3,2},{4,5},{5,4},{6,7},{7,6},{8,9},{9,8},{10,11... | collective-permute-start | bytes 3848 | tf_op jit(solution)/shard_map/ppermute | solution.py:153
  44.4 3.1 %collective-permute-start.39 = (f32[4,80]{1,0:T(4,128)S(1)}, f32[4,80]{1,0:T(4,128)S(1)}, u32[]{:S(2)}, u32[]{:S(2)}) collective-permute-start(f32[4,80]{1,0:T(4,128)S(1)} %get-tuple-element.739), channel_id=1, source_target_pairs={{0,3},{1,2},{2,1},{3,0},{4,7},{5,6},{6,5},{7,4},{8,11},{9,10},{10,... | collective-permute-start | bytes 3848 | tf_op jit(solution)/shard_map/ppermute | solution.py:153
  44.8 3.6 %collective-permute-start.40 = (f32[4,80]{1,0:T(4,128)S(1)}, f32[4,80]{1,0:T(4,128)S(1)}, u32[]{:S(2)}, u32[]{:S(2)}) collective-permute-start(f32[4,80]{1,0:T(4,128)S(1)} %get-tuple-element.740), channel_id=1, source_target_pairs={{0,2},{1,3},{2,0},{3,1},{4,6},{5,7},{6,4},{7,5},{8,10},{9,11},{10,... | collective-permute-start | bytes 3848 | tf_op jit(solution)/shard_map/ppermute | solution.py:153
  45.8 2.6 %collective-permute-start.41 = (f32[4,80]{1,0:T(4,128)S(1)}, f32[4,80]{1,0:T(4,128)S(1)}, u32[]{:S(2)}, u32[]{:S(2)}) collective-permute-start(f32[4,80]{1,0:T(4,128)S(1)} %get-tuple-element.741), channel_id=1, source_target_pairs={{0,1},{1,0},{2,3},{3,2},{4,5},{5,4},{6,7},{7,6},{8,9},{9,8},{10,11... | collective-permute-start | bytes 3848 | tf_op jit(solution)/shard_map/ppermute | solution.py:153
  48.5 3.7 %collective-permute-start.42 = (f32[16,80]{1,0:T(8,128)S(1)}, f32[16,80]{1,0:T(8,128)S(1)}, u32[]{:S(2)}, u32[]{:S(2)}) collective-permute-start(f32[16,80]{1,0:T(8,128)S(1)} %shard_map.100.refs_0_.refs_5_.refs_6_), channel_id=1, source_target_pairs={{0,4},{4,0},{8,12},{12,8},{16,20},{20,16},{24,28},{28,24},{1,5},{5... | collective-permute-start | bytes 15368 | tf_op jit(solution)/shard_map/ppermute | solution.py:598
  48.7 3.4 %collective-permute-start.43 = (f32[16,80]{1,0:T(8,128)S(1)}, f32[16,80]{1,0:T(8,128)S(1)}, u32[]{:S(2)}, u32[]{:S(2)}) collective-permute-start(f32[16,80]{1,0:T(8,128)S(1)} %shard_map.100.refs_0_.refs_5_.refs_6_), channel_id=1, source_target_pairs={{0,1},{1,0},{2,3},{3,2},{4,5},{5,4},{6,7},{7,6},{8,9},{9,8},{10,11... | collective-permute-start | bytes 15368 | tf_op jit(solution)/shard_map/ppermute | solution.py:598
  48.7 6.3 %collective-permute-start.44 = (f32[16,80]{1,0:T(8,128)S(1)}, f32[16,80]{1,0:T(8,128)S(1)}, u32[]{:S(2)}, u32[]{:S(2)}) collective-permute-start(f32[16,80]{1,0:T(8,128)S(1)} %shard_map.100.refs_0_.refs_5_.refs_6_), channel_id=1, source_target_pairs={{0,28},{4,8},{8,4},{12,16},{16,12},{20,24},{24,20},{28,0},{1,29},{... | collective-permute-start | bytes 15368 | tf_op jit(solution)/shard_map/ppermute | solution.py:597
  51.4 3.7 %collective-permute-start.45 = (f32[16,80]{1,0:T(8,128)S(1)}, f32[16,80]{1,0:T(8,128)S(1)}, u32[]{:S(2)}, u32[]{:S(2)}) collective-permute-start(f32[16,80]{1,0:T(8,128)S(1)} %shard_map.100.refs_0_.refs_5_.refs_6_), channel_id=1, source_target_pairs={{0,3},{1,2},{2,1},{3,0},{4,7},{5,6},{6,5},{7,4},{8,11},{9,10},{10,... | collective-permute-start | bytes 15368 | tf_op jit(solution)/shard_map/ppermute | solution.py:599
  (5 other events, 119.8 us)

commit v12 on v10

--- a/solution.py
+++ b/solution.py
@@ -238,12 +238,7 @@
     return [1 if lax.axis_size(a) % 2 else lax.axis_index(a) % 2 for a in ("span", "plane")]
 
 
-def early_blocks():
-    span_odd, plane_odd = parities()
-    return (1 + span_odd, 3 + plane_odd), (2 - span_odd, 4 - plane_odd)
-
-
-def pick_kernel(nspan, nplane, width, columns_ref, fold_ref, early_ref, late_ref, seg_ref, store_ref, sem):
+def pick_kernel(nspan, nplane, width, columns_ref, fold_ref, pick_ref, seg_ref, store_ref, sem):
     store = pltpu.make_async_copy(fold_ref, store_ref, sem)
     store.start()
     copies = seg_ref.shape[0] // width
@@ -260,14 +255,10 @@
     group = jnp.where(selector == 0, 0, jnp.where(selector <= 2, of_span, of_plane))
     at = (group * nfaces + face).astype(F32)
     eye = lax.broadcasted_iota(jnp.int32, (nfaces, nfaces), 0) == lax.broadcasted_iota(jnp.int32, (nfaces, nfaces), 1)
-    first, second = jnp.where(span_odd, at[2:3], at[1:2]), jnp.where(span_odd, at[1:2], at[2:3])
-    third, fourth = jnp.where(plane_odd, at[4:5], at[3:4]), jnp.where(plane_odd, at[3:4], at[4:5])
-    rest = [at[k : k + 1] for k in range(5, nblocks)]
-    for ref, rows in ((early_ref, [at[0:1], first, third]), (late_ref, [second, fourth, *rest])):
-        lane = lax.broadcasted_iota(jnp.int32, (nfaces, ref.shape[1]), 1) % (ref.shape[1] // 3)
-        for n, row in enumerate(rows):
-            column = jnp.sum(jnp.where(eye, row, 0.0), axis=1, keepdims=True).astype(jnp.int32)
-            ref[n * nfaces : (n + 1) * nfaces, :] = jnp.where(lane == column, 1.0, 0.0).astype(BF16)
+    lane = lax.broadcasted_iota(jnp.int32, (nfaces, pick_ref.shape[1]), 1) % (pick_ref.shape[1] // 3)
+    for k in range(nblocks):
+        column = jnp.sum(jnp.where(eye, at[k : k + 1], 0.0), axis=1, keepdims=True).astype(jnp.int32)
+        pick_ref[k * nfaces : (k + 1) * nfaces, :] = jnp.where(lane == column, 1.0, 0.0).astype(BF16)
     store.wait()
 
 
@@ -368,32 +359,15 @@
     return total[:, :width]
 
 
-def early_kernel(nblocks, blocks, pick, seg, *refs):
-    faces, (sum_ref, held, buf, x_scr, acc_scr, parts, sems) = refs[:3], refs[3:]
-    width = faces[0].shape[1]
-    area = width * width
-    early, late = early_blocks()
-
-    def fetch(k, count, dst, column, n):
-        start = pl.multiple_of(k * area, 128) if not isinstance(k, int) else k * area
-        return pltpu.make_async_copy(
-            blocks.at[:, pl.ds(start, count * area)], dst.at[:, pl.ds(column, count * area)], sems.at[n]
-        )
-
-    mine = [fetch(k, 1, buf, n * area, n) for n, k in enumerate((0, *early))]
-    kept = [fetch(k, 1, held, n * area, 3 + n) for n, k in enumerate(late)]
-    kept.append(fetch(5, nblocks - 5, held, 2 * area, 5))
-    for copy in mine + kept:
-        copy.start()
-    x_scr[...] = repeat_faces(faces, pick, x_scr.shape[1] // width)
-    work = [([(buf, n * area)], copy) for n, copy in enumerate(mine)]
-    sum_ref[...] = add_products(work, x_scr, acc_scr, parts, seg, width)
-    for copy in kept:
-        copy.wait()
+def hold_kernel(blocks, _, held, sem):
+    fetch = pltpu.make_async_copy(blocks, held, sem)
+    fetch.start()
+    fetch.wait()
 
 
 def late_kernel(nplane, last, *refs):
-    (slot, held, pick, seg, early_sum), faces, refs = refs[:5], refs[5:10], refs[10:]
+    (slot, other, plane_other, pair, plane_pair, held, pick, seg, mine), refs = refs[:9], refs[9:]
+    faces = (mine, pair, plane_pair, other, plane_other)
     nold = ITERS if last else 1
     olds, refs = refs[:nold], refs[nold:]
     next_ref, outs, (x_scr, acc_scr, parts, slot_scr, slot_sem) = refs[0], refs[1:-5], refs[-5:]
@@ -404,7 +378,7 @@
         slots.start()
     x_scr[...] = repeat_faces(faces, pick, x_scr.shape[1] // width)
     work = [([(held, column) for column in range(0, held.shape[1], area)], None)]
-    u_next = early_sum[...] + add_products(work, x_scr, acc_scr, parts, seg, width) - SHIFT * olds[-1][...]
+    u_next = add_products(work, x_scr, acc_scr, parts, seg, width) - SHIFT * olds[-1][...]
     next_ref[...] = u_next
     if last:
         gram_ref = outs[0]
@@ -532,7 +506,7 @@
     )
     us = [u_first]
     zs = []
-    picks = None
+    picks = held = None
     for step in range(ITERS):
         flat = pltpu.VMEM((nfaces, area), F32)
         squares = [(nfaces * width, width)] * 3
@@ -567,13 +541,12 @@
             *picks, fold = pl.pallas_call(
                 functools.partial(pick_kernel, nspan, nplane, width),
                 out_shape=[
-                    pltpu.VMEM((3 * nfaces, 9 * nfaces), BF16),
-                    pltpu.VMEM(((nblocks - 3) * nfaces, 15 * nfaces), BF16),
+                    pltpu.VMEM((nblocks * nfaces, 15 * nfaces), BF16),
                     pltpu.VMEM((math.lcm(width, 128), 128), BF16),
                     pltpu.HBM(squares[0], F32),
                 ],
                 in_specs=[pl.BlockSpec(memory_space=pltpu.VMEM)] * 2,
-                out_specs=[pl.BlockSpec(memory_space=pltpu.VMEM)] * 3 + [pl.BlockSpec(memory_space=pl.ANY)],
+                out_specs=[pl.BlockSpec(memory_space=pltpu.VMEM)] * 2 + [pl.BlockSpec(memory_space=pl.ANY)],
                 scratch_shapes=[pltpu.SemaphoreType.DMA],
                 compiler_params=pltpu.CompilerParams(vmem_limit_bytes=VMEM_LIMIT),
                 cost_estimate=pl.CostEstimate(flops=0, bytes_accessed=4 * nfaces * area, transcendentals=0),
@@ -587,8 +560,9 @@
         (mine,) = call(functools.partial(faces_kernel, nplane), args, [shape], spaces)
         zs.append(mine)
         other = lax.ppermute(mine, "span", span_others)
-        near = [mine, lax.ppermute(mine, "span", span_pairs), lax.ppermute(mine, "plane", plane_pairs)]
-        far = [other, lax.ppermute(mine, "plane", plane_others)]
+        pair = lax.ppermute(mine, "span", span_pairs)
+        plane_pair = lax.ppermute(mine, "plane", plane_pairs)
+        plane_other = lax.ppermute(mine, "plane", plane_others)
         chunk = math.lcm(width, 128)
 
         def scratch(count):
@@ -598,22 +572,16 @@
                 pltpu.VMEM((3 * nfaces * area // chunk, chunk), BF16),
             ]
 
-        early_sum, held = call(
-            functools.partial(early_kernel, nblocks),
-            [blocks, picks[0], picks[2], *near],
-            [shape, (nfaces, (nblocks - 3) * area)],
-            [pl.ANY] + [pltpu.VMEM] * 5,
-            [pltpu.VMEM((nfaces, 3 * area), F32)] + scratch(3) + [pltpu.SemaphoreType.DMA((6,))],
-            flops=6 * nfaces * area,
-        )
+        if step == 0:
+            (held,) = call(hold_kernel, [blocks, mine], [blocks.shape], [pl.ANY] * 2, [pltpu.SemaphoreType.DMA])
         last = step == ITERS - 1
-        args = [line_slot, held, picks[1], picks[2], early_sum, *near, *far, *(us if last else us[-1:])]
+        args = [line_slot, other, plane_other, pair, plane_pair, held, *picks, mine, *(us if last else us[-1:])]
         out = call(
             functools.partial(late_kernel, nplane, last),
             args,
             [shape] + ([(1, 128)] if last else [(per, width)] * nplane),
             [pl.ANY] + [pltpu.VMEM] * (len(args) - 1),
-            scratch(nblocks - 3) + [pltpu.SMEM(line_slot.shape, jnp.int32), pltpu.SemaphoreType.DMA],
+            scratch(nblocks) + [pltpu.SMEM(line_slot.shape, jnp.int32), pltpu.SemaphoreType.DMA],
             flops=2 * nblocks * nfaces * area,
         )
         us.append(out[0])

time: 67.9 us -> 67.6 us (level)
  Pallas kernels: 22.2 us -> 17.5 us
  waiting for transfers between devices: 8.77 us -> 13.1 us
    ppermute x3, waiting for transfers between devices: 0.68 us -> 5.6 us  [on_device(): other = lax.ppermute(mine, 'span', span_others)]
    pallas_call x17 -> x15, Pallas kernels: 20.7 us -> 15.9 us  [call(): pl.pallas_call(kernel, out_shape=[pltpu.VMEM(shape, F32) if pinned else j...]
    ppermute x3, starting transfers between devices: 9.01 us -> 9.82 us  [on_device(): other = lax.ppermute(mine, 'span', span_others)]
  transfers between devices with their start and end apart: 30 -> 30, of which waited for: 13 -> 12; matrix products, arithmetic and copies ran while one was open for 0% -> 0% of each run, Pallas kernels for 21% -> 14%
where the time goes in v12:
time: 67.6 us; the launch traced here: 67.3 us
  starting transfers between devices  25.3 us (37%)
  Pallas kernels  17.5 us (26%)
  waiting for transfers between devices  13.1 us (19%)
  blocking collectives  10.1 us (15%)
  between operations  1.08 us (2%)
    pallas_call x15, Pallas kernels, call(): pl.pallas_call(kernel, out_shape=[pltpu.VMEM(shape, F32) if pinned else j...  15.9 us
    ppermute x18, starting transfers between devices, exchange(): lax.ppermute(x, axis, [(i, partner(i, k, size)[0]) for i in range(size)])  12.8 us
    all_to_all x1, blocking collectives, add_up(): lax.all_to_all(rows, ('span', 'plane'), split_axis=0, concat_axis=0, tile...  10.1 us
    ppermute x3, starting transfers between devices, on_device(): other = lax.ppermute(mine, 'span', span_others)  9.82 us
    ppermute x18, waiting for transfers between devices, exchange(): lax.ppermute(x, axis, [(i, partner(i, k, size)[0]) for i in range(size)])  6.8 us
    ppermute x3, waiting for transfers between devices, on_device(): other = lax.ppermute(mine, 'span', span_others)  5.6 us
    ppermute x3, starting transfers between devices, on_device(): plane_pair = lax.ppermute(mine, 'plane', plane_pairs)  2.5 us
    pallas_call x1, Pallas kernels, on_device(): pl.pallas_call(functools.partial(pick_kernel, nspan, nplane, width), out_...  1.55 us
  transfers between devices with their start and end apart: 30, of which 12 were waited for; matrix products, arithmetic and copies ran while one was open for 0% of the time, Pallas kernels for 14%

profile of v12, /device:TPU:0, one launch (start us, length us, event | category | flops | bytes accessed | tf_op | source)
XLA Modules:
  0.0 67.3 jit_solution(6615224677160034654)
XLA Ops:
  0.6 0.8 %shard_map.86 = (f32[16,80]{1,0:T(8,128)S(1)}, f32[16,48]{1,0:T(8,128)S(1)}, f32[4,80]{1,0:T(4,128)S(1)}, f32[4,80]{1,0:T(4,128)S(1)}, f32[4,80]{1,0:T(4,128)S(1)}, /*index=5*/f32[4,80]{1,0:T(4,128)S(1)}) custom-call(s32[1,16]{1,0:T(1,128)} %refs_0_.5, f32[16,80]{1,0:T(8,128)} %bitcast.571), custom_call_target="tpu_custom_call" | custom-call | bytes 5184 | tf_op jit(solution)/shard_map/pallas_call | solution.py:465
  1.5 2.5 %collective-permute-start.16 = (f32[4,80]{1,0:T(4,128)S(1)}, f32[4,80]{1,0:T(4,128)S(1)}, u32[]{:S(2)}, u32[]{:S(2)}) collective-permute-start(f32[4,80]{1,0:T(4,128)S(1)} %get-tuple-element.695), channel_id=1, source_target_pairs={{0,3},{1,2},{2,1},{3,0},{4,7},{5,6},{6,5},{7,4},{8,11},{9,10},{10,... | collective-permute-start | bytes 3848 | tf_op jit(solution)/shard_map/ppermute | solution.py:153
  4.6 2.5 %shard_map.87 = (f32[1280,80]{1,0:T(8,128)S(1)}, f32[1280,80]{1,0:T(8,128)S(1)}, f32[1280,80]{1,0:T(8,128)S(1)}) custom-call(f32[16,6400]{1,0:T(8,128)} %low.5, f32[16,6400]{1,0:T(8,128)} %piv.5, f32[16,6400]{1,0:T(8,128)} %upp.1, f32[16,80]{1,0:T(8,128)S(1)} %get-tuple-element.699._.refs_9_.refs_0_), custom_call_target="tpu_custom_call" | custom-call | flops 8192000 | bytes 1233920 | tf_op jit(solution)/shard_map/pallas_call | solution.py:465
  7.5 0.9 %shard_map.88 = (f32[4,80]{1,0:T(4,128)S(1)}, f32[4,80]{1,0:T(4,128)S(1)}, f32[4,80]{1,0:T(4,128)S(1)}, f32[4,80]{1,0:T(4,128)S(1)}) custom-call(f32[4,80]{1,0:T(4,128)S(1)} %collective-permute-done.16.refs_0_, f32[4,80]{1,0:T(4,128)S(1)} %collective-permute-done.17.refs_1_, f32[4,80]{1,0:T(4,128)S(1)} %collective-permute-done.18.refs_2_, ...), custom_call_target="tpu_custom_call" | custom-call | flops 614400 | bytes 1233920 | tf_op jit(solution)/shard_map/pallas_call | solution.py:465
  8.5 1.2 %collective-permute-start.19 = (f32[4,80]{1,0:T(4,128)S(1)}, f32[4,80]{1,0:T(4,128)S(1)}, u32[]{:S(2)}, u32[]{:S(2)}) collective-permute-start(f32[4,80]{1,0:T(4,128)S(1)} %get-tuple-element.703), channel_id=1, source_target_pairs={{0,3},{1,2},{2,1},{3,0},{4,7},{5,6},{6,5},{7,4},{8,11},{9,10},{10,... | collective-permute-start | bytes 3848 | tf_op jit(solution)/shard_map/ppermute | solution.py:153
  10.4 1.6 %shard_map.89 = (bf16[176,240]{1,0:T(8,128)(2,1)S(1)}, bf16[640,128]{1,0:T(8,128)(2,1)S(1)}, f32[1280,80]{1,0:T(8,128)}) custom-call(s32[11,16]{1,0:T(8,128)} %columns_ref, f32[1280,80]{1,0:T(8,128)S(1)} %get-tuple-element.702.fold_ref), custom_call_target="tpu_custom_call" | custom-call | bytes 409600 | tf_op jit(solution)/shard_map/pallas_call | solution.py:541
  12.0 1.2 %collective-permute-done.20.refs_1_ = f32[4,80]{1,0:T(4,128)S(1)} collective-permute-done((f32[4,80]{1,0:T(4,128)S(1)}, f32[4,80]{1,0:T(4,128)S(1)}, u32[]{:S(2)}, u32[]{:S(2)}) %collective-permute-start.20) | collective-permute-done | bytes 1312 | tf_op jit(solution)/shard_map/ppermute | solution.py:153
  13.4 4.5 %collective-permute-start.22 = (f32[16,80]{1,0:T(8,128)S(1)}, f32[16,80]{1,0:T(8,128)S(1)}, u32[]{:S(2)}, u32[]{:S(2)}) collective-permute-start(f32[16,80]{1,0:T(8,128)S(1)} %shard_map.90._.refs_8_.refs_4_), channel_id=1, source_target_pairs={{0,28},{4,8},{8,4},{12,16},{16,12},{20,24},{24,20},{28,0},{1,29},{... | collective-permute-start | bytes 15368 | tf_op jit(solution)/shard_map/ppermute | solution.py:562
  17.9 0.8 %collective-permute-start.25 = (f32[16,80]{1,0:T(8,128)S(1)}, f32[16,80]{1,0:T(8,128)S(1)}, u32[]{:S(2)}, u32[]{:S(2)}) collective-permute-start(f32[16,80]{1,0:T(8,128)S(1)} %shard_map.90._.refs_8_.refs_4_), channel_id=1, source_target_pairs={{0,1},{1,0},{2,3},{3,2},{4,5},{5,4},{6,7},{7,6},{8,9},{9,8},{10,11... | collective-permute-start | bytes 15368 | tf_op jit(solution)/shard_map/ppermute | solution.py:564
  18.7 2.3 %shard_map.91.refs_5_ = f32[16,70400]{1,0:T(8,128)S(1)} custom-call(f32[16,70400]{1,0:T(8,128)} %blocks.1, f32[16,80]{1,0:T(8,128)S(1)} %shard_map.90._.refs_8_.refs_4_), custom_call_target="tpu_custom_call" | custom-call | bytes 4510720 | tf_op jit(solution)/shard_map/pallas_call | solution.py:465
  21.6 1.1 %shard_map.92 = (f32[16,80]{1,0:T(8,128)S(1)}, f32[4,80]{1,0:T(4,128)S(1)}, f32[4,80]{1,0:T(4,128)S(1)}, f32[4,80]{1,0:T(4,128)S(1)}, f32[4,80]{1,0:T(4,128)S(1)}) custom-call(s32[1,16]{1,0:T(1,128)S(1)} %copy-done.8, f32[16,80]{1,0:T(8,128)S(1)} %collective-permute-done.22.refs_1_, f32[16,80]{1,0:T(8,128)S(1)} %collective-permute-done.23.refs_2_, ...), custom_call_target="tpu_custom_call" | custom-call | flops 2252800 | bytes 4784704 | tf_op jit(solution)/shard_map/pallas_call | solution.py:465
  24.6 1.5 %shard_map.93 = (f32[1280,80]{1,0:T(8,128)S(1)}, f32[1280,80]{1,0:T(8,128)S(1)}, f32[1280,80]{1,0:T(8,128)S(1)}) custom-call(f32[16,6400]{1,0:T(8,128)S(1)} %copy-done.1, f32[16,6400]{1,0:T(8,128)S(1)} %copy-done.2, f32[1280,80]{1,0:T(8,128)S(1)} %copy-done, f32[16,80]{1,0:T(8,128)S(1)} %get-tuple-element.715._.refs_9_.refs_10_.refs_1_), custom_call_target="tpu_custom_call" | custom-call | flops 102400 | bytes 1233920 | tf_op jit(solution)/shard_map/pallas_call | solution.py:465
  26.1 0.8 %collective-permute-done.27.refs_1_ = f32[4,80]{1,0:T(4,128)S(1)} collective-permute-done((f32[4,80]{1,0:T(4,128)S(1)}, f32[4,80]{1,0:T(4,128)S(1)}, u32[]{:S(2)}, u32[]{:S(2)}) %collective-permute-start.27) | collective-permute-done | bytes 1312 | tf_op jit(solution)/shard_map/ppermute | solution.py:153
  26.9 0.9 %shard_map.94 = (f32[4,80]{1,0:T(4,128)S(1)}, f32[4,80]{1,0:T(4,128)S(1)}, f32[4,80]{1,0:T(4,128)S(1)}, f32[4,80]{1,0:T(4,128)S(1)}) custom-call(f32[4,80]{1,0:T(4,128)S(1)} %collective-permute-done.26.refs_0_, f32[4,80]{1,0:T(4,128)S(1)} %collective-permute-done.27.refs_1_, f32[4,80]{1,0:T(4,128)S(1)} %collective-permute-done.28.refs_2_, ...), custom_call_target="tpu_custom_call" | custom-call | flops 614400 | bytes 1233920 | tf_op jit(solution)/shard_map/pallas_call | solution.py:465
  28.0 0.8 %collective-permute-start.30 = (f32[4,80]{1,0:T(4,128)S(1)}, f32[4,80]{1,0:T(4,128)S(1)}, u32[]{:S(2)}, u32[]{:S(2)}) collective-permute-start(f32[4,80]{1,0:T(4,128)S(1)} %get-tuple-element.720), channel_id=1, source_target_pairs={{0,2},{1,3},{2,0},{3,1},{4,6},{5,7},{6,4},{7,5},{8,10},{9,11},{10,... | collective-permute-start | bytes 3848 | tf_op jit(solution)/shard_map/ppermute | solution.py:153
  28.8 0.9 %collective-permute-start.31 = (f32[4,80]{1,0:T(4,128)S(1)}, f32[4,80]{1,0:T(4,128)S(1)}, u32[]{:S(2)}, u32[]{:S(2)}) collective-permute-start(f32[4,80]{1,0:T(4,128)S(1)} %get-tuple-element.721), channel_id=1, source_target_pairs={{0,1},{1,0},{2,3},{3,2},{4,5},{5,4},{6,7},{7,6},{8,9},{9,8},{10,11... | collective-permute-start | bytes 3848 | tf_op jit(solution)/shard_map/ppermute | solution.py:153
  29.7 1.1 %collective-permute-done.29.refs_0_ = f32[4,80]{1,0:T(4,128)S(1)} collective-permute-done((f32[4,80]{1,0:T(4,128)S(1)}, f32[4,80]{1,0:T(4,128)S(1)}, u32[]{:S(2)}, u32[]{:S(2)}) %collective-permute-start.29) | collective-permute-done | bytes 1312 | tf_op jit(solution)/shard_map/ppermute | solution.py:153
  30.9 0.7 %collective-permute-done.30.refs_1_ = f32[4,80]{1,0:T(4,128)S(1)} collective-permute-done((f32[4,80]{1,0:T(4,128)S(1)}, f32[4,80]{1,0:T(4,128)S(1)}, u32[]{:S(2)}, u32[]{:S(2)}) %collective-permute-start.30) | collective-permute-done | bytes 1312 | tf_op jit(solution)/shard_map/ppermute | solution.py:153
  31.7 2.6 %collective-permute-start.32 = (f32[16,80]{1,0:T(8,128)S(1)}, f32[16,80]{1,0:T(8,128)S(1)}, u32[]{:S(2)}, u32[]{:S(2)}) collective-permute-start(f32[16,80]{1,0:T(8,128)S(1)} %shard_map.95.refs_8_.refs_5_), channel_id=1, source_target_pairs={{0,28},{4,8},{8,4},{12,16},{16,12},{20,24},{24,20},{28,0},{1,29},{... | collective-permute-start | bytes 15368 | tf_op jit(solution)/shard_map/ppermute | solution.py:562
  34.3 1.0 %collective-permute-start.35 = (f32[16,80]{1,0:T(8,128)S(1)}, f32[16,80]{1,0:T(8,128)S(1)}, u32[]{:S(2)}, u32[]{:S(2)}) collective-permute-start(f32[16,80]{1,0:T(8,128)S(1)} %shard_map.95.refs_8_.refs_5_), channel_id=1, source_target_pairs={{0,1},{1,0},{2,3},{3,2},{4,5},{5,4},{6,7},{7,6},{8,9},{9,8},{10,11... | collective-permute-start | bytes 15368 | tf_op jit(solution)/shard_map/ppermute | solution.py:564
  35.4 2.8 %collective-permute-done.32.refs_1_ = f32[16,80]{1,0:T(8,128)S(1)} collective-permute-done((f32[16,80]{1,0:T(8,128)S(1)}, f32[16,80]{1,0:T(8,128)S(1)}, u32[]{:S(2)}, u32[]{:S(2)}) %collective-permute-start.32) | collective-permute-done | bytes 5152 | tf_op jit(solution)/shard_map/ppermute | solution.py:562
  38.2 1.1 %shard_map.96 = (f32[16,80]{1,0:T(8,128)S(1)}, f32[4,80]{1,0:T(4,128)S(1)}, f32[4,80]{1,0:T(4,128)S(1)}, f32[4,80]{1,0:T(4,128)S(1)}, f32[4,80]{1,0:T(4,128)S(1)}) custom-call(s32[1,16]{1,0:T(1,128)S(1)} %copy-done.8, f32[16,80]{1,0:T(8,128)S(1)} %collective-permute-done.32.refs_1_, f32[16,80]{1,0:T(8,128)S(1)} %collective-permute-done.33.refs_2_, ...), custom_call_target="tpu_custom_call" | custom-call | flops 2252800 | bytes 4784704 | tf_op jit(solution)/shard_map/pallas_call | solution.py:465
  39.8 1.1 %collective-permute-start.37 = (f32[4,80]{1,0:T(4,128)S(1)}, f32[4,80]{1,0:T(4,128)S(1)}, u32[]{:S(2)}, u32[]{:S(2)}) collective-permute-start(f32[4,80]{1,0:T(4,128)S(1)} %get-tuple-element.724), channel_id=1, source_target_pairs={{0,2},{1,3},{2,0},{3,1},{4,6},{5,7},{6,4},{7,5},{8,10},{9,11},{10,... | collective-permute-start | bytes 3848 | tf_op jit(solution)/shard_map/ppermute | solution.py:153
  41.2 1.5 %shard_map.97 = (f32[1280,80]{1,0:T(8,128)S(1)}, f32[1280,80]{1,0:T(8,128)S(1)}, f32[1280,80]{1,0:T(8,128)S(1)}) custom-call(f32[16,6400]{1,0:T(8,128)S(1)} %copy-done.1, f32[16,6400]{1,0:T(8,128)S(1)} %copy-done.2, f32[1280,80]{1,0:T(8,128)S(1)} %copy-done, f32[16,80]{1,0:T(8,128)S(1)} %get-tuple-element.727._.refs_11_.refs_2_), custom_call_target="tpu_custom_call" | custom-call | flops 102400 | bytes 1233920 | tf_op jit(solution)/shard_map/pallas_call | solution.py:465
  43.4 0.9 %shard_map.98 = (f32[4,80]{1,0:T(4,128)S(1)}, f32[4,80]{1,0:T(4,128)S(1)}, f32[4,80]{1,0:T(4,128)S(1)}, f32[4,80]{1,0:T(4,128)S(1)}) custom-call(f32[4,80]{1,0:T(4,128)S(1)} %collective-permute-done.36.refs_0_, f32[4,80]{1,0:T(4,128)S(1)} %collective-permute-done.37.refs_1_, f32[4,80]{1,0:T(4,128)S(1)} %collective-permute-done.38.refs_2_, ...), custom_call_target="tpu_custom_call" | custom-call | flops 614400 | bytes 1233920 | tf_op jit(solution)/shard_map/pallas_call | solution.py:465
  44.5 1.1 %collective-permute-start.40 = (f32[4,80]{1,0:T(4,128)S(1)}, f32[4,80]{1,0:T(4,128)S(1)}, u32[]{:S(2)}, u32[]{:S(2)}) collective-permute-start(f32[4,80]{1,0:T(4,128)S(1)} %get-tuple-element.732), channel_id=1, source_target_pairs={{0,2},{1,3},{2,0},{3,1},{4,6},{5,7},{6,4},{7,5},{8,10},{9,11},{10,... | collective-permute-start | bytes 3848 | tf_op jit(solution)/shard_map/ppermute | solution.py:153
  46.3 1.1 %collective-permute-done.39.refs_0_ = f32[4,80]{1,0:T(4,128)S(1)} collective-permute-done((f32[4,80]{1,0:T(4,128)S(1)}, f32[4,80]{1,0:T(4,128)S(1)}, u32[]{:S(2)}, u32[]{:S(2)}) %collective-permute-start.39) | collective-permute-done | bytes 1312 | tf_op jit(solution)/shard_map/ppermute | solution.py:153
  48.2 2.7 %collective-permute-start.42 = (f32[16,80]{1,0:T(8,128)S(1)}, f32[16,80]{1,0:T(8,128)S(1)}, u32[]{:S(2)}, u32[]{:S(2)}) collective-permute-start(f32[16,80]{1,0:T(8,128)S(1)} %shard_map.99.refs_8_.refs_6_), channel_id=1, source_target_pairs={{0,28},{4,8},{8,4},{12,16},{16,12},{20,24},{24,20},{28,0},{1,29},{... | collective-permute-start | bytes 15368 | tf_op jit(solution)/shard_map/ppermute | solution.py:562
  51.8 2.8 %collective-permute-done.42.refs_1_ = f32[16,80]{1,0:T(8,128)S(1)} collective-permute-done((f32[16,80]{1,0:T(8,128)S(1)}, f32[16,80]{1,0:T(8,128)S(1)}, u32[]{:S(2)}, u32[]{:S(2)}) %collective-permute-start.42) | collective-permute-done | bytes 5152 | tf_op jit(solution)/shard_map/ppermute | solution.py:562
  54.7 1.1 %shard_map.100 = (f32[16,80]{1,0:T(8,128)S(1)}, f32[1,128]{1,0:T(1,128)S(1)}) custom-call(s32[1,16]{1,0:T(1,128)S(1)} %copy-done.8, f32[16,80]{1,0:T(8,128)S(1)} %collective-permute-done.42.refs_1_, f32[16,80]{1,0:T(8,128)S(1)} %collective-permute-done.43.refs_2_, f32[16,80]{1,0:T(8,128)S(1)} %collective-permute-done.44.refs_3_, ...), custom_call_target="tpu_custom_call" | custom-call | flops 2252800 | bytes 4794944 | tf_op jit(solution)/shard_map/pallas_call | solution.py:465
  55.9 10.1 %all_to_all.112 = f32[32,1,128]{2,1,0:T(1,128)S(1)} all-to-all(f32[32,1,128]{2,1,0:T(1,128)S(1)} %broadcast_in_dim.83), channel_id=1, replica_groups=mesh['span'=8,'plane'=4] {'span','plane'}, dimensions={0} | all-to-all | bytes 32768 | tf_op jit(solution)/shard_map/all_to_all | solution.py:479
  66.0 0.8 %shard_map.101 = (f32[16,80]{1,0:T(8,128)}, f32[16,80]{1,0:T(8,128)}, f32[1,128]{1,0:T(1,128)S(1)}) custom-call(f32[32,128]{1,0:T(8,128)S(1)} %bitcast.558, f32[16,80]{1,0:T(8,128)S(1)} %get-tuple-element.699._.refs_9_.refs_0_, f32[16,80]{1,0:T(8,128)S(1)} %get-tuple-element.715._.refs_9_.refs_10_.refs_1_, ...), custom_call_target="tpu_custom_call" | custom-call | bytes 52224 | tf_op jit(solution)/shard_map/pallas_call | solution.py:465
  (61 shorter events, 9.1 us)
Async XLA Ops:
  1.5 5.7 %collective-permute-start.16 = (f32[4,80]{1,0:T(4,128)S(1)}, f32[4,80]{1,0:T(4,128)S(1)}, u32[]{:S(2)}, u32[]{:S(2)}) collective-permute-start(f32[4,80]{1,0:T(4,128)S(1)} %get-tuple-element.695), channel_id=1, source_target_pairs={{0,3},{1,2},{2,1},{3,0},{4,7},{5,6},{6,5},{7,4},{8,11},{9,10},{10,... | collective-permute-start | bytes 3848 | tf_op jit(solution)/shard_map/ppermute | solution.py:153
  4.0 3.6 %collective-permute-start.17 = (f32[4,80]{1,0:T(4,128)S(1)}, f32[4,80]{1,0:T(4,128)S(1)}, u32[]{:S(2)}, u32[]{:S(2)}) collective-permute-start(f32[4,80]{1,0:T(4,128)S(1)} %get-tuple-element.696), channel_id=1, source_target_pairs={{0,2},{1,3},{2,0},{3,1},{4,6},{5,7},{6,4},{7,5},{8,10},{9,11},{10,... | collective-permute-start | bytes 3848 | tf_op jit(solution)/shard_map/ppermute | solution.py:153
  4.6 2.9 %collective-permute-start.18 = (f32[4,80]{1,0:T(4,128)S(1)}, f32[4,80]{1,0:T(4,128)S(1)}, u32[]{:S(2)}, u32[]{:S(2)}) collective-permute-start(f32[4,80]{1,0:T(4,128)S(1)} %get-tuple-element.697), channel_id=1, source_target_pairs={{0,1},{1,0},{2,3},{3,2},{4,5},{5,4},{6,7},{7,6},{8,9},{9,8},{10,11... | collective-permute-start | bytes 3848 | tf_op jit(solution)/shard_map/ppermute | solution.py:153
  8.5 3.5 %collective-permute-start.19 = (f32[4,80]{1,0:T(4,128)S(1)}, f32[4,80]{1,0:T(4,128)S(1)}, u32[]{:S(2)}, u32[]{:S(2)}) collective-permute-start(f32[4,80]{1,0:T(4,128)S(1)} %get-tuple-element.703), channel_id=1, source_target_pairs={{0,3},{1,2},{2,1},{3,0},{4,7},{5,6},{6,5},{7,4},{8,11},{9,10},{10,... | collective-permute-start | bytes 3848 | tf_op jit(solution)/shard_map/ppermute | solution.py:153
  9.6 3.6 %collective-permute-start.20 = (f32[4,80]{1,0:T(4,128)S(1)}, f32[4,80]{1,0:T(4,128)S(1)}, u32[]{:S(2)}, u32[]{:S(2)}) collective-permute-start(f32[4,80]{1,0:T(4,128)S(1)} %get-tuple-element.704), channel_id=1, source_target_pairs={{0,2},{1,3},{2,0},{3,1},{4,6},{5,7},{6,4},{7,5},{8,10},{9,11},{10,... | collective-permute-start | bytes 3848 | tf_op jit(solution)/shard_map/ppermute | solution.py:153
  10.3 2.9 %collective-permute-start.21 = (f32[4,80]{1,0:T(4,128)S(1)}, f32[4,80]{1,0:T(4,128)S(1)}, u32[]{:S(2)}, u32[]{:S(2)}) collective-permute-start(f32[4,80]{1,0:T(4,128)S(1)} %get-tuple-element.705), channel_id=1, source_target_pairs={{0,1},{1,0},{2,3},{3,2},{4,5},{5,4},{6,7},{7,6},{8,9},{9,8},{10,11... | collective-permute-start | bytes 3848 | tf_op jit(solution)/shard_map/ppermute | solution.py:153
  13.4 7.6 %collective-permute-start.22 = (f32[16,80]{1,0:T(8,128)S(1)}, f32[16,80]{1,0:T(8,128)S(1)}, u32[]{:S(2)}, u32[]{:S(2)}) collective-permute-start(f32[16,80]{1,0:T(8,128)S(1)} %shard_map.90._.refs_8_.refs_4_), channel_id=1, source_target_pairs={{0,28},{4,8},{8,4},{12,16},{16,12},{20,24},{24,20},{28,0},{1,29},{... | collective-permute-start | bytes 15368 | tf_op jit(solution)/shard_map/ppermute | solution.py:562
  17.9 3.1 %collective-permute-start.23 = (f32[16,80]{1,0:T(8,128)S(1)}, f32[16,80]{1,0:T(8,128)S(1)}, u32[]{:S(2)}, u32[]{:S(2)}) collective-permute-start(f32[16,80]{1,0:T(8,128)S(1)} %shard_map.90._.refs_8_.refs_4_), channel_id=1, source_target_pairs={{0,3},{1,2},{2,1},{3,0},{4,7},{5,6},{6,5},{7,4},{8,11},{9,10},{10,... | collective-permute-start | bytes 15368 | tf_op jit(solution)/shard_map/ppermute | solution.py:565
  17.9 3.7 %collective-permute-start.24 = (f32[16,80]{1,0:T(8,128)S(1)}, f32[16,80]{1,0:T(8,128)S(1)}, u32[]{:S(2)}, u32[]{:S(2)}) collective-permute-start(f32[16,80]{1,0:T(8,128)S(1)} %shard_map.90._.refs_8_.refs_4_), channel_id=1, source_target_pairs={{0,4},{4,0},{8,12},{12,8},{16,20},{20,16},{24,28},{28,24},{1,5},{5... | collective-permute-start | bytes 15368 | tf_op jit(solution)/shard_map/ppermute | solution.py:563
  17.9 3.7 %collective-permute-start.25 = (f32[16,80]{1,0:T(8,128)S(1)}, f32[16,80]{1,0:T(8,128)S(1)}, u32[]{:S(2)}, u32[]{:S(2)}) collective-permute-start(f32[16,80]{1,0:T(8,128)S(1)} %shard_map.90._.refs_8_.refs_4_), channel_id=1, source_target_pairs={{0,1},{1,0},{2,3},{3,2},{4,5},{5,4},{6,7},{7,6},{8,9},{9,8},{10,11... | collective-permute-start | bytes 15368 | tf_op jit(solution)/shard_map/ppermute | solution.py:564
  22.6 3.5 %collective-permute-start.26 = (f32[4,80]{1,0:T(4,128)S(1)}, f32[4,80]{1,0:T(4,128)S(1)}, u32[]{:S(2)}, u32[]{:S(2)}) collective-permute-start(f32[4,80]{1,0:T(4,128)S(1)} %get-tuple-element.710), channel_id=1, source_target_pairs={{0,3},{1,2},{2,1},{3,0},{4,7},{5,6},{6,5},{7,4},{8,11},{9,10},{10,... | collective-permute-start | bytes 3848 | tf_op jit(solution)/shard_map/ppermute | solution.py:153
  23.3 3.6 %collective-permute-start.27 = (f32[4,80]{1,0:T(4,128)S(1)}, f32[4,80]{1,0:T(4,128)S(1)}, u32[]{:S(2)}, u32[]{:S(2)}) collective-permute-start(f32[4,80]{1,0:T(4,128)S(1)} %get-tuple-element.711), channel_id=1, source_target_pairs={{0,2},{1,3},{2,0},{3,1},{4,6},{5,7},{6,4},{7,5},{8,10},{9,11},{10,... | collective-permute-start | bytes 3848 | tf_op jit(solution)/shard_map/ppermute | solution.py:153
  24.0 2.9 %collective-permute-start.28 = (f32[4,80]{1,0:T(4,128)S(1)}, f32[4,80]{1,0:T(4,128)S(1)}, u32[]{:S(2)}, u32[]{:S(2)}) collective-permute-start(f32[4,80]{1,0:T(4,128)S(1)} %get-tuple-element.712), channel_id=1, source_target_pairs={{0,1},{1,0},{2,3},{3,2},{4,5},{5,4},{6,7},{7,6},{8,9},{9,8},{10,11... | collective-permute-start | bytes 3848 | tf_op jit(solution)/shard_map/ppermute | solution.py:153
  26.9 40.0 %copy-start.5 = (f32[80,16]{0,1:T(8,128)S(1)}, f32[80,16]{0,1:T(8,128)}, u32[]{:S(2)}) copy-start(f32[80,16]{0,1:T(8,128)} %param.25) | copy-start | bytes 15364
  26.9 40.0 %copy-start.6 = (s32[11,16]{1,0:T(8,128)S(1)}, s32[11,16]{1,0:T(8,128)}, u32[]{:S(2)}) copy-start(s32[11,16]{1,0:T(8,128)} %columns_ref) | copy-start | bytes 2116
  27.8 3.1 %collective-permute-start.29 = (f32[4,80]{1,0:T(4,128)S(1)}, f32[4,80]{1,0:T(4,128)S(1)}, u32[]{:S(2)}, u32[]{:S(2)}) collective-permute-start(f32[4,80]{1,0:T(4,128)S(1)} %get-tuple-element.719), channel_id=1, source_target_pairs={{0,3},{1,2},{2,1},{3,0},{4,7},{5,6},{6,5},{7,4},{8,11},{9,10},{10,... | collective-permute-start | bytes 3848 | tf_op jit(solution)/shard_map/ppermute | solution.py:153
  28.0 3.6 %collective-permute-start.30 = (f32[4,80]{1,0:T(4,128)S(1)}, f32[4,80]{1,0:T(4,128)S(1)}, u32[]{:S(2)}, u32[]{:S(2)}) collective-permute-start(f32[4,80]{1,0:T(4,128)S(1)} %get-tuple-element.720), channel_id=1, source_target_pairs={{0,2},{1,3},{2,0},{3,1},{4,6},{5,7},{6,4},{7,5},{8,10},{9,11},{10,... | collective-permute-start | bytes 3848 | tf_op jit(solution)/shard_map/ppermute | solution.py:153
  28.8 2.8 %collective-permute-start.31 = (f32[4,80]{1,0:T(4,128)S(1)}, f32[4,80]{1,0:T(4,128)S(1)}, u32[]{:S(2)}, u32[]{:S(2)}) collective-permute-start(f32[4,80]{1,0:T(4,128)S(1)} %get-tuple-element.721), channel_id=1, source_target_pairs={{0,1},{1,0},{2,3},{3,2},{4,5},{5,4},{6,7},{7,6},{8,9},{9,8},{10,11... | collective-permute-start | bytes 3848 | tf_op jit(solution)/shard_map/ppermute | solution.py:153
  31.7 6.4 %collective-permute-start.32 = (f32[16,80]{1,0:T(8,128)S(1)}, f32[16,80]{1,0:T(8,128)S(1)}, u32[]{:S(2)}, u32[]{:S(2)}) collective-permute-start(f32[16,80]{1,0:T(8,128)S(1)} %shard_map.95.refs_8_.refs_5_), channel_id=1, source_target_pairs={{0,28},{4,8},{8,4},{12,16},{16,12},{20,24},{24,20},{28,0},{1,29},{... | collective-permute-start | bytes 15368 | tf_op jit(solution)/shard_map/ppermute | solution.py:562
  34.3 3.8 %collective-permute-start.33 = (f32[16,80]{1,0:T(8,128)S(1)}, f32[16,80]{1,0:T(8,128)S(1)}, u32[]{:S(2)}, u32[]{:S(2)}) collective-permute-start(f32[16,80]{1,0:T(8,128)S(1)} %shard_map.95.refs_8_.refs_5_), channel_id=1, source_target_pairs={{0,3},{1,2},{2,1},{3,0},{4,7},{5,6},{6,5},{7,4},{8,11},{9,10},{10,... | collective-permute-start | bytes 15368 | tf_op jit(solution)/shard_map/ppermute | solution.py:565
  34.3 3.8 %collective-permute-start.34 = (f32[16,80]{1,0:T(8,128)S(1)}, f32[16,80]{1,0:T(8,128)S(1)}, u32[]{:S(2)}, u32[]{:S(2)}) collective-permute-start(f32[16,80]{1,0:T(8,128)S(1)} %shard_map.95.refs_8_.refs_5_), channel_id=1, source_target_pairs={{0,4},{4,0},{8,12},{12,8},{16,20},{20,16},{24,28},{28,24},{1,5},{5... | collective-permute-start | bytes 15368 | tf_op jit(solution)/shard_map/ppermute | solution.py:563
  34.3 3.8 %collective-permute-start.35 = (f32[16,80]{1,0:T(8,128)S(1)}, f32[16,80]{1,0:T(8,128)S(1)}, u32[]{:S(2)}, u32[]{:S(2)}) collective-permute-start(f32[16,80]{1,0:T(8,128)S(1)} %shard_map.95.refs_8_.refs_5_), channel_id=1, source_target_pairs={{0,1},{1,0},{2,3},{3,2},{4,5},{5,4},{6,7},{7,6},{8,9},{9,8},{10,11... | collective-permute-start | bytes 15368 | tf_op jit(solution)/shard_map/ppermute | solution.py:564
  39.2 3.5 %collective-permute-start.36 = (f32[4,80]{1,0:T(4,128)S(1)}, f32[4,80]{1,0:T(4,128)S(1)}, u32[]{:S(2)}, u32[]{:S(2)}) collective-permute-start(f32[4,80]{1,0:T(4,128)S(1)} %get-tuple-element.723), channel_id=1, source_target_pairs={{0,3},{1,2},{2,1},{3,0},{4,7},{5,6},{6,5},{7,4},{8,11},{9,10},{10,... | collective-permute-start | bytes 3848 | tf_op jit(solution)/shard_map/ppermute | solution.py:153
  39.8 3.6 %collective-permute-start.37 = (f32[4,80]{1,0:T(4,128)S(1)}, f32[4,80]{1,0:T(4,128)S(1)}, u32[]{:S(2)}, u32[]{:S(2)}) collective-permute-start(f32[4,80]{1,0:T(4,128)S(1)} %get-tuple-element.724), channel_id=1, source_target_pairs={{0,2},{1,3},{2,0},{3,1},{4,6},{5,7},{6,4},{7,5},{8,10},{9,11},{10,... | collective-permute-start | bytes 3848 | tf_op jit(solution)/shard_map/ppermute | solution.py:153
  41.0 2.5 %collective-permute-start.38 = (f32[4,80]{1,0:T(4,128)S(1)}, f32[4,80]{1,0:T(4,128)S(1)}, u32[]{:S(2)}, u32[]{:S(2)}) collective-permute-start(f32[4,80]{1,0:T(4,128)S(1)} %get-tuple-element.725), channel_id=1, source_target_pairs={{0,1},{1,0},{2,3},{3,2},{4,5},{5,4},{6,7},{7,6},{8,9},{9,8},{10,11... | collective-permute-start | bytes 3848 | tf_op jit(solution)/shard_map/ppermute | solution.py:153
  44.3 3.1 %collective-permute-start.39 = (f32[4,80]{1,0:T(4,128)S(1)}, f32[4,80]{1,0:T(4,128)S(1)}, u32[]{:S(2)}, u32[]{:S(2)}) collective-permute-start(f32[4,80]{1,0:T(4,128)S(1)} %get-tuple-element.731), channel_id=1, source_target_pairs={{0,3},{1,2},{2,1},{3,0},{4,7},{5,6},{6,5},{7,4},{8,11},{9,10},{10,... | collective-permute-start | bytes 3848 | tf_op jit(solution)/shard_map/ppermute | solution.py:153
  44.5 3.6 %collective-permute-start.40 = (f32[4,80]{1,0:T(4,128)S(1)}, f32[4,80]{1,0:T(4,128)S(1)}, u32[]{:S(2)}, u32[]{:S(2)}) collective-permute-start(f32[4,80]{1,0:T(4,128)S(1)} %get-tuple-element.732), channel_id=1, source_target_pairs={{0,2},{1,3},{2,0},{3,1},{4,6},{5,7},{6,4},{7,5},{8,10},{9,11},{10,... | collective-permute-start | bytes 3848 | tf_op jit(solution)/shard_map/ppermute | solution.py:153
  45.6 2.4 %collective-permute-start.41 = (f32[4,80]{1,0:T(4,128)S(1)}, f32[4,80]{1,0:T(4,128)S(1)}, u32[]{:S(2)}, u32[]{:S(2)}) collective-permute-start(f32[4,80]{1,0:T(4,128)S(1)} %get-tuple-element.733), channel_id=1, source_target_pairs={{0,1},{1,0},{2,3},{3,2},{4,5},{5,4},{6,7},{7,6},{8,9},{9,8},{10,11... | collective-permute-start | bytes 3848 | tf_op jit(solution)/shard_map/ppermute | solution.py:153
  48.2 6.4 %collective-permute-start.42 = (f32[16,80]{1,0:T(8,128)S(1)}, f32[16,80]{1,0:T(8,128)S(1)}, u32[]{:S(2)}, u32[]{:S(2)}) collective-permute-start(f32[16,80]{1,0:T(8,128)S(1)} %shard_map.99.refs_8_.refs_6_), channel_id=1, source_target_pairs={{0,28},{4,8},{8,4},{12,16},{16,12},{20,24},{24,20},{28,0},{1,29},{... | collective-permute-start | bytes 15368 | tf_op jit(solution)/shard_map/ppermute | solution.py:562
  50.9 3.6 %collective-permute-start.43 = (f32[16,80]{1,0:T(8,128)S(1)}, f32[16,80]{1,0:T(8,128)S(1)}, u32[]{:S(2)}, u32[]{:S(2)}) collective-permute-start(f32[16,80]{1,0:T(8,128)S(1)} %shard_map.99.refs_8_.refs_6_), channel_id=1, source_target_pairs={{0,3},{1,2},{2,1},{3,0},{4,7},{5,6},{6,5},{7,4},{8,11},{9,10},{10,... | collective-permute-start | bytes 15368 | tf_op jit(solution)/shard_map/ppermute | solution.py:565
  51.1 3.7 %collective-permute-start.44 = (f32[16,80]{1,0:T(8,128)S(1)}, f32[16,80]{1,0:T(8,128)S(1)}, u32[]{:S(2)}, u32[]{:S(2)}) collective-permute-start(f32[16,80]{1,0:T(8,128)S(1)} %shard_map.99.refs_8_.refs_6_), channel_id=1, source_target_pairs={{0,4},{4,0},{8,12},{12,8},{16,20},{20,16},{24,28},{28,24},{1,5},{5... | collective-permute-start | bytes 15368 | tf_op jit(solution)/shard_map/ppermute | solution.py:563
  51.1 3.7 %collective-permute-start.45 = (f32[16,80]{1,0:T(8,128)S(1)}, f32[16,80]{1,0:T(8,128)S(1)}, u32[]{:S(2)}, u32[]{:S(2)}) collective-permute-start(f32[16,80]{1,0:T(8,128)S(1)} %shard_map.99.refs_8_.refs_6_), channel_id=1, source_target_pairs={{0,1},{1,0},{2,3},{3,2},{4,5},{5,4},{6,7},{7,6},{8,9},{9,8},{10,11... | collective-permute-start | bytes 15368 | tf_op jit(solution)/shard_map/ppermute | solution.py:564
  (5 other events, 98.7 us)

commit v13 on v12

--- a/solution.py
+++ b/solution.py
@@ -366,7 +366,7 @@
 
 
 def late_kernel(nplane, last, *refs):
-    (slot, other, plane_other, pair, plane_pair, held, pick, seg, mine), refs = refs[:9], refs[9:]
+    (slot, other, pair, plane_pair, plane_other, held, pick, seg, mine), refs = refs[:9], refs[9:]
     faces = (mine, pair, plane_pair, other, plane_other)
     nold = ITERS if last else 1
     olds, refs = refs[:nold], refs[nold:]
@@ -575,7 +575,7 @@
         if step == 0:
             (held,) = call(hold_kernel, [blocks, mine], [blocks.shape], [pl.ANY] * 2, [pltpu.SemaphoreType.DMA])
         last = step == ITERS - 1
-        args = [line_slot, other, plane_other, pair, plane_pair, held, *picks, mine, *(us if last else us[-1:])]
+        args = [line_slot, other, pair, plane_pair, plane_other, held, *picks, mine, *(us if last else us[-1:])]
         out = call(
             functools.partial(late_kernel, nplane, last),
             args,

time: 67.6 us -> 67.6 us (level)
    ppermute x3, starting transfers between devices: 2.5 us -> 0.01 us  [on_device(): plane_pair = lax.ppermute(mine, 'plane', plane_pairs)]
    ppermute x3, starting transfers between devices: 0.14 us -> 2.49 us  [on_device(): plane_other = lax.ppermute(mine, 'plane', plane_others)]
  transfers between devices with their start and end apart: 30 -> 30, of which waited for: 12 -> 13; matrix products, arithmetic and copies ran while one was open for 0% -> 0% of each run, Pallas kernels for 14% -> 14%
where the time goes in v13:
time: 67.6 us; the launch traced here: 67.4 us
  starting transfers between devices  25.5 us (38%)
  Pallas kernels  17.5 us (26%)
  waiting for transfers between devices  12.9 us (19%)
  blocking collectives  10.2 us (15%)
  between operations  1.07 us (2%)
    pallas_call x15, Pallas kernels, call(): pl.pallas_call(kernel, out_shape=[pltpu.VMEM(shape, F32) if pinned else j...  15.9 us
    ppermute x18, starting transfers between devices, exchange(): lax.ppermute(x, axis, [(i, partner(i, k, size)[0]) for i in range(size)])  12.8 us
    all_to_all x1, blocking collectives, add_up(): lax.all_to_all(rows, ('span', 'plane'), split_axis=0, concat_axis=0, tile...  10.2 us
    ppermute x3, starting transfers between devices, on_device(): other = lax.ppermute(mine, 'span', span_others)  10.1 us
    ppermute x18, waiting for transfers between devices, exchange(): lax.ppermute(x, axis, [(i, partner(i, k, size)[0]) for i in range(size)])  6.68 us
    ppermute x3, waiting for transfers between devices, on_device(): other = lax.ppermute(mine, 'span', span_others)  5.36 us
    ppermute x3, starting transfers between devices, on_device(): plane_other = lax.ppermute(mine, 'plane', plane_others)  2.49 us
    pallas_call x1, Pallas kernels, on_device(): pl.pallas_call(functools.partial(pick_kernel, nspan, nplane, width), out_...  1.55 us
  transfers between devices with their start and end apart: 30, of which 13 were waited for; matrix products, arithmetic and copies ran while one was open for 0% of the time, Pallas kernels for 14%

profile of v13, /device:TPU:0, one launch (start us, length us, event | category | flops | bytes accessed | tf_op | source)
XLA Modules:
  0.0 67.4 jit_solution(5060145007471151193)
XLA Ops:
  0.6 0.8 %shard_map.86 = (f32[16,80]{1,0:T(8,128)S(1)}, f32[16,48]{1,0:T(8,128)S(1)}, f32[4,80]{1,0:T(4,128)S(1)}, f32[4,80]{1,0:T(4,128)S(1)}, f32[4,80]{1,0:T(4,128)S(1)}, /*index=5*/f32[4,80]{1,0:T(4,128)S(1)}) custom-call(s32[1,16]{1,0:T(1,128)} %refs_0_.5, f32[16,80]{1,0:T(8,128)} %bitcast.571), custom_call_target="tpu_custom_call" | custom-call | bytes 5184 | tf_op jit(solution)/shard_map/pallas_call | solution.py:465
  1.5 2.5 %collective-permute-start.16 = (f32[4,80]{1,0:T(4,128)S(1)}, f32[4,80]{1,0:T(4,128)S(1)}, u32[]{:S(2)}, u32[]{:S(2)}) collective-permute-start(f32[4,80]{1,0:T(4,128)S(1)} %get-tuple-element.695), channel_id=1, source_target_pairs={{0,3},{1,2},{2,1},{3,0},{4,7},{5,6},{6,5},{7,4},{8,11},{9,10},{10,... | collective-permute-start | bytes 3848 | tf_op jit(solution)/shard_map/ppermute | solution.py:153
  4.6 2.5 %shard_map.87 = (f32[1280,80]{1,0:T(8,128)S(1)}, f32[1280,80]{1,0:T(8,128)S(1)}, f32[1280,80]{1,0:T(8,128)S(1)}) custom-call(f32[16,6400]{1,0:T(8,128)} %low.5, f32[16,6400]{1,0:T(8,128)} %piv.5, f32[16,6400]{1,0:T(8,128)} %upp.1, f32[16,80]{1,0:T(8,128)S(1)} %get-tuple-element.699._.refs_9_.refs_0_), custom_call_target="tpu_custom_call" | custom-call | flops 8192000 | bytes 1233920 | tf_op jit(solution)/shard_map/pallas_call | solution.py:465
  7.5 0.9 %shard_map.88 = (f32[4,80]{1,0:T(4,128)S(1)}, f32[4,80]{1,0:T(4,128)S(1)}, f32[4,80]{1,0:T(4,128)S(1)}, f32[4,80]{1,0:T(4,128)S(1)}) custom-call(f32[4,80]{1,0:T(4,128)S(1)} %collective-permute-done.16.refs_0_, f32[4,80]{1,0:T(4,128)S(1)} %collective-permute-done.17.refs_1_, f32[4,80]{1,0:T(4,128)S(1)} %collective-permute-done.18.refs_2_, ...), custom_call_target="tpu_custom_call" | custom-call | flops 614400 | bytes 1233920 | tf_op jit(solution)/shard_map/pallas_call | solution.py:465
  8.5 1.2 %collective-permute-start.19 = (f32[4,80]{1,0:T(4,128)S(1)}, f32[4,80]{1,0:T(4,128)S(1)}, u32[]{:S(2)}, u32[]{:S(2)}) collective-permute-start(f32[4,80]{1,0:T(4,128)S(1)} %get-tuple-element.703), channel_id=1, source_target_pairs={{0,3},{1,2},{2,1},{3,0},{4,7},{5,6},{6,5},{7,4},{8,11},{9,10},{10,... | collective-permute-start | bytes 3848 | tf_op jit(solution)/shard_map/ppermute | solution.py:153
  10.4 1.6 %shard_map.89 = (bf16[176,240]{1,0:T(8,128)(2,1)S(1)}, bf16[640,128]{1,0:T(8,128)(2,1)S(1)}, f32[1280,80]{1,0:T(8,128)}) custom-call(s32[11,16]{1,0:T(8,128)} %columns_ref, f32[1280,80]{1,0:T(8,128)S(1)} %get-tuple-element.702.fold_ref), custom_call_target="tpu_custom_call" | custom-call | bytes 409600 | tf_op jit(solution)/shard_map/pallas_call | solution.py:541
  12.0 1.2 %collective-permute-done.20.refs_1_ = f32[4,80]{1,0:T(4,128)S(1)} collective-permute-done((f32[4,80]{1,0:T(4,128)S(1)}, f32[4,80]{1,0:T(4,128)S(1)}, u32[]{:S(2)}, u32[]{:S(2)}) %collective-permute-start.20) | collective-permute-done | bytes 1312 | tf_op jit(solution)/shard_map/ppermute | solution.py:153
  13.4 4.5 %collective-permute-start.22 = (f32[16,80]{1,0:T(8,128)S(1)}, f32[16,80]{1,0:T(8,128)S(1)}, u32[]{:S(2)}, u32[]{:S(2)}) collective-permute-start(f32[16,80]{1,0:T(8,128)S(1)} %shard_map.90._.refs_8_.refs_4_), channel_id=1, source_target_pairs={{0,28},{4,8},{8,4},{12,16},{16,12},{20,24},{24,20},{28,0},{1,29},{... | collective-permute-start | bytes 15368 | tf_op jit(solution)/shard_map/ppermute | solution.py:562
  17.9 0.8 %collective-permute-start.25 = (f32[16,80]{1,0:T(8,128)S(1)}, f32[16,80]{1,0:T(8,128)S(1)}, u32[]{:S(2)}, u32[]{:S(2)}) collective-permute-start(f32[16,80]{1,0:T(8,128)S(1)} %shard_map.90._.refs_8_.refs_4_), channel_id=1, source_target_pairs={{0,3},{1,2},{2,1},{3,0},{4,7},{5,6},{6,5},{7,4},{8,11},{9,10},{10,... | collective-permute-start | bytes 15368 | tf_op jit(solution)/shard_map/ppermute | solution.py:565
  18.7 2.3 %shard_map.91.refs_5_ = f32[16,70400]{1,0:T(8,128)S(1)} custom-call(f32[16,70400]{1,0:T(8,128)} %blocks.1, f32[16,80]{1,0:T(8,128)S(1)} %shard_map.90._.refs_8_.refs_4_), custom_call_target="tpu_custom_call" | custom-call | bytes 4510720 | tf_op jit(solution)/shard_map/pallas_call | solution.py:465
  21.6 1.1 %shard_map.92 = (f32[16,80]{1,0:T(8,128)S(1)}, f32[4,80]{1,0:T(4,128)S(1)}, f32[4,80]{1,0:T(4,128)S(1)}, f32[4,80]{1,0:T(4,128)S(1)}, f32[4,80]{1,0:T(4,128)S(1)}) custom-call(s32[1,16]{1,0:T(1,128)S(1)} %copy-done.8, f32[16,80]{1,0:T(8,128)S(1)} %collective-permute-done.22.refs_1_, f32[16,80]{1,0:T(8,128)S(1)} %collective-permute-done.23.refs_2_, ...), custom_call_target="tpu_custom_call" | custom-call | flops 2252800 | bytes 4784704 | tf_op jit(solution)/shard_map/pallas_call | solution.py:465
  23.1 1.3 %collective-permute-start.27 = (f32[4,80]{1,0:T(4,128)S(1)}, f32[4,80]{1,0:T(4,128)S(1)}, u32[]{:S(2)}, u32[]{:S(2)}) collective-permute-start(f32[4,80]{1,0:T(4,128)S(1)} %get-tuple-element.711), channel_id=1, source_target_pairs={{0,2},{1,3},{2,0},{3,1},{4,6},{5,7},{6,4},{7,5},{8,10},{9,11},{10,... | collective-permute-start | bytes 3848 | tf_op jit(solution)/shard_map/ppermute | solution.py:153
  24.6 1.5 %shard_map.93 = (f32[1280,80]{1,0:T(8,128)S(1)}, f32[1280,80]{1,0:T(8,128)S(1)}, f32[1280,80]{1,0:T(8,128)S(1)}) custom-call(f32[16,6400]{1,0:T(8,128)S(1)} %copy-done.1, f32[16,6400]{1,0:T(8,128)S(1)} %copy-done.2, f32[1280,80]{1,0:T(8,128)S(1)} %copy-done, f32[16,80]{1,0:T(8,128)S(1)} %get-tuple-element.715._.refs_9_.refs_10_.refs_1_), custom_call_target="tpu_custom_call" | custom-call | flops 102400 | bytes 1233920 | tf_op jit(solution)/shard_map/pallas_call | solution.py:465
  26.7 0.9 %shard_map.94 = (f32[4,80]{1,0:T(4,128)S(1)}, f32[4,80]{1,0:T(4,128)S(1)}, f32[4,80]{1,0:T(4,128)S(1)}, f32[4,80]{1,0:T(4,128)S(1)}) custom-call(f32[4,80]{1,0:T(4,128)S(1)} %collective-permute-done.26.refs_0_, f32[4,80]{1,0:T(4,128)S(1)} %collective-permute-done.27.refs_1_, f32[4,80]{1,0:T(4,128)S(1)} %collective-permute-done.28.refs_2_, ...), custom_call_target="tpu_custom_call" | custom-call | flops 614400 | bytes 1233920 | tf_op jit(solution)/shard_map/pallas_call | solution.py:465
  27.9 1.3 %collective-permute-start.30 = (f32[4,80]{1,0:T(4,128)S(1)}, f32[4,80]{1,0:T(4,128)S(1)}, u32[]{:S(2)}, u32[]{:S(2)}) collective-permute-start(f32[4,80]{1,0:T(4,128)S(1)} %get-tuple-element.720), channel_id=1, source_target_pairs={{0,2},{1,3},{2,0},{3,1},{4,6},{5,7},{6,4},{7,5},{8,10},{9,11},{10,... | collective-permute-start | bytes 3848 | tf_op jit(solution)/shard_map/ppermute | solution.py:153
  29.6 1.2 %collective-permute-done.29.refs_0_ = f32[4,80]{1,0:T(4,128)S(1)} collective-permute-done((f32[4,80]{1,0:T(4,128)S(1)}, f32[4,80]{1,0:T(4,128)S(1)}, u32[]{:S(2)}, u32[]{:S(2)}) %collective-permute-start.29) | collective-permute-done | bytes 1312 | tf_op jit(solution)/shard_map/ppermute | solution.py:153
  30.7 0.7 %collective-permute-done.30.refs_1_ = f32[4,80]{1,0:T(4,128)S(1)} collective-permute-done((f32[4,80]{1,0:T(4,128)S(1)}, f32[4,80]{1,0:T(4,128)S(1)}, u32[]{:S(2)}, u32[]{:S(2)}) %collective-permute-start.30) | collective-permute-done | bytes 1312 | tf_op jit(solution)/shard_map/ppermute | solution.py:153
  31.6 2.9 %collective-permute-start.32 = (f32[16,80]{1,0:T(8,128)S(1)}, f32[16,80]{1,0:T(8,128)S(1)}, u32[]{:S(2)}, u32[]{:S(2)}) collective-permute-start(f32[16,80]{1,0:T(8,128)S(1)} %shard_map.95.refs_8_.refs_5_), channel_id=1, source_target_pairs={{0,28},{4,8},{8,4},{12,16},{16,12},{20,24},{24,20},{28,0},{1,29},{... | collective-permute-start | bytes 15368 | tf_op jit(solution)/shard_map/ppermute | solution.py:562
  34.5 0.9 %collective-permute-start.35 = (f32[16,80]{1,0:T(8,128)S(1)}, f32[16,80]{1,0:T(8,128)S(1)}, u32[]{:S(2)}, u32[]{:S(2)}) collective-permute-start(f32[16,80]{1,0:T(8,128)S(1)} %shard_map.95.refs_8_.refs_5_), channel_id=1, source_target_pairs={{0,3},{1,2},{2,1},{3,0},{4,7},{5,6},{6,5},{7,4},{8,11},{9,10},{10,... | collective-permute-start | bytes 15368 | tf_op jit(solution)/shard_map/ppermute | solution.py:565
  35.4 2.6 %collective-permute-done.32.refs_1_ = f32[16,80]{1,0:T(8,128)S(1)} collective-permute-done((f32[16,80]{1,0:T(8,128)S(1)}, f32[16,80]{1,0:T(8,128)S(1)}, u32[]{:S(2)}, u32[]{:S(2)}) %collective-permute-start.32) | collective-permute-done | bytes 5152 | tf_op jit(solution)/shard_map/ppermute | solution.py:562
  38.1 1.1 %shard_map.96 = (f32[16,80]{1,0:T(8,128)S(1)}, f32[4,80]{1,0:T(4,128)S(1)}, f32[4,80]{1,0:T(4,128)S(1)}, f32[4,80]{1,0:T(4,128)S(1)}, f32[4,80]{1,0:T(4,128)S(1)}) custom-call(s32[1,16]{1,0:T(1,128)S(1)} %copy-done.8, f32[16,80]{1,0:T(8,128)S(1)} %collective-permute-done.32.refs_1_, f32[16,80]{1,0:T(8,128)S(1)} %collective-permute-done.33.refs_2_, ...), custom_call_target="tpu_custom_call" | custom-call | flops 2252800 | bytes 4784704 | tf_op jit(solution)/shard_map/pallas_call | solution.py:465
  39.9 1.2 %collective-permute-start.37 = (f32[4,80]{1,0:T(4,128)S(1)}, f32[4,80]{1,0:T(4,128)S(1)}, u32[]{:S(2)}, u32[]{:S(2)}) collective-permute-start(f32[4,80]{1,0:T(4,128)S(1)} %get-tuple-element.724), channel_id=1, source_target_pairs={{0,2},{1,3},{2,0},{3,1},{4,6},{5,7},{6,4},{7,5},{8,10},{9,11},{10,... | collective-permute-start | bytes 3848 | tf_op jit(solution)/shard_map/ppermute | solution.py:153
  41.2 1.5 %shard_map.97 = (f32[1280,80]{1,0:T(8,128)S(1)}, f32[1280,80]{1,0:T(8,128)S(1)}, f32[1280,80]{1,0:T(8,128)S(1)}) custom-call(f32[16,6400]{1,0:T(8,128)S(1)} %copy-done.1, f32[16,6400]{1,0:T(8,128)S(1)} %copy-done.2, f32[1280,80]{1,0:T(8,128)S(1)} %copy-done, f32[16,80]{1,0:T(8,128)S(1)} %get-tuple-element.727._.refs_11_.refs_2_), custom_call_target="tpu_custom_call" | custom-call | flops 102400 | bytes 1233920 | tf_op jit(solution)/shard_map/pallas_call | solution.py:465
  43.4 0.9 %shard_map.98 = (f32[4,80]{1,0:T(4,128)S(1)}, f32[4,80]{1,0:T(4,128)S(1)}, f32[4,80]{1,0:T(4,128)S(1)}, f32[4,80]{1,0:T(4,128)S(1)}) custom-call(f32[4,80]{1,0:T(4,128)S(1)} %collective-permute-done.36.refs_0_, f32[4,80]{1,0:T(4,128)S(1)} %collective-permute-done.37.refs_1_, f32[4,80]{1,0:T(4,128)S(1)} %collective-permute-done.38.refs_2_, ...), custom_call_target="tpu_custom_call" | custom-call | flops 614400 | bytes 1233920 | tf_op jit(solution)/shard_map/pallas_call | solution.py:465
  44.5 1.2 %collective-permute-start.40 = (f32[4,80]{1,0:T(4,128)S(1)}, f32[4,80]{1,0:T(4,128)S(1)}, u32[]{:S(2)}, u32[]{:S(2)}) collective-permute-start(f32[4,80]{1,0:T(4,128)S(1)} %get-tuple-element.732), channel_id=1, source_target_pairs={{0,2},{1,3},{2,0},{3,1},{4,6},{5,7},{6,4},{7,5},{8,10},{9,11},{10,... | collective-permute-start | bytes 3848 | tf_op jit(solution)/shard_map/ppermute | solution.py:153
  46.3 1.1 %collective-permute-done.39.refs_0_ = f32[4,80]{1,0:T(4,128)S(1)} collective-permute-done((f32[4,80]{1,0:T(4,128)S(1)}, f32[4,80]{1,0:T(4,128)S(1)}, u32[]{:S(2)}, u32[]{:S(2)}) %collective-permute-start.39) | collective-permute-done | bytes 1312 | tf_op jit(solution)/shard_map/ppermute | solution.py:153
  48.3 2.7 %collective-permute-start.42 = (f32[16,80]{1,0:T(8,128)S(1)}, f32[16,80]{1,0:T(8,128)S(1)}, u32[]{:S(2)}, u32[]{:S(2)}) collective-permute-start(f32[16,80]{1,0:T(8,128)S(1)} %shard_map.99.refs_8_.refs_6_), channel_id=1, source_target_pairs={{0,28},{4,8},{8,4},{12,16},{16,12},{20,24},{24,20},{28,0},{1,29},{... | collective-permute-start | bytes 15368 | tf_op jit(solution)/shard_map/ppermute | solution.py:562
  51.0 0.9 %collective-permute-start.45 = (f32[16,80]{1,0:T(8,128)S(1)}, f32[16,80]{1,0:T(8,128)S(1)}, u32[]{:S(2)}, u32[]{:S(2)}) collective-permute-start(f32[16,80]{1,0:T(8,128)S(1)} %shard_map.99.refs_8_.refs_6_), channel_id=1, source_target_pairs={{0,3},{1,2},{2,1},{3,0},{4,7},{5,6},{6,5},{7,4},{8,11},{9,10},{10,... | collective-permute-start | bytes 15368 | tf_op jit(solution)/shard_map/ppermute | solution.py:565
  51.9 2.7 %collective-permute-done.42.refs_1_ = f32[16,80]{1,0:T(8,128)S(1)} collective-permute-done((f32[16,80]{1,0:T(8,128)S(1)}, f32[16,80]{1,0:T(8,128)S(1)}, u32[]{:S(2)}, u32[]{:S(2)}) %collective-permute-start.42) | collective-permute-done | bytes 5152 | tf_op jit(solution)/shard_map/ppermute | solution.py:562
  54.7 1.1 %shard_map.100 = (f32[16,80]{1,0:T(8,128)S(1)}, f32[1,128]{1,0:T(1,128)S(1)}) custom-call(s32[1,16]{1,0:T(1,128)S(1)} %copy-done.8, f32[16,80]{1,0:T(8,128)S(1)} %collective-permute-done.42.refs_1_, f32[16,80]{1,0:T(8,128)S(1)} %collective-permute-done.43.refs_2_, f32[16,80]{1,0:T(8,128)S(1)} %collective-permute-done.44.refs_3_, ...), custom_call_target="tpu_custom_call" | custom-call | flops 2252800 | bytes 4794944 | tf_op jit(solution)/shard_map/pallas_call | solution.py:465
  55.9 10.2 %all_to_all.112 = f32[32,1,128]{2,1,0:T(1,128)S(1)} all-to-all(f32[32,1,128]{2,1,0:T(1,128)S(1)} %broadcast_in_dim.83), channel_id=1, replica_groups=mesh['span'=8,'plane'=4] {'span','plane'}, dimensions={0} | all-to-all | bytes 32768 | tf_op jit(solution)/shard_map/all_to_all | solution.py:479
  66.0 0.8 %shard_map.101 = (f32[16,80]{1,0:T(8,128)}, f32[16,80]{1,0:T(8,128)}, f32[1,128]{1,0:T(1,128)S(1)}) custom-call(f32[32,128]{1,0:T(8,128)S(1)} %bitcast.558, f32[16,80]{1,0:T(8,128)S(1)} %get-tuple-element.699._.refs_9_.refs_0_, f32[16,80]{1,0:T(8,128)S(1)} %get-tuple-element.715._.refs_9_.refs_10_.refs_1_, ...), custom_call_target="tpu_custom_call" | custom-call | bytes 52224 | tf_op jit(solution)/shard_map/pallas_call | solution.py:465
  (61 shorter events, 8.2 us)
Async XLA Ops:
  1.5 5.7 %collective-permute-start.16 = (f32[4,80]{1,0:T(4,128)S(1)}, f32[4,80]{1,0:T(4,128)S(1)}, u32[]{:S(2)}, u32[]{:S(2)}) collective-permute-start(f32[4,80]{1,0:T(4,128)S(1)} %get-tuple-element.695), channel_id=1, source_target_pairs={{0,3},{1,2},{2,1},{3,0},{4,7},{5,6},{6,5},{7,4},{8,11},{9,10},{10,... | collective-permute-start | bytes 3848 | tf_op jit(solution)/shard_map/ppermute | solution.py:153
  4.0 3.6 %collective-permute-start.17 = (f32[4,80]{1,0:T(4,128)S(1)}, f32[4,80]{1,0:T(4,128)S(1)}, u32[]{:S(2)}, u32[]{:S(2)}) collective-permute-start(f32[4,80]{1,0:T(4,128)S(1)} %get-tuple-element.696), channel_id=1, source_target_pairs={{0,2},{1,3},{2,0},{3,1},{4,6},{5,7},{6,4},{7,5},{8,10},{9,11},{10,... | collective-permute-start | bytes 3848 | tf_op jit(solution)/shard_map/ppermute | solution.py:153
  4.6 2.9 %collective-permute-start.18 = (f32[4,80]{1,0:T(4,128)S(1)}, f32[4,80]{1,0:T(4,128)S(1)}, u32[]{:S(2)}, u32[]{:S(2)}) collective-permute-start(f32[4,80]{1,0:T(4,128)S(1)} %get-tuple-element.697), channel_id=1, source_target_pairs={{0,1},{1,0},{2,3},{3,2},{4,5},{5,4},{6,7},{7,6},{8,9},{9,8},{10,11... | collective-permute-start | bytes 3848 | tf_op jit(solution)/shard_map/ppermute | solution.py:153
  8.5 3.5 %collective-permute-start.19 = (f32[4,80]{1,0:T(4,128)S(1)}, f32[4,80]{1,0:T(4,128)S(1)}, u32[]{:S(2)}, u32[]{:S(2)}) collective-permute-start(f32[4,80]{1,0:T(4,128)S(1)} %get-tuple-element.703), channel_id=1, source_target_pairs={{0,3},{1,2},{2,1},{3,0},{4,7},{5,6},{6,5},{7,4},{8,11},{9,10},{10,... | collective-permute-start | bytes 3848 | tf_op jit(solution)/shard_map/ppermute | solution.py:153
  9.6 3.6 %collective-permute-start.20 = (f32[4,80]{1,0:T(4,128)S(1)}, f32[4,80]{1,0:T(4,128)S(1)}, u32[]{:S(2)}, u32[]{:S(2)}) collective-permute-start(f32[4,80]{1,0:T(4,128)S(1)} %get-tuple-element.704), channel_id=1, source_target_pairs={{0,2},{1,3},{2,0},{3,1},{4,6},{5,7},{6,4},{7,5},{8,10},{9,11},{10,... | collective-permute-start | bytes 3848 | tf_op jit(solution)/shard_map/ppermute | solution.py:153
  10.3 2.9 %collective-permute-start.21 = (f32[4,80]{1,0:T(4,128)S(1)}, f32[4,80]{1,0:T(4,128)S(1)}, u32[]{:S(2)}, u32[]{:S(2)}) collective-permute-start(f32[4,80]{1,0:T(4,128)S(1)} %get-tuple-element.705), channel_id=1, source_target_pairs={{0,1},{1,0},{2,3},{3,2},{4,5},{5,4},{6,7},{7,6},{8,9},{9,8},{10,11... | collective-permute-start | bytes 3848 | tf_op jit(solution)/shard_map/ppermute | solution.py:153
  13.4 7.6 %collective-permute-start.22 = (f32[16,80]{1,0:T(8,128)S(1)}, f32[16,80]{1,0:T(8,128)S(1)}, u32[]{:S(2)}, u32[]{:S(2)}) collective-permute-start(f32[16,80]{1,0:T(8,128)S(1)} %shard_map.90._.refs_8_.refs_4_), channel_id=1, source_target_pairs={{0,28},{4,8},{8,4},{12,16},{16,12},{20,24},{24,20},{28,0},{1,29},{... | collective-permute-start | bytes 15368 | tf_op jit(solution)/shard_map/ppermute | solution.py:562
  17.9 3.7 %collective-permute-start.23 = (f32[16,80]{1,0:T(8,128)S(1)}, f32[16,80]{1,0:T(8,128)S(1)}, u32[]{:S(2)}, u32[]{:S(2)}) collective-permute-start(f32[16,80]{1,0:T(8,128)S(1)} %shard_map.90._.refs_8_.refs_4_), channel_id=1, source_target_pairs={{0,4},{4,0},{8,12},{12,8},{16,20},{20,16},{24,28},{28,24},{1,5},{5... | collective-permute-start | bytes 15368 | tf_op jit(solution)/shard_map/ppermute | solution.py:563
  17.9 3.7 %collective-permute-start.24 = (f32[16,80]{1,0:T(8,128)S(1)}, f32[16,80]{1,0:T(8,128)S(1)}, u32[]{:S(2)}, u32[]{:S(2)}) collective-permute-start(f32[16,80]{1,0:T(8,128)S(1)} %shard_map.90._.refs_8_.refs_4_), channel_id=1, source_target_pairs={{0,1},{1,0},{2,3},{3,2},{4,5},{5,4},{6,7},{7,6},{8,9},{9,8},{10,11... | collective-permute-start | bytes 15368 | tf_op jit(solution)/shard_map/ppermute | solution.py:564
  17.9 3.7 %collective-permute-start.25 = (f32[16,80]{1,0:T(8,128)S(1)}, f32[16,80]{1,0:T(8,128)S(1)}, u32[]{:S(2)}, u32[]{:S(2)}) collective-permute-start(f32[16,80]{1,0:T(8,128)S(1)} %shard_map.90._.refs_8_.refs_4_), channel_id=1, source_target_pairs={{0,3},{1,2},{2,1},{3,0},{4,7},{5,6},{6,5},{7,4},{8,11},{9,10},{10,... | collective-permute-start | bytes 15368 | tf_op jit(solution)/shard_map/ppermute | solution.py:565
  22.6 3.5 %collective-permute-start.26 = (f32[4,80]{1,0:T(4,128)S(1)}, f32[4,80]{1,0:T(4,128)S(1)}, u32[]{:S(2)}, u32[]{:S(2)}) collective-permute-start(f32[4,80]{1,0:T(4,128)S(1)} %get-tuple-element.710), channel_id=1, source_target_pairs={{0,3},{1,2},{2,1},{3,0},{4,7},{5,6},{6,5},{7,4},{8,11},{9,10},{10,... | collective-permute-start | bytes 3848 | tf_op jit(solution)/shard_map/ppermute | solution.py:153
  23.1 3.6 %collective-permute-start.27 = (f32[4,80]{1,0:T(4,128)S(1)}, f32[4,80]{1,0:T(4,128)S(1)}, u32[]{:S(2)}, u32[]{:S(2)}) collective-permute-start(f32[4,80]{1,0:T(4,128)S(1)} %get-tuple-element.711), channel_id=1, source_target_pairs={{0,2},{1,3},{2,0},{3,1},{4,6},{5,7},{6,4},{7,5},{8,10},{9,11},{10,... | collective-permute-start | bytes 3848 | tf_op jit(solution)/shard_map/ppermute | solution.py:153
  24.4 2.3 %collective-permute-start.28 = (f32[4,80]{1,0:T(4,128)S(1)}, f32[4,80]{1,0:T(4,128)S(1)}, u32[]{:S(2)}, u32[]{:S(2)}) collective-permute-start(f32[4,80]{1,0:T(4,128)S(1)} %get-tuple-element.712), channel_id=1, source_target_pairs={{0,1},{1,0},{2,3},{3,2},{4,5},{5,4},{6,7},{7,6},{8,9},{9,8},{10,11... | collective-permute-start | bytes 3848 | tf_op jit(solution)/shard_map/ppermute | solution.py:153
  26.7 40.2 %copy-start.5 = (f32[80,16]{0,1:T(8,128)S(1)}, f32[80,16]{0,1:T(8,128)}, u32[]{:S(2)}) copy-start(f32[80,16]{0,1:T(8,128)} %param.25) | copy-start | bytes 15364
  26.7 40.2 %copy-start.6 = (s32[11,16]{1,0:T(8,128)S(1)}, s32[11,16]{1,0:T(8,128)}, u32[]{:S(2)}) copy-start(s32[11,16]{1,0:T(8,128)} %columns_ref) | copy-start | bytes 2116
  27.7 3.1 %collective-permute-start.29 = (f32[4,80]{1,0:T(4,128)S(1)}, f32[4,80]{1,0:T(4,128)S(1)}, u32[]{:S(2)}, u32[]{:S(2)}) collective-permute-start(f32[4,80]{1,0:T(4,128)S(1)} %get-tuple-element.719), channel_id=1, source_target_pairs={{0,3},{1,2},{2,1},{3,0},{4,7},{5,6},{6,5},{7,4},{8,11},{9,10},{10,... | collective-permute-start | bytes 3848 | tf_op jit(solution)/shard_map/ppermute | solution.py:153
  27.9 3.6 %collective-permute-start.30 = (f32[4,80]{1,0:T(4,128)S(1)}, f32[4,80]{1,0:T(4,128)S(1)}, u32[]{:S(2)}, u32[]{:S(2)}) collective-permute-start(f32[4,80]{1,0:T(4,128)S(1)} %get-tuple-element.720), channel_id=1, source_target_pairs={{0,2},{1,3},{2,0},{3,1},{4,6},{5,7},{6,4},{7,5},{8,10},{9,11},{10,... | collective-permute-start | bytes 3848 | tf_op jit(solution)/shard_map/ppermute | solution.py:153
  29.2 2.3 %collective-permute-start.31 = (f32[4,80]{1,0:T(4,128)S(1)}, f32[4,80]{1,0:T(4,128)S(1)}, u32[]{:S(2)}, u32[]{:S(2)}) collective-permute-start(f32[4,80]{1,0:T(4,128)S(1)} %get-tuple-element.721), channel_id=1, source_target_pairs={{0,1},{1,0},{2,3},{3,2},{4,5},{5,4},{6,7},{7,6},{8,9},{9,8},{10,11... | collective-permute-start | bytes 3848 | tf_op jit(solution)/shard_map/ppermute | solution.py:153
  31.6 6.4 %collective-permute-start.32 = (f32[16,80]{1,0:T(8,128)S(1)}, f32[16,80]{1,0:T(8,128)S(1)}, u32[]{:S(2)}, u32[]{:S(2)}) collective-permute-start(f32[16,80]{1,0:T(8,128)S(1)} %shard_map.95.refs_8_.refs_5_), channel_id=1, source_target_pairs={{0,28},{4,8},{8,4},{12,16},{16,12},{20,24},{24,20},{28,0},{1,29},{... | collective-permute-start | bytes 15368 | tf_op jit(solution)/shard_map/ppermute | solution.py:562
  34.5 3.7 %collective-permute-start.33 = (f32[16,80]{1,0:T(8,128)S(1)}, f32[16,80]{1,0:T(8,128)S(1)}, u32[]{:S(2)}, u32[]{:S(2)}) collective-permute-start(f32[16,80]{1,0:T(8,128)S(1)} %shard_map.95.refs_8_.refs_5_), channel_id=1, source_target_pairs={{0,4},{4,0},{8,12},{12,8},{16,20},{20,16},{24,28},{28,24},{1,5},{5... | collective-permute-start | bytes 15368 | tf_op jit(solution)/shard_map/ppermute | solution.py:563
  34.5 3.7 %collective-permute-start.34 = (f32[16,80]{1,0:T(8,128)S(1)}, f32[16,80]{1,0:T(8,128)S(1)}, u32[]{:S(2)}, u32[]{:S(2)}) collective-permute-start(f32[16,80]{1,0:T(8,128)S(1)} %shard_map.95.refs_8_.refs_5_), channel_id=1, source_target_pairs={{0,1},{1,0},{2,3},{3,2},{4,5},{5,4},{6,7},{7,6},{8,9},{9,8},{10,11... | collective-permute-start | bytes 15368 | tf_op jit(solution)/shard_map/ppermute | solution.py:564
  34.5 3.7 %collective-permute-start.35 = (f32[16,80]{1,0:T(8,128)S(1)}, f32[16,80]{1,0:T(8,128)S(1)}, u32[]{:S(2)}, u32[]{:S(2)}) collective-permute-start(f32[16,80]{1,0:T(8,128)S(1)} %shard_map.95.refs_8_.refs_5_), channel_id=1, source_target_pairs={{0,3},{1,2},{2,1},{3,0},{4,7},{5,6},{6,5},{7,4},{8,11},{9,10},{10,... | collective-permute-start | bytes 15368 | tf_op jit(solution)/shard_map/ppermute | solution.py:565
  39.2 3.5 %collective-permute-start.36 = (f32[4,80]{1,0:T(4,128)S(1)}, f32[4,80]{1,0:T(4,128)S(1)}, u32[]{:S(2)}, u32[]{:S(2)}) collective-permute-start(f32[4,80]{1,0:T(4,128)S(1)} %get-tuple-element.723), channel_id=1, source_target_pairs={{0,3},{1,2},{2,1},{3,0},{4,7},{5,6},{6,5},{7,4},{8,11},{9,10},{10,... | collective-permute-start | bytes 3848 | tf_op jit(solution)/shard_map/ppermute | solution.py:153
  39.9 3.6 %collective-permute-start.37 = (f32[4,80]{1,0:T(4,128)S(1)}, f32[4,80]{1,0:T(4,128)S(1)}, u32[]{:S(2)}, u32[]{:S(2)}) collective-permute-start(f32[4,80]{1,0:T(4,128)S(1)} %get-tuple-element.724), channel_id=1, source_target_pairs={{0,2},{1,3},{2,0},{3,1},{4,6},{5,7},{6,4},{7,5},{8,10},{9,11},{10,... | collective-permute-start | bytes 3848 | tf_op jit(solution)/shard_map/ppermute | solution.py:153
  41.0 2.4 %collective-permute-start.38 = (f32[4,80]{1,0:T(4,128)S(1)}, f32[4,80]{1,0:T(4,128)S(1)}, u32[]{:S(2)}, u32[]{:S(2)}) collective-permute-start(f32[4,80]{1,0:T(4,128)S(1)} %get-tuple-element.725), channel_id=1, source_target_pairs={{0,1},{1,0},{2,3},{3,2},{4,5},{5,4},{6,7},{7,6},{8,9},{9,8},{10,11... | collective-permute-start | bytes 3848 | tf_op jit(solution)/shard_map/ppermute | solution.py:153
  44.4 3.1 %collective-permute-start.39 = (f32[4,80]{1,0:T(4,128)S(1)}, f32[4,80]{1,0:T(4,128)S(1)}, u32[]{:S(2)}, u32[]{:S(2)}) collective-permute-start(f32[4,80]{1,0:T(4,128)S(1)} %get-tuple-element.731), channel_id=1, source_target_pairs={{0,3},{1,2},{2,1},{3,0},{4,7},{5,6},{6,5},{7,4},{8,11},{9,10},{10,... | collective-permute-start | bytes 3848 | tf_op jit(solution)/shard_map/ppermute | solution.py:153
  44.5 3.6 %collective-permute-start.40 = (f32[4,80]{1,0:T(4,128)S(1)}, f32[4,80]{1,0:T(4,128)S(1)}, u32[]{:S(2)}, u32[]{:S(2)}) collective-permute-start(f32[4,80]{1,0:T(4,128)S(1)} %get-tuple-element.732), channel_id=1, source_target_pairs={{0,2},{1,3},{2,0},{3,1},{4,6},{5,7},{6,4},{7,5},{8,10},{9,11},{10,... | collective-permute-start | bytes 3848 | tf_op jit(solution)/shard_map/ppermute | solution.py:153
  45.7 2.4 %collective-permute-start.41 = (f32[4,80]{1,0:T(4,128)S(1)}, f32[4,80]{1,0:T(4,128)S(1)}, u32[]{:S(2)}, u32[]{:S(2)}) collective-permute-start(f32[4,80]{1,0:T(4,128)S(1)} %get-tuple-element.733), channel_id=1, source_target_pairs={{0,1},{1,0},{2,3},{3,2},{4,5},{5,4},{6,7},{7,6},{8,9},{9,8},{10,11... | collective-permute-start | bytes 3848 | tf_op jit(solution)/shard_map/ppermute | solution.py:153
  48.3 6.4 %collective-permute-start.42 = (f32[16,80]{1,0:T(8,128)S(1)}, f32[16,80]{1,0:T(8,128)S(1)}, u32[]{:S(2)}, u32[]{:S(2)}) collective-permute-start(f32[16,80]{1,0:T(8,128)S(1)} %shard_map.99.refs_8_.refs_6_), channel_id=1, source_target_pairs={{0,28},{4,8},{8,4},{12,16},{16,12},{20,24},{24,20},{28,0},{1,29},{... | collective-permute-start | bytes 15368 | tf_op jit(solution)/shard_map/ppermute | solution.py:562
  51.0 3.7 %collective-permute-start.43 = (f32[16,80]{1,0:T(8,128)S(1)}, f32[16,80]{1,0:T(8,128)S(1)}, u32[]{:S(2)}, u32[]{:S(2)}) collective-permute-start(f32[16,80]{1,0:T(8,128)S(1)} %shard_map.99.refs_8_.refs_6_), channel_id=1, source_target_pairs={{0,4},{4,0},{8,12},{12,8},{16,20},{20,16},{24,28},{28,24},{1,5},{5... | collective-permute-start | bytes 15368 | tf_op jit(solution)/shard_map/ppermute | solution.py:563
  51.0 3.7 %collective-permute-start.44 = (f32[16,80]{1,0:T(8,128)S(1)}, f32[16,80]{1,0:T(8,128)S(1)}, u32[]{:S(2)}, u32[]{:S(2)}) collective-permute-start(f32[16,80]{1,0:T(8,128)S(1)} %shard_map.99.refs_8_.refs_6_), channel_id=1, source_target_pairs={{0,1},{1,0},{2,3},{3,2},{4,5},{5,4},{6,7},{7,6},{8,9},{9,8},{10,11... | collective-permute-start | bytes 15368 | tf_op jit(solution)/shard_map/ppermute | solution.py:564
  51.0 3.7 %collective-permute-start.45 = (f32[16,80]{1,0:T(8,128)S(1)}, f32[16,80]{1,0:T(8,128)S(1)}, u32[]{:S(2)}, u32[]{:S(2)}) collective-permute-start(f32[16,80]{1,0:T(8,128)S(1)} %shard_map.99.refs_8_.refs_6_), channel_id=1, source_target_pairs={{0,3},{1,2},{2,1},{3,0},{4,7},{5,6},{6,5},{7,4},{8,11},{9,10},{10,... | collective-permute-start | bytes 15368 | tf_op jit(solution)/shard_map/ppermute | solution.py:565
  (5 other events, 99.0 us)
